TPU v7x, 32 devices: a whole 2x2x4 slice. The times are simulated.
32 devices in a mesh: tm: 8 (over z, y), state: 4 (over x, core).
Axes of the slice: x: 2, y: 2, z: 4, core: 2. Of those that a mesh axis runs over, the one named last changes fastest.
Arguments:
- filtered_covariance: float32 [32, 512, 512], P('tm', 'state'), may hold values from -1 to 2.5, as said below
- pred_prec: float32 [32, 512, 512], P('tm', 'state'), may hold values from -1 to 3, as said below
- transition: float32 [512, 512], P('state'), may hold values from -1 to 1.5
- filt_means: float32 [32, 512], P('tm'), may hold values from -6 to 6
- terminal_mean: float32 [512], replicated, may hold values from -6 to 6
Outputs:
- smoothed: float32 [32, 512], P('tm', 'state')
Inputs may be any that keep to these rules, and one draw needn't show every extreme that they name: `filtered_covariance`: each step's matrix is symmetric and positive definite. `pred_prec`: each step's matrix is symmetric and positive definite.
All inputs are finite; a program needn't handle non-finite values.
Results may differ from a plain program's by a relative error of at most 0.0003.
Values sent between devices are 32-bit elements; how exact they have to be, the bound alone decides.
No kernel may reach another device: no remote copies, remote signals or barrier semaphores. Data moves between devices by JAX's collectives and lax.ppermute only.
A program may use at most 128 MiB of HBM per device.

v0:
```python
import jax
import jax.numpy as jnp
from jax import lax
from jax.sharding import PartitionSpec as P

HIGHEST = lax.Precision.HIGHEST


def prefix(shard, axis, combine, identity):
    devices, index = (lax.axis_size(axis), lax.axis_index(axis))
    everything = jax.tree.map(lambda part: lax.all_gather(part, axis), shard)
    start = jax.tree.map(
        lambda part, zero: jnp.broadcast_to(jnp.asarray(zero, part.dtype), part.shape),
        shard,
        identity,
    )

    def step(k, before):
        at = devices - 1 - k
        reached = at > index
        new = combine(before, jax.tree.map(lambda part: part[at], everything))
        return jax.tree.map(lambda a, b: jnp.where(reached, a, b), new, before)

    return lax.fori_loop(0, devices, step, start)


def local(filtered_covariance, pred_prec, transition, filt_means, terminal_mean):
    step_count, panel_size, order_size = filtered_covariance.shape
    full_trans = lax.all_gather(transition, "state", axis=0, tiled=True)
    cov_trans = jnp.einsum("krj,ij->kri", filtered_covariance, full_trans, precision=HIGHEST)
    gains = jnp.einsum(
        "krc,kcj->krj",
        cov_trans,
        lax.all_gather(pred_prec, "state", axis=1, tiled=True),
        precision=HIGHEST,
    )
    first_row = lax.axis_index("state") * panel_size
    pred_means = jnp.dot(filt_means, full_trans.T, precision=HIGHEST)
    own_means = lax.dynamic_slice_in_dim(filt_means, first_row, panel_size, 1)
    offsets = own_means - jnp.einsum("krj,kj->kr", gains, pred_means, precision=HIGHEST)
    identity_matrix = jnp.eye(order_size, dtype=jnp.float32)
    zero_vector = jnp.zeros((order_size,), jnp.float32)

    def compose_rows(running, element):
        matrix, column_vector = running
        step_gain, offset = element
        new_rows = jnp.dot(step_gain, matrix, precision=HIGHEST)
        new_entries = jnp.dot(step_gain, column_vector, precision=HIGHEST) + offset
        return (
            (
                lax.all_gather(new_rows, "state", axis=0, tiled=True),
                lax.all_gather(new_entries, "state", axis=0, tiled=True),
            ),
            None,
        )

    (block_matrix, block_vector), _ = lax.scan(
        compose_rows, (identity_matrix, zero_vector), (gains, offsets), reverse=True
    )

    def combine(earlier, latter):
        return (
            jnp.dot(latter[0], earlier[0], precision=HIGHEST),
            jnp.dot(latter[0], earlier[1], precision=HIGHEST) + latter[1],
        )

    after_matrix, after_vector = prefix(
        (block_matrix, block_vector), "tm", combine, (identity_matrix, zero_vector)
    )
    incoming = jnp.dot(after_matrix, terminal_mean, precision=HIGHEST) + after_vector

    def backward_rows(state_mean, element):
        step_gain, offset = element
        local_portion = jnp.dot(step_gain, state_mean, precision=HIGHEST) + offset
        return (lax.all_gather(local_portion, "state", axis=0, tiled=True), local_portion)

    _, smoothed = lax.scan(backward_rows, incoming, (gains, offsets), reverse=True)
    return smoothed


def solution(mesh):
    return jax.shard_map(
        local,
        mesh=mesh,
        in_specs=(
            P("tm", "state", None),
            P("tm", "state", None),
            P("state", None),
            P("tm", None),
            P(),
        ),
        out_specs=P("tm", "state"),
        check_vma=False,
    )
```

profile of v0, /device:TPU:0, one launch (start us, length us, event | category | flops | bytes accessed | tf_op | source)
XLA Modules:
  0.0 351.0 jit_solution(12539354520768308768)
XLA Ops:
  9.2 19.2 %all-gather.14.cloned.1.call-done = f32[512,512]{1,0:T(8,128)} async-done(((f32[128,512]{1,0:T(8,128)}), f32[512,512]{1,0:T(8,128)}) %all-gather.14.cloned.1.call-update) | async-done | bytes 1048592 | tf_op jit(solution)/shard_map/all_gather | solution.py:29
  30.6 4.1 %fusion.21 = f32[4,128,512]{2,1,0:T(8,128)} fusion(f32[4,128,512]{2,1,0:T(8,128)S(1)} %copy-done, f32[512,512]{1,0:T(8,128)} %all-gather.14.cloned.1.call-done), kind=kOutput, calls=%fused_computation.29 | convolution fusion | flops 1610612736 | bytes 3145728 | tf_op jit(solution)/shard_map/krj,ij->kri/dot_general | solution.py:30
  34.7 29.8 %all-gather.16.cloned.1.call-done = f32[4,512,512]{2,1,0:T(8,128)} async-done(((f32[4,128,512]{2,1,0:T(8,128)}), f32[4,512,512]{2,1,0:T(8,128)}) %all-gather.16.cloned.1.call-update) | async-done | bytes 4194320 | tf_op jit(solution)/shard_map/all_gather | solution.py:34
  64.4 5.0 %fusion.26 = f32[4,128,512]{2,1,0:T(8,128)S(1)} fusion(f32[4,128,512]{2,1,0:T(8,128)} %fusion.21, f32[4,512,512]{2,1,0:T(8,128)} %all-gather.16.cloned.1.call-done), kind=kOutput, calls=%fused_computation.37 | convolution fusion | flops 1610612736 | bytes 6291456 | tf_op jit(solution)/shard_map/krc,kcj->krj/dot_general | solution.py:31
  71.1 78.1 %while.50 = (s32[]{:T(128)}, f32[512,512]{1,0:T(8,128)}, f32[512]{0:T(512)S(1)}, f32[4,128,512]{2,1,0:T(8,128)S(1)}, f32[4,128]{1,0:T(4,128)S(1)}, /*index=5*/s32[]{:T(128)}, s32[]{:T(128)}) while((s32[]{:T(128)}, f32[512,512]{1,0:T(8,128)}, f32[512]{0:T(512)S(1)}, f32[4,128,512]{2,1,0:T(8,128)S(1)}, f32[4,128]{1,0:T(4,128)S(1)}, ...), condition=%wide.region_1.2_spmd, body=%wide.region_0.1_spmd.sunk | while | flops 403439744 | bytes 5773957 | solution.py:57
  71.1 2.6 fusion.59
  74.0 5.1 %all-gather.7 = f32[4,1,128]{2,1,0:T(1,128)S(1)} all-gather(f32[1,1,128]{2,1,0:T(1,128)S(1)} %fusion.60), channel_id=1, replica_groups=mesh['tm'=8,'state'=4] {'state'}, dimensions={0}, use_global_device_ids=true | all-gather | bytes 2560 | tf_op jit(solution)/shard_map/while/body/eval_jaxpr/all_gather | solution.py:52
  79.1 11.5 %all-gather.20.cloned.1.call-done = f32[512,512]{1,0:T(8,128)} async-done(((f32[128,512]{1,0:T(8,128)}), f32[512,512]{1,0:T(8,128)}) %all-gather.20.cloned.1.call-update) | async-done | bytes 1048592 | tf_op jit(solution)/shard_map/while/body/eval_jaxpr/all_gather | solution.py:51
  90.6 2.6 fusion.59
  93.6 5.1 %all-gather.7 = f32[4,1,128]{2,1,0:T(1,128)S(1)} all-gather(f32[1,1,128]{2,1,0:T(1,128)S(1)} %fusion.60), channel_id=1, replica_groups=mesh['tm'=8,'state'=4] {'state'}, dimensions={0}, use_global_device_ids=true | all-gather | bytes 2560 | tf_op jit(solution)/shard_map/while/body/eval_jaxpr/all_gather | solution.py:52
  98.7 11.5 %all-gather.20.cloned.1.call-done = f32[512,512]{1,0:T(8,128)} async-done(((f32[128,512]{1,0:T(8,128)}), f32[512,512]{1,0:T(8,128)}) %all-gather.20.cloned.1.call-update) | async-done | bytes 1048592 | tf_op jit(solution)/shard_map/while/body/eval_jaxpr/all_gather | solution.py:51
  113.1 5.1 %all-gather.7 = f32[4,1,128]{2,1,0:T(1,128)S(1)} all-gather(f32[1,1,128]{2,1,0:T(1,128)S(1)} %fusion.60), channel_id=1, replica_groups=mesh['tm'=8,'state'=4] {'state'}, dimensions={0}, use_global_device_ids=true | all-gather | bytes 2560 | tf_op jit(solution)/shard_map/while/body/eval_jaxpr/all_gather | solution.py:52
  118.2 11.5 %all-gather.20.cloned.1.call-done = f32[512,512]{1,0:T(8,128)} async-done(((f32[128,512]{1,0:T(8,128)}), f32[512,512]{1,0:T(8,128)}) %all-gather.20.cloned.1.call-update) | async-done | bytes 1048592 | tf_op jit(solution)/shard_map/while/body/eval_jaxpr/all_gather | solution.py:51
  129.7 2.6 fusion.59
  132.6 5.1 %all-gather.7 = f32[4,1,128]{2,1,0:T(1,128)S(1)} all-gather(f32[1,1,128]{2,1,0:T(1,128)S(1)} %fusion.60), channel_id=1, replica_groups=mesh['tm'=8,'state'=4] {'state'}, dimensions={0}, use_global_device_ids=true | all-gather | bytes 2560 | tf_op jit(solution)/shard_map/while/body/eval_jaxpr/all_gather | solution.py:52
  137.7 11.5 %all-gather.20.cloned.1.call-done = f32[512,512]{1,0:T(8,128)} async-done(((f32[128,512]{1,0:T(8,128)}), f32[512,512]{1,0:T(8,128)}) %all-gather.20.cloned.1.call-update) | async-done | bytes 1048592 | tf_op jit(solution)/shard_map/while/body/eval_jaxpr/all_gather | solution.py:51
  150.0 26.6 %all-gather.4 = f32[8,1,512]{2,1,0:T(1,128)S(1)} all-gather(f32[1,1,512]{2,1,0:T(1,128)S(1)} %bitcast.123), channel_id=3, replica_groups=mesh['tm'=8,'state'=4] {'tm'}, dimensions={0}, use_global_device_ids=true | all-gather | bytes 18432 | tf_op jit(solution)/shard_map/all_gather | solution.py:11
  176.6 100.8 %all-gather.18.cloned.1.call-done = f32[4096,512]{1,0:T(8,128)} async-done(((f32[512,512]{1,0:T(8,128)}), f32[4096,512]{1,0:T(8,128)}) %all-gather.18.cloned.1.call-update) | async-done | bytes 8388624 | tf_op jit(solution)/shard_map/all_gather | solution.py:11
  277.4 43.5 %while.52 = (s32[]{:T(128)}, f32[512,512]{1,0:T(8,128)S(1)}, f32[512]{0:T(512)S(1)}, s32[]{:T(128)}, f32[8,512,512]{2,1,0:T(8,128)}, /*index=5*/f32[8,512]{1,0:T...) while((s32[]{:T(128)}, f32[512,512]{1,0:T(8,128)S(1)}, f32[512]{0:T(512)S(1)}, s32[]{:T(128)}, ...), condition=%wide.region_3.4_spmd.clone, body=%wide.region_2.3_spmd.clone.sunk | while | flops 1614022656 | bytes 7360693 | solution.py:24
  279.7 3.1 convolution_select_fusion.2
  285.2 3.1 convolution_select_fusion.2
  290.6 3.1 convolution_select_fusion.2
  296.1 3.1 convolution_select_fusion.2
  301.5 3.1 convolution_select_fusion.2
  307.0 3.1 convolution_select_fusion.2
  312.4 3.1 convolution_select_fusion.2
  317.8 3.1 convolution_select_fusion.2
  321.9 21.6 %while.51 = (s32[]{:T(128)}, f32[512]{0:T(512)S(1)}, f32[4,128]{1,0:T(4,128)S(1)}, f32[4,128,512]{2,1,0:T(8,128)S(1)}, f32[4,128]{1,0:T(4,128)S(1)}, /*index=5*/s32[]{:T(128)}, s32[]{:T(128)}, s32[]{:T(128)}) while((s32[]{:T(128)}, f32[512]{0:T(512)S(1)}, f32[4,128]{1,0:T(4,128)S(1)}, f32[4,128,512]{2,1,0:T(8,128)S(1)}, ...), condition=%wide.region_5.6_spmd, body=%wide.region_4.5_spmd.sunk | while | flops 786563 | bytes 269925 | solution.py:77
  322.3 5.0 %all-gather.8 = f32[4,1,128]{2,1,0:T(1,128)S(1)} all-gather(f32[1,1,128]{2,1,0:T(1,128)S(1)} %bitcast.120), channel_id=1, replica_groups=mesh['tm'=8,'state'=4] {'state'}, dimensions={0}, use_global_device_ids=true | all-gather | bytes 2560 | tf_op jit(solution)/shard_map/while/body/eval_jaxpr/all_gather | solution.py:75
  327.7 5.0 %all-gather.8 = f32[4,1,128]{2,1,0:T(1,128)S(1)} all-gather(f32[1,1,128]{2,1,0:T(1,128)S(1)} %bitcast.120), channel_id=1, replica_groups=mesh['tm'=8,'state'=4] {'state'}, dimensions={0}, use_global_device_ids=true | all-gather | bytes 2560 | tf_op jit(solution)/shard_map/while/body/eval_jaxpr/all_gather | solution.py:75
  333.1 5.0 %all-gather.8 = f32[4,1,128]{2,1,0:T(1,128)S(1)} all-gather(f32[1,1,128]{2,1,0:T(1,128)S(1)} %bitcast.120), channel_id=1, replica_groups=mesh['tm'=8,'state'=4] {'state'}, dimensions={0}, use_global_device_ids=true | all-gather | bytes 2560 | tf_op jit(solution)/shard_map/while/body/eval_jaxpr/all_gather | solution.py:75
  338.5 5.0 %all-gather.8 = f32[4,1,128]{2,1,0:T(1,128)S(1)} all-gather(f32[1,1,128]{2,1,0:T(1,128)S(1)} %bitcast.120), channel_id=1, replica_groups=mesh['tm'=8,'state'=4] {'state'}, dimensions={0}, use_global_device_ids=true | all-gather | bytes 2560 | tf_op jit(solution)/shard_map/while/body/eval_jaxpr/all_gather | solution.py:75
  (84 shorter events, 32.4 us)
Async XLA Ops:
  6.5 24.0 %copy-start = (f32[4,128,512]{2,1,0:T(8,128)S(1)}, f32[4,128,512]{2,1,0:T(8,128)}, u32[]{:S(2)}) copy-start(f32[4,128,512]{2,1,0:T(8,128)} %param.11) | copy-start | bytes 3145732
  6.5 21.8 %all-gather.14.cloned.1.call-start = ((), (), s32[]{:S(2)}) async-start(), calls=%async_computation | async-start | bytes 1310720 | tf_op jit(solution)/shard_map/all_gather | solution.py:29
  7.3 57.2 %all-gather.16.cloned.1.call-start = ((), (), s32[]{:S(2)}) async-start(), calls=%async_computation.1 | async-start | bytes 5242880 | tf_op jit(solution)/shard_map/all_gather | solution.py:34
  71.1 19.5 %all-gather.20.cloned.1.call-start = ((), (), s32[]{:S(2)}) async-start(), calls=%async_computation.3 | async-start | bytes 1310720 | tf_op jit(solution)/shard_map/while/body/eval_jaxpr/all_gather | solution.py:51
  90.6 19.5 %all-gather.20.cloned.1.call-start = ((), (), s32[]{:S(2)}) async-start(), calls=%async_computation.3 | async-start | bytes 1310720 | tf_op jit(solution)/shard_map/while/body/eval_jaxpr/all_gather | solution.py:51
  110.2 19.5 %all-gather.20.cloned.1.call-start = ((), (), s32[]{:S(2)}) async-start(), calls=%async_computation.3 | async-start | bytes 1310720 | tf_op jit(solution)/shard_map/while/body/eval_jaxpr/all_gather | solution.py:51
  129.7 19.5 %all-gather.20.cloned.1.call-start = ((), (), s32[]{:S(2)}) async-start(), calls=%async_computation.3 | async-start | bytes 1310720 | tf_op jit(solution)/shard_map/while/body/eval_jaxpr/all_gather | solution.py:51
  149.3 128.2 %all-gather.18.cloned.1.call-start = ((), (), s32[]{:S(2)}) async-start(), calls=%async_computation.2 | async-start | bytes 9437184 | tf_op jit(solution)/shard_map/all_gather | solution.py:11
  277.4 43.5 %copy-start.1 = (f32[512]{0:T(512)S(1)}, f32[512]{0:T(512)}, u32[]{:S(2)}) copy-start(f32[512]{0:T(512)} %param.15) | copy-start | bytes 6148
  343.5 0.6 copy-start.2
Sparse Core Ops, SparseCore 0:
  8.9 19.4 all-gather.13
  29.9 34.4 all-gather.15
  73.9 16.7 all-gather.19
  93.4 16.7 all-gather.19
  113.0 16.7 all-gather.19
  132.5 16.7 all-gather.19
  152.2 125.1 all-gather.17
where the time goes:
time: 352 us; the launch traced here: 351 us
  waiting for transfers between devices  198 us (56%)
  matrix products  67.9 us (19%)
  blocking collectives  67.2 us (19%)
  between operations  13.5 us (4%)
    all_gather x1, waiting for transfers between devices, prefix(): everything = jax.tree.map(lambda part: lax.all_gather(part, axis), shard)  101 us
    all_gather x4, waiting for transfers between devices, compose_rows(): lax.all_gather(new_rows, 'state', axis=0, tiled=True)  46.1 us
    all_gather x1, waiting for transfers between devices, local(): lax.all_gather(pred_prec, 'state', axis=1, tiled=True)  29.8 us
    all_gather x1, blocking collectives, prefix(): everything = jax.tree.map(lambda part: lax.all_gather(part, axis), shard)  26.6 us
    dot_general x8, matrix products, combine(): jnp.dot(latter[0], earlier[0], precision=HIGHEST)  24.6 us
    all_gather x4, blocking collectives, compose_rows(): lax.all_gather(new_entries, 'state', axis=0, tiled=True)  20.4 us
    all_gather x4, blocking collectives, backward_rows(): lax.all_gather(local_portion, 'state', axis=0, tiled=True)  20.2 us
    all_gather x1, waiting for transfers between devices, local(): full_trans = lax.all_gather(transition, 'state', axis=0, tiled=True)  19.2 us
  transfers between devices with their start and end apart: 7, of which 7 were waited for; matrix products, arithmetic and copies ran while one was open for 2% of the time, Pallas kernels for 0%

commit v1 on v0

v1 whole, which is shorter than its diff:
```python
import functools

import jax
import jax.numpy as jnp
from jax import lax
from jax.experimental import pallas as pl
from jax.experimental.pallas import tpu as pltpu
from jax.sharding import PartitionSpec as P

F32, BF16 = jnp.float32, jnp.bfloat16
NN = (((1,), (0,)), ((), ()))
NT = (((1,), (1,)), ((), ()))
ANY = pl.BlockSpec(memory_space=pl.ANY)
VMEM = pl.BlockSpec(memory_space=pltpu.VMEM)
LIMIT = 40 * 1024 * 1024


def split(x):
    high = x.astype(BF16)
    return high, (x - high.astype(F32)).astype(BF16)


def dot3(a, b, dims):
    (ah, al), (bh, bl) = split(a), split(b)
    dot = functools.partial(lax.dot_general, dimension_numbers=dims, preferred_element_type=F32)
    return dot(ah, bh) + (dot(ah, bl) + dot(al, bh))


def matvec(matrix, row):
    order = matrix.shape[1]
    total = matrix[:, :128] * row[:, :128]
    for j in range(128, order, 128):
        total += matrix[:, j : j + 128] * row[:, j : j + 128]
    return jnp.sum(total.T, axis=0, keepdims=True)


def gain_kernel(devices, repeat, *refs):
    half = devices // 2
    cov, prec, means, trans = refs[:4]
    arrived = refs[4 : 4 + devices - 1]
    gain, pred, pf, lf, af, sems = refs[4 + devices - 1 :]
    panel, order = cov.shape[1:]
    wide = order // 2
    s = lax.axis_index("state")
    side = s // half
    step = s // repeat

    copies = []

    def start(source, target):
        copy = pltpu.make_async_copy(source, target, sems.at[len(copies)])
        copy.start()
        copies.append(copy)

    def rows(i):
        return pl.ds(pl.multiple_of(i * panel, panel), panel)

    other = pl.multiple_of((1 - side) * wide, wide)
    own = pl.multiple_of(side * wide, wide)
    start(trans, af)
    start(cov.at[step], pf.at[rows(s), :])
    start(prec.at[step], lf.at[rows(s), :])
    for off in range(1, devices):
        i = s ^ off
        for which, full in enumerate((pf, lf)):
            place = full.at[rows(i), :] if off < half else full.at[rows(i), pl.ds(other, wide)]
            start(arrived[off - 1].at[which], place)
    steps = means.shape[0]
    pf[order:, :] = jnp.concatenate([means[...], jnp.zeros((16 - steps, order), F32)], axis=0)
    for copy in copies:
        copy.wait()
    for full in (pf, lf):
        full[pl.ds(other, wide), pl.ds(own, wide)] = full[pl.ds(own, wide), pl.ds(other, wide)].T
    cov_trans = dot3(pf[...], af[...], NT)
    pred[...] = cov_trans[order : order + 8]
    gain[...] = dot3(cov_trans[:order], lf[...], NN)


def pair_kernel(repeat, own, partner, means, pred, c_ref, late_ref, vec_ref, slots, sems):
    step = lax.axis_index("state") // repeat
    bit = step % 2
    first = pltpu.make_async_copy(own, slots.at[bit], sems.at[0])
    second = pltpu.make_async_copy(partner, slots.at[1 - bit], sems.at[1])
    first.start()
    second.start()
    a = step - bit
    mean_a, mean_b = means[pl.ds(a, 1), :], means[pl.ds(a + 1, 1), :]
    pred_a, pred_b = pred[pl.ds(a, 1), :], pred[pl.ds(a + 1, 1), :]
    first.wait()
    second.wait()
    ga, gb = slots[0], slots[1]
    vec_ref[...] = jnp.concatenate(
        [mean_a + matvec(ga, mean_b - pred_a), mean_b, pred_b, jnp.zeros((5, ga.shape[1]), F32)], axis=0
    )
    c_ref[...] = dot3(ga, gb, NN)
    late_ref[...] = gb


def hop_kernel(x_ref, c_ref, vec_ref, out_ref):
    vec = vec_ref[...]
    out_ref[...] = vec[0:1] + matvec(c_ref[...], x_ref[...] - vec[2:3])


def last_kernel(x_ref, c_ref, late_ref, vec_ref, out_ref):
    vec = vec_ref[...]
    gap = x_ref[...] - vec[2:3]
    out_ref[0:1, :] = vec[0:1] + matvec(c_ref[...], gap)
    out_ref[1:2, :] = vec[1:2] + matvec(late_ref[...], gap)


def params():
    return pltpu.CompilerParams(vmem_limit_bytes=LIMIT)


def local(filtered_covariance, pred_prec, transition, filt_means, terminal_mean):
    steps, panel, order = filtered_covariance.shape
    devices, blocks = lax.axis_size("state"), lax.axis_size("tm")
    repeat, half, wide = devices // steps, devices // 2, order // 2
    s, b = lax.axis_index("state"), lax.axis_index("tm")
    side = s // half

    def swap(x, off):
        return lax.ppermute(x, "state", [(i, i ^ off) for i in range(devices)])

    across = swap(transition, half)
    both = jnp.stack([transition, across])
    parts = [both] + [swap(both, off) for off in range(1, half)]
    parts = jnp.concatenate(parts, axis=0).reshape(half, 2, panel, order)
    full = jnp.zeros((devices, panel, order), F32)
    for o in range(half):
        for h in range(2):
            full = lax.dynamic_update_slice_in_dim(full, parts[o, h][None], s ^ o ^ (h * half), 0)
    trans = full.reshape(order, order)

    arrived = []
    for off in range(1, devices):
        target = (s ^ off) // repeat
        piece = [lax.dynamic_index_in_dim(m, target, 0, False) for m in (filtered_covariance, pred_prec)]
        if off >= half:
            piece = [lax.dynamic_slice_in_dim(m, side * wide, wide, 1) for m in piece]
        arrived.append(swap(jnp.stack(piece), off))

    count = 3 + 2 * (devices - 1)
    gain, pred = pl.pallas_call(
        functools.partial(gain_kernel, devices, repeat),
        out_shape=(jax.ShapeDtypeStruct((order, order), F32), jax.ShapeDtypeStruct((8, order), F32)),
        in_specs=[ANY, ANY, VMEM, ANY] + [ANY] * (devices - 1),
        out_specs=(VMEM, VMEM),
        scratch_shapes=[
            pltpu.VMEM((order + 16, order), F32),
            pltpu.VMEM((order, order), F32),
            pltpu.VMEM((order, order), F32),
            pltpu.SemaphoreType.DMA((count,)),
        ],
        compiler_params=params(),
        name="gain",
    )(filtered_covariance, pred_prec, filt_means, trans, *arrived)

    partner = swap(gain, repeat)
    c, late, vec = pl.pallas_call(
        functools.partial(pair_kernel, repeat),
        out_shape=(
            jax.ShapeDtypeStruct((order, order), F32),
            jax.ShapeDtypeStruct((order, order), F32),
            jax.ShapeDtypeStruct((8, order), F32),
        ),
        in_specs=[ANY, ANY, VMEM, VMEM],
        out_specs=(VMEM, VMEM, VMEM),
        scratch_shapes=[pltpu.VMEM((2, order, order), F32), pltpu.SemaphoreType.DMA((2,))],
        compiler_params=params(),
        name="pair",
    )(gain, partner, filt_means, pred)

    hop = pl.pallas_call(
        hop_kernel,
        out_shape=jax.ShapeDtypeStruct((1, order), F32),
        in_specs=[VMEM] * 3,
        out_specs=VMEM,
        compiler_params=params(),
        name="hop",
    )

    def flat(tm, state):
        return tm * devices + state

    lower, upper = range(half), range(half, devices)
    start = jnp.where((b == blocks - 1) & (side == 1), terminal_mean, 0.0)[None]
    incoming, total = start, start
    for tm in range(blocks - 1, -1, -1):
        for to, members in ((tm, upper), (tm - 1, lower)):
            if to < 0:
                break
            pairs = [(flat(tm, i), flat(to, i ^ half)) for i in members]
            incoming = lax.ppermute(hop(incoming, c, vec), ("tm", "state"), pairs)
            total = total + incoming

    both = pl.pallas_call(
        last_kernel,
        out_shape=jax.ShapeDtypeStruct((2, order), F32),
        in_specs=[VMEM] * 4,
        out_specs=VMEM,
        compiler_params=params(),
        name="last",
    )(total, c, late, vec)
    theirs = swap(lax.dynamic_slice_in_dim(both, (s ^ half) * panel, panel, 1), half)
    mine = lax.dynamic_slice_in_dim(both, s * panel, panel, 1)
    return jnp.where(
        side == 0, jnp.concatenate([mine, theirs], axis=0), jnp.concatenate([theirs, mine], axis=0)
    )


def solution(mesh):
    return jax.shard_map(
        local,
        mesh=mesh,
        in_specs=(
            P("tm", "state", None),
            P("tm", "state", None),
            P("state", None),
            P("tm", None),
            P(),
        ),
        out_specs=P("tm", "state"),
        check_vma=False,
    )
```

time: 352 us -> 113 us (0.32)
  waiting for transfers between devices: 198 us -> 76.1 us
  matrix products: 67.9 us -> 0 us
  blocking collectives: 67.2 us -> 0 us
  starting transfers between devices: 0.05 us -> 16.1 us
  between operations: 13.5 us -> 0.44 us
  Pallas kernels: 0 us -> 6.03 us
  local copies, waits for them, and re-layouts: 2.76 us -> 7.96 us
  other arithmetic: 0.96 us -> 5.98 us
    all_gather x7 -> x0, waiting for transfers between devices: 196 us -> none  [the longest x1 101 us: prefix(): everything = jax.tree.map(lambda part: lax.all_gather(part, axis), shard)]
    ppermute x0 -> x22, waiting for transfers between devices: none -> 76.1 us  [the longest x15 55.6 us: local(): incoming = lax.ppermute(hop(incoming, c, vec), ('tm', 'state'), pairs)]
    dot_general x33 -> x0, matrix products: 67.9 us -> none  [the longest x8 24.6 us: combine(): jnp.dot(latter[0], earlier[0], precision=HIGHEST)]
    all_gather x9 -> x0, blocking collectives: 67.2 us -> none  [the longest x1 26.6 us: prefix(): everything = jax.tree.map(lambda part: lax.all_gather(part, axis), shard)]
    ppermute x0 -> x22, starting transfers between devices: none -> 16.1 us  [the longest x15 10.6 us: local(): incoming = lax.ppermute(hop(incoming, c, vec), ('tm', 'state'), pairs)]
    pallas_call x0 -> x18, Pallas kernels: none -> 6.03 us  [the longest x15 2.36 us: local(): incoming = lax.ppermute(hop(incoming, c, vec), ('tm', 'state'), pairs)]
    unnamed x8 -> x20, local copies, waits for them, and re-layouts: 1.64 us -> 6.38 us
    another operation x0 -> x4, other arithmetic: none -> 4.11 us  [the longest x3 2.26 us: local(): arrived.append(swap(jnp.stack(piece), off))]
  transfers between devices with their start and end apart: 7 -> 22, of which waited for: 7 -> 6; matrix products, arithmetic and copies ran while one was open for 2% -> 5% of each run, Pallas kernels for 0% -> 0%
where the time goes in v1:
time: 113 us
  waiting for transfers between devices  76.1 us (67%)
  starting transfers between devices  16.1 us (14%)
  local copies, waits for them, and re-layouts  7.96 us (7%)
  Pallas kernels  6.03 us (5%)
  other arithmetic  5.98 us (5%)
    ppermute x15, waiting for transfers between devices, local(): incoming = lax.ppermute(hop(incoming, c, vec), ('tm', 'state'), pairs)  55.6 us
    ppermute x7, waiting for transfers between devices, swap(): return lax.ppermute(x, 'state', [(i, i ^ off) for i in range(devices)])  20.6 us
    ppermute x15, starting transfers between devices, local(): incoming = lax.ppermute(hop(incoming, c, vec), ('tm', 'state'), pairs)  10.6 us
    unnamed x20, local copies, waits for them, and re-layouts  6.38 us
    ppermute x7, starting transfers between devices, swap(): return lax.ppermute(x, 'state', [(i, i ^ off) for i in range(devices)])  5.51 us
    pallas_call x15, Pallas kernels, local(): incoming = lax.ppermute(hop(incoming, c, vec), ('tm', 'state'), pairs)  2.36 us
    another operation x3, other arithmetic, local(): arrived.append(swap(jnp.stack(piece), off))  2.26 us
  transfers between devices with their start and end apart: 22, of which 6 were waited for; matrix products, arithmetic and copies ran while one was open for 5% of the time, Pallas kernels for 0%

profile of v1, /device:TPU:0, one launch (start us, length us, event | category | flops | bytes accessed | tf_op | source)
XLA Modules:
  0.0 112.6 jit_solution(6590243072254732986)
XLA Ops:
  0.0 2.9 %collective-permute-start = (f32[128,512]{1,0:T(8,128)}, f32[128,512]{1,0:T(8,128)}, u32[]{:S(2)}, u32[]{:S(2)}) collective-permute-start(f32[128,512]{1,0:T(8,128)} %param.7), channel_id=1, source_target_pairs={{0,2},{1,3},{2,0},{3,1},{4,6},{5,7},{6,4},{7,5},{8,10},{9,11},{10,... | collective-permute-start | bytes 786440 | tf_op jit(solution)/shard_map/ppermute | solution.py:123
  2.9 6.6 %collective-permute-done = f32[128,512]{1,0:T(8,128)} collective-permute-done((f32[128,512]{1,0:T(8,128)}, f32[128,512]{1,0:T(8,128)}, u32[]{:S(2)}, u32[]{:S(2)}) %collective-permute-start) | collective-permute-done | bytes 262176 | tf_op jit(solution)/shard_map/ppermute | solution.py:123
  9.6 1.8 %pad_maximum_fusion.1 = f32[2,128,512]{2,1,0:T(8,128)} fusion(f32[1,128,512]{2,1,0:T(8,128)} %bitcast.2, f32[1,128,512]{2,1,0:T(8,128)} %bitcast.28), kind=kLoop, calls=%fused_computation.1 | loop fusion | flops 131072 | bytes 1048576 | tf_op jit(solution)/shard_map/stack | solution.py:126
  11.4 1.3 %constant_dynamic-slice_fusion.2 = (f32[1,128,256]{2,1,0:T(8,128)S(1)}, f32[1,128,256]{2,1,0:T(8,128)S(1)}, f32[1,128,256]{2,1,0:T(8,128)S(1)}, f32[1,128,256]{2,1,0:T(8,128)S(1)}) fusion(f32[4,128,512]{2,1,0:T(8,128)} %refs_1_.1, s32[]{:T(128)S(6)} %select_n.75, s32[]{:T(128)S(6)} %select_n.73, s32[]{:T(128)S(6)} %select_n.71, f32[4,128,512]{2,1,0:T(8,128)S(1)} %copy-done), kind=kLoop, calls=%fused_computation.15 | loop fusion | bytes 1048588 | tf_op jit(solution)/shard_map/dynamic_slice | solution.py:140
  12.7 0.7 pad_maximum_fusion.3
  13.5 1.7 %collective-permute-start.3 = (f32[2,128,256]{2,1,0:T(8,128)}, f32[2,128,256]{2,1,0:T(8,128)S(1)}, u32[]{:S(2)}, u32[]{:S(2)}) collective-permute-start(f32[2,128,256]{2,1,0:T(8,128)} %pad_maximum_fusion.3), channel_id=1, source_target_pairs={{0,2},{1,3},{2,0},{3,1},{4,6},{5,7},{6,4},{7,5},{8,10},{9,11},{10,... | collective-permute-start | bytes 786440 | tf_op jit(solution)/shard_map/ppermute | solution.py:123
  15.1 0.7 pad_maximum_fusion.4
  16.0 0.8 pad_maximum_fusion.2
  17.2 1.3 %pad_maximum_fusion = f32[4,128,512]{2,1,0:T(8,128)S(1)} fusion(f32[2,128,512]{2,1,0:T(8,128)} %collective-permute-done.1, f32[1,128,512]{2,1,0:T(8,128)} %bitcast.2, f32[1,128,512]{2,1,0:T(8,128)} %bitcast.29), kind=kLoop, calls=%fused_computation | loop fusion | flops 524288 | bytes 2097152 | tf_op jit(solution)/shard_map/concatenate | solution.py:128
  18.7 4.1 %collective-permute-done.3.refs_5_ = f32[2,128,256]{2,1,0:T(8,128)S(1)} collective-permute-done((f32[2,128,256]{2,1,0:T(8,128)}, f32[2,128,256]{2,1,0:T(8,128)S(1)}, u32[]{:S(2)}, u32[]{:S(2)}) %collective-permute-start.3) | collective-permute-done | bytes 262176 | tf_op jit(solution)/shard_map/ppermute | solution.py:123
  22.8 4.7 %collective-permute-done.4.refs_6_ = f32[2,128,256]{2,1,0:T(8,128)S(1)} collective-permute-done((f32[2,128,256]{2,1,0:T(8,128)}, f32[2,128,256]{2,1,0:T(8,128)S(1)}, u32[]{:S(2)}, u32[]{:S(2)}) %collective-permute-start.4) | collective-permute-done | bytes 262176 | tf_op jit(solution)/shard_map/ppermute | solution.py:123
  27.4 0.7 copy-done.6
  28.1 0.8 copy-done.4
  28.9 1.0 copy-done.5
  30.0 0.9 copy-done.7
  30.9 2.2 %gain.1 = (f32[512,512]{1,0:T(8,128)S(1)}, f32[8,512]{1,0:T(8,128)S(1)}) custom-call(f32[4,128,512]{2,1,0:T(8,128)S(1)} %copy-done, f32[4,128,512]{2,1,0:T(8,128)S(1)} %copy-done.1, f32[4,512]{1,0:T(4,128)S(1)} %copy-done.8, f32[512,512]{1,0:T(8,128)S(1)} %bitcast.21, f32[2,128,512]{2,1,0:T(8,128)S(1)} %copy-done.5, ...), custom_call_target="tpu_custom_call" | custom-call | tf_op jit(solution)/shard_map/gain/pallas_call | solution.py:144
  33.6 0.7 copy-done.9
  34.2 1.7 %collective-permute-done.5.partner = f32[512,512]{1,0:T(8,128)S(1)} collective-permute-done((f32[512,512]{1,0:T(8,128)S(1)}, f32[512,512]{1,0:T(8,128)S(1)}, u32[]{:S(2)}, u32[]{:S(2)}) %collective-permute-start.5) | collective-permute-done | bytes 1048608 | tf_op jit(solution)/shard_map/ppermute | solution.py:123
  35.9 1.0 copy-done.2
  36.9 1.2 %copy-done.3 = f32[512,512]{1,0:T(8,128)S(1)} copy-done((f32[512,512]{1,0:T(8,128)S(1)}, f32[512,512]{1,0:T(8,128)}, u32[]{:S(2)}) %copy-start.3) | copy-done | bytes 1048600
  38.1 1.2 %pair.1 = (f32[512,512]{1,0:T(8,128)S(1)}, f32[512,512]{1,0:T(8,128)S(1)}, f32[8,512]{1,0:T(8,128)S(1)}) custom-call(f32[512,512]{1,0:T(8,128)S(1)} %get-tuple-element.10.own, f32[512,512]{1,0:T(8,128)S(1)} %copy-done.3, f32[4,512]{1,0:T(4,128)S(1)} %copy-done.8, f32[8,512]{1,0:T(8,128)S(1)} %get-tuple-element.11.pred), custom_call_target="tpu_custom_call" | custom-call | tf_op jit(solution)/shard_map/pair/pallas_call | solution.py:160
  39.5 0.7 collective-permute-start.6
  40.3 0.7 collective-permute-start.7
  41.2 0.7 collective-permute-start.8
  42.0 0.7 collective-permute-start.9
  42.9 0.7 collective-permute-start.10
  43.7 0.7 collective-permute-start.11
  44.5 0.7 collective-permute-start.12
  45.4 0.7 collective-permute-start.13
  51.3 1.3 %collective-permute-start.20 = (f32[1,512]{1,0:T(1,128)S(1)}, f32[1,512]{1,0:T(1,128)S(1)}, u32[]{:S(2)}, u32[]{:S(2)}) collective-permute-start(f32[1,512]{1,0:T(1,128)S(1)} %hop.29), channel_id=1, source_target_pairs={{2,0},{3,1}} | collective-permute-start | bytes 6152 | tf_op jit(solution)/shard_map/ppermute | solution.py:194
  52.6 55.5 %collective-permute-done.20 = f32[1,512]{1,0:T(1,128)S(1)} collective-permute-done((f32[1,512]{1,0:T(1,128)S(1)}, f32[1,512]{1,0:T(1,128)S(1)}, u32[]{:S(2)}, u32[]{:S(2)}) %collective-permute-start.20) | collective-permute-done | bytes 2080 | tf_op jit(solution)/shard_map/ppermute | solution.py:194
  108.5 3.6 %collective-permute-done.21 = f32[2,128]{1,0:T(2,128)S(1)} collective-permute-done((f32[2,128]{1,0:T(2,128)S(1)}, f32[2,128]{1,0:T(2,128)S(1)}, u32[]{:S(2)}, u32[]{:S(2)}) %collective-permute-start.21) | collective-permute-done | bytes 1056 | tf_op jit(solution)/shard_map/ppermute | solution.py:123
  (66 shorter events, 8.4 us)
Async XLA Ops:
  0.0 11.4 %copy-start = (f32[4,128,512]{2,1,0:T(8,128)S(1)}, f32[4,128,512]{2,1,0:T(8,128)}, u32[]{:S(2)}) copy-start(f32[4,128,512]{2,1,0:T(8,128)} %refs_0_.1) | copy-start | bytes 3145732
  0.0 9.6 %collective-permute-start = (f32[128,512]{1,0:T(8,128)}, f32[128,512]{1,0:T(8,128)}, u32[]{:S(2)}, u32[]{:S(2)}) collective-permute-start(f32[128,512]{1,0:T(8,128)} %param.7), channel_id=1, source_target_pairs={{0,2},{1,3},{2,0},{3,1},{4,6},{5,7},{6,4},{7,5},{8,10},{9,11},{10,... | collective-permute-start | bytes 786440 | tf_op jit(solution)/shard_map/ppermute | solution.py:123
  11.4 4.5 %copy-start.1 = (f32[4,128,512]{2,1,0:T(8,128)S(1)}, f32[4,128,512]{2,1,0:T(8,128)}, u32[]{:S(2)}) copy-start(f32[4,128,512]{2,1,0:T(8,128)} %refs_1_.1) | copy-start | bytes 3145732
  11.4 5.8 %collective-permute-start.1 = (f32[2,128,512]{2,1,0:T(8,128)}, f32[2,128,512]{2,1,0:T(8,128)}, u32[]{:S(2)}, u32[]{:S(2)}) collective-permute-start(f32[2,128,512]{2,1,0:T(8,128)} %pad_maximum_fusion.1), channel_id=1, source_target_pairs={{0,1},{1,0},{2,3},{3,2},{4,5},{5,4},{6,7},{7,6},{8,9},{9,8},{10,11... | collective-permute-start | bytes 1572872 | tf_op jit(solution)/shard_map/ppermute | solution.py:123
  13.5 9.3 %collective-permute-start.3 = (f32[2,128,256]{2,1,0:T(8,128)}, f32[2,128,256]{2,1,0:T(8,128)S(1)}, u32[]{:S(2)}, u32[]{:S(2)}) collective-permute-start(f32[2,128,256]{2,1,0:T(8,128)} %pad_maximum_fusion.3), channel_id=1, source_target_pairs={{0,2},{1,3},{2,0},{3,1},{4,6},{5,7},{6,4},{7,5},{8,10},{9,11},{10,... | collective-permute-start | bytes 786440 | tf_op jit(solution)/shard_map/ppermute | solution.py:123
  15.9 11.6 %collective-permute-start.4 = (f32[2,128,256]{2,1,0:T(8,128)}, f32[2,128,256]{2,1,0:T(8,128)S(1)}, u32[]{:S(2)}, u32[]{:S(2)}) collective-permute-start(f32[2,128,256]{2,1,0:T(8,128)} %pad_maximum_fusion.4), channel_id=1, source_target_pairs={{0,3},{1,2},{2,1},{3,0},{4,7},{5,6},{6,5},{7,4},{8,11},{9,10},{10,... | collective-permute-start | bytes 786440 | tf_op jit(solution)/shard_map/ppermute | solution.py:123
  16.8 11.3 %collective-permute-start.2 = (f32[2,128,512]{2,1,0:T(8,128)}, f32[2,128,512]{2,1,0:T(8,128)S(1)}, u32[]{:S(2)}, u32[]{:S(2)}) collective-permute-start(f32[2,128,512]{2,1,0:T(8,128)} %pad_maximum_fusion.2), channel_id=1, source_target_pairs={{0,1},{1,0},{2,3},{3,2},{4,5},{5,4},{6,7},{7,6},{8,9},{9,8},{10,11... | collective-permute-start | bytes 1572872 | tf_op jit(solution)/shard_map/ppermute | solution.py:123
  18.7 10.3 %copy-start.8 = (f32[4,512]{1,0:T(4,128)S(1)}, f32[4,512]{1,0:T(4,128)}, u32[]{:S(2)}) copy-start(f32[4,512]{1,0:T(4,128)} %means.1) | copy-start | bytes 24580
  27.4 0.7 copy-start.6
  28.1 0.8 copy-start.4
  28.9 1.0 copy-start.5
  30.0 0.9 copy-start.7
  33.2 2.7 %collective-permute-start.5 = (f32[512,512]{1,0:T(8,128)S(1)}, f32[512,512]{1,0:T(8,128)S(1)}, u32[]{:S(2)}, u32[]{:S(2)}) collective-permute-start(f32[512,512]{1,0:T(8,128)S(1)} %get-tuple-element.10.own), channel_id=1, source_target_pairs={{0,1},{1,0},{2,3},{3,2},{4,5},{5,4},{6,7},{7,6},{8,9},{9,8},{10,11... | collective-permute-start | bytes 3145736 | tf_op jit(solution)/shard_map/ppermute | solution.py:123
  33.6 0.7 copy-start.9
  35.9 1.0 copy-start.2
  36.9 1.2 %copy-start.3 = (f32[512,512]{1,0:T(8,128)S(1)}, f32[512,512]{1,0:T(8,128)}, u32[]{:S(2)}) copy-start(f32[512,512]{1,0:T(8,128)} %copy-done.2) | copy-start | bytes 3145732
  39.5 0.7 collective-permute-start.6
  40.3 0.7 collective-permute-start.7
  41.2 0.7 collective-permute-start.8
  42.0 0.7 collective-permute-start.9
  42.9 0.7 collective-permute-start.10
  43.7 0.7 collective-permute-start.11
  44.5 0.7 collective-permute-start.12
  45.4 0.7 collective-permute-start.13
  46.2 0.7 collective-permute-start.14
  47.1 0.7 collective-permute-start.15
  47.9 0.7 collective-permute-start.16
  48.8 0.7 collective-permute-start.17
  49.6 0.7 collective-permute-start.18
  50.4 0.7 collective-permute-start.19
  51.3 56.8 %collective-permute-start.20 = (f32[1,512]{1,0:T(1,128)S(1)}, f32[1,512]{1,0:T(1,128)S(1)}, u32[]{:S(2)}, u32[]{:S(2)}) collective-permute-start(f32[1,512]{1,0:T(1,128)S(1)} %hop.29), channel_id=1, source_target_pairs={{2,0},{3,1}} | collective-permute-start | bytes 6152 | tf_op jit(solution)/shard_map/ppermute | solution.py:194
  108.4 3.6 %collective-permute-start.21 = (f32[2,128]{1,0:T(2,128)S(1)}, f32[2,128]{1,0:T(2,128)S(1)}, u32[]{:S(2)}, u32[]{:S(2)}) collective-permute-start(f32[2,128]{1,0:T(2,128)S(1)} %get-tuple-element.20), channel_id=1, source_target_pairs={{0,2},{1,3},{2,0},{3,1},{4,6},{5,7},{6,4},{7,5},{8,10},{9,11},{10,... | collective-permute-start | bytes 3080 | tf_op jit(solution)/shard_map/ppermute | solution.py:123

commit v2 on v1

v2 whole, which is shorter than its diff:
```python
import functools

import jax
import jax.numpy as jnp
from jax import lax
from jax.experimental import pallas as pl
from jax.experimental.pallas import tpu as pltpu
from jax.sharding import PartitionSpec as P

F32, BF16 = jnp.float32, jnp.bfloat16
NN = (((1,), (0,)), ((), ()))
NT = (((1,), (1,)), ((), ()))
ANY = pl.BlockSpec(memory_space=pl.ANY)
HBM = pl.BlockSpec(memory_space=pltpu.HBM)
VMEM = pl.BlockSpec(memory_space=pltpu.VMEM)


def split(x):
    high = x.astype(BF16)
    return high, (x - high.astype(F32)).astype(BF16)


def dot3(a, b, dims):
    (ah, al), (bh, bl) = split(a), split(b)
    dot = functools.partial(lax.dot_general, dimension_numbers=dims, preferred_element_type=F32)
    return dot(ah, bh) + (dot(ah, bl) + dot(al, bh))


def matvec(matrix, row):
    order = matrix.shape[1]
    total = matrix[:, :128] * row[:, :128]
    for j in range(128, order, 128):
        total += matrix[:, j : j + 128] * row[:, j : j + 128]
    return jnp.sum(total.T, axis=0, keepdims=True)


def rows(i, panel):
    return pl.ds(pl.multiple_of(i * panel, panel), panel)


def starter(sems):
    copies = []

    def start(source, target):
        copy = pltpu.make_async_copy(source, target, sems.at[len(copies)])
        copy.start()
        copies.append(copy)

    return start, copies


def width(devices, panel, order, off):
    if off < devices // 2:
        return order
    return panel if off == devices - 1 and panel % 128 == 0 else order // 2


def pack_kernel(devices, repeat, cov, prec, *refs):
    outs, sems = refs[:-1], refs[-1]
    panel, order = cov.shape[1:]
    half, wide = devices // 2, order // 2
    s = lax.axis_index("state")
    start, copies = starter(sems)
    for off in list(range(half, devices)) + list(range(1, half)):
        step = (s ^ off) // repeat
        w = width(devices, panel, order, off)
        for which, matrix in enumerate((cov, prec)):
            if w == order:
                source = matrix.at[step]
            else:
                first = pl.multiple_of((s // half) * wide if w == wide else s * panel, w)
                source = matrix.at[step, :, pl.ds(first, w)]
            start(source, outs[off - 1].at[which])
    for copy in copies:
        copy.wait()


def gain_kernel(devices, repeat, *refs):
    half = devices // 2
    cov, prec, means, trans, across = refs[:5]
    near, far = refs[5 : 5 + half - 1], refs[4 + half : 4 + half + half - 1]
    arrived = refs[3 + 2 * half : 3 + 2 * half + devices - 1]
    gain, pred, pf, lf, af, sems = refs[3 + 2 * half + devices - 1 :]
    panel, order = cov.shape[1:]
    wide = order // 2
    s = lax.axis_index("state")
    side = s // half
    step = s // repeat
    start, copies = starter(sems)
    other = pl.multiple_of((1 - side) * wide, wide)
    own = pl.multiple_of(side * wide, wide)
    start(trans, af.at[rows(s, panel), :])
    start(across, af.at[rows(s ^ half, panel), :])
    for off in range(1, half):
        start(near[off - 1], af.at[rows(s ^ off, panel), :])
        start(far[off - 1], af.at[rows(s ^ off ^ half, panel), :])
    start(cov.at[step], pf.at[rows(s, panel), :])
    start(prec.at[step], lf.at[rows(s, panel), :])
    for off in range(1, devices):
        i = s ^ off
        w = width(devices, panel, order, off)
        for which, full in enumerate((pf, lf)):
            place = full.at[rows(i, panel), :]
            if w < order:
                first = other if w == wide else pl.multiple_of(i * panel, panel)
                place = full.at[rows(i, panel), pl.ds(first, w)]
            start(arrived[off - 1].at[which], place)
    steps = means.shape[0]
    pf[order:, :] = jnp.concatenate([means[...], jnp.zeros((16 - steps, order), F32)], axis=0)
    for copy in copies:
        copy.wait()
    for full in (pf, lf):
        full[pl.ds(other, wide), pl.ds(own, wide)] = full[pl.ds(own, wide), pl.ds(other, wide)].T
        if width(devices, panel, order, devices - 1) < wide:
            i = s ^ (devices - 1)
            for off in range(half, devices - 1):
                j = s ^ off
                full[rows(i, panel), rows(j, panel)] = full[rows(j, panel), rows(i, panel)].T
    cov_trans = dot3(pf[...], af[...], NT)
    pred[...] = cov_trans[order : order + 8]
    gain[...] = dot3(cov_trans[:order], lf[...], NN)


def pair_kernel(repeat, own, partner, means, pred, c_ref, late_ref, vec_ref, slots, sems):
    step = lax.axis_index("state") // repeat
    bit = step % 2
    first = pltpu.make_async_copy(own, slots.at[bit], sems.at[0])
    second = pltpu.make_async_copy(partner, slots.at[1 - bit], sems.at[1])
    first.start()
    second.start()
    a = step - bit
    mean_a, mean_b = means[pl.ds(a, 1), :], means[pl.ds(a + 1, 1), :]
    pred_a, pred_b = pred[pl.ds(a, 1), :], pred[pl.ds(a + 1, 1), :]
    first.wait()
    second.wait()
    ga, gb = slots[0], slots[1]
    vec_ref[...] = jnp.concatenate(
        [mean_a + matvec(ga, mean_b - pred_a), mean_b, pred_b, jnp.zeros((5, ga.shape[1]), F32)], axis=0
    )
    c_ref[...] = dot3(ga, gb, NN)
    late_ref[...] = gb


def hop_kernel(x_ref, c_ref, vec_ref, out_ref):
    vec = vec_ref[...]
    out_ref[...] = vec[0:1] + matvec(c_ref[...], x_ref[...] - vec[2:3])


def last_kernel(x_ref, c_ref, late_ref, vec_ref, out_ref):
    vec = vec_ref[...]
    gap = x_ref[...] - vec[2:3]
    out_ref[0:1, :] = vec[0:1] + matvec(c_ref[...], gap)
    out_ref[1:2, :] = vec[1:2] + matvec(late_ref[...], gap)


def params(mebibytes):
    return pltpu.CompilerParams(vmem_limit_bytes=mebibytes * 2**20)


def local(filtered_covariance, pred_prec, transition, filt_means, terminal_mean):
    steps, panel, order = filtered_covariance.shape
    devices, blocks = lax.axis_size("state"), lax.axis_size("tm")
    repeat, half, wide = devices // steps, devices // 2, order // 2
    s, b = lax.axis_index("state"), lax.axis_index("tm")
    side = s // half

    def swap(x, off):
        return lax.ppermute(x, "state", [(i, i ^ off) for i in range(devices)])

    across = swap(transition, half)
    near = [swap(transition, off) for off in range(1, half)]

    widths = [width(devices, panel, order, off) for off in range(1, devices)]
    pieces = pl.pallas_call(
        functools.partial(pack_kernel, devices, repeat),
        out_shape=[jax.ShapeDtypeStruct((2, panel, w), F32) for w in widths],
        in_specs=[HBM, HBM],
        out_specs=[VMEM] * (devices - 1),
        scratch_shapes=[pltpu.SemaphoreType.DMA((2 * devices - 2,))],
        compiler_params=params(4),
        name="pack",
    )(filtered_covariance, pred_prec)
    arrived = [swap(piece, off) for off, piece in enumerate(pieces, 1)]
    far = [swap(across, off) for off in range(1, half)]

    gain, pred = pl.pallas_call(
        functools.partial(gain_kernel, devices, repeat),
        out_shape=(jax.ShapeDtypeStruct((order, order), F32), jax.ShapeDtypeStruct((8, order), F32)),
        in_specs=[HBM, HBM, VMEM, HBM] + [ANY] * (2 * half + devices - 2),
        out_specs=(VMEM, VMEM),
        scratch_shapes=[
            pltpu.VMEM((order + 16, order), F32),
            pltpu.VMEM((order, order), F32),
            pltpu.VMEM((order, order), F32),
            pltpu.SemaphoreType.DMA((2 * half + 2 * devices,)),
        ],
        compiler_params=params(16),
        name="gain",
    )(filtered_covariance, pred_prec, filt_means, transition, across, *near, *far, *arrived)

    partner = swap(gain, repeat)
    c, late, vec = pl.pallas_call(
        functools.partial(pair_kernel, repeat),
        out_shape=(
            jax.ShapeDtypeStruct((order, order), F32),
            jax.ShapeDtypeStruct((order, order), F32),
            jax.ShapeDtypeStruct((8, order), F32),
        ),
        in_specs=[ANY, ANY, VMEM, VMEM],
        out_specs=(VMEM, VMEM, VMEM),
        scratch_shapes=[pltpu.VMEM((2, order, order), F32), pltpu.SemaphoreType.DMA((2,))],
        compiler_params=params(12),
        name="pair",
    )(gain, partner, filt_means, pred)

    hop = pl.pallas_call(
        hop_kernel,
        out_shape=jax.ShapeDtypeStruct((1, order), F32),
        in_specs=[VMEM] * 3,
        out_specs=VMEM,
        compiler_params=params(6),
        name="hop",
    )

    everyone = range(blocks * devices)
    lead = (half - 1, devices - 1)
    start = jnp.where((b == blocks - 1) & (s == lead[1]), terminal_mean, 0.0)[None]
    arrives = [(tm, h) for tm in range(blocks - 1, -1, -1) for h in (1, 0)]
    incoming, total = start, start
    for (tm, h), (to, g) in zip(arrives, arrives[1:]):
        u, v = tm * devices + lead[h], to * devices + lead[g]
        change = {u: v, v: u}
        swapped = lax.ppermute(hop(incoming, c, vec), ("tm", "state"), [(i, change.get(i, i)) for i in everyone])
        incoming = swapped
        total = jnp.where((b == to) & (s == lead[g]), swapped, total)

    both = pl.pallas_call(
        last_kernel,
        out_shape=jax.ShapeDtypeStruct((2, order), F32),
        in_specs=[VMEM] * 4,
        out_specs=VMEM,
        compiler_params=params(6),
        name="last",
    )(total, c, late, vec)

    def columns(i):
        return lax.dynamic_slice_in_dim(both, i * panel, panel, 1)

    theirs = [columns(s)] + [swap(columns(s ^ off), off) for off in range(1, devices)]
    away = [s ^ lead[h] for h in range(2)]
    return jnp.concatenate([sum(jnp.where(a == off, x, 0.0) for off, x in enumerate(theirs)) for a in away], axis=0)


def solution(mesh):
    return jax.shard_map(
        local,
        mesh=mesh,
        in_specs=(
            P("tm", "state", None),
            P("tm", "state", None),
            P("state", None),
            P("tm", None),
            P(),
        ),
        out_specs=P("tm", "state"),
        check_vma=False,
    )
```

time: 113 us -> 102 us (0.903)
  waiting for transfers between devices: 76.1 us -> 18.6 us
  starting transfers between devices: 16.1 us -> 68.8 us
  other arithmetic: 5.98 us -> 0.64 us
  local copies, waits for them, and re-layouts: 7.96 us -> 6.32 us
    ppermute x15, waiting for transfers between devices: 55.6 us -> 0.04 us  [local(): lax.ppermute(hop(incoming, c, vec), ('tm', 'state'), [(i, change.get(i, i...]
    ppermute x7 -> x10, starting transfers between devices: 5.51 us -> 58.9 us  [swap(): return lax.ppermute(x, 'state', [(i, i ^ off) for i in range(devices)])]
    another operation x4 -> x0, other arithmetic: 4.11 us -> none  [the longest x3 2.26 us: local(): arrived.append(swap(jnp.stack(piece), off))]
    ppermute x7 -> x10, waiting for transfers between devices: 20.6 us -> 18.6 us  [swap(): return lax.ppermute(x, 'state', [(i, i ^ off) for i in range(devices)])]
    dynamic_slice x3 -> x1, local copies, waits for them, and re-layouts: 1.37 us -> 0.01 us  [columns(): return lax.dynamic_slice_in_dim(both, i * panel, panel, 1)]
    pallas_call x15 -> x16, Pallas kernels: 2.36 us -> 2.52 us  [the longest x15 2.36 us: local(): hop(incoming, c, vec)]
  transfers between devices with their start and end apart: 22 -> 25, of which waited for: 6 -> 5; matrix products, arithmetic and copies ran while one was open for 5% -> 0% of each run, Pallas kernels for 0% -> 0%
where the time goes in v2:
time: 102 us; the launch traced here: 101 us
  starting transfers between devices  68.8 us (67%)
  waiting for transfers between devices  18.6 us (18%)
  Pallas kernels  6.33 us (6%)
  local copies, waits for them, and re-layouts  6.32 us (6%)
    ppermute x10, starting transfers between devices, swap(): return lax.ppermute(x, 'state', [(i, i ^ off) for i in range(devices)])  58.9 us
    ppermute x10, waiting for transfers between devices, swap(): return lax.ppermute(x, 'state', [(i, i ^ off) for i in range(devices)])  18.6 us
    ppermute x15, starting transfers between devices, local(): lax.ppermute(hop(incoming, c, vec), ('tm', 'state'), [(i, change.get(i, i...  9.92 us
    unnamed x20, local copies, waits for them, and re-layouts  6.31 us
    pallas_call x1, Pallas kernels, local(): pl.pallas_call(functools.partial(gain_kernel, devices, repeat), out_shape...  2.39 us
    pallas_call x15, Pallas kernels, local(): hop(incoming, c, vec)  2.36 us
  transfers between devices with their start and end apart: 25, of which 5 were waited for; matrix products, arithmetic and copies ran while one was open for 0% of the time, Pallas kernels for 0%

profile of v2, /device:TPU:0, one launch (start us, length us, event | category | flops | bytes accessed | tf_op | source)
XLA Modules:
  0.0 101.2 jit_solution(4152980509137335597)
XLA Ops:
  0.0 1.2 %copy-done = f32[4,128,512]{2,1,0:T(8,128)S(1)} copy-done((f32[4,128,512]{2,1,0:T(8,128)S(1)}, f32[4,128,512]{2,1,0:T(8,128)}, u32[]{:S(2)}) %copy-start) | copy-done | bytes 1048600
  1.2 1.2 %copy-done.2 = f32[4,128,512]{2,1,0:T(8,128)S(1)} copy-done((f32[4,128,512]{2,1,0:T(8,128)S(1)}, f32[4,128,512]{2,1,0:T(8,128)}, u32[]{:S(2)}) %copy-start.2) | copy-done | bytes 1048600
  3.1 2.6 %collective-permute-start = (f32[128,512]{1,0:T(8,128)}, f32[128,512]{1,0:T(8,128)S(1)}, u32[]{:S(2)}, u32[]{:S(2)}) collective-permute-start(f32[128,512]{1,0:T(8,128)} %refs_3_.1), channel_id=1, source_target_pairs={{0,2},{1,3},{2,0},{3,1},{4,6},{5,7},{6,4},{7,5},{8,10},{9,11},{10,... | collective-permute-start | bytes 786440 | tf_op jit(solution)/shard_map/ppermute | solution.py:168
  5.9 7.2 %collective-permute-done.refs_4_ = f32[128,512]{1,0:T(8,128)S(1)} collective-permute-done((f32[128,512]{1,0:T(8,128)}, f32[128,512]{1,0:T(8,128)S(1)}, u32[]{:S(2)}, u32[]{:S(2)}) %collective-permute-start) | collective-permute-done | bytes 262176 | tf_op jit(solution)/shard_map/ppermute | solution.py:168
  13.1 2.1 %collective-permute-start.5 = (f32[2,128,128]{2,1,0:T(8,128)S(1)}, f32[2,128,128]{2,1,0:T(8,128)S(1)}, u32[]{:S(2)}, u32[]{:S(2)}) collective-permute-start(f32[2,128,128]{2,1,0:T(8,128)S(1)} %get-tuple-element.15), channel_id=1, source_target_pairs={{0,3},{1,2},{2,1},{3,0},{4,7},{5,6},{6,5},{7,4},{8,11},{9,10},{10,... | collective-permute-start | bytes 393224 | tf_op jit(solution)/shard_map/ppermute | solution.py:168
  15.1 5.8 %collective-permute-done.5.refs_9_ = f32[2,128,128]{2,1,0:T(8,128)S(1)} collective-permute-done((f32[2,128,128]{2,1,0:T(8,128)S(1)}, f32[2,128,128]{2,1,0:T(8,128)S(1)}, u32[]{:S(2)}, u32[]{:S(2)}) %collective-permute-start.5) | collective-permute-done | bytes 131104 | tf_op jit(solution)/shard_map/ppermute | solution.py:168
  21.0 0.9 copy-done.6
  22.0 0.7 copy-done.7
  22.7 2.4 %gain.1 = (f32[512,512]{1,0:T(8,128)S(1)}, f32[8,512]{1,0:T(8,128)S(1)}) custom-call(f32[4,128,512]{2,1,0:T(8,128)S(1)} %copy-done.1, f32[4,128,512]{2,1,0:T(8,128)S(1)} %copy-done.3, f32[4,512]{1,0:T(4,128)S(1)} %copy-done.7, f32[128,512]{1,0:T(8,128)S(1)} %copy-done.6, f32[128,512]{1,0:T(8,128)S(1)} %collective-permute-done.refs_4_, ...), custom_call_target="tpu_custom_call" | custom-call | tf_op jit(solution)/shard_map/gain/pallas_call | solution.py:186
  25.3 2.5 %collective-permute-done.6.partner = f32[512,512]{1,0:T(8,128)S(1)} collective-permute-done((f32[512,512]{1,0:T(8,128)S(1)}, f32[512,512]{1,0:T(8,128)S(1)}, u32[]{:S(2)}, u32[]{:S(2)}) %collective-permute-start.6) | collective-permute-done | bytes 1048608 | tf_op jit(solution)/shard_map/ppermute | solution.py:168
  27.8 1.0 copy-done.4
  28.8 1.2 %copy-done.5 = f32[512,512]{1,0:T(8,128)S(1)} copy-done((f32[512,512]{1,0:T(8,128)S(1)}, f32[512,512]{1,0:T(8,128)}, u32[]{:S(2)}) %copy-start.5) | copy-done | bytes 1048600
  30.0 1.2 %pair.1 = (f32[512,512]{1,0:T(8,128)S(1)}, f32[512,512]{1,0:T(8,128)S(1)}, f32[8,512]{1,0:T(8,128)S(1)}) custom-call(f32[512,512]{1,0:T(8,128)S(1)} %get-tuple-element.16.own, f32[512,512]{1,0:T(8,128)S(1)} %copy-done.5, f32[4,512]{1,0:T(4,128)S(1)} %copy-done.8, f32[8,512]{1,0:T(8,128)S(1)} %get-tuple-element.17.pred), custom_call_target="tpu_custom_call" | custom-call | tf_op jit(solution)/shard_map/pair/pallas_call | solution.py:202
  31.4 0.7 collective-permute-start.7
  32.2 0.7 collective-permute-start.8
  33.0 0.7 collective-permute-start.9
  33.9 0.7 collective-permute-start.10
  34.7 0.7 collective-permute-start.11
  35.6 0.7 collective-permute-start.12
  36.4 0.7 collective-permute-start.13
  37.3 0.7 collective-permute-start.14
  38.1 0.7 collective-permute-start.15
  39.0 0.7 collective-permute-start.16
  39.8 0.7 collective-permute-start.17
  40.6 0.7 collective-permute-start.18
  41.5 0.7 collective-permute-start.19
  42.3 0.7 collective-permute-start.20
  43.2 0.7 collective-permute-start.21
  44.2 51.7 %collective-permute-start.22 = (f32[2,128]{1,0:T(2,128)S(1)}, f32[2,128]{1,0:T(2,128)S(1)}, u32[]{:S(2)}, u32[]{:S(2)}) collective-permute-start(f32[2,128]{1,0:T(2,128)S(1)} %get-tuple-element.23), channel_id=1, source_target_pairs={{0,1},{1,0},{2,3},{3,2},{4,5},{5,4},{6,7},{7,6},{8,9},{9,8},{10,11... | collective-permute-start | bytes 3080 | tf_op jit(solution)/shard_map/ppermute | solution.py:168
  95.9 1.7 %collective-permute-start.23 = (f32[2,128]{1,0:T(2,128)S(1)}, f32[2,128]{1,0:T(2,128)S(1)}, u32[]{:S(2)}, u32[]{:S(2)}) collective-permute-start(f32[2,128]{1,0:T(2,128)S(1)} %get-tuple-element.25), channel_id=1, source_target_pairs={{0,2},{1,3},{2,0},{3,1},{4,6},{5,7},{6,4},{7,5},{8,10},{9,11},{10,... | collective-permute-start | bytes 3080 | tf_op jit(solution)/shard_map/ppermute | solution.py:168
  97.6 1.8 %collective-permute-done.23 = f32[2,128]{1,0:T(2,128)S(1)} collective-permute-done((f32[2,128]{1,0:T(2,128)S(1)}, f32[2,128]{1,0:T(2,128)S(1)}, u32[]{:S(2)}, u32[]{:S(2)}) %collective-permute-start.23) | collective-permute-done | bytes 1056 | tf_op jit(solution)/shard_map/ppermute | solution.py:168
  99.5 1.2 %collective-permute-done.24 = f32[2,128]{1,0:T(2,128)S(1)} collective-permute-done((f32[2,128]{1,0:T(2,128)S(1)}, f32[2,128]{1,0:T(2,128)S(1)}, u32[]{:S(2)}, u32[]{:S(2)}) %collective-permute-start.24) | collective-permute-done | bytes 1056 | tf_op jit(solution)/shard_map/ppermute | solution.py:168
  (62 shorter events, 4.4 us)
Async XLA Ops:
  0.0 1.2 %copy-start = (f32[4,128,512]{2,1,0:T(8,128)S(1)}, f32[4,128,512]{2,1,0:T(8,128)}, u32[]{:S(2)}) copy-start(f32[4,128,512]{2,1,0:T(8,128)} %refs_0_.1) | copy-start | bytes 3145732
  1.2 1.2 %copy-start.2 = (f32[4,128,512]{2,1,0:T(8,128)S(1)}, f32[4,128,512]{2,1,0:T(8,128)}, u32[]{:S(2)}) copy-start(f32[4,128,512]{2,1,0:T(8,128)} %refs_1_.1) | copy-start | bytes 3145732
  2.5 18.5 %copy-start.1 = (f32[4,128,512]{2,1,0:T(8,128)S(1)}, f32[4,128,512]{2,1,0:T(8,128)}, u32[]{:S(2)}) copy-start(f32[4,128,512]{2,1,0:T(8,128)} %refs_0_.1) | copy-start | bytes 3145732
  2.5 18.6 %copy-start.3 = (f32[4,128,512]{2,1,0:T(8,128)S(1)}, f32[4,128,512]{2,1,0:T(8,128)}, u32[]{:S(2)}) copy-start(f32[4,128,512]{2,1,0:T(8,128)} %refs_1_.1) | copy-start | bytes 3145732
  2.6 18.4 %collective-permute-start.3 = (f32[2,128,512]{2,1,0:T(8,128)S(1)}, f32[2,128,512]{2,1,0:T(8,128)S(1)}, u32[]{:S(2)}, u32[]{:S(2)}) collective-permute-start(f32[2,128,512]{2,1,0:T(8,128)S(1)} %get-tuple-element.13), channel_id=1, source_target_pairs={{0,1},{1,0},{2,3},{3,2},{4,5},{5,4},{6,7},{7,6},{8,9},{9,8},{10,11... | collective-permute-start | bytes 1572872 | tf_op jit(solution)/shard_map/ppermute | solution.py:168
  3.1 9.9 %collective-permute-start = (f32[128,512]{1,0:T(8,128)}, f32[128,512]{1,0:T(8,128)S(1)}, u32[]{:S(2)}, u32[]{:S(2)}) collective-permute-start(f32[128,512]{1,0:T(8,128)} %refs_3_.1), channel_id=1, source_target_pairs={{0,2},{1,3},{2,0},{3,1},{4,6},{5,7},{6,4},{7,5},{8,10},{9,11},{10,... | collective-permute-start | bytes 786440 | tf_op jit(solution)/shard_map/ppermute | solution.py:168
  5.7 15.3 %collective-permute-start.4 = (f32[2,128,256]{2,1,0:T(8,128)S(1)}, f32[2,128,256]{2,1,0:T(8,128)S(1)}, u32[]{:S(2)}, u32[]{:S(2)}) collective-permute-start(f32[2,128,256]{2,1,0:T(8,128)S(1)} %get-tuple-element.14), channel_id=1, source_target_pairs={{0,2},{1,3},{2,0},{3,1},{4,6},{5,7},{6,4},{7,5},{8,10},{9,11},{10,... | collective-permute-start | bytes 786440 | tf_op jit(solution)/shard_map/ppermute | solution.py:168
  5.8 15.2 %collective-permute-start.1 = (f32[128,512]{1,0:T(8,128)}, f32[128,512]{1,0:T(8,128)S(1)}, u32[]{:S(2)}, u32[]{:S(2)}) collective-permute-start(f32[128,512]{1,0:T(8,128)} %refs_3_.1), channel_id=1, source_target_pairs={{0,1},{1,0},{2,3},{3,2},{4,5},{5,4},{6,7},{7,6},{8,9},{9,8},{10,11... | collective-permute-start | bytes 786440 | tf_op jit(solution)/shard_map/ppermute | solution.py:168
  13.1 7.9 %collective-permute-start.2 = (f32[128,512]{1,0:T(8,128)S(1)}, f32[128,512]{1,0:T(8,128)S(1)}, u32[]{:S(2)}, u32[]{:S(2)}) collective-permute-start(f32[128,512]{1,0:T(8,128)S(1)} %collective-permute-done.refs_4_), channel_id=1, source_target_pairs={{0,1},{1,0},{2,3},{3,2},{4,5},{5,4},{6,7},{7,6},{8,9},{9,8},{10,11... | collective-permute-start | bytes 786440 | tf_op jit(solution)/shard_map/ppermute | solution.py:168
  13.1 7.9 %collective-permute-start.5 = (f32[2,128,128]{2,1,0:T(8,128)S(1)}, f32[2,128,128]{2,1,0:T(8,128)S(1)}, u32[]{:S(2)}, u32[]{:S(2)}) collective-permute-start(f32[2,128,128]{2,1,0:T(8,128)S(1)} %get-tuple-element.15), channel_id=1, source_target_pairs={{0,3},{1,2},{2,1},{3,0},{4,7},{5,6},{6,5},{7,4},{8,11},{9,10},{10,... | collective-permute-start | bytes 393224 | tf_op jit(solution)/shard_map/ppermute | solution.py:168
  22.7 2.6 %copy-start.9 = (f32[512]{0:T(512)S(1)}, f32[512]{0:T(512)}, u32[]{:S(2)}) copy-start(f32[512]{0:T(512)} %param.9) | copy-start | bytes 6148
  25.1 2.7 %collective-permute-start.6 = (f32[512,512]{1,0:T(8,128)S(1)}, f32[512,512]{1,0:T(8,128)S(1)}, u32[]{:S(2)}, u32[]{:S(2)}) collective-permute-start(f32[512,512]{1,0:T(8,128)S(1)} %get-tuple-element.16.own), channel_id=1, source_target_pairs={{0,1},{1,0},{2,3},{3,2},{4,5},{5,4},{6,7},{7,6},{8,9},{9,8},{10,11... | collective-permute-start | bytes 3145736 | tf_op jit(solution)/shard_map/ppermute | solution.py:168
  25.2 3.5 %copy-start.8 = (f32[4,512]{1,0:T(4,128)S(1)}, f32[4,512]{1,0:T(4,128)}, u32[]{:S(2)}) copy-start(f32[4,512]{1,0:T(4,128)} %means.1) | copy-start | bytes 24580
  28.8 1.2 %copy-start.5 = (f32[512,512]{1,0:T(8,128)S(1)}, f32[512,512]{1,0:T(8,128)}, u32[]{:S(2)}) copy-start(f32[512,512]{1,0:T(8,128)} %copy-done.4) | copy-start | bytes 3145732
  31.4 0.7 collective-permute-start.7
  32.2 0.7 collective-permute-start.8
  33.0 0.7 collective-permute-start.9
  33.9 0.7 collective-permute-start.10
  34.7 0.7 collective-permute-start.11
  35.6 0.7 collective-permute-start.12
  36.4 0.7 collective-permute-start.13
  37.3 0.7 collective-permute-start.14
  38.1 0.7 collective-permute-start.15
  39.0 0.7 collective-permute-start.16
  39.8 0.7 collective-permute-start.17
  40.6 0.7 collective-permute-start.18
  41.5 0.7 collective-permute-start.19
  42.3 0.7 collective-permute-start.20
  43.2 0.7 collective-permute-start.21
  44.2 53.4 %collective-permute-start.22 = (f32[2,128]{1,0:T(2,128)S(1)}, f32[2,128]{1,0:T(2,128)S(1)}, u32[]{:S(2)}, u32[]{:S(2)}) collective-permute-start(f32[2,128]{1,0:T(2,128)S(1)} %get-tuple-element.23), channel_id=1, source_target_pairs={{0,1},{1,0},{2,3},{3,2},{4,5},{5,4},{6,7},{7,6},{8,9},{9,8},{10,11... | collective-permute-start | bytes 3080 | tf_op jit(solution)/shard_map/ppermute | solution.py:168
  95.9 3.6 %collective-permute-start.23 = (f32[2,128]{1,0:T(2,128)S(1)}, f32[2,128]{1,0:T(2,128)S(1)}, u32[]{:S(2)}, u32[]{:S(2)}) collective-permute-start(f32[2,128]{1,0:T(2,128)S(1)} %get-tuple-element.25), channel_id=1, source_target_pairs={{0,2},{1,3},{2,0},{3,1},{4,6},{5,7},{6,4},{7,5},{8,10},{9,11},{10,... | collective-permute-start | bytes 3080 | tf_op jit(solution)/shard_map/ppermute | solution.py:168
  97.6 3.0 %collective-permute-start.24 = (f32[2,128]{1,0:T(2,128)S(1)}, f32[2,128]{1,0:T(2,128)S(1)}, u32[]{:S(2)}, u32[]{:S(2)}) collective-permute-start(f32[2,128]{1,0:T(2,128)S(1)} %get-tuple-element.24), channel_id=1, source_target_pairs={{0,3},{1,2},{2,1},{3,0},{4,7},{5,6},{6,5},{7,4},{8,11},{9,10},{10,... | collective-permute-start | bytes 3080 | tf_op jit(solution)/shard_map/ppermute | solution.py:168
  (3 other events, 2.6 us)

commit v3 on v2

v3 whole, which is shorter than its diff:
```python
import functools

import jax
import jax.numpy as jnp
from jax import lax
from jax.experimental import pallas as pl
from jax.experimental.pallas import tpu as pltpu
from jax.sharding import PartitionSpec as P

F32, BF16 = jnp.float32, jnp.bfloat16
NN = (((1,), (0,)), ((), ()))
NT = (((1,), (1,)), ((), ()))
ANY = pl.BlockSpec(memory_space=pl.ANY)
HBM = pl.BlockSpec(memory_space=pltpu.HBM)
VMEM = pl.BlockSpec(memory_space=pltpu.VMEM)


def split(x):
    high = x.astype(BF16)
    return high, (x - high.astype(F32)).astype(BF16)


def dot3(a, b, dims):
    (ah, al), (bh, bl) = split(a), split(b)
    dot = functools.partial(lax.dot_general, dimension_numbers=dims, preferred_element_type=F32)
    return dot(ah, bh) + (dot(ah, bl) + dot(al, bh))


def matvec(matrix, row):
    order = matrix.shape[1]
    total = matrix[:, :128] * row[:, :128]
    for j in range(128, order, 128):
        total += matrix[:, j : j + 128] * row[:, j : j + 128]
    return jnp.sum(total.T, axis=0, keepdims=True)


def rows(i, panel):
    return pl.ds(pl.multiple_of(i * panel, panel), panel)


def starter(sems):
    copies = []

    def start(source, target):
        copy = pltpu.make_async_copy(source, target, sems.at[len(copies)])
        copy.start()
        copies.append(copy)

    return start, copies


def width(devices, panel, order, off):
    if off < devices // 2:
        return order
    return panel if off == devices - 1 and panel % 128 == 0 else order // 2


def place():
    b, s, half = lax.axis_index("tm"), lax.axis_index("state"), lax.axis_size("state") // 2
    return b, s, s ^ ((b % 2) * half)


def owned(b, s, repeat):
    return (s ^ ((b % 2) * (lax.axis_size("state") // 2))) // repeat


def pack_kernel(devices, repeat, cov, prec, trans, terminal, *refs):
    pieces, trans_half, first, sems = refs[: devices - 1], *refs[devices - 1 :]
    panel, order = cov.shape[1:]
    half, wide = devices // 2, order // 2
    b, s, _ = place()
    start, copies = starter(sems)
    start(trans.at[pl.ds(pl.multiple_of((b % 2) * (panel // 2), panel // 2), panel // 2), :], trans_half)
    for off in list(range(half, devices)) + list(range(1, half)):
        step = owned(b, s ^ off, repeat)
        w = width(devices, panel, order, off)
        for which, matrix in enumerate((cov, prec)):
            if w == order:
                source = matrix.at[step]
            else:
                column = pl.multiple_of((s // half) * wide if w == wide else s * panel, w)
                source = matrix.at[step, :, pl.ds(column, w)]
            start(source, pieces[off - 1].at[which])
    first[...] = jnp.where(b == lax.axis_size("tm") - 1, terminal[...], 0.0)
    for copy in copies:
        copy.wait()


def gain_kernel(devices, repeat, *refs):
    half = devices // 2
    cov, prec, means, trans, across, around = refs[:6]
    near = refs[6 : 6 + 3 * (half - 1)]
    arrived = refs[6 + 3 * (half - 1) : 5 + 3 * (half - 1) + devices]
    gain, info, pf, lf, af, sems = refs[5 + 3 * (half - 1) + devices :]
    steps, panel, order = cov.shape
    wide = order // 2
    b, s, _ = place()
    side = s // half
    step = owned(b, s, repeat)
    start, copies = starter(sems)
    other = pl.multiple_of((1 - side) * wide, wide)
    own = pl.multiple_of(side * wide, wide)

    def halves(i):
        first = i * panel + (b % 2) * (panel // 2)
        second = i * panel + (1 - b % 2) * (panel // 2)
        return [af.at[pl.ds(pl.multiple_of(at, panel // 2), panel // 2), :] for at in (first, second)]

    start(trans, af.at[rows(s, panel), :])
    for piece, target in zip((across, around), halves(s ^ half)):
        start(piece, target)
    for off in range(1, half):
        mine, one, two = near[3 * off - 3 : 3 * off]
        start(mine, af.at[rows(s ^ off, panel), :])
        for piece, target in zip((one, two), halves(s ^ off ^ half)):
            start(piece, target)
    start(means, pf.at[pl.ds(order, steps), :])
    start(cov.at[step], pf.at[rows(s, panel), :])
    start(prec.at[step], lf.at[rows(s, panel), :])
    for off in range(1, devices):
        i = s ^ off
        w = width(devices, panel, order, off)
        for which, full in enumerate((pf, lf)):
            target = full.at[rows(i, panel), :]
            if w < order:
                column = other if w == wide else pl.multiple_of(i * panel, panel)
                target = full.at[rows(i, panel), pl.ds(column, w)]
            start(arrived[off - 1].at[which], target)
    pf[order + 8 :, :] = jnp.zeros((8, order), F32)
    for copy in copies:
        copy.wait()
    pf[order + steps : order + 8, :] = jnp.zeros((8 - steps, order), F32)
    for full in (pf, lf):
        full[pl.ds(other, wide), pl.ds(own, wide)] = full[pl.ds(own, wide), pl.ds(other, wide)].T
        if width(devices, panel, order, devices - 1) < wide:
            i = s ^ (devices - 1)
            for off in range(half, devices - 1):
                j = s ^ off
                full[rows(i, panel), rows(j, panel)] = full[rows(j, panel), rows(i, panel)].T
    cov_trans = dot3(pf[...], af[...], NT)
    info[:8] = pf[order : order + 8, :]
    info[8:] = cov_trans[order : order + 8]
    gain[...] = dot3(cov_trans[:order], lf[...], NN)


def pair_kernel(repeat, own, partner, info, c_ref, late_ref, vec_ref, slots, sems):
    b, s, _ = place()
    step = owned(b, s, repeat)
    bit = step % 2
    first = pltpu.make_async_copy(own, slots.at[bit], sems.at[0])
    second = pltpu.make_async_copy(partner, slots.at[1 - bit], sems.at[1])
    first.start()
    second.start()
    a = step - bit
    mean_a, mean_b = info[pl.ds(a, 1), :], info[pl.ds(a + 1, 1), :]
    pred_a, pred_b = info[pl.ds(a + 8, 1), :], info[pl.ds(a + 9, 1), :]
    first.wait()
    second.wait()
    ga, gb = slots[0], slots[1]
    vec_ref[...] = jnp.concatenate(
        [mean_a + matvec(ga, mean_b - pred_a), mean_b, pred_b, jnp.zeros((5, ga.shape[1]), F32)], axis=0
    )
    c_ref[...] = dot3(ga, gb, NN)
    late_ref[...] = gb


def hop_kernel(x_ref, c_ref, vec_ref, out_ref):
    vec = vec_ref[...]
    out_ref[...] = vec[0:1] + matvec(c_ref[...], x_ref[...] - vec[2:3])


def last_kernel(devices, *refs):
    incoming, (c_ref, late_ref, vec_ref, mine_ref, theirs_ref, both) = refs[:-6], refs[-6:]
    panel = mine_ref.shape[1]
    half = devices // 2
    b, s, t = place()
    arrival = 2 * (lax.axis_size("tm") - 1 - b) + 1 - t // half
    x = incoming[0][...]
    for k, ref in enumerate(incoming[1:], 1):
        x = jnp.where(arrival == k, ref[...], x)
    vec = vec_ref[...]
    gap = x - vec[2:3]
    full = jnp.concatenate(
        [vec[0:1] + matvec(c_ref[...], gap), vec[1:2] + matvec(late_ref[...], gap)], axis=0
    )
    for i in range(devices):
        both[i] = full[:, i * panel : (i + 1) * panel]
    mine_ref[...] = both[s]
    theirs_ref[...] = both[s ^ half ^ 1]


def out_kernel(devices, mine_ref, theirs_ref, out_ref):
    _, _, t = place()
    low = t < devices // 2
    mine, theirs = mine_ref[...], theirs_ref[...]
    out_ref[...] = jnp.concatenate([jnp.where(low, mine, theirs), jnp.where(low, theirs, mine)], axis=0)


def params(mebibytes):
    return pltpu.CompilerParams(vmem_limit_bytes=mebibytes * 2**20)


def local(filtered_covariance, pred_prec, transition, filt_means, terminal_mean):
    steps, panel, order = filtered_covariance.shape
    devices, blocks = lax.axis_size("state"), lax.axis_size("tm")
    repeat, half = devices // steps, devices // 2

    def swap(x, off):
        return lax.ppermute(x, "state", [(i, i ^ off) for i in range(devices)])

    def swap_blocks(x, off):
        return lax.ppermute(x, "tm", [(i, i ^ off) for i in range(blocks)])

    def shape(*dims):
        return jax.ShapeDtypeStruct(dims, F32)

    cov, prec, trans, means = (
        pltpu.with_memory_space_constraint(x, pltpu.HBM)
        for x in (filtered_covariance, pred_prec, transition, filt_means)
    )
    widths = [width(devices, panel, order, off) for off in range(1, devices)]
    *pieces, trans_half, first = pl.pallas_call(
        functools.partial(pack_kernel, devices, repeat),
        out_shape=[shape(2, panel, w) for w in widths] + [shape(panel // 2, order), shape(1, order)],
        in_specs=[HBM, HBM, HBM, VMEM],
        out_specs=[VMEM] * (devices + 1),
        scratch_shapes=[pltpu.SemaphoreType.DMA((2 * devices,))],
        compiler_params=params(4),
        name="pack",
    )(cov, prec, trans, terminal_mean[None])

    across = swap(trans_half, half)
    arrived = [swap(piece, off) for off, piece in enumerate(pieces, 1)]
    around = swap_blocks(across, 1)
    near = [swap(x, off) for off in range(1, half) for x in (transition, across, around)]

    gain, info = pl.pallas_call(
        functools.partial(gain_kernel, devices, repeat),
        out_shape=(shape(order, order), shape(16, order)),
        in_specs=[HBM] * 4 + [ANY] * (2 + len(near) + len(arrived)),
        out_specs=(VMEM, VMEM),
        scratch_shapes=[
            pltpu.VMEM((order + 16, order), F32),
            pltpu.VMEM((order, order), F32),
            pltpu.VMEM((order, order), F32),
            pltpu.SemaphoreType.DMA((6 + len(near) + 2 * len(arrived),)),
        ],
        compiler_params=params(16),
        name="gain",
    )(cov, prec, means, trans, across, around, *near, *arrived)

    partner = swap(gain, repeat)
    c, late, vec = pl.pallas_call(
        functools.partial(pair_kernel, repeat),
        out_shape=(shape(order, order), shape(order, order), shape(8, order)),
        in_specs=[ANY, ANY, VMEM],
        out_specs=(VMEM, VMEM, VMEM),
        scratch_shapes=[pltpu.VMEM((2, order, order), F32), pltpu.SemaphoreType.DMA((2,))],
        compiler_params=params(12),
        name="pair",
    )(gain, partner, info)

    hop = pl.pallas_call(
        hop_kernel,
        out_shape=shape(1, order),
        in_specs=[VMEM] * 3,
        out_specs=VMEM,
        compiler_params=params(4),
        name="hop",
    )
    incoming = [first]
    for block in range(blocks - 1, -1, -1):
        incoming.append(swap(hop(incoming[-1], c, vec), half ^ 1))
        if block:
            incoming.append(swap_blocks(hop(incoming[-1], c, vec), block ^ (block - 1)))

    mine, theirs = pl.pallas_call(
        functools.partial(last_kernel, devices),
        out_shape=(shape(2, panel), shape(2, panel)),
        in_specs=[VMEM] * (len(incoming) + 3),
        out_specs=(VMEM, VMEM),
        scratch_shapes=[pltpu.VMEM((devices, 2, panel), F32)],
        compiler_params=params(6),
        name="last",
    )(*incoming, c, late, vec)
    return pl.pallas_call(
        functools.partial(out_kernel, devices),
        out_shape=shape(steps, panel),
        in_specs=[VMEM, VMEM],
        out_specs=VMEM,
        compiler_params=params(4),
        name="out",
    )(mine, swap(theirs, half ^ 1))


def solution(mesh):
    return jax.shard_map(
        local,
        mesh=mesh,
        in_specs=(
            P("tm", "state", None),
            P("tm", "state", None),
            P("state", None),
            P("tm", None),
            P(),
        ),
        out_specs=P("tm", "state"),
        check_vma=False,
    )
```

time: 102 us -> 86.9 us (0.85)
  starting transfers between devices: 68.8 us -> 26 us
  waiting for transfers between devices: 18.6 us -> 50.1 us
  local copies, waits for them, and re-layouts: 6.32 us -> 0.68 us
  Pallas kernels: 6.33 us -> 9.72 us
    ppermute x10 -> x17, starting transfers between devices: 58.9 us -> 8.1 us  [swap(): return lax.ppermute(x, 'state', [(i, i ^ off) for i in range(devices)])]
    ppermute x15 -> x8, waiting for transfers between devices: 0.04 us -> 16.6 us  [swap_blocks(): return lax.ppermute(x, 'tm', [(i, i ^ off) for i in range(blocks)])]
    ppermute x10 -> x17, waiting for transfers between devices: 18.6 us -> 33.5 us  [swap(): return lax.ppermute(x, 'state', [(i, i ^ off) for i in range(devices)])]
    ppermute x15 -> x8, starting transfers between devices: 9.92 us -> 17.9 us  [swap_blocks(): return lax.ppermute(x, 'tm', [(i, i ^ off) for i in range(blocks)])]
    unnamed x20 -> x4, local copies, waits for them, and re-layouts: 6.31 us -> 0.68 us
    pallas_call x1, Pallas kernels: 2.39 us -> 3.96 us  [local(): pl.pallas_call(functools.partial(gain_kernel, devices, repeat), out_shape...]
    pallas_call x1, Pallas kernels: 0.16 us -> 1.4 us  [local(): pl.pallas_call(functools.partial(pack_kernel, devices, repeat), out_shape...]
    pallas_call x17 -> x18, Pallas kernels: 3.79 us -> 4.36 us  [the longest x8 1.26 us: local(): incoming.append(swap(hop(incoming[-1], c, vec), half ^ 1))]
  transfers between devices with their start and end apart: 25 -> 25, of which waited for: 5 -> 21; matrix products, arithmetic and copies ran while one was open for 0% -> 0% of each run, Pallas kernels for 0% -> 0%
where the time goes in v3:
time: 86.9 us; the launch traced here: 86.7 us
  waiting for transfers between devices  50.1 us (58%)
  starting transfers between devices  26 us (30%)
  Pallas kernels  9.72 us (11%)
    ppermute x17, waiting for transfers between devices, swap(): return lax.ppermute(x, 'state', [(i, i ^ off) for i in range(devices)])  33.5 us
    ppermute x8, starting transfers between devices, swap_blocks(): return lax.ppermute(x, 'tm', [(i, i ^ off) for i in range(blocks)])  17.9 us
    ppermute x8, waiting for transfers between devices, swap_blocks(): return lax.ppermute(x, 'tm', [(i, i ^ off) for i in range(blocks)])  16.6 us
    ppermute x17, starting transfers between devices, swap(): return lax.ppermute(x, 'state', [(i, i ^ off) for i in range(devices)])  8.1 us
    pallas_call x1, Pallas kernels, local(): pl.pallas_call(functools.partial(gain_kernel, devices, repeat), out_shape...  3.96 us
  transfers between devices with their start and end apart: 25, of which 21 were waited for; matrix products, arithmetic and copies ran while one was open for 0% of the time, Pallas kernels for 0%

profile of v3, /device:TPU:0, one launch (start us, length us, event | category | flops | bytes accessed | tf_op | source)
XLA Modules:
  0.0 86.7 jit_solution(3221251801320046024)
XLA Ops:
  0.7 1.4 %pack.1 = (f32[2,128,512]{2,1,0:T(8,128)S(1)}, f32[2,128,256]{2,1,0:T(8,128)S(1)}, f32[2,128,128]{2,1,0:T(8,128)S(1)}, f32[64,512]{1,0:T(8,128)S(1)}, f32[1,512]{1,0:T(1,128)S(1)}) custom-call(f32[4,128,512]{2,1,0:T(8,128)} %refs_0_.1, f32[4,128,512]{2,1,0:T(8,128)} %refs_1_.1, f32[128,512]{1,0:T(8,128)} %refs_3_.1, f32[1,512]{1,0:T(1,128)S(1)} %bitcast.1), custom_call_target="tpu_custom_call" | custom-call | tf_op jit(solution)/shard_map/pack/pallas_call | solution.py:222
  2.6 2.6 %collective-permute-start = (f32[64,512]{1,0:T(8,128)S(1)}, f32[64,512]{1,0:T(8,128)S(1)}, u32[]{:S(2)}, u32[]{:S(2)}) collective-permute-start(f32[64,512]{1,0:T(8,128)S(1)} %get-tuple-element.18), channel_id=1, source_target_pairs={{0,2},{1,3},{2,0},{3,1},{4,6},{5,7},{6,4},{7,5},{8,10},{9,11},{10,... | collective-permute-start | bytes 393224 | tf_op jit(solution)/shard_map/ppermute | solution.py:209
  5.4 1.9 %collective-permute-start.6 = (f32[2,128,256]{2,1,0:T(8,128)S(1)}, f32[2,128,256]{2,1,0:T(8,128)S(1)}, u32[]{:S(2)}, u32[]{:S(2)}) collective-permute-start(f32[2,128,256]{2,1,0:T(8,128)S(1)} %get-tuple-element.20), channel_id=1, source_target_pairs={{0,2},{1,3},{2,0},{3,1},{4,6},{5,7},{6,4},{7,5},{8,10},{9,11},{10,... | collective-permute-start | bytes 786440 | tf_op jit(solution)/shard_map/ppermute | solution.py:209
  7.3 2.2 %collective-permute-done.refs_4_ = f32[64,512]{1,0:T(8,128)S(1)} collective-permute-done((f32[64,512]{1,0:T(8,128)S(1)}, f32[64,512]{1,0:T(8,128)S(1)}, u32[]{:S(2)}, u32[]{:S(2)}) %collective-permute-start) | collective-permute-done | bytes 131104 | tf_op jit(solution)/shard_map/ppermute | solution.py:209
  9.5 2.0 %collective-permute-start.1 = (f32[64,512]{1,0:T(8,128)S(1)}, f32[64,512]{1,0:T(8,128)S(1)}, u32[]{:S(2)}, u32[]{:S(2)}) collective-permute-start(f32[64,512]{1,0:T(8,128)S(1)} %collective-permute-done.refs_4_), channel_id=1, source_target_pairs={{0,4},{4,0},{8,12},{12,8},{16,20},{20,16},{24,28},{28,24},{1,5},{5... | collective-permute-start | bytes 393224 | tf_op jit(solution)/shard_map/ppermute | solution.py:212
  12.1 2.4 %collective-permute-done.1.refs_5_ = f32[64,512]{1,0:T(8,128)S(1)} collective-permute-done((f32[64,512]{1,0:T(8,128)S(1)}, f32[64,512]{1,0:T(8,128)S(1)}, u32[]{:S(2)}, u32[]{:S(2)}) %collective-permute-start.1) | collective-permute-done | bytes 131104 | tf_op jit(solution)/shard_map/ppermute | solution.py:212
  14.5 3.2 %collective-permute-done.6.refs_10_ = f32[2,128,256]{2,1,0:T(8,128)S(1)} collective-permute-done((f32[2,128,256]{2,1,0:T(8,128)S(1)}, f32[2,128,256]{2,1,0:T(8,128)S(1)}, u32[]{:S(2)}, u32[]{:S(2)}) %collective-permute-start.6) | collective-permute-done | bytes 262176 | tf_op jit(solution)/shard_map/ppermute | solution.py:209
  17.7 4.0 %gain.1 = (f32[512,512]{1,0:T(8,128)S(1)}, f32[16,512]{1,0:T(8,128)S(1)}) custom-call(f32[4,128,512]{2,1,0:T(8,128)} %refs_0_.1, f32[4,128,512]{2,1,0:T(8,128)} %refs_1_.1, f32[4,512]{1,0:T(4,128)} %refs_2_.1, f32[128,512]{1,0:T(8,128)} %refs_3_.1, f32[64,512]{1,0:T(8,128)S(1)} %collective-permute-done.refs_4_, ...), custom_call_target="tpu_custom_call" | custom-call | tf_op jit(solution)/shard_map/gain/pallas_call | solution.py:237
  21.7 2.6 %collective-permute-done.8.partner = f32[512,512]{1,0:T(8,128)S(1)} collective-permute-done((f32[512,512]{1,0:T(8,128)S(1)}, f32[512,512]{1,0:T(8,128)S(1)}, u32[]{:S(2)}, u32[]{:S(2)}) %collective-permute-start.8) | collective-permute-done | bytes 1048608 | tf_op jit(solution)/shard_map/ppermute | solution.py:209
  25.7 1.6 %collective-permute-start.9 = (f32[1,512]{1,0:T(1,128)S(1)}, f32[1,512]{1,0:T(1,128)S(1)}, u32[]{:S(2)}, u32[]{:S(2)}) collective-permute-start(f32[1,512]{1,0:T(1,128)S(1)} %hop.15), channel_id=1, source_target_pairs={{0,3},{1,2},{2,1},{3,0},{4,7},{5,6},{6,5},{7,4},{8,11},{9,10},{10,... | collective-permute-start | bytes 6152 | tf_op jit(solution)/shard_map/ppermute | solution.py:209
  27.3 1.5 %collective-permute-done.9.x_ref.refs_1_ = f32[1,512]{1,0:T(1,128)S(1)} collective-permute-done((f32[1,512]{1,0:T(1,128)S(1)}, f32[1,512]{1,0:T(1,128)S(1)}, u32[]{:S(2)}, u32[]{:S(2)}) %collective-permute-start.9) | collective-permute-done | bytes 2080 | tf_op jit(solution)/shard_map/ppermute | solution.py:209
  29.0 1.9 %collective-permute-start.10 = (f32[1,512]{1,0:T(1,128)S(1)}, f32[1,512]{1,0:T(1,128)S(1)}, u32[]{:S(2)}, u32[]{:S(2)}) collective-permute-start(f32[1,512]{1,0:T(1,128)S(1)} %hop.16), channel_id=1, source_target_pairs={{0,4},{4,0},{8,12},{12,8},{16,20},{20,16},{24,28},{28,24},{1,5},{5... | collective-permute-start | bytes 6152 | tf_op jit(solution)/shard_map/ppermute | solution.py:212
  30.8 1.8 %collective-permute-done.10.x_ref.refs_2_ = f32[1,512]{1,0:T(1,128)S(1)} collective-permute-done((f32[1,512]{1,0:T(1,128)S(1)}, f32[1,512]{1,0:T(1,128)S(1)}, u32[]{:S(2)}, u32[]{:S(2)}) %collective-permute-start.10) | collective-permute-done | bytes 2080 | tf_op jit(solution)/shard_map/ppermute | solution.py:212
  33.2 2.7 %collective-permute-done.11.x_ref.refs_3_ = f32[1,512]{1,0:T(1,128)S(1)} collective-permute-done((f32[1,512]{1,0:T(1,128)S(1)}, f32[1,512]{1,0:T(1,128)S(1)}, u32[]{:S(2)}, u32[]{:S(2)}) %collective-permute-start.11) | collective-permute-done | bytes 2080 | tf_op jit(solution)/shard_map/ppermute | solution.py:209
  36.0 2.9 %collective-permute-start.12 = (f32[1,512]{1,0:T(1,128)S(1)}, f32[1,512]{1,0:T(1,128)S(1)}, u32[]{:S(2)}, u32[]{:S(2)}) collective-permute-start(f32[1,512]{1,0:T(1,128)S(1)} %hop.18), channel_id=1, source_target_pairs={{0,12},{4,8},{8,4},{12,0},{16,28},{20,24},{24,20},{28,16},{1,13},{... | collective-permute-start | bytes 6152 | tf_op jit(solution)/shard_map/ppermute | solution.py:212
  38.9 1.7 %collective-permute-done.12.x_ref.refs_4_ = f32[1,512]{1,0:T(1,128)S(1)} collective-permute-done((f32[1,512]{1,0:T(1,128)S(1)}, f32[1,512]{1,0:T(1,128)S(1)}, u32[]{:S(2)}, u32[]{:S(2)}) %collective-permute-start.12) | collective-permute-done | bytes 2080 | tf_op jit(solution)/shard_map/ppermute | solution.py:212
  40.8 3.0 %collective-permute-done.13.x_ref.refs_5_ = f32[1,512]{1,0:T(1,128)S(1)} collective-permute-done((f32[1,512]{1,0:T(1,128)S(1)}, f32[1,512]{1,0:T(1,128)S(1)}, u32[]{:S(2)}, u32[]{:S(2)}) %collective-permute-start.13) | collective-permute-done | bytes 2080 | tf_op jit(solution)/shard_map/ppermute | solution.py:209
  44.0 1.9 %collective-permute-start.14 = (f32[1,512]{1,0:T(1,128)S(1)}, f32[1,512]{1,0:T(1,128)S(1)}, u32[]{:S(2)}, u32[]{:S(2)}) collective-permute-start(f32[1,512]{1,0:T(1,128)S(1)} %hop.20), channel_id=1, source_target_pairs={{0,4},{4,0},{8,12},{12,8},{16,20},{20,16},{24,28},{28,24},{1,5},{5... | collective-permute-start | bytes 6152 | tf_op jit(solution)/shard_map/ppermute | solution.py:212
  45.8 1.8 %collective-permute-done.14.x_ref.refs_6_ = f32[1,512]{1,0:T(1,128)S(1)} collective-permute-done((f32[1,512]{1,0:T(1,128)S(1)}, f32[1,512]{1,0:T(1,128)S(1)}, u32[]{:S(2)}, u32[]{:S(2)}) %collective-permute-start.14) | collective-permute-done | bytes 2080 | tf_op jit(solution)/shard_map/ppermute | solution.py:212
  47.9 3.0 %collective-permute-done.15.x_ref.refs_7_ = f32[1,512]{1,0:T(1,128)S(1)} collective-permute-done((f32[1,512]{1,0:T(1,128)S(1)}, f32[1,512]{1,0:T(1,128)S(1)}, u32[]{:S(2)}, u32[]{:S(2)}) %collective-permute-start.15) | collective-permute-done | bytes 2080 | tf_op jit(solution)/shard_map/ppermute | solution.py:209
  51.0 4.9 %collective-permute-start.16 = (f32[1,512]{1,0:T(1,128)S(1)}, f32[1,512]{1,0:T(1,128)S(1)}, u32[]{:S(2)}, u32[]{:S(2)}) collective-permute-start(f32[1,512]{1,0:T(1,128)S(1)} %hop.22), channel_id=1, source_target_pairs={{0,28},{4,24},{8,20},{12,16},{16,12},{20,8},{24,4},{28,0},{1,29},{... | collective-permute-start | bytes 6152 | tf_op jit(solution)/shard_map/ppermute | solution.py:212
  55.9 1.6 %collective-permute-done.16.x_ref.refs_8_ = f32[1,512]{1,0:T(1,128)S(1)} collective-permute-done((f32[1,512]{1,0:T(1,128)S(1)}, f32[1,512]{1,0:T(1,128)S(1)}, u32[]{:S(2)}, u32[]{:S(2)}) %collective-permute-start.16) | collective-permute-done | bytes 2080 | tf_op jit(solution)/shard_map/ppermute | solution.py:212
  57.7 3.0 %collective-permute-done.17.x_ref.refs_9_ = f32[1,512]{1,0:T(1,128)S(1)} collective-permute-done((f32[1,512]{1,0:T(1,128)S(1)}, f32[1,512]{1,0:T(1,128)S(1)}, u32[]{:S(2)}, u32[]{:S(2)}) %collective-permute-start.17) | collective-permute-done | bytes 2080 | tf_op jit(solution)/shard_map/ppermute | solution.py:209
  60.9 1.7 %collective-permute-start.18 = (f32[1,512]{1,0:T(1,128)S(1)}, f32[1,512]{1,0:T(1,128)S(1)}, u32[]{:S(2)}, u32[]{:S(2)}) collective-permute-start(f32[1,512]{1,0:T(1,128)S(1)} %hop.24), channel_id=1, source_target_pairs={{0,4},{4,0},{8,12},{12,8},{16,20},{20,16},{24,28},{28,24},{1,5},{5... | collective-permute-start | bytes 6152 | tf_op jit(solution)/shard_map/ppermute | solution.py:212
  62.6 1.9 %collective-permute-done.18.x_ref.refs_10_ = f32[1,512]{1,0:T(1,128)S(1)} collective-permute-done((f32[1,512]{1,0:T(1,128)S(1)}, f32[1,512]{1,0:T(1,128)S(1)}, u32[]{:S(2)}, u32[]{:S(2)}) %collective-permute-start.18) | collective-permute-done | bytes 2080 | tf_op jit(solution)/shard_map/ppermute | solution.py:212
  64.8 3.0 %collective-permute-done.19.x_ref.refs_11_ = f32[1,512]{1,0:T(1,128)S(1)} collective-permute-done((f32[1,512]{1,0:T(1,128)S(1)}, f32[1,512]{1,0:T(1,128)S(1)}, u32[]{:S(2)}, u32[]{:S(2)}) %collective-permute-start.19) | collective-permute-done | bytes 2080 | tf_op jit(solution)/shard_map/ppermute | solution.py:209
  68.9 3.6 %collective-permute-done.20.x_ref.refs_12_ = f32[1,512]{1,0:T(1,128)S(1)} collective-permute-done((f32[1,512]{1,0:T(1,128)S(1)}, f32[1,512]{1,0:T(1,128)S(1)}, u32[]{:S(2)}, u32[]{:S(2)}) %collective-permute-start.20) | collective-permute-done | bytes 2080 | tf_op jit(solution)/shard_map/ppermute | solution.py:212
  72.7 3.0 %collective-permute-done.21.x_ref.refs_13_ = f32[1,512]{1,0:T(1,128)S(1)} collective-permute-done((f32[1,512]{1,0:T(1,128)S(1)}, f32[1,512]{1,0:T(1,128)S(1)}, u32[]{:S(2)}, u32[]{:S(2)}) %collective-permute-start.21) | collective-permute-done | bytes 2080 | tf_op jit(solution)/shard_map/ppermute | solution.py:209
  75.9 1.7 %collective-permute-start.22 = (f32[1,512]{1,0:T(1,128)S(1)}, f32[1,512]{1,0:T(1,128)S(1)}, u32[]{:S(2)}, u32[]{:S(2)}) collective-permute-start(f32[1,512]{1,0:T(1,128)S(1)} %hop.28), channel_id=1, source_target_pairs={{0,4},{4,0},{8,12},{12,8},{16,20},{20,16},{24,28},{28,24},{1,5},{5... | collective-permute-start | bytes 6152 | tf_op jit(solution)/shard_map/ppermute | solution.py:212
  77.7 1.9 %collective-permute-done.22.x_ref.refs_14_ = f32[1,512]{1,0:T(1,128)S(1)} collective-permute-done((f32[1,512]{1,0:T(1,128)S(1)}, f32[1,512]{1,0:T(1,128)S(1)}, u32[]{:S(2)}, u32[]{:S(2)}) %collective-permute-start.22) | collective-permute-done | bytes 2080 | tf_op jit(solution)/shard_map/ppermute | solution.py:212
  79.8 3.0 %collective-permute-done.23.refs_15_ = f32[1,512]{1,0:T(1,128)S(1)} collective-permute-done((f32[1,512]{1,0:T(1,128)S(1)}, f32[1,512]{1,0:T(1,128)S(1)}, u32[]{:S(2)}, u32[]{:S(2)}) %collective-permute-start.23) | collective-permute-done | bytes 2080 | tf_op jit(solution)/shard_map/ppermute | solution.py:209
  83.1 3.0 %collective-permute-done.24.theirs_ref = f32[2,128]{1,0:T(2,128)S(1)} collective-permute-done((f32[2,128]{1,0:T(2,128)S(1)}, f32[2,128]{1,0:T(2,128)S(1)}, u32[]{:S(2)}, u32[]{:S(2)}) %collective-permute-start.24) | collective-permute-done | bytes 1056 | tf_op jit(solution)/shard_map/ppermute | solution.py:209
  (42 shorter events, 8.4 us)
Async XLA Ops:
  0.0 0.7 copy-start
  0.7 4.5 %copy-start.1 = (f32[128,512]{1,0:T(8,128)S(1)}, f32[128,512]{1,0:T(8,128)}, u32[]{:S(2)}) copy-start(f32[128,512]{1,0:T(8,128)} %refs_3_.1) | copy-start | bytes 786436
  2.1 15.6 %collective-permute-start.5 = (f32[2,128,512]{2,1,0:T(8,128)S(1)}, f32[2,128,512]{2,1,0:T(8,128)S(1)}, u32[]{:S(2)}, u32[]{:S(2)}) collective-permute-start(f32[2,128,512]{2,1,0:T(8,128)S(1)} %get-tuple-element.19), channel_id=1, source_target_pairs={{0,1},{1,0},{2,3},{3,2},{4,5},{5,4},{6,7},{7,6},{8,9},{9,8},{10,11... | collective-permute-start | bytes 1572872 | tf_op jit(solution)/shard_map/ppermute | solution.py:209
  2.6 6.9 %collective-permute-start = (f32[64,512]{1,0:T(8,128)S(1)}, f32[64,512]{1,0:T(8,128)S(1)}, u32[]{:S(2)}, u32[]{:S(2)}) collective-permute-start(f32[64,512]{1,0:T(8,128)S(1)} %get-tuple-element.18), channel_id=1, source_target_pairs={{0,2},{1,3},{2,0},{3,1},{4,6},{5,7},{6,4},{7,5},{8,10},{9,11},{10,... | collective-permute-start | bytes 393224 | tf_op jit(solution)/shard_map/ppermute | solution.py:209
  5.2 9.3 %collective-permute-start.2 = (f32[128,512]{1,0:T(8,128)S(1)}, f32[128,512]{1,0:T(8,128)S(1)}, u32[]{:S(2)}, u32[]{:S(2)}) collective-permute-start(f32[128,512]{1,0:T(8,128)S(1)} %copy-done.1), channel_id=1, source_target_pairs={{0,1},{1,0},{2,3},{3,2},{4,5},{5,4},{6,7},{7,6},{8,9},{9,8},{10,11... | collective-permute-start | bytes 786440 | tf_op jit(solution)/shard_map/ppermute | solution.py:209
  5.3 6.5 %collective-permute-start.7 = (f32[2,128,128]{2,1,0:T(8,128)S(1)}, f32[2,128,128]{2,1,0:T(8,128)S(1)}, u32[]{:S(2)}, u32[]{:S(2)}) collective-permute-start(f32[2,128,128]{2,1,0:T(8,128)S(1)} %get-tuple-element.21), channel_id=1, source_target_pairs={{0,3},{1,2},{2,1},{3,0},{4,7},{5,6},{6,5},{7,4},{8,11},{9,10},{10,... | collective-permute-start | bytes 393224 | tf_op jit(solution)/shard_map/ppermute | solution.py:209
  5.4 12.3 %collective-permute-start.6 = (f32[2,128,256]{2,1,0:T(8,128)S(1)}, f32[2,128,256]{2,1,0:T(8,128)S(1)}, u32[]{:S(2)}, u32[]{:S(2)}) collective-permute-start(f32[2,128,256]{2,1,0:T(8,128)S(1)} %get-tuple-element.20), channel_id=1, source_target_pairs={{0,2},{1,3},{2,0},{3,1},{4,6},{5,7},{6,4},{7,5},{8,10},{9,11},{10,... | collective-permute-start | bytes 786440 | tf_op jit(solution)/shard_map/ppermute | solution.py:209
  9.5 5.0 %collective-permute-start.1 = (f32[64,512]{1,0:T(8,128)S(1)}, f32[64,512]{1,0:T(8,128)S(1)}, u32[]{:S(2)}, u32[]{:S(2)}) collective-permute-start(f32[64,512]{1,0:T(8,128)S(1)} %collective-permute-done.refs_4_), channel_id=1, source_target_pairs={{0,4},{4,0},{8,12},{12,8},{16,20},{20,16},{24,28},{28,24},{1,5},{5... | collective-permute-start | bytes 393224 | tf_op jit(solution)/shard_map/ppermute | solution.py:212
  11.8 2.7 %collective-permute-start.3 = (f32[64,512]{1,0:T(8,128)S(1)}, f32[64,512]{1,0:T(8,128)S(1)}, u32[]{:S(2)}, u32[]{:S(2)}) collective-permute-start(f32[64,512]{1,0:T(8,128)S(1)} %collective-permute-done.refs_4_), channel_id=1, source_target_pairs={{0,1},{1,0},{2,3},{3,2},{4,5},{5,4},{6,7},{7,6},{8,9},{9,8},{10,11... | collective-permute-start | bytes 393224 | tf_op jit(solution)/shard_map/ppermute | solution.py:209
  14.5 3.2 %collective-permute-start.4 = (f32[64,512]{1,0:T(8,128)S(1)}, f32[64,512]{1,0:T(8,128)S(1)}, u32[]{:S(2)}, u32[]{:S(2)}) collective-permute-start(f32[64,512]{1,0:T(8,128)S(1)} %collective-permute-done.1.refs_5_), channel_id=1, source_target_pairs={{0,1},{1,0},{2,3},{3,2},{4,5},{5,4},{6,7},{7,6},{8,9},{9,8},{10,11... | collective-permute-start | bytes 393224 | tf_op jit(solution)/shard_map/ppermute | solution.py:209
  21.7 2.7 %collective-permute-start.8 = (f32[512,512]{1,0:T(8,128)S(1)}, f32[512,512]{1,0:T(8,128)S(1)}, u32[]{:S(2)}, u32[]{:S(2)}) collective-permute-start(f32[512,512]{1,0:T(8,128)S(1)} %get-tuple-element.22.own), channel_id=1, source_target_pairs={{0,1},{1,0},{2,3},{3,2},{4,5},{5,4},{6,7},{7,6},{8,9},{9,8},{10,11... | collective-permute-start | bytes 3145736 | tf_op jit(solution)/shard_map/ppermute | solution.py:209
  25.7 3.1 %collective-permute-start.9 = (f32[1,512]{1,0:T(1,128)S(1)}, f32[1,512]{1,0:T(1,128)S(1)}, u32[]{:S(2)}, u32[]{:S(2)}) collective-permute-start(f32[1,512]{1,0:T(1,128)S(1)} %hop.15), channel_id=1, source_target_pairs={{0,3},{1,2},{2,1},{3,0},{4,7},{5,6},{6,5},{7,4},{8,11},{9,10},{10,... | collective-permute-start | bytes 6152 | tf_op jit(solution)/shard_map/ppermute | solution.py:209
  29.0 3.7 %collective-permute-start.10 = (f32[1,512]{1,0:T(1,128)S(1)}, f32[1,512]{1,0:T(1,128)S(1)}, u32[]{:S(2)}, u32[]{:S(2)}) collective-permute-start(f32[1,512]{1,0:T(1,128)S(1)} %hop.16), channel_id=1, source_target_pairs={{0,4},{4,0},{8,12},{12,8},{16,20},{20,16},{24,28},{28,24},{1,5},{5... | collective-permute-start | bytes 6152 | tf_op jit(solution)/shard_map/ppermute | solution.py:212
  32.8 3.1 %collective-permute-start.11 = (f32[1,512]{1,0:T(1,128)S(1)}, f32[1,512]{1,0:T(1,128)S(1)}, u32[]{:S(2)}, u32[]{:S(2)}) collective-permute-start(f32[1,512]{1,0:T(1,128)S(1)} %hop.17), channel_id=1, source_target_pairs={{0,3},{1,2},{2,1},{3,0},{4,7},{5,6},{6,5},{7,4},{8,11},{9,10},{10,... | collective-permute-start | bytes 6152 | tf_op jit(solution)/shard_map/ppermute | solution.py:209
  36.0 4.5 %collective-permute-start.12 = (f32[1,512]{1,0:T(1,128)S(1)}, f32[1,512]{1,0:T(1,128)S(1)}, u32[]{:S(2)}, u32[]{:S(2)}) collective-permute-start(f32[1,512]{1,0:T(1,128)S(1)} %hop.18), channel_id=1, source_target_pairs={{0,12},{4,8},{8,4},{12,0},{16,28},{20,24},{24,20},{28,16},{1,13},{... | collective-permute-start | bytes 6152 | tf_op jit(solution)/shard_map/ppermute | solution.py:212
  40.8 3.1 %collective-permute-start.13 = (f32[1,512]{1,0:T(1,128)S(1)}, f32[1,512]{1,0:T(1,128)S(1)}, u32[]{:S(2)}, u32[]{:S(2)}) collective-permute-start(f32[1,512]{1,0:T(1,128)S(1)} %hop.19), channel_id=1, source_target_pairs={{0,3},{1,2},{2,1},{3,0},{4,7},{5,6},{6,5},{7,4},{8,11},{9,10},{10,... | collective-permute-start | bytes 6152 | tf_op jit(solution)/shard_map/ppermute | solution.py:209
  44.0 3.7 %collective-permute-start.14 = (f32[1,512]{1,0:T(1,128)S(1)}, f32[1,512]{1,0:T(1,128)S(1)}, u32[]{:S(2)}, u32[]{:S(2)}) collective-permute-start(f32[1,512]{1,0:T(1,128)S(1)} %hop.20), channel_id=1, source_target_pairs={{0,4},{4,0},{8,12},{12,8},{16,20},{20,16},{24,28},{28,24},{1,5},{5... | collective-permute-start | bytes 6152 | tf_op jit(solution)/shard_map/ppermute | solution.py:212
  47.8 3.1 %collective-permute-start.15 = (f32[1,512]{1,0:T(1,128)S(1)}, f32[1,512]{1,0:T(1,128)S(1)}, u32[]{:S(2)}, u32[]{:S(2)}) collective-permute-start(f32[1,512]{1,0:T(1,128)S(1)} %hop.21), channel_id=1, source_target_pairs={{0,3},{1,2},{2,1},{3,0},{4,7},{5,6},{6,5},{7,4},{8,11},{9,10},{10,... | collective-permute-start | bytes 6152 | tf_op jit(solution)/shard_map/ppermute | solution.py:209
  51.0 6.5 %collective-permute-start.16 = (f32[1,512]{1,0:T(1,128)S(1)}, f32[1,512]{1,0:T(1,128)S(1)}, u32[]{:S(2)}, u32[]{:S(2)}) collective-permute-start(f32[1,512]{1,0:T(1,128)S(1)} %hop.22), channel_id=1, source_target_pairs={{0,28},{4,24},{8,20},{12,16},{16,12},{20,8},{24,4},{28,0},{1,29},{... | collective-permute-start | bytes 6152 | tf_op jit(solution)/shard_map/ppermute | solution.py:212
  57.7 3.1 %collective-permute-start.17 = (f32[1,512]{1,0:T(1,128)S(1)}, f32[1,512]{1,0:T(1,128)S(1)}, u32[]{:S(2)}, u32[]{:S(2)}) collective-permute-start(f32[1,512]{1,0:T(1,128)S(1)} %hop.23), channel_id=1, source_target_pairs={{0,3},{1,2},{2,1},{3,0},{4,7},{5,6},{6,5},{7,4},{8,11},{9,10},{10,... | collective-permute-start | bytes 6152 | tf_op jit(solution)/shard_map/ppermute | solution.py:209
  60.9 3.7 %collective-permute-start.18 = (f32[1,512]{1,0:T(1,128)S(1)}, f32[1,512]{1,0:T(1,128)S(1)}, u32[]{:S(2)}, u32[]{:S(2)}) collective-permute-start(f32[1,512]{1,0:T(1,128)S(1)} %hop.24), channel_id=1, source_target_pairs={{0,4},{4,0},{8,12},{12,8},{16,20},{20,16},{24,28},{28,24},{1,5},{5... | collective-permute-start | bytes 6152 | tf_op jit(solution)/shard_map/ppermute | solution.py:212
  64.7 3.1 %collective-permute-start.19 = (f32[1,512]{1,0:T(1,128)S(1)}, f32[1,512]{1,0:T(1,128)S(1)}, u32[]{:S(2)}, u32[]{:S(2)}) collective-permute-start(f32[1,512]{1,0:T(1,128)S(1)} %hop.25), channel_id=1, source_target_pairs={{0,3},{1,2},{2,1},{3,0},{4,7},{5,6},{6,5},{7,4},{8,11},{9,10},{10,... | collective-permute-start | bytes 6152 | tf_op jit(solution)/shard_map/ppermute | solution.py:209
  68.0 4.5 %collective-permute-start.20 = (f32[1,512]{1,0:T(1,128)S(1)}, f32[1,512]{1,0:T(1,128)S(1)}, u32[]{:S(2)}, u32[]{:S(2)}) collective-permute-start(f32[1,512]{1,0:T(1,128)S(1)} %hop.26), channel_id=1, source_target_pairs={{0,12},{4,8},{8,4},{12,0},{16,28},{20,24},{24,20},{28,16},{1,13},{... | collective-permute-start | bytes 6152 | tf_op jit(solution)/shard_map/ppermute | solution.py:212
  72.7 3.1 %collective-permute-start.21 = (f32[1,512]{1,0:T(1,128)S(1)}, f32[1,512]{1,0:T(1,128)S(1)}, u32[]{:S(2)}, u32[]{:S(2)}) collective-permute-start(f32[1,512]{1,0:T(1,128)S(1)} %hop.27), channel_id=1, source_target_pairs={{0,3},{1,2},{2,1},{3,0},{4,7},{5,6},{6,5},{7,4},{8,11},{9,10},{10,... | collective-permute-start | bytes 6152 | tf_op jit(solution)/shard_map/ppermute | solution.py:209
  75.9 3.7 %collective-permute-start.22 = (f32[1,512]{1,0:T(1,128)S(1)}, f32[1,512]{1,0:T(1,128)S(1)}, u32[]{:S(2)}, u32[]{:S(2)}) collective-permute-start(f32[1,512]{1,0:T(1,128)S(1)} %hop.28), channel_id=1, source_target_pairs={{0,4},{4,0},{8,12},{12,8},{16,20},{20,16},{24,28},{28,24},{1,5},{5... | collective-permute-start | bytes 6152 | tf_op jit(solution)/shard_map/ppermute | solution.py:212
  79.7 3.1 %collective-permute-start.23 = (f32[1,512]{1,0:T(1,128)S(1)}, f32[1,512]{1,0:T(1,128)S(1)}, u32[]{:S(2)}, u32[]{:S(2)}) collective-permute-start(f32[1,512]{1,0:T(1,128)S(1)} %hop.29), channel_id=1, source_target_pairs={{0,3},{1,2},{2,1},{3,0},{4,7},{5,6},{6,5},{7,4},{8,11},{9,10},{10,... | collective-permute-start | bytes 6152 | tf_op jit(solution)/shard_map/ppermute | solution.py:209
  83.0 3.1 %collective-permute-start.24 = (f32[2,128]{1,0:T(2,128)S(1)}, f32[2,128]{1,0:T(2,128)S(1)}, u32[]{:S(2)}, u32[]{:S(2)}) collective-permute-start(f32[2,128]{1,0:T(2,128)S(1)} %get-tuple-element.28), channel_id=1, source_target_pairs={{0,3},{1,2},{2,1},{3,0},{4,7},{5,6},{6,5},{7,4},{8,11},{9,10},{10,... | collective-permute-start | bytes 3080 | tf_op jit(solution)/shard_map/ppermute | solution.py:209

commit v4 on v0

v4 whole, which is shorter than its diff:
```python
import functools

import jax
import jax.numpy as jnp
from jax import lax
from jax.experimental import pallas as pl
from jax.experimental.pallas import tpu as pltpu
from jax.sharding import PartitionSpec as P

F32, BF16 = jnp.float32, jnp.bfloat16
NN = (((1,), (0,)), ((), ()))
NT = (((1,), (1,)), ((), ()))
ANY = pl.BlockSpec(memory_space=pl.ANY)
HBM = pl.BlockSpec(memory_space=pltpu.HBM)
VMEM = pl.BlockSpec(memory_space=pltpu.VMEM)


def split(x):
    high = x.astype(BF16)
    return high, (x - high.astype(F32)).astype(BF16)


def dot3(a, b, dims):
    (ah, al), (bh, bl) = split(a), split(b)
    dot = functools.partial(lax.dot_general, dimension_numbers=dims, preferred_element_type=F32)
    return dot(ah, bh) + (dot(ah, bl) + dot(al, bh))


def matvec(matrix, row):
    order = matrix.shape[1]
    total = matrix[:, :128] * row[:, :128]
    for j in range(128, order, 128):
        total += matrix[:, j : j + 128] * row[:, j : j + 128]
    return jnp.sum(total.T, axis=0, keepdims=True)


def rows(i, panel):
    return pl.ds(pl.multiple_of(i * panel, panel), panel)


def starter(sems):
    copies = []

    def start(source, target):
        copy = pltpu.make_async_copy(source, target, sems.at[len(copies)])
        copy.start()
        copies.append(copy)

    return start, copies


def width(devices, panel, order, off):
    if off < 2:
        return order
    return panel if devices == 4 and off == 3 and panel % 128 == 0 else order - 2 * panel


def pack_kernel(devices, cov, prec, trans, terminal, *refs):
    pieces, trans_half, first, vector, sems = refs[: 2 * devices - 4], *refs[2 * devices - 4 :]
    steps, panel, order = cov.shape
    b, s = lax.axis_index("tm"), lax.axis_index("state")
    start, copies = starter(sems)
    start(terminal, vector)
    start(trans.at[pl.ds(pl.multiple_of((b % 2) * (panel // 2), panel // 2), panel // 2), :], trans_half)
    for which, matrix in enumerate((cov, prec)):
        for off in range(2, devices):
            mine = pl.ds(((s ^ off) % 2) * (steps // 2), steps // 2)
            w = width(devices, panel, order, off)
            column = 2 * panel if w == order - 2 * panel else pl.multiple_of(s * panel, panel)
            start(matrix.at[mine, :, pl.ds(column, w)], pieces[which * (devices - 2) + off - 2])
    copies[0].wait()
    first[...] = jnp.where(b == lax.axis_size("tm") - 1, vector[...], 0.0)
    for copy in copies[1:]:
        copy.wait()


def load_kernel(cov, prec, trans, means, after, near_cov, near_prec, own_cov, own_prec, own_trans, own_means, sems):
    count = cov.shape[0] // 2
    s = lax.axis_index("state")
    start, copies = starter(sems)
    for matrix, near, own in ((cov, near_cov, own_cov), (prec, near_prec, own_prec)):
        start(matrix.at[pl.ds((1 - s % 2) * count, count)], near)
        start(matrix.at[pl.ds((s % 2) * count, count)], own)
    start(trans, own_trans)
    start(means, own_means)
    for copy in copies:
        copy.wait()


def assemble(devices, start, full, k, own, arrived):
    panel, order = own.shape[1:]
    s = lax.axis_index("state")
    start(own.at[k], full.at[rows(s, panel), :])
    for off, piece in enumerate(arrived, 1):
        i = s ^ off
        w = width(devices, panel, order, off)
        target = full.at[rows(i, panel), :]
        if w < order:
            column = 2 * panel if w == order - 2 * panel else pl.multiple_of(i * panel, panel)
            target = full.at[rows(i, panel), pl.ds(column, w)]
        start(piece.at[k], target)


def mirror(devices, full, panel, order):
    s, known = lax.axis_index("state"), 2 * panel
    full[known:order, :known] = full[:known, known:order].T
    if width(devices, panel, order, 3) < order - known:
        i, j = s ^ 3, s ^ 2
        full[rows(i, panel), rows(j, panel)] = full[rows(j, panel), rows(i, panel)].T


def cov_kernel(devices, *refs):
    own, means, trans, *arrived = refs[: 2 + devices]
    moved = refs[2 + devices : -5]
    out, info, pf, af, sems = refs[-5:]
    count, panel, order = own.shape
    steps = means.shape[0]
    b, s = lax.axis_index("tm"), lax.axis_index("state")
    start, copies = starter(sems)
    for k in range(count):
        assemble(devices, start, pf.at[pl.ds(k * order, order), :], k, own, arrived)
    start(trans, af.at[rows(s, panel), :])
    start(moved[0], af.at[rows(s ^ 1, panel), :])
    spots = [(off ^ near, half) for off in range(2, devices, 2) for near in range(2) for half in range(2)]
    for piece, (off, half) in zip(moved[1:], spots):
        at = (s ^ off) * panel + (b % 2 if half == 0 else 1 - b % 2) * (panel // 2)
        start(piece, af.at[pl.ds(pl.multiple_of(at, panel // 2), panel // 2), :])
    pf[count * order :, :] = jnp.concatenate([means[...], jnp.zeros((16 - steps, order), F32)], axis=0)
    for copy in copies:
        copy.wait()
    for k in range(count):
        mirror(devices, pf.at[pl.ds(k * order, order), :], panel, order)
    product = dot3(pf[...], af[...], NT)
    out[...] = product[: count * order]
    info[:8] = pf[count * order : count * order + 8, :]
    info[8:] = product[count * order : count * order + 8]


def gain_kernel(devices, *refs):
    cov_trans, info, own, *arrived = refs[: 2 + devices]
    map_ref, late_ref, lf, sems = refs[2 + devices :]
    count, panel, order = own.shape
    s = lax.axis_index("state")
    start, copies = starter(sems)
    for k in range(count):
        assemble(devices, start, lf.at[k], k, own, arrived)
    for copy in copies:
        copy.wait()
    for k in range(count):
        mirror(devices, lf.at[k], panel, order)
    ga = dot3(cov_trans[:order], lf[0], NN)
    gb = dot3(cov_trans[order:], lf[1], NN)
    a = (s % 2) * count
    mean_a, mean_b = info[pl.ds(a, 1), :], info[pl.ds(a + 1, 1), :]
    pred_a, pred_b = info[pl.ds(a + 8, 1), :], info[pl.ds(a + 9, 1), :]
    map_ref[order:, :] = jnp.concatenate(
        [mean_a + matvec(ga, mean_b - pred_a), mean_b, pred_b, jnp.zeros((5, order), F32)], axis=0
    )
    map_ref[:order, :] = dot3(ga, gb, NN)
    late_ref[...] = gb


def block_kernel(own, partner, map_ref, slots, sems):
    s, order = lax.axis_index("state"), own.shape[1]
    start, copies = starter(sems)
    start(own, slots.at[s % 2])
    start(partner, slots.at[1 - s % 2])
    for copy in copies:
        copy.wait()
    early, late = slots.at[0], slots.at[1]
    shift = early[order : order + 1, :] + matvec(early[:order, :], late[order : order + 1, :] - early[order + 2 : order + 3, :])
    map_ref[order:, :] = jnp.concatenate([shift, jnp.zeros((1, order), F32), late[order + 2 :, :]], axis=0)
    map_ref[:order, :] = dot3(early[:order, :], late[:order, :], NN)


def apply(map_ref, x):
    order = x.shape[1]
    vec = map_ref[order : order + 8, :]
    return vec[0:1] + matvec(map_ref[:order, :], x - vec[2:3])


def hop_kernel(x_ref, map_ref, out_ref):
    out_ref[...] = apply(map_ref, x_ref[...])


def last_kernel(devices, *refs):
    blocks = len(refs) - 4 - devices
    incoming, (own, partner, late_ref), outs, both = refs[:blocks], refs[blocks : blocks + 3], refs[blocks + 3 : -1], refs[-1]
    order, panel = own.shape[1], outs[0].shape[1]
    b, s = lax.axis_index("tm"), lax.axis_index("state")
    x = incoming[0][...]
    for k, ref in enumerate(incoming[1:], 1):
        x = jnp.where(lax.axis_size("tm") - 1 - b == k, ref[...], x)

    def give(x):
        vec = own[order : order + 8, :]
        later = vec[1:2] + matvec(late_ref[...], x - vec[2:3])
        pair = jnp.concatenate([apply(own, x), later], axis=0)
        for i in range(devices):
            both[i] = pair[:, i * panel : (i + 1) * panel]

    @pl.when(s % 2 == 0)
    def _():
        give(apply(partner, x))

    @pl.when(s % 2 == 1)
    def _():
        give(x)

    for off, out in enumerate(outs):
        out[...] = both[s ^ off]


def out_kernel(*refs):
    given, out_ref = refs[:-1], refs[-1]
    s = lax.axis_index("state")

    def pick(off):
        x = given[0][...]
        for k, ref in enumerate(given[1:], 1):
            x = jnp.where(off == k, ref[...], x)
        return x

    out_ref[...] = jnp.concatenate([pick(s), pick(s ^ 1)], axis=0)


def params(mebibytes):
    return pltpu.CompilerParams(vmem_limit_bytes=mebibytes * 2**20)


def local(filtered_covariance, pred_prec, transition, filt_means, terminal_mean):
    steps, panel, order = filtered_covariance.shape
    devices, blocks = lax.axis_size("state"), lax.axis_size("tm")
    count = steps // 2

    def swap(x, off, block_off=0):
        pairs = [(i, i ^ (block_off * devices + off)) for i in range(blocks * devices)]
        return lax.ppermute(x, ("tm", "state"), pairs)

    def shape(*dims):
        return jax.ShapeDtypeStruct(dims, F32)

    def call(kernel, name, mebibytes, outs, in_specs, scratch, args):
        return pl.pallas_call(
            kernel,
            out_shape=outs,
            in_specs=in_specs,
            out_specs=[VMEM] * len(outs),
            scratch_shapes=scratch,
            compiler_params=params(mebibytes),
            name=name,
        )(*args)

    cov, prec, trans, means, terminal = (
        pltpu.with_memory_space_constraint(x, pltpu.HBM)
        for x in (filtered_covariance, pred_prec, transition, filt_means, terminal_mean[None])
    )
    semaphores = pltpu.SemaphoreType.DMA((8 * devices,))
    far = [shape(count, panel, width(devices, panel, order, off)) for off in range(2, devices)]
    *pieces, trans_half, first = call(
        functools.partial(pack_kernel, devices),
        "pack",
        4,
        far + far + [shape(panel // 2, order), shape(1, order)],
        [HBM] * 4,
        [pltpu.VMEM((1, order), F32), semaphores],
        (cov, prec, trans, terminal),
    )
    whole = shape(count, panel, order)
    near_cov, near_prec, own_cov, own_prec, own_trans, own_means = call(
        load_kernel,
        "load",
        4,
        [whole] * 4 + [shape(panel, order), shape(steps, order)],
        [HBM] * 4 + [VMEM],
        [semaphores],
        (cov, prec, trans, means, first),
    )

    moved = [swap(own_trans, 1)]
    for off in range(2, devices, 2):
        across = swap(trans_half, off)
        around = swap(across, 0, 1)
        moved += [across, around, swap(across, 1), swap(around, 1)]
    cov_pieces = [swap(near_cov, 1)] + [swap(x, off) for off, x in enumerate(pieces[: devices - 2], 2)]
    prec_pieces = [swap(near_prec, 1)] + [swap(x, off) for off, x in enumerate(pieces[devices - 2 :], 2)]

    cov_trans, info = call(
        functools.partial(cov_kernel, devices),
        "cov",
        24,
        [shape(count * order, order), shape(16, order)],
        [ANY, VMEM] + [ANY] * (devices + len(moved)),
        [pltpu.VMEM((count * order + 16, order), F32), pltpu.VMEM((order, order), F32), semaphores],
        (own_cov, own_means, own_trans, *cov_pieces, *moved),
    )
    pair_map, late = call(
        functools.partial(gain_kernel, devices),
        "gain",
        24,
        [shape(order + 8, order), shape(order, order)],
        [VMEM, VMEM] + [ANY] * devices,
        [pltpu.VMEM((count, order, order), F32), semaphores],
        (cov_trans, info, own_prec, *prec_pieces),
    )
    partner_map = swap(pair_map, 1)
    (block_map,) = call(
        block_kernel,
        "block",
        12,
        [shape(order + 8, order)],
        [ANY, ANY],
        [pltpu.VMEM((2, order + 8, order), F32), semaphores],
        (pair_map, partner_map),
    )

    incoming = [first]
    for block in range(blocks - 1, 0, -1):
        (x,) = call(hop_kernel, "hop", 4, [shape(1, order)], [VMEM, VMEM], [], (incoming[-1], block_map))
        incoming.append(swap(x, 1, block ^ (block - 1)))

    given = call(
        functools.partial(last_kernel, devices),
        "last",
        6,
        [shape(count, panel)] * devices,
        [VMEM] * (blocks + 3),
        [pltpu.VMEM((devices, count, panel), F32)],
        (*incoming, pair_map, partner_map, late),
    )
    given = [given[0]] + [swap(x, off) for off, x in enumerate(given[1:], 1)]
    (out,) = call(out_kernel, "out", 4, [shape(steps, panel)], [VMEM] * devices, [], given)
    return out


def solution(mesh):
    return jax.shard_map(
        local,
        mesh=mesh,
        in_specs=(
            P("tm", "state", None),
            P("tm", "state", None),
            P("state", None),
            P("tm", None),
            P(),
        ),
        out_specs=P("tm", "state"),
        check_vma=False,
    )
```

time: 352 us -> 67.5 us (0.19)
  waiting for transfers between devices: 198 us -> 26.2 us
  matrix products: 67.9 us -> 0 us
  blocking collectives: 67.2 us -> 0 us
  starting transfers between devices: 0.05 us -> 27 us
  Pallas kernels: 0 us -> 13.9 us
  between operations: 13.5 us -> 0.11 us
    all_gather x7 -> x0, waiting for transfers between devices: 196 us -> none  [the longest x1 101 us: prefix(): everything = jax.tree.map(lambda part: lax.all_gather(part, axis), shard)]
    dot_general x33 -> x0, matrix products: 67.9 us -> none  [the longest x8 24.6 us: combine(): jnp.dot(latter[0], earlier[0], precision=HIGHEST)]
    all_gather x9 -> x0, blocking collectives: 67.2 us -> none  [the longest x1 26.6 us: prefix(): everything = jax.tree.map(lambda part: lax.all_gather(part, axis), shard)]
    ppermute x0 -> x22, starting transfers between devices: none -> 27 us  [swap(): return lax.ppermute(x, ('tm', 'state'), pairs)]
    ppermute x0 -> x22, waiting for transfers between devices: none -> 26.2 us  [swap(): return lax.ppermute(x, ('tm', 'state'), pairs)]
    pallas_call x0 -> x14, Pallas kernels: none -> 13.9 us  [call(): pl.pallas_call(kernel, out_shape=outs, in_specs=in_specs, out_specs=[VMEM...]
  transfers between devices with their start and end apart: 7 -> 22, of which waited for: 7 -> 13; matrix products, arithmetic and copies ran while one was open for 2% -> 0% of each run, Pallas kernels for 0% -> 8%
where the time goes in v4:
time: 67.5 us; the launch traced here: 67.3 us
  starting transfers between devices  27 us (40%)
  waiting for transfers between devices  26.2 us (39%)
  Pallas kernels  13.9 us (21%)
    ppermute x22, starting transfers between devices, swap(): return lax.ppermute(x, ('tm', 'state'), pairs)  27 us
    ppermute x22, waiting for transfers between devices, swap(): return lax.ppermute(x, ('tm', 'state'), pairs)  26.2 us
    pallas_call x14, Pallas kernels, call(): pl.pallas_call(kernel, out_shape=outs, in_specs=in_specs, out_specs=[VMEM...  13.9 us
  transfers between devices with their start and end apart: 22, of which 13 were waited for; matrix products, arithmetic and copies ran while one was open for 0% of the time, Pallas kernels for 8%

profile of v4, /device:TPU:0, one launch (start us, length us, event | category | flops | bytes accessed | tf_op | source)
XLA Modules:
  0.0 67.3 jit_solution(13118691135938233456)
XLA Ops:
  0.0 1.5 %pack.1 = (f32[2,128,256]{2,1,0:T(8,128)S(1)}, f32[2,128,128]{2,1,0:T(8,128)S(1)}, f32[2,128,256]{2,1,0:T(8,128)S(1)}, f32[2,128,128]{2,1,0:T(8,128)S(1)}, f32[64,512]{1,0:T(8,128)S(1)}, /*index=5*/f32[1,512]{1,0:T(1,128)S(1)}) custom-call(f32[4,128,512]{2,1,0:T(8,128)} %cov.4, f32[4,128,512]{2,1,0:T(8,128)} %prec.3, f32[128,512]{1,0:T(8,128)} %trans.3, ...), custom_call_target="tpu_custom_call" | custom-call | tf_op jit(solution)/shard_map/pack/pallas_call | solution.py:244
  1.5 3.0 %collective-permute-start.4 = (f32[64,512]{1,0:T(8,128)S(1)}, f32[64,512]{1,0:T(8,128)S(1)}, u32[]{:S(2)}, u32[]{:S(2)}) collective-permute-start(f32[64,512]{1,0:T(8,128)S(1)} %get-tuple-element.32), channel_id=1, source_target_pairs={{0,2},{1,3},{2,0},{3,1},{4,6},{5,7},{6,4},{7,5},{8,10},{9,11},{10,... | collective-permute-start | bytes 393224 | tf_op jit(solution)/shard_map/ppermute | solution.py:238
  4.5 1.9 %load.1 = (f32[2,128,512]{2,1,0:T(8,128)S(1)}, f32[2,128,512]{2,1,0:T(8,128)S(1)}, f32[2,128,512]{2,1,0:T(8,128)S(1)}, f32[2,128,512]{2,1,0:T(8,128)S(1)}, f32[128,512]{1,0:T(8,128)S(1)}, /*index=5*/f32[4,512]{1,0:T(4,128)S(1)}) custom-call(f32[4,128,512]{2,1,0:T(8,128)} %cov.4, f32[4,128,512]{2,1,0:T(8,128)} %prec.3, f32[128,512]{1,0:T(8,128)} %trans.3, ...), custom_call_target="tpu_custom_call" | custom-call | tf_op jit(solution)/shard_map/load/pallas_call | solution.py:244
  6.6 1.8 %collective-permute-done.4.refs_7_ = f32[64,512]{1,0:T(8,128)S(1)} collective-permute-done((f32[64,512]{1,0:T(8,128)S(1)}, f32[64,512]{1,0:T(8,128)S(1)}, u32[]{:S(2)}, u32[]{:S(2)}) %collective-permute-start.4) | collective-permute-done | bytes 131104 | tf_op jit(solution)/shard_map/ppermute | solution.py:238
  8.4 0.5 collective-permute-start.8
  9.0 2.4 %collective-permute-start.1 = (f32[2,128,256]{2,1,0:T(8,128)S(1)}, f32[2,128,256]{2,1,0:T(8,128)S(1)}, u32[]{:S(2)}, u32[]{:S(2)}) collective-permute-start(f32[2,128,256]{2,1,0:T(8,128)S(1)} %get-tuple-element.30), channel_id=1, source_target_pairs={{0,2},{1,3},{2,0},{3,1},{4,6},{5,7},{6,4},{7,5},{8,10},{9,11},{10,... | collective-permute-start | bytes 786440 | tf_op jit(solution)/shard_map/ppermute | solution.py:238
  11.4 1.6 %collective-permute-start.5 = (f32[64,512]{1,0:T(8,128)S(1)}, f32[64,512]{1,0:T(8,128)S(1)}, u32[]{:S(2)}, u32[]{:S(2)}) collective-permute-start(f32[64,512]{1,0:T(8,128)S(1)} %collective-permute-done.4.refs_7_), channel_id=1, source_target_pairs={{0,4},{1,5},{2,6},{3,7},{4,0},{5,1},{6,2},{7,3},{8,12},{9,13},{10,... | collective-permute-start | bytes 393224 | tf_op jit(solution)/shard_map/ppermute | solution.py:238
  13.0 4.3 %collective-permute-done.5.refs_8_ = f32[64,512]{1,0:T(8,128)S(1)} collective-permute-done((f32[64,512]{1,0:T(8,128)S(1)}, f32[64,512]{1,0:T(8,128)S(1)}, u32[]{:S(2)}, u32[]{:S(2)}) %collective-permute-start.5) | collective-permute-done | bytes 131104 | tf_op jit(solution)/shard_map/ppermute | solution.py:238
  17.9 1.9 %collective-permute-start.10 = (f32[2,128,128]{2,1,0:T(8,128)S(1)}, f32[2,128,128]{2,1,0:T(8,128)S(1)}, u32[]{:S(2)}, u32[]{:S(2)}) collective-permute-start(f32[2,128,128]{2,1,0:T(8,128)S(1)} %get-tuple-element.38), channel_id=1, source_target_pairs={{0,3},{1,2},{2,1},{3,0},{4,7},{5,6},{6,5},{7,4},{8,11},{9,10},{10,... | collective-permute-start | bytes 393224 | tf_op jit(solution)/shard_map/ppermute | solution.py:238
  19.7 3.4 %cov.5 = (f32[1024,512]{1,0:T(8,128)S(1)}, f32[16,512]{1,0:T(8,128)S(1)}) custom-call(f32[2,128,512]{2,1,0:T(8,128)S(1)} %get-tuple-element.26.refs_0_, f32[4,512]{1,0:T(4,128)S(1)} %get-tuple-element.27.refs_1_, f32[128,512]{1,0:T(8,128)S(1)} %get-tuple-element.28.refs_2_, f32[2,128,512]{2,1,0:T(8,128)S(1)} %collective-permute-done.refs_3_, ...), custom_call_target="tpu_custom_call" | custom-call | tf_op jit(solution)/shard_map/cov/pallas_call | solution.py:244
  23.2 3.4 %collective-permute-done.10.refs_5_ = f32[2,128,128]{2,1,0:T(8,128)S(1)} collective-permute-done((f32[2,128,128]{2,1,0:T(8,128)S(1)}, f32[2,128,128]{2,1,0:T(8,128)S(1)}, u32[]{:S(2)}, u32[]{:S(2)}) %collective-permute-start.10) | collective-permute-done | bytes 131104 | tf_op jit(solution)/shard_map/ppermute | solution.py:238
  26.6 3.6 %gain.1 = (f32[520,512]{1,0:T(8,128)S(1)}, f32[512,512]{1,0:T(8,128)S(1)}) custom-call(f32[1024,512]{1,0:T(8,128)S(1)} %get-tuple-element.33.refs_0_, f32[16,512]{1,0:T(8,128)S(1)} %get-tuple-element.34.refs_1_, f32[2,128,512]{2,1,0:T(8,128)S(1)} %get-tuple-element.35.refs_2_, f32[2,128,512]{2,1,0:T(8,128)S(1)} %collective-permute-done.8.refs_3_, ...), custom_call_target="tpu_custom_call" | custom-call | tf_op jit(solution)/shard_map/gain/pallas_call | solution.py:244
  30.3 1.2 %collective-permute-start.11 = (f32[520,512]{1,0:T(8,128)S(1)}, f32[520,512]{1,0:T(8,128)S(1)}, u32[]{:S(2)}, u32[]{:S(2)}) collective-permute-start(f32[520,512]{1,0:T(8,128)S(1)} %get-tuple-element.39.own.refs_8_), channel_id=1, source_target_pairs={{0,1},{1,0},{2,3},{3,2},{4,5},{5,4},{6,7},{7,6},{8,9},{9,8},{10,11... | collective-permute-start | bytes 3194888 | tf_op jit(solution)/shard_map/ppermute | solution.py:238
  31.5 2.3 %collective-permute-done.11.partner.refs_9_ = f32[520,512]{1,0:T(8,128)S(1)} collective-permute-done((f32[520,512]{1,0:T(8,128)S(1)}, f32[520,512]{1,0:T(8,128)S(1)}, u32[]{:S(2)}, u32[]{:S(2)}) %collective-permute-start.11) | collective-permute-done | bytes 1064992 | tf_op jit(solution)/shard_map/ppermute | solution.py:238
  33.8 1.5 %block.1.map_ref = f32[520,512]{1,0:T(8,128)S(1)} custom-call(f32[520,512]{1,0:T(8,128)S(1)} %get-tuple-element.39.own.refs_8_, f32[520,512]{1,0:T(8,128)S(1)} %collective-permute-done.11.partner.refs_9_), custom_call_target="tpu_custom_call" | custom-call | tf_op jit(solution)/shard_map/block/pallas_call | solution.py:244
  35.4 1.6 %collective-permute-start.12 = (f32[1,512]{1,0:T(1,128)S(1)}, f32[1,512]{1,0:T(1,128)S(1)}, u32[]{:S(2)}, u32[]{:S(2)}) collective-permute-start(f32[1,512]{1,0:T(1,128)S(1)} %hop.7), channel_id=1, source_target_pairs={{0,5},{1,4},{2,7},{3,6},{4,1},{5,0},{6,3},{7,2},{8,13},{9,12},{10,... | collective-permute-start | bytes 6152 | tf_op jit(solution)/shard_map/ppermute | solution.py:238
  37.0 1.5 %collective-permute-done.12.x_ref.refs_1_ = f32[1,512]{1,0:T(1,128)S(1)} collective-permute-done((f32[1,512]{1,0:T(1,128)S(1)}, f32[1,512]{1,0:T(1,128)S(1)}, u32[]{:S(2)}, u32[]{:S(2)}) %collective-permute-start.12) | collective-permute-done | bytes 2080 | tf_op jit(solution)/shard_map/ppermute | solution.py:238
  38.7 2.6 %collective-permute-start.13 = (f32[1,512]{1,0:T(1,128)S(1)}, f32[1,512]{1,0:T(1,128)S(1)}, u32[]{:S(2)}, u32[]{:S(2)}) collective-permute-start(f32[1,512]{1,0:T(1,128)S(1)} %hop.8), channel_id=1, source_target_pairs={{0,13},{1,12},{2,15},{3,14},{4,9},{5,8},{6,11},{7,10},{8,5},{9,4},... | collective-permute-start | bytes 6152 | tf_op jit(solution)/shard_map/ppermute | solution.py:238
  41.3 1.4 %collective-permute-done.13.x_ref.refs_2_ = f32[1,512]{1,0:T(1,128)S(1)} collective-permute-done((f32[1,512]{1,0:T(1,128)S(1)}, f32[1,512]{1,0:T(1,128)S(1)}, u32[]{:S(2)}, u32[]{:S(2)}) %collective-permute-start.13) | collective-permute-done | bytes 2080 | tf_op jit(solution)/shard_map/ppermute | solution.py:238
  42.9 1.5 %collective-permute-start.14 = (f32[1,512]{1,0:T(1,128)S(1)}, f32[1,512]{1,0:T(1,128)S(1)}, u32[]{:S(2)}, u32[]{:S(2)}) collective-permute-start(f32[1,512]{1,0:T(1,128)S(1)} %hop.9), channel_id=1, source_target_pairs={{0,5},{1,4},{2,7},{3,6},{4,1},{5,0},{6,3},{7,2},{8,13},{9,12},{10,... | collective-permute-start | bytes 6152 | tf_op jit(solution)/shard_map/ppermute | solution.py:238
  44.4 1.5 %collective-permute-done.14.x_ref.refs_3_ = f32[1,512]{1,0:T(1,128)S(1)} collective-permute-done((f32[1,512]{1,0:T(1,128)S(1)}, f32[1,512]{1,0:T(1,128)S(1)}, u32[]{:S(2)}, u32[]{:S(2)}) %collective-permute-start.14) | collective-permute-done | bytes 2080 | tf_op jit(solution)/shard_map/ppermute | solution.py:238
  46.1 4.6 %collective-permute-start.15 = (f32[1,512]{1,0:T(1,128)S(1)}, f32[1,512]{1,0:T(1,128)S(1)}, u32[]{:S(2)}, u32[]{:S(2)}) collective-permute-start(f32[1,512]{1,0:T(1,128)S(1)} %hop.10), channel_id=1, source_target_pairs={{0,29},{1,28},{2,31},{3,30},{4,25},{5,24},{6,27},{7,26},{8,21},{9,... | collective-permute-start | bytes 6152 | tf_op jit(solution)/shard_map/ppermute | solution.py:238
  50.7 1.3 %collective-permute-done.15.x_ref.refs_4_ = f32[1,512]{1,0:T(1,128)S(1)} collective-permute-done((f32[1,512]{1,0:T(1,128)S(1)}, f32[1,512]{1,0:T(1,128)S(1)}, u32[]{:S(2)}, u32[]{:S(2)}) %collective-permute-start.15) | collective-permute-done | bytes 2080 | tf_op jit(solution)/shard_map/ppermute | solution.py:238
  52.1 1.4 %collective-permute-start.16 = (f32[1,512]{1,0:T(1,128)S(1)}, f32[1,512]{1,0:T(1,128)S(1)}, u32[]{:S(2)}, u32[]{:S(2)}) collective-permute-start(f32[1,512]{1,0:T(1,128)S(1)} %hop.11), channel_id=1, source_target_pairs={{0,5},{1,4},{2,7},{3,6},{4,1},{5,0},{6,3},{7,2},{8,13},{9,12},{10,... | collective-permute-start | bytes 6152 | tf_op jit(solution)/shard_map/ppermute | solution.py:238
  53.6 1.7 %collective-permute-done.16.x_ref.refs_5_ = f32[1,512]{1,0:T(1,128)S(1)} collective-permute-done((f32[1,512]{1,0:T(1,128)S(1)}, f32[1,512]{1,0:T(1,128)S(1)}, u32[]{:S(2)}, u32[]{:S(2)}) %collective-permute-start.16) | collective-permute-done | bytes 2080 | tf_op jit(solution)/shard_map/ppermute | solution.py:238
  55.4 0.6 collective-permute-start.17
  56.0 3.3 %collective-permute-done.17.x_ref.refs_6_ = f32[1,512]{1,0:T(1,128)S(1)} collective-permute-done((f32[1,512]{1,0:T(1,128)S(1)}, f32[1,512]{1,0:T(1,128)S(1)}, u32[]{:S(2)}, u32[]{:S(2)}) %collective-permute-start.17) | collective-permute-done | bytes 2080 | tf_op jit(solution)/shard_map/ppermute | solution.py:238
  59.5 1.4 %collective-permute-start.18 = (f32[1,512]{1,0:T(1,128)S(1)}, f32[1,512]{1,0:T(1,128)S(1)}, u32[]{:S(2)}, u32[]{:S(2)}) collective-permute-start(f32[1,512]{1,0:T(1,128)S(1)} %hop.13), channel_id=1, source_target_pairs={{0,5},{1,4},{2,7},{3,6},{4,1},{5,0},{6,3},{7,2},{8,13},{9,12},{10,... | collective-permute-start | bytes 6152 | tf_op jit(solution)/shard_map/ppermute | solution.py:238
  60.9 1.7 %collective-permute-done.18.refs_7_ = f32[1,512]{1,0:T(1,128)S(1)} collective-permute-done((f32[1,512]{1,0:T(1,128)S(1)}, f32[1,512]{1,0:T(1,128)S(1)}, u32[]{:S(2)}, u32[]{:S(2)}) %collective-permute-start.18) | collective-permute-done | bytes 2080 | tf_op jit(solution)/shard_map/ppermute | solution.py:238
  63.4 1.5 %collective-permute-start.21 = (f32[2,128]{1,0:T(2,128)S(1)}, f32[2,128]{1,0:T(2,128)S(1)}, u32[]{:S(2)}, u32[]{:S(2)}) collective-permute-start(f32[2,128]{1,0:T(2,128)S(1)} %get-tuple-element.44), channel_id=1, source_target_pairs={{0,3},{1,2},{2,1},{3,0},{4,7},{5,6},{6,5},{7,4},{8,11},{9,10},{10,... | collective-permute-start | bytes 3080 | tf_op jit(solution)/shard_map/ppermute | solution.py:238
  64.9 1.8 %collective-permute-done.20.refs_2_ = f32[2,128]{1,0:T(2,128)S(1)} collective-permute-done((f32[2,128]{1,0:T(2,128)S(1)}, f32[2,128]{1,0:T(2,128)S(1)}, u32[]{:S(2)}, u32[]{:S(2)}) %collective-permute-start.20) | collective-permute-done | bytes 1056 | tf_op jit(solution)/shard_map/ppermute | solution.py:238
  66.7 0.6 out.1
  (26 shorter events, 2.8 us)
Async XLA Ops:
  1.5 6.9 %collective-permute-start.4 = (f32[64,512]{1,0:T(8,128)S(1)}, f32[64,512]{1,0:T(8,128)S(1)}, u32[]{:S(2)}, u32[]{:S(2)}) collective-permute-start(f32[64,512]{1,0:T(8,128)S(1)} %get-tuple-element.32), channel_id=1, source_target_pairs={{0,2},{1,3},{2,0},{3,1},{4,6},{5,7},{6,4},{7,5},{8,10},{9,11},{10,... | collective-permute-start | bytes 393224 | tf_op jit(solution)/shard_map/ppermute | solution.py:238
  4.5 6.9 %collective-permute-start.2 = (f32[2,128,128]{2,1,0:T(8,128)S(1)}, f32[2,128,128]{2,1,0:T(8,128)S(1)}, u32[]{:S(2)}, u32[]{:S(2)}) collective-permute-start(f32[2,128,128]{2,1,0:T(8,128)S(1)} %get-tuple-element.31), channel_id=1, source_target_pairs={{0,3},{1,2},{2,1},{3,0},{4,7},{5,6},{6,5},{7,4},{8,11},{9,10},{10,... | collective-permute-start | bytes 393224 | tf_op jit(solution)/shard_map/ppermute | solution.py:238
  6.4 13.4 %collective-permute-start = (f32[2,128,512]{2,1,0:T(8,128)S(1)}, f32[2,128,512]{2,1,0:T(8,128)S(1)}, u32[]{:S(2)}, u32[]{:S(2)}) collective-permute-start(f32[2,128,512]{2,1,0:T(8,128)S(1)} %get-tuple-element.29), channel_id=1, source_target_pairs={{0,1},{1,0},{2,3},{3,2},{4,5},{5,4},{6,7},{7,6},{8,9},{9,8},{10,11... | collective-permute-start | bytes 1572872 | tf_op jit(solution)/shard_map/ppermute | solution.py:238
  8.4 3.0 %collective-permute-start.6 = (f32[64,512]{1,0:T(8,128)S(1)}, f32[64,512]{1,0:T(8,128)S(1)}, u32[]{:S(2)}, u32[]{:S(2)}) collective-permute-start(f32[64,512]{1,0:T(8,128)S(1)} %collective-permute-done.4.refs_7_), channel_id=1, source_target_pairs={{0,1},{1,0},{2,3},{3,2},{4,5},{5,4},{6,7},{7,6},{8,9},{9,8},{10,11... | collective-permute-start | bytes 393224 | tf_op jit(solution)/shard_map/ppermute | solution.py:238
  8.4 18.2 %collective-permute-start.8 = (f32[2,128,512]{2,1,0:T(8,128)S(1)}, f32[2,128,512]{2,1,0:T(8,128)S(1)}, u32[]{:S(2)}, u32[]{:S(2)}) collective-permute-start(f32[2,128,512]{2,1,0:T(8,128)S(1)} %get-tuple-element.36), channel_id=1, source_target_pairs={{0,1},{1,0},{2,3},{3,2},{4,5},{5,4},{6,7},{7,6},{8,9},{9,8},{10,11... | collective-permute-start | bytes 1572872 | tf_op jit(solution)/shard_map/ppermute | solution.py:238
  9.0 8.9 %collective-permute-start.1 = (f32[2,128,256]{2,1,0:T(8,128)S(1)}, f32[2,128,256]{2,1,0:T(8,128)S(1)}, u32[]{:S(2)}, u32[]{:S(2)}) collective-permute-start(f32[2,128,256]{2,1,0:T(8,128)S(1)} %get-tuple-element.30), channel_id=1, source_target_pairs={{0,2},{1,3},{2,0},{3,1},{4,6},{5,7},{6,4},{7,5},{8,10},{9,11},{10,... | collective-permute-start | bytes 786440 | tf_op jit(solution)/shard_map/ppermute | solution.py:238
  11.4 6.5 %collective-permute-start.3 = (f32[128,512]{1,0:T(8,128)S(1)}, f32[128,512]{1,0:T(8,128)S(1)}, u32[]{:S(2)}, u32[]{:S(2)}) collective-permute-start(f32[128,512]{1,0:T(8,128)S(1)} %get-tuple-element.28.refs_2_), channel_id=1, source_target_pairs={{0,1},{1,0},{2,3},{3,2},{4,5},{5,4},{6,7},{7,6},{8,9},{9,8},{10,11... | collective-permute-start | bytes 786440 | tf_op jit(solution)/shard_map/ppermute | solution.py:238
  11.4 5.9 %collective-permute-start.5 = (f32[64,512]{1,0:T(8,128)S(1)}, f32[64,512]{1,0:T(8,128)S(1)}, u32[]{:S(2)}, u32[]{:S(2)}) collective-permute-start(f32[64,512]{1,0:T(8,128)S(1)} %collective-permute-done.4.refs_7_), channel_id=1, source_target_pairs={{0,4},{1,5},{2,6},{3,7},{4,0},{5,1},{6,2},{7,3},{8,12},{9,13},{10,... | collective-permute-start | bytes 393224 | tf_op jit(solution)/shard_map/ppermute | solution.py:238
  17.3 9.3 %collective-permute-start.9 = (f32[2,128,256]{2,1,0:T(8,128)S(1)}, f32[2,128,256]{2,1,0:T(8,128)S(1)}, u32[]{:S(2)}, u32[]{:S(2)}) collective-permute-start(f32[2,128,256]{2,1,0:T(8,128)S(1)} %get-tuple-element.37), channel_id=1, source_target_pairs={{0,2},{1,3},{2,0},{3,1},{4,6},{5,7},{6,4},{7,5},{8,10},{9,11},{10,... | collective-permute-start | bytes 786440 | tf_op jit(solution)/shard_map/ppermute | solution.py:238
  17.9 1.9 %collective-permute-start.7 = (f32[64,512]{1,0:T(8,128)S(1)}, f32[64,512]{1,0:T(8,128)S(1)}, u32[]{:S(2)}, u32[]{:S(2)}) collective-permute-start(f32[64,512]{1,0:T(8,128)S(1)} %collective-permute-done.5.refs_8_), channel_id=1, source_target_pairs={{0,1},{1,0},{2,3},{3,2},{4,5},{5,4},{6,7},{7,6},{8,9},{9,8},{10,11... | collective-permute-start | bytes 393224 | tf_op jit(solution)/shard_map/ppermute | solution.py:238
  17.9 8.7 %collective-permute-start.10 = (f32[2,128,128]{2,1,0:T(8,128)S(1)}, f32[2,128,128]{2,1,0:T(8,128)S(1)}, u32[]{:S(2)}, u32[]{:S(2)}) collective-permute-start(f32[2,128,128]{2,1,0:T(8,128)S(1)} %get-tuple-element.38), channel_id=1, source_target_pairs={{0,3},{1,2},{2,1},{3,0},{4,7},{5,6},{6,5},{7,4},{8,11},{9,10},{10,... | collective-permute-start | bytes 393224 | tf_op jit(solution)/shard_map/ppermute | solution.py:238
  30.3 3.6 %collective-permute-start.11 = (f32[520,512]{1,0:T(8,128)S(1)}, f32[520,512]{1,0:T(8,128)S(1)}, u32[]{:S(2)}, u32[]{:S(2)}) collective-permute-start(f32[520,512]{1,0:T(8,128)S(1)} %get-tuple-element.39.own.refs_8_), channel_id=1, source_target_pairs={{0,1},{1,0},{2,3},{3,2},{4,5},{5,4},{6,7},{7,6},{8,9},{9,8},{10,11... | collective-permute-start | bytes 3194888 | tf_op jit(solution)/shard_map/ppermute | solution.py:238
  35.4 3.1 %collective-permute-start.12 = (f32[1,512]{1,0:T(1,128)S(1)}, f32[1,512]{1,0:T(1,128)S(1)}, u32[]{:S(2)}, u32[]{:S(2)}) collective-permute-start(f32[1,512]{1,0:T(1,128)S(1)} %hop.7), channel_id=1, source_target_pairs={{0,5},{1,4},{2,7},{3,6},{4,1},{5,0},{6,3},{7,2},{8,13},{9,12},{10,... | collective-permute-start | bytes 6152 | tf_op jit(solution)/shard_map/ppermute | solution.py:238
  38.7 4.0 %collective-permute-start.13 = (f32[1,512]{1,0:T(1,128)S(1)}, f32[1,512]{1,0:T(1,128)S(1)}, u32[]{:S(2)}, u32[]{:S(2)}) collective-permute-start(f32[1,512]{1,0:T(1,128)S(1)} %hop.8), channel_id=1, source_target_pairs={{0,13},{1,12},{2,15},{3,14},{4,9},{5,8},{6,11},{7,10},{8,5},{9,4},... | collective-permute-start | bytes 6152 | tf_op jit(solution)/shard_map/ppermute | solution.py:238
  42.9 3.1 %collective-permute-start.14 = (f32[1,512]{1,0:T(1,128)S(1)}, f32[1,512]{1,0:T(1,128)S(1)}, u32[]{:S(2)}, u32[]{:S(2)}) collective-permute-start(f32[1,512]{1,0:T(1,128)S(1)} %hop.9), channel_id=1, source_target_pairs={{0,5},{1,4},{2,7},{3,6},{4,1},{5,0},{6,3},{7,2},{8,13},{9,12},{10,... | collective-permute-start | bytes 6152 | tf_op jit(solution)/shard_map/ppermute | solution.py:238
  46.1 5.9 %collective-permute-start.15 = (f32[1,512]{1,0:T(1,128)S(1)}, f32[1,512]{1,0:T(1,128)S(1)}, u32[]{:S(2)}, u32[]{:S(2)}) collective-permute-start(f32[1,512]{1,0:T(1,128)S(1)} %hop.10), channel_id=1, source_target_pairs={{0,29},{1,28},{2,31},{3,30},{4,25},{5,24},{6,27},{7,26},{8,21},{9,... | collective-permute-start | bytes 6152 | tf_op jit(solution)/shard_map/ppermute | solution.py:238
  52.1 3.1 %collective-permute-start.16 = (f32[1,512]{1,0:T(1,128)S(1)}, f32[1,512]{1,0:T(1,128)S(1)}, u32[]{:S(2)}, u32[]{:S(2)}) collective-permute-start(f32[1,512]{1,0:T(1,128)S(1)} %hop.11), channel_id=1, source_target_pairs={{0,5},{1,4},{2,7},{3,6},{4,1},{5,0},{6,3},{7,2},{8,13},{9,12},{10,... | collective-permute-start | bytes 6152 | tf_op jit(solution)/shard_map/ppermute | solution.py:238
  55.4 4.0 %collective-permute-start.17 = (f32[1,512]{1,0:T(1,128)S(1)}, f32[1,512]{1,0:T(1,128)S(1)}, u32[]{:S(2)}, u32[]{:S(2)}) collective-permute-start(f32[1,512]{1,0:T(1,128)S(1)} %hop.12), channel_id=1, source_target_pairs={{0,13},{1,12},{2,15},{3,14},{4,9},{5,8},{6,11},{7,10},{8,5},{9,4},... | collective-permute-start | bytes 6152 | tf_op jit(solution)/shard_map/ppermute | solution.py:238
  59.5 3.1 %collective-permute-start.18 = (f32[1,512]{1,0:T(1,128)S(1)}, f32[1,512]{1,0:T(1,128)S(1)}, u32[]{:S(2)}, u32[]{:S(2)}) collective-permute-start(f32[1,512]{1,0:T(1,128)S(1)} %hop.13), channel_id=1, source_target_pairs={{0,5},{1,4},{2,7},{3,6},{4,1},{5,0},{6,3},{7,2},{8,13},{9,12},{10,... | collective-permute-start | bytes 6152 | tf_op jit(solution)/shard_map/ppermute | solution.py:238
  63.0 1.9 %collective-permute-start.19 = (f32[2,128]{1,0:T(2,128)S(1)}, f32[2,128]{1,0:T(2,128)S(1)}, u32[]{:S(2)}, u32[]{:S(2)}) collective-permute-start(f32[2,128]{1,0:T(2,128)S(1)} %get-tuple-element.42), channel_id=1, source_target_pairs={{0,1},{1,0},{2,3},{3,2},{4,5},{5,4},{6,7},{7,6},{8,9},{9,8},{10,11... | collective-permute-start | bytes 3080 | tf_op jit(solution)/shard_map/ppermute | solution.py:238
  63.1 3.6 %collective-permute-start.20 = (f32[2,128]{1,0:T(2,128)S(1)}, f32[2,128]{1,0:T(2,128)S(1)}, u32[]{:S(2)}, u32[]{:S(2)}) collective-permute-start(f32[2,128]{1,0:T(2,128)S(1)} %get-tuple-element.43), channel_id=1, source_target_pairs={{0,2},{1,3},{2,0},{3,1},{4,6},{5,7},{6,4},{7,5},{8,10},{9,11},{10,... | collective-permute-start | bytes 3080 | tf_op jit(solution)/shard_map/ppermute | solution.py:238
  63.4 3.3 %collective-permute-start.21 = (f32[2,128]{1,0:T(2,128)S(1)}, f32[2,128]{1,0:T(2,128)S(1)}, u32[]{:S(2)}, u32[]{:S(2)}) collective-permute-start(f32[2,128]{1,0:T(2,128)S(1)} %get-tuple-element.44), channel_id=1, source_target_pairs={{0,3},{1,2},{2,1},{3,0},{4,7},{5,6},{6,5},{7,4},{8,11},{9,10},{10,... | collective-permute-start | bytes 3080 | tf_op jit(solution)/shard_map/ppermute | solution.py:238

commit v5 on v4

v5 whole, which is shorter than its diff:
```python
import functools

import jax
import jax.numpy as jnp
from jax import lax
from jax.experimental import pallas as pl
from jax.experimental.pallas import tpu as pltpu
from jax.sharding import PartitionSpec as P

F32, BF16 = jnp.float32, jnp.bfloat16
NN = (((1,), (0,)), ((), ()))
NT = (((1,), (1,)), ((), ()))
ANY = pl.BlockSpec(memory_space=pl.ANY)
HBM = pl.BlockSpec(memory_space=pltpu.HBM)
VMEM = pl.BlockSpec(memory_space=pltpu.VMEM)


def split(x):
    high = x.astype(BF16)
    return high, (x - high.astype(F32)).astype(BF16)


def dot3(a, b, dims):
    (ah, al), (bh, bl) = split(a), split(b)
    dot = functools.partial(lax.dot_general, dimension_numbers=dims, preferred_element_type=F32)
    return dot(ah, bh) + (dot(ah, bl) + dot(al, bh))


def matvec(matrix, row):
    order = matrix.shape[1]
    total = matrix[:, :128] * row[:, :128]
    for j in range(128, order, 128):
        total += matrix[:, j : j + 128] * row[:, j : j + 128]
    return jnp.sum(total.T, axis=0, keepdims=True)


def rows(i, panel):
    return pl.ds(pl.multiple_of(i * panel, panel), panel)


def starter(sems):
    copies = []

    def start(source, target):
        copy = pltpu.make_async_copy(source, target, sems.at[len(copies)])
        copy.start()
        copies.append(copy)

    return start, copies


def width(devices, panel, order, off):
    if off < 2:
        return order
    return panel if devices == 4 and off == 3 and panel % 128 == 0 else order - 2 * panel


def pack_kernel(devices, cov, prec, trans, terminal, *refs):
    far, (trans_half, first, vector, sems) = refs[:-4], refs[-4:]
    steps, panel, order = cov.shape
    b, s = lax.axis_index("tm"), lax.axis_index("state")
    start, copies = starter(sems)
    start(terminal, vector)
    start(trans.at[pl.ds(pl.multiple_of((b % 2) * (panel // 2), panel // 2), panel // 2), :], trans_half)
    pieces = iter(far)
    for matrix, groups in ((cov, 1), (prec, 2)):
        for group in range(groups):
            for off in range(2, devices):
                piece = next(pieces)
                count = piece.shape[0]
                step = ((s ^ off) % 2) * (steps // 2) + (groups - 1 - group) * count
                w = width(devices, panel, order, off)
                column = 2 * panel if w == order - 2 * panel else pl.multiple_of(s * panel, panel)
                start(matrix.at[pl.ds(step, count), :, pl.ds(column, w)], piece)
    copies[0].wait()
    first[...] = jnp.where(b == lax.axis_size("tm") - 1, vector[...], 0.0)
    for copy in copies[1:]:
        copy.wait()


def load_kernel(cov, prec, trans, means, after, near, own, own_means, sems):
    count = cov.shape[0] // 2
    s = lax.axis_index("state")
    start, copies = starter(sems)
    for target, half in ((near, 1 - s % 2), (own, s % 2)):
        start(cov.at[pl.ds(half * count, count)], target.at[pl.ds(0, count)])
        start(prec.at[pl.ds(half * count, count)], target.at[pl.ds(count, count)])
        start(trans, target.at[2 * count])
    start(means, own_means)
    for copy in copies:
        copy.wait()


def assemble(devices, start, full, panels):
    panel, order = panels[0].shape
    s = lax.axis_index("state")
    for off, piece in enumerate(panels):
        i = s ^ off
        w = width(devices, panel, order, off)
        target = full.at[rows(i, panel), :]
        if w < order:
            column = 2 * panel if w == order - 2 * panel else pl.multiple_of(i * panel, panel)
            target = full.at[rows(i, panel), pl.ds(column, w)]
        start(piece, target)


def mirror(devices, full, panel, order):
    s, known = lax.axis_index("state"), 2 * panel
    full[known:order, :known] = full[:known, known:order].T
    if width(devices, panel, order, 3) < order - known:
        i, j = s ^ 3, s ^ 2
        full[rows(i, panel), rows(j, panel)] = full[rows(j, panel), rows(i, panel)].T


def cov_kernel(devices, means, own, near, *refs):
    far, moved, (out, info, pf, af, sems) = refs[: devices - 2], refs[devices - 2 : -5], refs[-5:]
    _, panel, order = own.shape
    count = far[0].shape[0]
    steps = means.shape[0]
    b, s = lax.axis_index("tm"), lax.axis_index("state")
    start, copies = starter(sems)
    for k in range(count):
        panels = [own.at[k], near.at[k]] + [piece.at[k] for piece in far]
        assemble(devices, start, pf.at[pl.ds(k * order, order), :], panels)
    start(own.at[2 * count], af.at[rows(s, panel), :])
    start(near.at[2 * count], af.at[rows(s ^ 1, panel), :])
    spots = [(off ^ beside, half) for off in range(2, devices, 2) for beside in range(2) for half in range(2)]
    for piece, (off, half) in zip(moved, spots):
        at = (s ^ off) * panel + (b % 2 if half == 0 else 1 - b % 2) * (panel // 2)
        start(piece, af.at[pl.ds(pl.multiple_of(at, panel // 2), panel // 2), :])
    pf[count * order :, :] = jnp.concatenate([means[...], jnp.zeros((16 - steps, order), F32)], axis=0)
    for copy in copies:
        copy.wait()
    for k in range(count):
        mirror(devices, pf.at[pl.ds(k * order, order), :], panel, order)
    product = dot3(pf[...], af[...], NT)
    out[...] = product[: count * order]
    info[:8] = pf[count * order : count * order + 8, :]
    info[8:] = product[count * order : count * order + 8]


def gain_kernel(devices, k, cov_trans, own, near, *refs):
    far, (gain, lf, sems) = refs[: devices - 2], refs[-3:]
    count, (_, panel, order) = own.shape[0] // 2, own.shape
    start, copies = starter(sems)
    assemble(devices, start, lf, [own.at[count + k], near.at[count + k]] + [piece.at[0] for piece in far])
    for copy in copies:
        copy.wait()
    mirror(devices, lf, panel, order)
    gain[...] = dot3(cov_trans[k * order : (k + 1) * order, :], lf[...], NN)


def three_kernel(info, g1, g2, g3, c_ref, n_ref, vec_ref):
    mean, pred = info[0:4, :], info[8:12, :]
    late = mean[2:3] + matvec(g2[...], mean[3:4] - pred[2:3])
    early = mean[1:2] + matvec(g1[...], late - pred[1:2])
    vec_ref[...] = jnp.concatenate([pred[3:4], mean[3:4], late, early, mean[0:1], pred[0:1], mean[0:2]], axis=0)
    c = dot3(g2[...], g3[...], NN)
    c_ref[...] = c
    n_ref[...] = dot3(g1[...], c, NN)


def four_kernel(vec, n, g0, m_ref, out_ref):
    shift = vec[4:5, :] + matvec(g0[...], vec[3:4, :] - vec[5:6, :])
    out_ref[...] = jnp.concatenate([vec[0:1, :], shift, vec[0:6, :]], axis=0)
    m_ref[...] = dot3(g0[...], n[...], NN)


def hop_kernel(x, m, vec, out_ref):
    out_ref[...] = vec[1:2, :] + matvec(m[...], x[...] - vec[0:1, :])


def last_kernel(devices, *refs):
    blocks = len(refs) - 6 - devices
    incoming, (m, n, c, g3, vec), outs, cut = refs[:blocks], refs[blocks : blocks + 5], refs[blocks + 5 : -1], refs[-1]
    panel = outs[0].shape[1]
    b, s = lax.axis_index("tm"), lax.axis_index("state")
    x = incoming[0][...]
    for k, ref in enumerate(incoming[1:], 1):
        x = jnp.where(lax.axis_size("tm") - 1 - b == k, ref[...], x)
    gap = x - vec[0:1, :]
    shifts = (vec[1:2, :], vec[5:6, :], vec[4:5, :], vec[3:4, :])
    full = jnp.concatenate([v + matvec(g[...], gap) for v, g in zip(shifts, (m, n, c, g3))], axis=0)
    for i in range(devices):
        cut[i] = full[:, i * panel : (i + 1) * panel]
    for off, out in enumerate(outs):
        out[...] = cut[s ^ off]


def out_kernel(*refs):
    given, out_ref = refs[:-1], refs[-1]
    off = lax.axis_index("state") ^ 1
    x = given[0][...]
    for k, ref in enumerate(given[1:], 1):
        x = jnp.where(off == k, ref[...], x)
    out_ref[...] = x


def params(mebibytes):
    return pltpu.CompilerParams(vmem_limit_bytes=mebibytes * 2**20)


def local(filtered_covariance, pred_prec, transition, filt_means, terminal_mean):
    steps, panel, order = filtered_covariance.shape
    devices, blocks = lax.axis_size("state"), lax.axis_size("tm")
    count = steps // 2

    def swap(x, off, block_off=0):
        pairs = [(i, i ^ (block_off * devices + off)) for i in range(blocks * devices)]
        return lax.ppermute(x, ("tm", "state"), pairs)

    def shape(*dims):
        return jax.ShapeDtypeStruct(dims, F32)

    def call(kernel, name, mebibytes, outs, in_specs, scratch, args):
        return pl.pallas_call(
            kernel,
            out_shape=outs,
            in_specs=in_specs,
            out_specs=[VMEM] * len(outs),
            scratch_shapes=scratch,
            compiler_params=params(mebibytes),
            name=name,
        )(*args)

    cov, prec, trans, means, terminal = (
        pltpu.with_memory_space_constraint(x, pltpu.HBM)
        for x in (filtered_covariance, pred_prec, transition, filt_means, terminal_mean[None])
    )
    semaphores = pltpu.SemaphoreType.DMA((8 * devices,))
    square = shape(order, order)

    def far(k):
        return [shape(k, panel, width(devices, panel, order, off)) for off in range(2, devices)]

    *pieces, trans_half, first = call(
        functools.partial(pack_kernel, devices),
        "pack",
        4,
        far(count) + far(1) * count + [shape(panel // 2, order), shape(1, order)],
        [HBM] * 4,
        [pltpu.VMEM((1, order), F32), semaphores],
        (cov, prec, trans, terminal),
    )
    panels = shape(2 * count + 1, panel, order)
    near, own, own_means = call(
        load_kernel,
        "load",
        4,
        [panels, panels, shape(steps, order)],
        [HBM] * 4 + [VMEM],
        [semaphores],
        (cov, prec, trans, means, first),
    )

    across = [swap(trans_half, off) for off in range(2, devices, 2)]
    arrived = []
    for group in range(1 + count):
        at = group * (devices - 2)
        arrived.append([swap(x, off) for off, x in enumerate(pieces[at : at + devices - 2], 2)])
    near = swap(near, 1)
    moved = []
    for x in across:
        around = swap(x, 0, 1)
        moved += [x, around, swap(x, 1), swap(around, 1)]

    cov_trans, info = call(
        functools.partial(cov_kernel, devices),
        "cov",
        24,
        [shape(count * order, order), shape(16, order)],
        [VMEM] + [ANY] * (devices + len(moved)),
        [pltpu.VMEM((count * order + 16, order), F32), pltpu.VMEM((order, order), F32), semaphores],
        (own_means, own, near, *arrived[0], *moved),
    )

    def gain(k, far):
        (out,) = call(
            functools.partial(gain_kernel, devices, k),
            "gain",
            16,
            [square],
            [VMEM] + [ANY] * devices,
            [pltpu.VMEM((order, order), F32), semaphores],
            (cov_trans, own, near, *far),
        )
        return out

    g3 = gain(1, arrived[1])
    g1 = swap(g3, 1)
    g2 = gain(0, arrived[2])
    g0 = swap(g2, 1)
    c, n, vec = call(
        three_kernel, "three", 12, [square, square, shape(8, order)], [VMEM] * 4, [], (info, g1, g2, g3)
    )
    m, vec = call(four_kernel, "four", 12, [square, shape(8, order)], [VMEM] * 3, [], (vec, n, g0))

    incoming = [first]
    for block in range(blocks - 1, 0, -1):
        (x,) = call(hop_kernel, "hop", 4, [shape(1, order)], [VMEM] * 3, [], (incoming[-1], m, vec))
        if block % 2:
            x = swap(x, 0, 1)
        else:
            x = lax.ppermute(x, ("tm", "state"), [(block * devices + 1, (block - 1) * devices + 1)])
        incoming.append(x)

    given = call(
        functools.partial(last_kernel, devices),
        "last",
        8,
        [shape(steps, panel)] * devices,
        [VMEM] * (blocks + 5),
        [pltpu.VMEM((devices, steps, panel), F32)],
        (*incoming, m, n, c, g3, vec),
    )
    given = [given[0]] + [swap(x, off) for off, x in enumerate(given[1:], 1)]
    (out,) = call(out_kernel, "out", 4, [shape(steps, panel)], [VMEM] * devices, [], given)
    return out


def solution(mesh):
    return jax.shard_map(
        local,
        mesh=mesh,
        in_specs=(
            P("tm", "state", None),
            P("tm", "state", None),
            P("state", None),
            P("tm", None),
            P(),
        ),
        out_specs=P("tm", "state"),
        check_vma=False,
    )
```

time: 67.5 us -> 64.3 us (0.953)
  waiting for transfers between devices: 26.2 us -> 20.9 us
  Pallas kernels: 13.9 us -> 15 us
  starting transfers between devices: 27 us -> 28 us
    ppermute x22 -> x20, waiting for transfers between devices: 26.2 us -> 20.9 us  [swap(): return lax.ppermute(x, ('tm', 'state'), pairs)]
    ppermute x0 -> x3, starting transfers between devices: none -> 1.98 us  [local(): lax.ppermute(x, ('tm', 'state'), [(block * devices + 1, (block - 1) * dev...]
    pallas_call x14 -> x16, Pallas kernels: 13.9 us -> 15 us  [call(): pl.pallas_call(kernel, out_shape=outs, in_specs=in_specs, out_specs=[VMEM...]
    ppermute x22 -> x20, starting transfers between devices: 27 us -> 26 us  [swap(): return lax.ppermute(x, ('tm', 'state'), pairs)]
  transfers between devices with their start and end apart: 22 -> 23, of which waited for: 13 -> 11; matrix products, arithmetic and copies ran while one was open for 0% -> 0% of each run, Pallas kernels for 8% -> 13%
where the time goes in v5:
time: 64.3 us; the launch traced here: 64 us
  starting transfers between devices  28 us (44%)
  waiting for transfers between devices  20.9 us (33%)
  Pallas kernels  15 us (23%)
    ppermute x20, starting transfers between devices, swap(): return lax.ppermute(x, ('tm', 'state'), pairs)  26 us
    ppermute x20, waiting for transfers between devices, swap(): return lax.ppermute(x, ('tm', 'state'), pairs)  20.9 us
    pallas_call x16, Pallas kernels, call(): pl.pallas_call(kernel, out_shape=outs, in_specs=in_specs, out_specs=[VMEM...  15 us
    ppermute x3, starting transfers between devices, local(): lax.ppermute(x, ('tm', 'state'), [(block * devices + 1, (block - 1) * dev...  1.98 us
  transfers between devices with their start and end apart: 23, of which 11 were waited for; matrix products, arithmetic and copies ran while one was open for 0% of the time, Pallas kernels for 13%

profile of v5, /device:TPU:0, one launch (start us, length us, event | category | flops | bytes accessed | tf_op | source)
XLA Modules:
  0.0 64.0 jit_solution(7265708384557204989)
XLA Ops:
  0.0 1.5 %pack.1 = (f32[2,128,256]{2,1,0:T(8,128)S(1)}, f32[2,128,128]{2,1,0:T(8,128)S(1)}, f32[1,128,256]{2,1,0:T(8,128)S(1)}, f32[1,128,128]{2,1,0:T(8,128)S(1)}, f32[1...) custom-call(f32[4,128,512]{2,1,0:T(8,128)} %cov.4, ...), custom_call_target="tpu_custom_call" | custom-call | tf_op jit(solution)/shard_map/pack/pallas_call | solution.py:216
  1.5 2.0 %load.1 = (f32[5,128,512]{2,1,0:T(8,128)S(1)}, f32[5,128,512]{2,1,0:T(8,128)S(1)}, f32[4,512]{1,0:T(4,128)S(1)}) custom-call(f32[4,128,512]{2,1,0:T(8,128)} %cov.4, f32[4,128,512]{2,1,0:T(8,128)} %prec.3, f32[128,512]{1,0:T(8,128)} %trans.3, f32[4,512]{1,0:T(4,128)} %means.1, f32[1,512]{1,0:T(1,128)S(1)} %get-tuple-element.27.after.x.refs_0_), custom_call_target="tpu_custom_call" | custom-call | tf_op jit(solution)/shard_map/load/pallas_call | solution.py:216
  4.0 2.6 %collective-permute-start.3 = (f32[64,512]{1,0:T(8,128)S(1)}, f32[64,512]{1,0:T(8,128)S(1)}, u32[]{:S(2)}, u32[]{:S(2)}) collective-permute-start(f32[64,512]{1,0:T(8,128)S(1)} %get-tuple-element.33), channel_id=1, source_target_pairs={{0,2},{1,3},{2,0},{3,1},{4,6},{5,7},{6,4},{7,5},{8,10},{9,11},{10,... | collective-permute-start | bytes 393224 | tf_op jit(solution)/shard_map/ppermute | solution.py:210
  6.6 4.3 %collective-permute-done.3.refs_2_ = f32[64,512]{1,0:T(8,128)S(1)} collective-permute-done((f32[64,512]{1,0:T(8,128)S(1)}, f32[64,512]{1,0:T(8,128)S(1)}, u32[]{:S(2)}, u32[]{:S(2)}) %collective-permute-start.3) | collective-permute-done | bytes 131104 | tf_op jit(solution)/shard_map/ppermute | solution.py:210
  10.9 2.0 %collective-permute-start.4 = (f32[64,512]{1,0:T(8,128)S(1)}, f32[64,512]{1,0:T(8,128)S(1)}, u32[]{:S(2)}, u32[]{:S(2)}) collective-permute-start(f32[64,512]{1,0:T(8,128)S(1)} %collective-permute-done.3.refs_2_), channel_id=1, source_target_pairs={{0,4},{1,5},{2,6},{3,7},{4,0},{5,1},{6,2},{7,3},{8,12},{9,13},{10,... | collective-permute-start | bytes 393224 | tf_op jit(solution)/shard_map/ppermute | solution.py:210
  12.9 1.6 %collective-permute-start.5 = (f32[64,512]{1,0:T(8,128)S(1)}, f32[64,512]{1,0:T(8,128)S(1)}, u32[]{:S(2)}, u32[]{:S(2)}) collective-permute-start(f32[64,512]{1,0:T(8,128)S(1)} %collective-permute-done.3.refs_2_), channel_id=1, source_target_pairs={{0,1},{1,0},{2,3},{3,2},{4,5},{5,4},{6,7},{7,6},{8,9},{9,8},{10,11... | collective-permute-start | bytes 393224 | tf_op jit(solution)/shard_map/ppermute | solution.py:210
  14.5 1.4 %collective-permute-done.4.refs_3_ = f32[64,512]{1,0:T(8,128)S(1)} collective-permute-done((f32[64,512]{1,0:T(8,128)S(1)}, f32[64,512]{1,0:T(8,128)S(1)}, u32[]{:S(2)}, u32[]{:S(2)}) %collective-permute-start.4) | collective-permute-done | bytes 131104 | tf_op jit(solution)/shard_map/ppermute | solution.py:210
  15.9 2.9 %collective-permute-done.2.refs_1_ = f32[2,128,128]{2,1,0:T(8,128)S(1)} collective-permute-done((f32[2,128,128]{2,1,0:T(8,128)S(1)}, f32[2,128,128]{2,1,0:T(8,128)S(1)}, u32[]{:S(2)}, u32[]{:S(2)}) %collective-permute-start.2) | collective-permute-done | bytes 131104 | tf_op jit(solution)/shard_map/ppermute | solution.py:210
  18.8 1.6 %collective-permute-start.7 = (f32[1,128,256]{2,1,0:T(8,128)S(1)}, f32[1,128,256]{2,1,0:T(8,128)S(1)}, u32[]{:S(2)}, u32[]{:S(2)}) collective-permute-start(f32[1,128,256]{2,1,0:T(8,128)S(1)} %get-tuple-element.36), channel_id=1, source_target_pairs={{0,2},{1,3},{2,0},{3,1},{4,6},{5,7},{6,4},{7,5},{8,10},{9,11},{10,... | collective-permute-start | bytes 393224 | tf_op jit(solution)/shard_map/ppermute | solution.py:210
  20.8 0.9 %collective-permute-start.8 = (f32[1,128,128]{2,1,0:T(8,128)S(1)}, f32[1,128,128]{2,1,0:T(8,128)S(1)}, u32[]{:S(2)}, u32[]{:S(2)}) collective-permute-start(f32[1,128,128]{2,1,0:T(8,128)S(1)} %get-tuple-element.37), channel_id=1, source_target_pairs={{0,3},{1,2},{2,1},{3,0},{4,7},{5,6},{6,5},{7,4},{8,11},{9,10},{10,... | collective-permute-start | bytes 196616 | tf_op jit(solution)/shard_map/ppermute | solution.py:210
  21.7 0.9 %collective-permute-start.11 = (f32[1,128,128]{2,1,0:T(8,128)S(1)}, f32[1,128,128]{2,1,0:T(8,128)S(1)}, u32[]{:S(2)}, u32[]{:S(2)}) collective-permute-start(f32[1,128,128]{2,1,0:T(8,128)S(1)} %get-tuple-element.39), channel_id=1, source_target_pairs={{0,3},{1,2},{2,1},{3,0},{4,7},{5,6},{6,5},{7,4},{8,11},{9,10},{10,... | collective-permute-start | bytes 196616 | tf_op jit(solution)/shard_map/ppermute | solution.py:210
  22.6 3.4 %cov.5 = (f32[1024,512]{1,0:T(8,128)S(1)}, f32[16,512]{1,0:T(8,128)S(1)}) custom-call(f32[4,512]{1,0:T(4,128)S(1)} %get-tuple-element.28.means, f32[5,128,512]{2,1,0:T(8,128)S(1)} %get-tuple-element.29.own, f32[5,128,512]{2,1,0:T(8,128)S(1)} %collective-permute-done.near, f32[2,128,256]{2,1,0:T(8,128)S(1)} %collective-permute-done.1.refs_0_, ...), custom_call_target="tpu_custom_call" | custom-call | tf_op jit(solution)/shard_map/cov/pallas_call | solution.py:216
  26.0 2.4 %collective-permute-done.8.refs_1_ = f32[1,128,128]{2,1,0:T(8,128)S(1)} collective-permute-done((f32[1,128,128]{2,1,0:T(8,128)S(1)}, f32[1,128,128]{2,1,0:T(8,128)S(1)}, u32[]{:S(2)}, u32[]{:S(2)}) %collective-permute-start.8) | collective-permute-done | bytes 65568 | tf_op jit(solution)/shard_map/ppermute | solution.py:210
  28.4 1.6 %gain.2.g3.refs_11_ = f32[512,512]{1,0:T(8,128)S(1)} custom-call(f32[1024,512]{1,0:T(8,128)S(1)} %get-tuple-element.35.cov_trans, f32[5,128,512]{2,1,0:T(8,128)S(1)} %get-tuple-element.29.own, f32[5,128,512]{2,1,0:T(8,128)S(1)} %collective-permute-done.near, f32[1,128,256]{2,1,0:T(8,128)S(1)} %collective-permute-done.7.refs_0_, ...), custom_call_target="tpu_custom_call" | custom-call | tf_op jit(solution)/shard_map/gain/pallas_call | solution.py:216
  30.0 0.9 %collective-permute-start.9 = (f32[512,512]{1,0:T(8,128)S(1)}, f32[512,512]{1,0:T(8,128)S(1)}, u32[]{:S(2)}, u32[]{:S(2)}) collective-permute-start(f32[512,512]{1,0:T(8,128)S(1)} %gain.2.g3.refs_11_), channel_id=1, source_target_pairs={{0,1},{1,0},{2,3},{3,2},{4,5},{5,4},{6,7},{7,6},{8,9},{9,8},{10,11... | collective-permute-start | bytes 3145736 | tf_op jit(solution)/shard_map/ppermute | solution.py:210
  30.9 1.6 %gain.3.g2 = f32[512,512]{1,0:T(8,128)S(1)} custom-call(f32[1024,512]{1,0:T(8,128)S(1)} %get-tuple-element.35.cov_trans, f32[5,128,512]{2,1,0:T(8,128)S(1)} %get-tuple-element.29.own, f32[5,128,512]{2,1,0:T(8,128)S(1)} %collective-permute-done.near, f32[1,128,256]{2,1,0:T(8,128)S(1)} %collective-permute-done.10.refs_0_, ...), custom_call_target="tpu_custom_call" | custom-call | tf_op jit(solution)/shard_map/gain/pallas_call | solution.py:216
  33.2 1.9 %three.1 = (f32[512,512]{1,0:T(8,128)S(1)}, f32[512,512]{1,0:T(8,128)S(1)}, f32[8,512]{1,0:T(8,128)S(1)}) custom-call(f32[16,512]{1,0:T(8,128)S(1)} %get-tuple-element.34.info, f32[512,512]{1,0:T(8,128)S(1)} %collective-permute-done.9.g1, f32[512,512]{1,0:T(8,128)S(1)} %gain.3.g2, f32[512,512]{1,0:T(8,128)S(1)} %gain.2.g3.refs_11_), custom_call_target="tpu_custom_call" | custom-call | tf_op jit(solution)/shard_map/three/pallas_call | solution.py:216
  35.2 1.0 %four.1 = (f32[512,512]{1,0:T(8,128)S(1)}, f32[8,512]{1,0:T(8,128)S(1)}) custom-call(f32[8,512]{1,0:T(8,128)S(1)} %get-tuple-element.40.vec, f32[512,512]{1,0:T(8,128)S(1)} %get-tuple-element.41.n.refs_9_, f32[512,512]{1,0:T(8,128)S(1)} %collective-permute-done.12.g0), custom_call_target="tpu_custom_call" | custom-call | tf_op jit(solution)/shard_map/four/pallas_call | solution.py:216
  36.4 1.9 %collective-permute-start.13 = (f32[1,512]{1,0:T(1,128)S(1)}, f32[1,512]{1,0:T(1,128)S(1)}, u32[]{:S(2)}, u32[]{:S(2)}) collective-permute-start(f32[1,512]{1,0:T(1,128)S(1)} %hop.7), channel_id=1, source_target_pairs={{0,4},{1,5},{2,6},{3,7},{4,0},{5,1},{6,2},{7,3},{8,12},{9,13},{10,... | collective-permute-start | bytes 6152 | tf_op jit(solution)/shard_map/ppermute | solution.py:210
  38.3 1.8 %collective-permute-done.13.x.refs_1_ = f32[1,512]{1,0:T(1,128)S(1)} collective-permute-done((f32[1,512]{1,0:T(1,128)S(1)}, f32[1,512]{1,0:T(1,128)S(1)}, u32[]{:S(2)}, u32[]{:S(2)}) %collective-permute-start.13) | collective-permute-done | bytes 2080 | tf_op jit(solution)/shard_map/ppermute | solution.py:210
  40.2 0.7 %collective-permute-start.14 = (f32[1,512]{1,0:T(1,128)S(1)}, f32[1,512]{1,0:T(1,128)S(1)}, u32[]{:S(2)}, u32[]{:S(2)}) collective-permute-start(f32[1,512]{1,0:T(1,128)S(1)} %hop.8), channel_id=1, source_target_pairs={{25,21}} | collective-permute-start | bytes 6152 | tf_op jit(solution)/shard_map/ppermute | solution.py:304
  41.0 1.9 %collective-permute-start.15 = (f32[1,512]{1,0:T(1,128)S(1)}, f32[1,512]{1,0:T(1,128)S(1)}, u32[]{:S(2)}, u32[]{:S(2)}) collective-permute-start(f32[1,512]{1,0:T(1,128)S(1)} %hop.9), channel_id=1, source_target_pairs={{0,4},{1,5},{2,6},{3,7},{4,0},{5,1},{6,2},{7,3},{8,12},{9,13},{10,... | collective-permute-start | bytes 6152 | tf_op jit(solution)/shard_map/ppermute | solution.py:210
  42.9 1.8 %collective-permute-done.15.x.refs_3_ = f32[1,512]{1,0:T(1,128)S(1)} collective-permute-done((f32[1,512]{1,0:T(1,128)S(1)}, f32[1,512]{1,0:T(1,128)S(1)}, u32[]{:S(2)}, u32[]{:S(2)}) %collective-permute-start.15) | collective-permute-done | bytes 2080 | tf_op jit(solution)/shard_map/ppermute | solution.py:210
  44.8 0.7 %collective-permute-start.16 = (f32[1,512]{1,0:T(1,128)S(1)}, f32[1,512]{1,0:T(1,128)S(1)}, u32[]{:S(2)}, u32[]{:S(2)}) collective-permute-start(f32[1,512]{1,0:T(1,128)S(1)} %hop.10), channel_id=1, source_target_pairs={{17,13}} | collective-permute-start | bytes 6152 | tf_op jit(solution)/shard_map/ppermute | solution.py:304
  45.7 1.9 %collective-permute-start.17 = (f32[1,512]{1,0:T(1,128)S(1)}, f32[1,512]{1,0:T(1,128)S(1)}, u32[]{:S(2)}, u32[]{:S(2)}) collective-permute-start(f32[1,512]{1,0:T(1,128)S(1)} %hop.11), channel_id=1, source_target_pairs={{0,4},{1,5},{2,6},{3,7},{4,0},{5,1},{6,2},{7,3},{8,12},{9,13},{10,... | collective-permute-start | bytes 6152 | tf_op jit(solution)/shard_map/ppermute | solution.py:210
  47.6 1.8 %collective-permute-done.17.x.refs_5_ = f32[1,512]{1,0:T(1,128)S(1)} collective-permute-done((f32[1,512]{1,0:T(1,128)S(1)}, f32[1,512]{1,0:T(1,128)S(1)}, u32[]{:S(2)}, u32[]{:S(2)}) %collective-permute-start.17) | collective-permute-done | bytes 2080 | tf_op jit(solution)/shard_map/ppermute | solution.py:210
  49.5 0.7 %collective-permute-start.18 = (f32[1,512]{1,0:T(1,128)S(1)}, f32[1,512]{1,0:T(1,128)S(1)}, u32[]{:S(2)}, u32[]{:S(2)}) collective-permute-start(f32[1,512]{1,0:T(1,128)S(1)} %hop.12), channel_id=1, source_target_pairs={{9,5}} | collective-permute-start | bytes 6152 | tf_op jit(solution)/shard_map/ppermute | solution.py:304
  50.3 1.9 %collective-permute-start.19 = (f32[1,512]{1,0:T(1,128)S(1)}, f32[1,512]{1,0:T(1,128)S(1)}, u32[]{:S(2)}, u32[]{:S(2)}) collective-permute-start(f32[1,512]{1,0:T(1,128)S(1)} %hop.13), channel_id=1, source_target_pairs={{0,4},{1,5},{2,6},{3,7},{4,0},{5,1},{6,2},{7,3},{8,12},{9,13},{10,... | collective-permute-start | bytes 6152 | tf_op jit(solution)/shard_map/ppermute | solution.py:210
  52.2 1.8 %collective-permute-done.19.refs_7_ = f32[1,512]{1,0:T(1,128)S(1)} collective-permute-done((f32[1,512]{1,0:T(1,128)S(1)}, f32[1,512]{1,0:T(1,128)S(1)}, u32[]{:S(2)}, u32[]{:S(2)}) %collective-permute-start.19) | collective-permute-done | bytes 2080 | tf_op jit(solution)/shard_map/ppermute | solution.py:210
  54.3 5.5 %collective-permute-start.20 = (f32[4,128]{1,0:T(4,128)S(1)}, f32[4,128]{1,0:T(4,128)S(1)}, u32[]{:S(2)}, u32[]{:S(2)}) collective-permute-start(f32[4,128]{1,0:T(4,128)S(1)} %get-tuple-element.46), channel_id=1, source_target_pairs={{0,1},{1,0},{2,3},{3,2},{4,5},{5,4},{6,7},{7,6},{8,9},{9,8},{10,11... | collective-permute-start | bytes 6152 | tf_op jit(solution)/shard_map/ppermute | solution.py:210
  59.9 1.4 %collective-permute-start.22 = (f32[4,128]{1,0:T(4,128)S(1)}, f32[4,128]{1,0:T(4,128)S(1)}, u32[]{:S(2)}, u32[]{:S(2)}) collective-permute-start(f32[4,128]{1,0:T(4,128)S(1)} %get-tuple-element.48), channel_id=1, source_target_pairs={{0,3},{1,2},{2,1},{3,0},{4,7},{5,6},{6,5},{7,4},{8,11},{9,10},{10,... | collective-permute-start | bytes 6152 | tf_op jit(solution)/shard_map/ppermute | solution.py:210
  61.3 2.2 %collective-permute-done.21.refs_2_ = f32[4,128]{1,0:T(4,128)S(1)} collective-permute-done((f32[4,128]{1,0:T(4,128)S(1)}, f32[4,128]{1,0:T(4,128)S(1)}, u32[]{:S(2)}, u32[]{:S(2)}) %collective-permute-start.21) | collective-permute-done | bytes 2080 | tf_op jit(solution)/shard_map/ppermute | solution.py:210
  (30 shorter events, 4.0 us)
Async XLA Ops:
  3.5 19.1 %collective-permute-start = (f32[5,128,512]{2,1,0:T(8,128)S(1)}, f32[5,128,512]{2,1,0:T(8,128)S(1)}, u32[]{:S(2)}, u32[]{:S(2)}) collective-permute-start(f32[5,128,512]{2,1,0:T(8,128)S(1)} %get-tuple-element.30), channel_id=1, source_target_pairs={{0,1},{1,0},{2,3},{3,2},{4,5},{5,4},{6,7},{7,6},{8,9},{9,8},{10,11... | collective-permute-start | bytes 3932168 | tf_op jit(solution)/shard_map/ppermute | solution.py:210
  4.0 6.9 %collective-permute-start.3 = (f32[64,512]{1,0:T(8,128)S(1)}, f32[64,512]{1,0:T(8,128)S(1)}, u32[]{:S(2)}, u32[]{:S(2)}) collective-permute-start(f32[64,512]{1,0:T(8,128)S(1)} %get-tuple-element.33), channel_id=1, source_target_pairs={{0,2},{1,3},{2,0},{3,1},{4,6},{5,7},{6,4},{7,5},{8,10},{9,11},{10,... | collective-permute-start | bytes 393224 | tf_op jit(solution)/shard_map/ppermute | solution.py:210
  6.5 14.3 %collective-permute-start.1 = (f32[2,128,256]{2,1,0:T(8,128)S(1)}, f32[2,128,256]{2,1,0:T(8,128)S(1)}, u32[]{:S(2)}, u32[]{:S(2)}) collective-permute-start(f32[2,128,256]{2,1,0:T(8,128)S(1)} %get-tuple-element.31), channel_id=1, source_target_pairs={{0,2},{1,3},{2,0},{3,1},{4,6},{5,7},{6,4},{7,5},{8,10},{9,11},{10,... | collective-permute-start | bytes 786440 | tf_op jit(solution)/shard_map/ppermute | solution.py:210
  10.9 5.0 %collective-permute-start.4 = (f32[64,512]{1,0:T(8,128)S(1)}, f32[64,512]{1,0:T(8,128)S(1)}, u32[]{:S(2)}, u32[]{:S(2)}) collective-permute-start(f32[64,512]{1,0:T(8,128)S(1)} %collective-permute-done.3.refs_2_), channel_id=1, source_target_pairs={{0,4},{1,5},{2,6},{3,7},{4,0},{5,1},{6,2},{7,3},{8,12},{9,13},{10,... | collective-permute-start | bytes 393224 | tf_op jit(solution)/shard_map/ppermute | solution.py:210
  12.9 5.9 %collective-permute-start.2 = (f32[2,128,128]{2,1,0:T(8,128)S(1)}, f32[2,128,128]{2,1,0:T(8,128)S(1)}, u32[]{:S(2)}, u32[]{:S(2)}) collective-permute-start(f32[2,128,128]{2,1,0:T(8,128)S(1)} %get-tuple-element.32), channel_id=1, source_target_pairs={{0,3},{1,2},{2,1},{3,0},{4,7},{5,6},{6,5},{7,4},{8,11},{9,10},{10,... | collective-permute-start | bytes 393224 | tf_op jit(solution)/shard_map/ppermute | solution.py:210
  12.9 7.5 %collective-permute-start.5 = (f32[64,512]{1,0:T(8,128)S(1)}, f32[64,512]{1,0:T(8,128)S(1)}, u32[]{:S(2)}, u32[]{:S(2)}) collective-permute-start(f32[64,512]{1,0:T(8,128)S(1)} %collective-permute-done.3.refs_2_), channel_id=1, source_target_pairs={{0,1},{1,0},{2,3},{3,2},{4,5},{5,4},{6,7},{7,6},{8,9},{9,8},{10,11... | collective-permute-start | bytes 393224 | tf_op jit(solution)/shard_map/ppermute | solution.py:210
  15.9 5.8 %collective-permute-start.6 = (f32[64,512]{1,0:T(8,128)S(1)}, f32[64,512]{1,0:T(8,128)S(1)}, u32[]{:S(2)}, u32[]{:S(2)}) collective-permute-start(f32[64,512]{1,0:T(8,128)S(1)} %collective-permute-done.4.refs_3_), channel_id=1, source_target_pairs={{0,1},{1,0},{2,3},{3,2},{4,5},{5,4},{6,7},{7,6},{8,9},{9,8},{10,11... | collective-permute-start | bytes 393224 | tf_op jit(solution)/shard_map/ppermute | solution.py:210
  18.8 9.6 %collective-permute-start.7 = (f32[1,128,256]{2,1,0:T(8,128)S(1)}, f32[1,128,256]{2,1,0:T(8,128)S(1)}, u32[]{:S(2)}, u32[]{:S(2)}) collective-permute-start(f32[1,128,256]{2,1,0:T(8,128)S(1)} %get-tuple-element.36), channel_id=1, source_target_pairs={{0,2},{1,3},{2,0},{3,1},{4,6},{5,7},{6,4},{7,5},{8,10},{9,11},{10,... | collective-permute-start | bytes 393224 | tf_op jit(solution)/shard_map/ppermute | solution.py:210
  20.4 10.5 %collective-permute-start.10 = (f32[1,128,256]{2,1,0:T(8,128)S(1)}, f32[1,128,256]{2,1,0:T(8,128)S(1)}, u32[]{:S(2)}, u32[]{:S(2)}) collective-permute-start(f32[1,128,256]{2,1,0:T(8,128)S(1)} %get-tuple-element.38), channel_id=1, source_target_pairs={{0,2},{1,3},{2,0},{3,1},{4,6},{5,7},{6,4},{7,5},{8,10},{9,11},{10,... | collective-permute-start | bytes 393224 | tf_op jit(solution)/shard_map/ppermute | solution.py:210
  20.8 7.6 %collective-permute-start.8 = (f32[1,128,128]{2,1,0:T(8,128)S(1)}, f32[1,128,128]{2,1,0:T(8,128)S(1)}, u32[]{:S(2)}, u32[]{:S(2)}) collective-permute-start(f32[1,128,128]{2,1,0:T(8,128)S(1)} %get-tuple-element.37), channel_id=1, source_target_pairs={{0,3},{1,2},{2,1},{3,0},{4,7},{5,6},{6,5},{7,4},{8,11},{9,10},{10,... | collective-permute-start | bytes 196616 | tf_op jit(solution)/shard_map/ppermute | solution.py:210
  21.7 9.2 %collective-permute-start.11 = (f32[1,128,128]{2,1,0:T(8,128)S(1)}, f32[1,128,128]{2,1,0:T(8,128)S(1)}, u32[]{:S(2)}, u32[]{:S(2)}) collective-permute-start(f32[1,128,128]{2,1,0:T(8,128)S(1)} %get-tuple-element.39), channel_id=1, source_target_pairs={{0,3},{1,2},{2,1},{3,0},{4,7},{5,6},{6,5},{7,4},{8,11},{9,10},{10,... | collective-permute-start | bytes 196616 | tf_op jit(solution)/shard_map/ppermute | solution.py:210
  30.0 3.1 %collective-permute-start.9 = (f32[512,512]{1,0:T(8,128)S(1)}, f32[512,512]{1,0:T(8,128)S(1)}, u32[]{:S(2)}, u32[]{:S(2)}) collective-permute-start(f32[512,512]{1,0:T(8,128)S(1)} %gain.2.g3.refs_11_), channel_id=1, source_target_pairs={{0,1},{1,0},{2,3},{3,2},{4,5},{5,4},{6,7},{7,6},{8,9},{9,8},{10,11... | collective-permute-start | bytes 3145736 | tf_op jit(solution)/shard_map/ppermute | solution.py:210
  32.5 2.7 %collective-permute-start.12 = (f32[512,512]{1,0:T(8,128)S(1)}, f32[512,512]{1,0:T(8,128)S(1)}, u32[]{:S(2)}, u32[]{:S(2)}) collective-permute-start(f32[512,512]{1,0:T(8,128)S(1)} %gain.3.g2), channel_id=1, source_target_pairs={{0,1},{1,0},{2,3},{3,2},{4,5},{5,4},{6,7},{7,6},{8,9},{9,8},{10,11... | collective-permute-start | bytes 3145736 | tf_op jit(solution)/shard_map/ppermute | solution.py:210
  36.4 3.7 %collective-permute-start.13 = (f32[1,512]{1,0:T(1,128)S(1)}, f32[1,512]{1,0:T(1,128)S(1)}, u32[]{:S(2)}, u32[]{:S(2)}) collective-permute-start(f32[1,512]{1,0:T(1,128)S(1)} %hop.7), channel_id=1, source_target_pairs={{0,4},{1,5},{2,6},{3,7},{4,0},{5,1},{6,2},{7,3},{8,12},{9,13},{10,... | collective-permute-start | bytes 6152 | tf_op jit(solution)/shard_map/ppermute | solution.py:210
  40.2 0.7 %collective-permute-start.14 = (f32[1,512]{1,0:T(1,128)S(1)}, f32[1,512]{1,0:T(1,128)S(1)}, u32[]{:S(2)}, u32[]{:S(2)}) collective-permute-start(f32[1,512]{1,0:T(1,128)S(1)} %hop.8), channel_id=1, source_target_pairs={{25,21}} | collective-permute-start | bytes 6152 | tf_op jit(solution)/shard_map/ppermute | solution.py:304
  41.0 3.7 %collective-permute-start.15 = (f32[1,512]{1,0:T(1,128)S(1)}, f32[1,512]{1,0:T(1,128)S(1)}, u32[]{:S(2)}, u32[]{:S(2)}) collective-permute-start(f32[1,512]{1,0:T(1,128)S(1)} %hop.9), channel_id=1, source_target_pairs={{0,4},{1,5},{2,6},{3,7},{4,0},{5,1},{6,2},{7,3},{8,12},{9,13},{10,... | collective-permute-start | bytes 6152 | tf_op jit(solution)/shard_map/ppermute | solution.py:210
  44.8 0.7 %collective-permute-start.16 = (f32[1,512]{1,0:T(1,128)S(1)}, f32[1,512]{1,0:T(1,128)S(1)}, u32[]{:S(2)}, u32[]{:S(2)}) collective-permute-start(f32[1,512]{1,0:T(1,128)S(1)} %hop.10), channel_id=1, source_target_pairs={{17,13}} | collective-permute-start | bytes 6152 | tf_op jit(solution)/shard_map/ppermute | solution.py:304
  45.7 3.7 %collective-permute-start.17 = (f32[1,512]{1,0:T(1,128)S(1)}, f32[1,512]{1,0:T(1,128)S(1)}, u32[]{:S(2)}, u32[]{:S(2)}) collective-permute-start(f32[1,512]{1,0:T(1,128)S(1)} %hop.11), channel_id=1, source_target_pairs={{0,4},{1,5},{2,6},{3,7},{4,0},{5,1},{6,2},{7,3},{8,12},{9,13},{10,... | collective-permute-start | bytes 6152 | tf_op jit(solution)/shard_map/ppermute | solution.py:210
  49.5 0.7 %collective-permute-start.18 = (f32[1,512]{1,0:T(1,128)S(1)}, f32[1,512]{1,0:T(1,128)S(1)}, u32[]{:S(2)}, u32[]{:S(2)}) collective-permute-start(f32[1,512]{1,0:T(1,128)S(1)} %hop.12), channel_id=1, source_target_pairs={{9,5}} | collective-permute-start | bytes 6152 | tf_op jit(solution)/shard_map/ppermute | solution.py:304
  50.3 3.7 %collective-permute-start.19 = (f32[1,512]{1,0:T(1,128)S(1)}, f32[1,512]{1,0:T(1,128)S(1)}, u32[]{:S(2)}, u32[]{:S(2)}) collective-permute-start(f32[1,512]{1,0:T(1,128)S(1)} %hop.13), channel_id=1, source_target_pairs={{0,4},{1,5},{2,6},{3,7},{4,0},{5,1},{6,2},{7,3},{8,12},{9,13},{10,... | collective-permute-start | bytes 6152 | tf_op jit(solution)/shard_map/ppermute | solution.py:210
  54.3 7.0 %collective-permute-start.20 = (f32[4,128]{1,0:T(4,128)S(1)}, f32[4,128]{1,0:T(4,128)S(1)}, u32[]{:S(2)}, u32[]{:S(2)}) collective-permute-start(f32[4,128]{1,0:T(4,128)S(1)} %get-tuple-element.46), channel_id=1, source_target_pairs={{0,1},{1,0},{2,3},{3,2},{4,5},{5,4},{6,7},{7,6},{8,9},{9,8},{10,11... | collective-permute-start | bytes 6152 | tf_op jit(solution)/shard_map/ppermute | solution.py:210
  59.9 3.6 %collective-permute-start.21 = (f32[4,128]{1,0:T(4,128)S(1)}, f32[4,128]{1,0:T(4,128)S(1)}, u32[]{:S(2)}, u32[]{:S(2)}) collective-permute-start(f32[4,128]{1,0:T(4,128)S(1)} %get-tuple-element.47), channel_id=1, source_target_pairs={{0,2},{1,3},{2,0},{3,1},{4,6},{5,7},{6,4},{7,5},{8,10},{9,11},{10,... | collective-permute-start | bytes 6152 | tf_op jit(solution)/shard_map/ppermute | solution.py:210
  59.9 3.6 %collective-permute-start.22 = (f32[4,128]{1,0:T(4,128)S(1)}, f32[4,128]{1,0:T(4,128)S(1)}, u32[]{:S(2)}, u32[]{:S(2)}) collective-permute-start(f32[4,128]{1,0:T(4,128)S(1)} %get-tuple-element.48), channel_id=1, source_target_pairs={{0,3},{1,2},{2,1},{3,0},{4,7},{5,6},{6,5},{7,4},{8,11},{9,10},{10,... | collective-permute-start | bytes 6152 | tf_op jit(solution)/shard_map/ppermute | solution.py:210

commit v6 on v5

v6 whole, which is shorter than its diff:
```python
import functools

import jax
import jax.numpy as jnp
from jax import lax
from jax.experimental import pallas as pl
from jax.experimental.pallas import tpu as pltpu
from jax.sharding import PartitionSpec as P

F32, BF16 = jnp.float32, jnp.bfloat16
NN = (((1,), (0,)), ((), ()))
NT = (((1,), (1,)), ((), ()))
ANY = pl.BlockSpec(memory_space=pl.ANY)
HBM = pl.BlockSpec(memory_space=pltpu.HBM)
VMEM = pl.BlockSpec(memory_space=pltpu.VMEM)


def split(x):
    high = x.astype(BF16)
    return high, (x - high.astype(F32)).astype(BF16)


def dot3(a, b, dims):
    (ah, al), (bh, bl) = split(a), split(b)
    dot = functools.partial(lax.dot_general, dimension_numbers=dims, preferred_element_type=F32)
    return dot(ah, bh) + (dot(ah, bl) + dot(al, bh))


def matvec(matrix, row):
    order = matrix.shape[1]
    total = matrix[:, :128] * row[:, :128]
    for j in range(128, order, 128):
        total += matrix[:, j : j + 128] * row[:, j : j + 128]
    return jnp.sum(total.T, axis=0, keepdims=True)


def rows(i, panel):
    return pl.ds(pl.multiple_of(i * panel, panel), panel)


def starter(sems):
    copies = []

    def start(source, target):
        copy = pltpu.make_async_copy(source, target, sems.at[len(copies)])
        copy.start()
        copies.append(copy)

    return start, copies


def width(devices, panel, order, off):
    if off < 2:
        return order
    return panel if devices == 4 and off == 3 and panel % 128 == 0 else order - 2 * panel


def far_copies(devices, start, matrix, far):
    steps, panel, order = matrix.shape
    s = lax.axis_index("state")
    for off, piece in enumerate(far, 2):
        w = width(devices, panel, order, off)
        column = 2 * panel if w == order - 2 * panel else pl.multiple_of(s * panel, panel)
        mine = pl.ds(((s ^ off) % 2) * (steps // 2), steps // 2)
        start(matrix.at[mine, :, pl.ds(column, w)], piece)


def pack_kernel(devices, cov, prec, trans, means, terminal, *refs):
    far, (trans_half, first, near, own, own_means, vector, sems) = refs[: 2 * devices - 4], refs[2 * devices - 4 :]
    count, panel = cov.shape[0] // 2, cov.shape[1]
    b, s = lax.axis_index("tm"), lax.axis_index("state")
    start, copies = starter(sems)
    start(terminal, vector)
    start(trans.at[pl.ds(pl.multiple_of((b % 2) * (panel // 2), panel // 2), panel // 2), :], trans_half)
    far_copies(devices, start, cov, far[: devices - 2])
    far_copies(devices, start, prec, far[devices - 2 :])
    for target, half in ((near, 1 - s % 2), (own, s % 2)):
        start(cov.at[pl.ds(half * count, count)], target.at[pl.ds(0, count)])
        start(prec.at[pl.ds(half * count, count)], target.at[pl.ds(count, count)])
        start(trans, target.at[2 * count])
    start(means, own_means)
    copies[0].wait()
    first[...] = jnp.where(b == lax.axis_size("tm") - 1, vector[...], 0.0)
    for copy in copies[1:]:
        copy.wait()


def join_kernel(*refs):
    moved, (joined, sems) = refs[:-2], refs[-2:]
    half = moved[0].shape[0]
    b = lax.axis_index("tm")
    start, copies = starter(sems)
    for k, piece in enumerate(moved):
        at = (b % 2 if k % 2 == 0 else 1 - b % 2) * half
        start(piece, joined.at[k // 2, pl.ds(pl.multiple_of(at, half), half), :])
    for copy in copies:
        copy.wait()


def cov_kernel(means, own, near, joined, joined_near, *refs):
    far, (gains, late, info, pf, af, lf, sems) = refs[:-7], refs[-7:]
    _, panel, order = own.shape
    count, known = far[0].shape[0], 2 * panel
    steps = means.shape[0]
    e = lax.axis_index("state") % 2
    start, copies = starter(sems)
    for k in range(count):
        full = pf.at[pl.ds(k * order, order), :]
        start(own.at[k], full.at[rows(e, panel), :])
        start(near.at[k], full.at[rows(1 - e, panel), :])
        start(own.at[count + k], lf.at[k, rows(e, panel), :])
        start(near.at[count + k], lf.at[k, rows(1 - e, panel), :])
        for off, piece in enumerate(far, 2):
            i = e ^ off
            w = piece.shape[2]
            column = known if w == order - known else pl.multiple_of(i * panel, panel)
            start(piece.at[k], full.at[rows(i, panel), pl.ds(column, w)])
    for j in range(order // (2 * panel)):
        mine, theirs = (own.at[2 * count], near.at[2 * count]) if j == 0 else (joined.at[j - 1], joined_near.at[j - 1])
        start(mine, af.at[rows(e ^ (2 * j), panel), :])
        start(theirs, af.at[rows(e ^ (2 * j) ^ 1, panel), :])
    pf[count * order :, :] = jnp.concatenate([means[...], jnp.zeros((16 - steps, order), F32)], axis=0)
    for copy in copies:
        copy.wait()
    for k in range(count):
        full = pf.at[pl.ds(k * order, order), :]
        full[known:order, :known] = full[:known, known:order].T
        if far[-1].shape[2] < order - known:
            i, j = e ^ 3, e ^ 2
            full[rows(i, panel), rows(j, panel)] = full[rows(j, panel), rows(i, panel)].T
    product = dot3(pf[...], af[...], NT)
    info[:8] = pf[count * order : count * order + 8, :]
    info[8:] = product[count * order : count * order + 8]
    late[...] = product[: count * order, known:]
    for k in range(count):
        part = product[k * order : (k + 1) * order]
        partial = dot3(part[:, :known], lf[k], NN)
        gains[k, :, :known] = partial[:, :known] + dot3(part[:, known:], lf[k, :, known:], NT)
        gains[k, :, known:] = partial[:, known:]


def gain_kernel(info, gains, late, *refs):
    far, (map_ref, gain_ref, ff) = refs[:-3], refs[-3:]
    count, panel, _ = far[0].shape
    order = gains.shape[1]
    known = 2 * panel
    s = lax.axis_index("state")
    e = s % 2
    for k in range(count):
        for off, piece in enumerate(far, 2):
            i = (e ^ off) - 2
            if piece.shape[2] == order - known:
                ff[k, rows(i, panel), :] = piece[k]
            else:
                ff[k, rows(i, panel), rows(i, panel)] = piece[k]
        if far[-1].shape[2] < order - known:
            i, j = (e ^ 3) - 2, (e ^ 2) - 2
            ff[k, rows(i, panel), rows(j, panel)] = ff[k, rows(j, panel), rows(i, panel)].T

    def complete(k):
        rest = gains[k, :, known:] + dot3(late[k * order : (k + 1) * order, :], ff[k], NN)
        return jnp.concatenate([gains[k, :, :known], rest], axis=1)

    ga, gb = complete(0), complete(1)
    gain_ref[...] = gb
    a = e * count
    mean_a, mean_b = info[pl.ds(a, 1), :], info[pl.ds(a + 1, 1), :]
    pred_a, pred_b = info[pl.ds(a + 8, 1), :], info[pl.ds(a + 9, 1), :]
    map_ref[order:, :] = jnp.concatenate(
        [mean_a + matvec(ga, mean_b - pred_a), mean_b, pred_b, jnp.zeros((5, order), F32)], axis=0
    )
    map_ref[:order, :] = dot3(ga, gb, NN)


def block_kernel(late, early, m_ref, vec_ref):
    order = late.shape[1]
    shift = early[order : order + 1, :] + matvec(
        early[:order, :], late[order : order + 1, :] - early[order + 2 : order + 3, :]
    )
    vec_ref[...] = jnp.concatenate([late[order + 2 : order + 3, :], shift, jnp.zeros((6, order), F32)], axis=0)
    m_ref[...] = dot3(early[:order, :], late[:order, :], NN)


def hop_kernel(x, m, vec, out_ref):
    out_ref[...] = vec[1:2, :] + matvec(m[...], x[...] - vec[0:1, :])


def last_kernel(devices, *refs):
    blocks = len(refs) - 7 - devices
    incoming, (m, vec, late, g3, early, g1), outs, cut = refs[:blocks], refs[blocks : blocks + 6], refs[blocks + 6 : -1], refs[-1]
    order, panel = m.shape[1], outs[0].shape[1]
    b, s = lax.axis_index("tm"), lax.axis_index("state")
    x = incoming[0][...]
    for k, ref in enumerate(incoming[1:], 1):
        x = jnp.where(lax.axis_size("tm") - 1 - b == k, ref[...], x)
    gap = x - vec[0:1, :]
    x3 = late[order + 1 : order + 2, :] + matvec(g3[...], gap)
    x2 = late[order : order + 1, :] + matvec(late[:order, :], gap)
    x0 = vec[1:2, :] + matvec(m[...], gap)
    x1 = early[order + 1 : order + 2, :] + matvec(g1[...], x2 - early[order + 2 : order + 3, :])
    full = jnp.concatenate([x0, x1, x2, x3], axis=0)
    for i in range(devices):
        cut[i] = full[:, i * panel : (i + 1) * panel]
    for off, out in enumerate(outs):
        out[...] = cut[s ^ off]


def out_kernel(*refs):
    given, out_ref = refs[:-1], refs[-1]
    off = lax.axis_index("state") ^ 1
    x = given[0][...]
    for k, ref in enumerate(given[1:], 1):
        x = jnp.where(off == k, ref[...], x)
    out_ref[...] = x


def params(mebibytes):
    return pltpu.CompilerParams(vmem_limit_bytes=mebibytes * 2**20)


def local(filtered_covariance, pred_prec, transition, filt_means, terminal_mean):
    steps, panel, order = filtered_covariance.shape
    devices, blocks = lax.axis_size("state"), lax.axis_size("tm")
    count = steps // 2

    def swap(x, off, block_off=0):
        pairs = [(i, i ^ (block_off * devices + off)) for i in range(blocks * devices)]
        return lax.ppermute(x, ("tm", "state"), pairs)

    def shape(*dims):
        return jax.ShapeDtypeStruct(dims, F32)

    def call(kernel, name, mebibytes, outs, in_specs, scratch, args):
        return pl.pallas_call(
            kernel,
            out_shape=outs,
            in_specs=in_specs,
            out_specs=[VMEM] * len(outs),
            scratch_shapes=scratch,
            compiler_params=params(mebibytes),
            name=name,
        )(*args)

    cov, prec, trans, means, terminal = (
        pltpu.with_memory_space_constraint(x, pltpu.HBM)
        for x in (filtered_covariance, pred_prec, transition, filt_means, terminal_mean[None])
    )
    semaphores = pltpu.SemaphoreType.DMA((8 * devices,))
    square = shape(order, order)

    far = [shape(count, panel, width(devices, panel, order, off)) for off in range(2, devices)]
    panels = shape(2 * count + 1, panel, order)
    *far, trans_half, first, near, own, own_means = call(
        functools.partial(pack_kernel, devices),
        "pack",
        4,
        far + far + [shape(panel // 2, order), shape(1, order), panels, panels, shape(steps, order)],
        [HBM] * 5,
        [pltpu.VMEM((1, order), F32), semaphores],
        (cov, prec, trans, means, terminal),
    )
    across = [swap(trans_half, off) for off in range(2, devices, 2)]
    cov_far, prec_far = ([swap(x, off) for off, x in enumerate(part, 2)] for part in (far[: devices - 2], far[devices - 2 :]))
    near = swap(near, 1)
    moved = [y for x in across for y in (x, swap(x, 0, 1))]
    (joined,) = call(
        join_kernel, "join", 4, [shape(devices // 2 - 1, panel, order)], [ANY] * len(moved), [semaphores], moved
    )
    joined_near = swap(joined, 1)

    gains, late, info = call(
        cov_kernel,
        "cov",
        28,
        [shape(count, order, order), shape(count * order, order - 2 * panel), shape(16, order)],
        [VMEM] + [ANY] * (devices + 2),
        [
            pltpu.VMEM((count * order + 16, order), F32),
            pltpu.VMEM((order, order), F32),
            pltpu.VMEM((count, 2 * panel, order), F32),
            semaphores,
        ],
        (own_means, own, near, joined, joined_near, *cov_far),
    )
    late_map, g3 = call(
        gain_kernel,
        "gain",
        20,
        [shape(order + 8, order), square],
        [VMEM] * (1 + devices),
        [pltpu.VMEM((count, order - 2 * panel, order - 2 * panel), F32)],
        (info, gains, late, *prec_far),
    )
    early_map = swap(late_map, 1)
    m, vec = call(block_kernel, "block", 12, [square, shape(8, order)], [VMEM] * 2, [], (late_map, early_map))

    incoming = [first]
    for block in range(blocks - 1, 0, -1):
        (x,) = call(hop_kernel, "hop", 4, [shape(1, order)], [VMEM] * 3, [], (incoming[-1], m, vec))
        if block % 2:
            x = swap(x, 0, 1)
        else:
            x = lax.ppermute(x, ("tm", "state"), [(block * devices + 1, (block - 1) * devices + 1)])
        incoming.append(x)
    g1 = swap(lax.optimization_barrier((g3, incoming[1]))[0], 1)

    given = list(call(
        functools.partial(last_kernel, devices),
        "last",
        8,
        [shape(steps, panel)] * devices,
        [VMEM] * (blocks + 6),
        [pltpu.VMEM((devices, steps, panel), F32)],
        (*incoming, m, vec, late_map, g3, early_map, g1),
    ))
    for off in range(devices - 1, 0, -1):
        given[off] = swap(given[off], off)
    (out,) = call(out_kernel, "out", 4, [shape(steps, panel)], [VMEM] * devices, [], given)
    return out


def solution(mesh):
    return jax.shard_map(
        local,
        mesh=mesh,
        in_specs=(
            P("tm", "state", None),
            P("tm", "state", None),
            P("state", None),
            P("tm", None),
            P(),
        ),
        out_specs=P("tm", "state"),
        check_vma=False,
    )
```

time: 64.3 us -> 64.1 us (level)
  waiting for transfers between devices: 20.9 us -> 26.9 us
  starting transfers between devices: 28 us -> 24.4 us
  Pallas kernels: 15 us -> 12.4 us
    ppermute x20 -> x17, waiting for transfers between devices: 20.9 us -> 26.9 us  [swap(): return lax.ppermute(x, ('tm', 'state'), pairs)]
    ppermute x20 -> x17, starting transfers between devices: 26 us -> 22.4 us  [swap(): return lax.ppermute(x, ('tm', 'state'), pairs)]
    pallas_call x16 -> x14, Pallas kernels: 15 us -> 12.4 us  [call(): pl.pallas_call(kernel, out_shape=outs, in_specs=in_specs, out_specs=[VMEM...]
  transfers between devices with their start and end apart: 23 -> 20, of which waited for: 11 -> 10; matrix products, arithmetic and copies ran while one was open for 0% -> 0% of each run, Pallas kernels for 13% -> 10%
where the time goes in v6:
time: 64.1 us; the launch traced here: 63.9 us
  waiting for transfers between devices  26.9 us (42%)
  starting transfers between devices  24.4 us (38%)
  Pallas kernels  12.4 us (19%)
    ppermute x17, waiting for transfers between devices, swap(): return lax.ppermute(x, ('tm', 'state'), pairs)  26.9 us
    ppermute x17, starting transfers between devices, swap(): return lax.ppermute(x, ('tm', 'state'), pairs)  22.4 us
    pallas_call x14, Pallas kernels, call(): pl.pallas_call(kernel, out_shape=outs, in_specs=in_specs, out_specs=[VMEM...  12.4 us
    ppermute x3, starting transfers between devices, local(): lax.ppermute(x, ('tm', 'state'), [(block * devices + 1, (block - 1) * dev...  1.98 us
  transfers between devices with their start and end apart: 20, of which 10 were waited for; matrix products, arithmetic and copies ran while one was open for 0% of the time, Pallas kernels for 10%

profile of v6, /device:TPU:0, one launch (start us, length us, event | category | flops | bytes accessed | tf_op | source)
XLA Modules:
  0.0 63.9 jit_solution(8932101492200699262)
XLA Ops:
  0.0 2.3 %pack.1 = (f32[2,128,256]{2,1,0:T(8,128)S(1)}, f32[2,128,128]{2,1,0:T(8,128)S(1)}, f32[2,128,256]{2,1,0:T(8,128)S(1)}, f32[2,128,128]{2,1,0:T(8,128)S(1)}, f32[6...) custom-call(f32[4,128,512]{2,1,0:T(8,128)} %cov.2, ...), custom_call_target="tpu_custom_call" | custom-call | tf_op jit(solution)/shard_map/pack/pallas_call | solution.py:234
  2.3 0.5 collective-permute-start
  2.9 2.7 %collective-permute-start.1 = (f32[64,512]{1,0:T(8,128)S(1)}, f32[64,512]{1,0:T(8,128)S(1)}, u32[]{:S(2)}, u32[]{:S(2)}) collective-permute-start(f32[64,512]{1,0:T(8,128)S(1)} %get-tuple-element.30), channel_id=1, source_target_pairs={{0,2},{1,3},{2,0},{3,1},{4,6},{5,7},{6,4},{7,5},{8,10},{9,11},{10,... | collective-permute-start | bytes 393224 | tf_op jit(solution)/shard_map/ppermute | solution.py:228
  5.5 4.1 %collective-permute-done.1.refs_0_ = f32[64,512]{1,0:T(8,128)S(1)} collective-permute-done((f32[64,512]{1,0:T(8,128)S(1)}, f32[64,512]{1,0:T(8,128)S(1)}, u32[]{:S(2)}, u32[]{:S(2)}) %collective-permute-start.1) | collective-permute-done | bytes 131104 | tf_op jit(solution)/shard_map/ppermute | solution.py:228
  9.6 1.7 %collective-permute-start.2 = (f32[64,512]{1,0:T(8,128)S(1)}, f32[64,512]{1,0:T(8,128)S(1)}, u32[]{:S(2)}, u32[]{:S(2)}) collective-permute-start(f32[64,512]{1,0:T(8,128)S(1)} %collective-permute-done.1.refs_0_), channel_id=1, source_target_pairs={{0,4},{1,5},{2,6},{3,7},{4,0},{5,1},{6,2},{7,3},{8,12},{9,13},{10,... | collective-permute-start | bytes 393224 | tf_op jit(solution)/shard_map/ppermute | solution.py:228
  11.3 1.6 %collective-permute-start.4 = (f32[2,128,256]{2,1,0:T(8,128)S(1)}, f32[2,128,256]{2,1,0:T(8,128)S(1)}, u32[]{:S(2)}, u32[]{:S(2)}) collective-permute-start(f32[2,128,256]{2,1,0:T(8,128)S(1)} %get-tuple-element.31), channel_id=1, source_target_pairs={{0,2},{1,3},{2,0},{3,1},{4,6},{5,7},{6,4},{7,5},{8,10},{9,11},{10,... | collective-permute-start | bytes 786440 | tf_op jit(solution)/shard_map/ppermute | solution.py:228
  12.9 2.0 %collective-permute-done.2.refs_1_ = f32[64,512]{1,0:T(8,128)S(1)} collective-permute-done((f32[64,512]{1,0:T(8,128)S(1)}, f32[64,512]{1,0:T(8,128)S(1)}, u32[]{:S(2)}, u32[]{:S(2)}) %collective-permute-start.2) | collective-permute-done | bytes 131104 | tf_op jit(solution)/shard_map/ppermute | solution.py:228
  14.9 0.6 join.1.joined
  15.5 1.7 %collective-permute-start.5 = (f32[2,128,128]{2,1,0:T(8,128)S(1)}, f32[2,128,128]{2,1,0:T(8,128)S(1)}, u32[]{:S(2)}, u32[]{:S(2)}) collective-permute-start(f32[2,128,128]{2,1,0:T(8,128)S(1)} %get-tuple-element.32), channel_id=1, source_target_pairs={{0,3},{1,2},{2,1},{3,0},{4,7},{5,6},{6,5},{7,4},{8,11},{9,10},{10,... | collective-permute-start | bytes 393224 | tf_op jit(solution)/shard_map/ppermute | solution.py:228
  17.2 0.5 collective-permute-start.6
  17.7 3.7 %collective-permute-done.5.refs_1_ = f32[2,128,128]{2,1,0:T(8,128)S(1)} collective-permute-done((f32[2,128,128]{2,1,0:T(8,128)S(1)}, f32[2,128,128]{2,1,0:T(8,128)S(1)}, u32[]{:S(2)}, u32[]{:S(2)}) %collective-permute-start.5) | collective-permute-done | bytes 131104 | tf_op jit(solution)/shard_map/ppermute | solution.py:228
  21.4 1.6 %collective-permute-start.7 = (f32[2,128,128]{2,1,0:T(8,128)S(1)}, f32[2,128,128]{2,1,0:T(8,128)S(1)}, u32[]{:S(2)}, u32[]{:S(2)}) collective-permute-start(f32[2,128,128]{2,1,0:T(8,128)S(1)} %get-tuple-element.37), channel_id=1, source_target_pairs={{0,3},{1,2},{2,1},{3,0},{4,7},{5,6},{6,5},{7,4},{8,11},{9,10},{10,... | collective-permute-start | bytes 393224 | tf_op jit(solution)/shard_map/ppermute | solution.py:228
  23.0 4.8 %cov.3 = (f32[2,512,512]{2,1,0:T(8,128)S(1)}, f32[1024,256]{1,0:T(8,128)S(1)}, f32[16,512]{1,0:T(8,128)S(1)}) custom-call(f32[4,512]{1,0:T(4,128)S(1)} %get-tuple-element.27.means, f32[5,128,512]{2,1,0:T(8,128)S(1)} %get-tuple-element.28.own, f32[5,128,512]{2,1,0:T(8,128)S(1)} %collective-permute-done.near, f32[1,128,512]{2,1,0:T(8,128)S(1)} %join.1.joined, ...), custom_call_target="tpu_custom_call" | custom-call | tf_op jit(solution)/shard_map/cov/pallas_call | solution.py:234
  27.8 2.0 %collective-permute-done.7.refs_1_ = f32[2,128,128]{2,1,0:T(8,128)S(1)} collective-permute-done((f32[2,128,128]{2,1,0:T(8,128)S(1)}, f32[2,128,128]{2,1,0:T(8,128)S(1)}, u32[]{:S(2)}, u32[]{:S(2)}) %collective-permute-start.7) | collective-permute-done | bytes 131104 | tf_op jit(solution)/shard_map/ppermute | solution.py:228
  29.8 1.7 %gain.1 = (f32[520,512]{1,0:T(8,128)S(1)}, f32[512,512]{1,0:T(8,128)S(1)}) custom-call(f32[16,512]{1,0:T(8,128)S(1)} %get-tuple-element.33.info, f32[2,512,512]{2,1,0:T(8,128)S(1)} %get-tuple-element.34.gains, f32[1024,256]{1,0:T(8,128)S(1)} %get-tuple-element.35.late, f32[2,128,256]{2,1,0:T(8,128)S(1)} %collective-permute-done.6.refs_0_, ...), custom_call_target="tpu_custom_call" | custom-call | tf_op jit(solution)/shard_map/gain/pallas_call | solution.py:234
  31.7 2.6 %collective-permute-done.8.early.refs_12_ = f32[520,512]{1,0:T(8,128)S(1)} collective-permute-done((f32[520,512]{1,0:T(8,128)S(1)}, f32[520,512]{1,0:T(8,128)S(1)}, u32[]{:S(2)}, u32[]{:S(2)}) %collective-permute-start.8) | collective-permute-done | bytes 1064992 | tf_op jit(solution)/shard_map/ppermute | solution.py:228
  34.3 1.0 %block.1 = (f32[512,512]{1,0:T(8,128)S(1)}, f32[8,512]{1,0:T(8,128)S(1)}) custom-call(f32[520,512]{1,0:T(8,128)S(1)} %get-tuple-element.38.late.refs_10_, f32[520,512]{1,0:T(8,128)S(1)} %collective-permute-done.8.early.refs_12_), custom_call_target="tpu_custom_call" | custom-call | tf_op jit(solution)/shard_map/block/pallas_call | solution.py:234
  35.4 1.0 %collective-permute-start.9 = (f32[1,512]{1,0:T(1,128)S(1)}, f32[1,512]{1,0:T(1,128)S(1)}, u32[]{:S(2)}, u32[]{:S(2)}) collective-permute-start(f32[1,512]{1,0:T(1,128)S(1)} %hop.7), channel_id=1, source_target_pairs={{0,4},{1,5},{2,6},{3,7},{4,0},{5,1},{6,2},{7,3},{8,12},{9,13},{10,... | collective-permute-start | bytes 6152 | tf_op jit(solution)/shard_map/ppermute | solution.py:228
  36.5 2.6 %collective-permute-done.9.x.refs_1_ = f32[1,512]{1,0:T(1,128)S(1)} collective-permute-done((f32[1,512]{1,0:T(1,128)S(1)}, f32[1,512]{1,0:T(1,128)S(1)}, u32[]{:S(2)}, u32[]{:S(2)}) %collective-permute-start.9) | collective-permute-done | bytes 2080 | tf_op jit(solution)/shard_map/ppermute | solution.py:228
  39.3 0.7 %collective-permute-start.10 = (f32[1,512]{1,0:T(1,128)S(1)}, f32[1,512]{1,0:T(1,128)S(1)}, u32[]{:S(2)}, u32[]{:S(2)}) collective-permute-start(f32[1,512]{1,0:T(1,128)S(1)} %hop.8), channel_id=1, source_target_pairs={{25,21}} | collective-permute-start | bytes 6152 | tf_op jit(solution)/shard_map/ppermute | solution.py:303
  40.1 1.0 %collective-permute-start.11 = (f32[1,512]{1,0:T(1,128)S(1)}, f32[1,512]{1,0:T(1,128)S(1)}, u32[]{:S(2)}, u32[]{:S(2)}) collective-permute-start(f32[1,512]{1,0:T(1,128)S(1)} %hop.9), channel_id=1, source_target_pairs={{0,4},{1,5},{2,6},{3,7},{4,0},{5,1},{6,2},{7,3},{8,12},{9,13},{10,... | collective-permute-start | bytes 6152 | tf_op jit(solution)/shard_map/ppermute | solution.py:228
  41.1 2.6 %collective-permute-done.11.x.refs_3_ = f32[1,512]{1,0:T(1,128)S(1)} collective-permute-done((f32[1,512]{1,0:T(1,128)S(1)}, f32[1,512]{1,0:T(1,128)S(1)}, u32[]{:S(2)}, u32[]{:S(2)}) %collective-permute-start.11) | collective-permute-done | bytes 2080 | tf_op jit(solution)/shard_map/ppermute | solution.py:228
  43.9 0.7 %collective-permute-start.12 = (f32[1,512]{1,0:T(1,128)S(1)}, f32[1,512]{1,0:T(1,128)S(1)}, u32[]{:S(2)}, u32[]{:S(2)}) collective-permute-start(f32[1,512]{1,0:T(1,128)S(1)} %hop.10), channel_id=1, source_target_pairs={{17,13}} | collective-permute-start | bytes 6152 | tf_op jit(solution)/shard_map/ppermute | solution.py:303
  44.7 1.0 %collective-permute-start.13 = (f32[1,512]{1,0:T(1,128)S(1)}, f32[1,512]{1,0:T(1,128)S(1)}, u32[]{:S(2)}, u32[]{:S(2)}) collective-permute-start(f32[1,512]{1,0:T(1,128)S(1)} %hop.11), channel_id=1, source_target_pairs={{0,4},{1,5},{2,6},{3,7},{4,0},{5,1},{6,2},{7,3},{8,12},{9,13},{10,... | collective-permute-start | bytes 6152 | tf_op jit(solution)/shard_map/ppermute | solution.py:228
  45.8 2.6 %collective-permute-done.13.x.refs_5_ = f32[1,512]{1,0:T(1,128)S(1)} collective-permute-done((f32[1,512]{1,0:T(1,128)S(1)}, f32[1,512]{1,0:T(1,128)S(1)}, u32[]{:S(2)}, u32[]{:S(2)}) %collective-permute-start.13) | collective-permute-done | bytes 2080 | tf_op jit(solution)/shard_map/ppermute | solution.py:228
  48.5 0.7 %collective-permute-start.14 = (f32[1,512]{1,0:T(1,128)S(1)}, f32[1,512]{1,0:T(1,128)S(1)}, u32[]{:S(2)}, u32[]{:S(2)}) collective-permute-start(f32[1,512]{1,0:T(1,128)S(1)} %hop.12), channel_id=1, source_target_pairs={{9,5}} | collective-permute-start | bytes 6152 | tf_op jit(solution)/shard_map/ppermute | solution.py:303
  49.4 1.0 %collective-permute-start.15 = (f32[1,512]{1,0:T(1,128)S(1)}, f32[1,512]{1,0:T(1,128)S(1)}, u32[]{:S(2)}, u32[]{:S(2)}) collective-permute-start(f32[1,512]{1,0:T(1,128)S(1)} %hop.13), channel_id=1, source_target_pairs={{0,4},{1,5},{2,6},{3,7},{4,0},{5,1},{6,2},{7,3},{8,12},{9,13},{10,... | collective-permute-start | bytes 6152 | tf_op jit(solution)/shard_map/ppermute | solution.py:228
  50.4 2.6 %collective-permute-done.15.refs_7_ = f32[1,512]{1,0:T(1,128)S(1)} collective-permute-done((f32[1,512]{1,0:T(1,128)S(1)}, f32[1,512]{1,0:T(1,128)S(1)}, u32[]{:S(2)}, u32[]{:S(2)}) %collective-permute-start.15) | collective-permute-done | bytes 2080 | tf_op jit(solution)/shard_map/ppermute | solution.py:228
  53.4 6.2 %collective-permute-start.17 = (f32[4,128]{1,0:T(4,128)S(1)}, f32[4,128]{1,0:T(4,128)S(1)}, u32[]{:S(2)}, u32[]{:S(2)}) collective-permute-start(f32[4,128]{1,0:T(4,128)S(1)} %get-tuple-element.44), channel_id=1, source_target_pairs={{0,1},{1,0},{2,3},{3,2},{4,5},{5,4},{6,7},{7,6},{8,9},{9,8},{10,11... | collective-permute-start | bytes 6152 | tf_op jit(solution)/shard_map/ppermute | solution.py:228
  59.7 1.4 %collective-permute-start.19 = (f32[4,128]{1,0:T(4,128)S(1)}, f32[4,128]{1,0:T(4,128)S(1)}, u32[]{:S(2)}, u32[]{:S(2)}) collective-permute-start(f32[4,128]{1,0:T(4,128)S(1)} %get-tuple-element.46), channel_id=1, source_target_pairs={{0,3},{1,2},{2,1},{3,0},{4,7},{5,6},{6,5},{7,4},{8,11},{9,10},{10,... | collective-permute-start | bytes 6152 | tf_op jit(solution)/shard_map/ppermute | solution.py:228
  61.1 2.2 %collective-permute-done.18.refs_2_ = f32[4,128]{1,0:T(4,128)S(1)} collective-permute-done((f32[4,128]{1,0:T(4,128)S(1)}, f32[4,128]{1,0:T(4,128)S(1)}, u32[]{:S(2)}, u32[]{:S(2)}) %collective-permute-start.18) | collective-permute-done | bytes 2080 | tf_op jit(solution)/shard_map/ppermute | solution.py:228
  63.3 0.6 out.1
  (22 shorter events, 1.8 us)
Async XLA Ops:
  2.3 20.7 %collective-permute-start = (f32[5,128,512]{2,1,0:T(8,128)S(1)}, f32[5,128,512]{2,1,0:T(8,128)S(1)}, u32[]{:S(2)}, u32[]{:S(2)}) collective-permute-start(f32[5,128,512]{2,1,0:T(8,128)S(1)} %get-tuple-element.29), channel_id=1, source_target_pairs={{0,1},{1,0},{2,3},{3,2},{4,5},{5,4},{6,7},{7,6},{8,9},{9,8},{10,11... | collective-permute-start | bytes 3932168 | tf_op jit(solution)/shard_map/ppermute | solution.py:228
  2.9 6.7 %collective-permute-start.1 = (f32[64,512]{1,0:T(8,128)S(1)}, f32[64,512]{1,0:T(8,128)S(1)}, u32[]{:S(2)}, u32[]{:S(2)}) collective-permute-start(f32[64,512]{1,0:T(8,128)S(1)} %get-tuple-element.30), channel_id=1, source_target_pairs={{0,2},{1,3},{2,0},{3,1},{4,6},{5,7},{6,4},{7,5},{8,10},{9,11},{10,... | collective-permute-start | bytes 393224 | tf_op jit(solution)/shard_map/ppermute | solution.py:228
  9.6 5.3 %collective-permute-start.2 = (f32[64,512]{1,0:T(8,128)S(1)}, f32[64,512]{1,0:T(8,128)S(1)}, u32[]{:S(2)}, u32[]{:S(2)}) collective-permute-start(f32[64,512]{1,0:T(8,128)S(1)} %collective-permute-done.1.refs_0_), channel_id=1, source_target_pairs={{0,4},{1,5},{2,6},{3,7},{4,0},{5,1},{6,2},{7,3},{8,12},{9,13},{10,... | collective-permute-start | bytes 393224 | tf_op jit(solution)/shard_map/ppermute | solution.py:228
  11.3 11.7 %collective-permute-start.4 = (f32[2,128,256]{2,1,0:T(8,128)S(1)}, f32[2,128,256]{2,1,0:T(8,128)S(1)}, u32[]{:S(2)}, u32[]{:S(2)}) collective-permute-start(f32[2,128,256]{2,1,0:T(8,128)S(1)} %get-tuple-element.31), channel_id=1, source_target_pairs={{0,2},{1,3},{2,0},{3,1},{4,6},{5,7},{6,4},{7,5},{8,10},{9,11},{10,... | collective-permute-start | bytes 786440 | tf_op jit(solution)/shard_map/ppermute | solution.py:228
  15.5 7.6 %collective-permute-start.3 = (f32[1,128,512]{2,1,0:T(8,128)S(1)}, f32[1,128,512]{2,1,0:T(8,128)S(1)}, u32[]{:S(2)}, u32[]{:S(2)}) collective-permute-start(f32[1,128,512]{2,1,0:T(8,128)S(1)} %join.1.joined), channel_id=1, source_target_pairs={{0,1},{1,0},{2,3},{3,2},{4,5},{5,4},{6,7},{7,6},{8,9},{9,8},{10,11... | collective-permute-start | bytes 786440 | tf_op jit(solution)/shard_map/ppermute | solution.py:228
  15.5 5.8 %collective-permute-start.5 = (f32[2,128,128]{2,1,0:T(8,128)S(1)}, f32[2,128,128]{2,1,0:T(8,128)S(1)}, u32[]{:S(2)}, u32[]{:S(2)}) collective-permute-start(f32[2,128,128]{2,1,0:T(8,128)S(1)} %get-tuple-element.32), channel_id=1, source_target_pairs={{0,3},{1,2},{2,1},{3,0},{4,7},{5,6},{6,5},{7,4},{8,11},{9,10},{10,... | collective-permute-start | bytes 393224 | tf_op jit(solution)/shard_map/ppermute | solution.py:228
  17.2 12.6 %collective-permute-start.6 = (f32[2,128,256]{2,1,0:T(8,128)S(1)}, f32[2,128,256]{2,1,0:T(8,128)S(1)}, u32[]{:S(2)}, u32[]{:S(2)}) collective-permute-start(f32[2,128,256]{2,1,0:T(8,128)S(1)} %get-tuple-element.36), channel_id=1, source_target_pairs={{0,2},{1,3},{2,0},{3,1},{4,6},{5,7},{6,4},{7,5},{8,10},{9,11},{10,... | collective-permute-start | bytes 786440 | tf_op jit(solution)/shard_map/ppermute | solution.py:228
  21.4 8.4 %collective-permute-start.7 = (f32[2,128,128]{2,1,0:T(8,128)S(1)}, f32[2,128,128]{2,1,0:T(8,128)S(1)}, u32[]{:S(2)}, u32[]{:S(2)}) collective-permute-start(f32[2,128,128]{2,1,0:T(8,128)S(1)} %get-tuple-element.37), channel_id=1, source_target_pairs={{0,3},{1,2},{2,1},{3,0},{4,7},{5,6},{6,5},{7,4},{8,11},{9,10},{10,... | collective-permute-start | bytes 393224 | tf_op jit(solution)/shard_map/ppermute | solution.py:228
  31.6 2.7 %collective-permute-start.8 = (f32[520,512]{1,0:T(8,128)S(1)}, f32[520,512]{1,0:T(8,128)S(1)}, u32[]{:S(2)}, u32[]{:S(2)}) collective-permute-start(f32[520,512]{1,0:T(8,128)S(1)} %get-tuple-element.38.late.refs_10_), channel_id=1, source_target_pairs={{0,1},{1,0},{2,3},{3,2},{4,5},{5,4},{6,7},{7,6},{8,9},{9,8},{10,11... | collective-permute-start | bytes 3194888 | tf_op jit(solution)/shard_map/ppermute | solution.py:228
  35.4 3.7 %collective-permute-start.9 = (f32[1,512]{1,0:T(1,128)S(1)}, f32[1,512]{1,0:T(1,128)S(1)}, u32[]{:S(2)}, u32[]{:S(2)}) collective-permute-start(f32[1,512]{1,0:T(1,128)S(1)} %hop.7), channel_id=1, source_target_pairs={{0,4},{1,5},{2,6},{3,7},{4,0},{5,1},{6,2},{7,3},{8,12},{9,13},{10,... | collective-permute-start | bytes 6152 | tf_op jit(solution)/shard_map/ppermute | solution.py:228
  39.1 13.9 %collective-permute-start.16 = (f32[512,512]{1,0:T(8,128)S(1)}, f32[512,512]{1,0:T(8,128)S(1)}, u32[]{:S(2)}, u32[]{:S(2)}) collective-permute-start(f32[512,512]{1,0:T(8,128)S(1)} %get-tuple-element.42.refs_11_), channel_id=1, source_target_pairs={{0,1},{1,0},{2,3},{3,2},{4,5},{5,4},{6,7},{7,6},{8,9},{9,8},{10,11... | collective-permute-start | bytes 3145736 | tf_op jit(solution)/shard_map/ppermute | solution.py:228
  39.3 0.7 %collective-permute-start.10 = (f32[1,512]{1,0:T(1,128)S(1)}, f32[1,512]{1,0:T(1,128)S(1)}, u32[]{:S(2)}, u32[]{:S(2)}) collective-permute-start(f32[1,512]{1,0:T(1,128)S(1)} %hop.8), channel_id=1, source_target_pairs={{25,21}} | collective-permute-start | bytes 6152 | tf_op jit(solution)/shard_map/ppermute | solution.py:303
  40.1 3.7 %collective-permute-start.11 = (f32[1,512]{1,0:T(1,128)S(1)}, f32[1,512]{1,0:T(1,128)S(1)}, u32[]{:S(2)}, u32[]{:S(2)}) collective-permute-start(f32[1,512]{1,0:T(1,128)S(1)} %hop.9), channel_id=1, source_target_pairs={{0,4},{1,5},{2,6},{3,7},{4,0},{5,1},{6,2},{7,3},{8,12},{9,13},{10,... | collective-permute-start | bytes 6152 | tf_op jit(solution)/shard_map/ppermute | solution.py:228
  43.9 0.7 %collective-permute-start.12 = (f32[1,512]{1,0:T(1,128)S(1)}, f32[1,512]{1,0:T(1,128)S(1)}, u32[]{:S(2)}, u32[]{:S(2)}) collective-permute-start(f32[1,512]{1,0:T(1,128)S(1)} %hop.10), channel_id=1, source_target_pairs={{17,13}} | collective-permute-start | bytes 6152 | tf_op jit(solution)/shard_map/ppermute | solution.py:303
  44.7 3.7 %collective-permute-start.13 = (f32[1,512]{1,0:T(1,128)S(1)}, f32[1,512]{1,0:T(1,128)S(1)}, u32[]{:S(2)}, u32[]{:S(2)}) collective-permute-start(f32[1,512]{1,0:T(1,128)S(1)} %hop.11), channel_id=1, source_target_pairs={{0,4},{1,5},{2,6},{3,7},{4,0},{5,1},{6,2},{7,3},{8,12},{9,13},{10,... | collective-permute-start | bytes 6152 | tf_op jit(solution)/shard_map/ppermute | solution.py:228
  48.5 0.7 %collective-permute-start.14 = (f32[1,512]{1,0:T(1,128)S(1)}, f32[1,512]{1,0:T(1,128)S(1)}, u32[]{:S(2)}, u32[]{:S(2)}) collective-permute-start(f32[1,512]{1,0:T(1,128)S(1)} %hop.12), channel_id=1, source_target_pairs={{9,5}} | collective-permute-start | bytes 6152 | tf_op jit(solution)/shard_map/ppermute | solution.py:303
  49.4 3.7 %collective-permute-start.15 = (f32[1,512]{1,0:T(1,128)S(1)}, f32[1,512]{1,0:T(1,128)S(1)}, u32[]{:S(2)}, u32[]{:S(2)}) collective-permute-start(f32[1,512]{1,0:T(1,128)S(1)} %hop.13), channel_id=1, source_target_pairs={{0,4},{1,5},{2,6},{3,7},{4,0},{5,1},{6,2},{7,3},{8,12},{9,13},{10,... | collective-permute-start | bytes 6152 | tf_op jit(solution)/shard_map/ppermute | solution.py:228
  53.4 7.7 %collective-permute-start.17 = (f32[4,128]{1,0:T(4,128)S(1)}, f32[4,128]{1,0:T(4,128)S(1)}, u32[]{:S(2)}, u32[]{:S(2)}) collective-permute-start(f32[4,128]{1,0:T(4,128)S(1)} %get-tuple-element.44), channel_id=1, source_target_pairs={{0,1},{1,0},{2,3},{3,2},{4,5},{5,4},{6,7},{7,6},{8,9},{9,8},{10,11... | collective-permute-start | bytes 6152 | tf_op jit(solution)/shard_map/ppermute | solution.py:228
  59.7 3.6 %collective-permute-start.18 = (f32[4,128]{1,0:T(4,128)S(1)}, f32[4,128]{1,0:T(4,128)S(1)}, u32[]{:S(2)}, u32[]{:S(2)}) collective-permute-start(f32[4,128]{1,0:T(4,128)S(1)} %get-tuple-element.45), channel_id=1, source_target_pairs={{0,2},{1,3},{2,0},{3,1},{4,6},{5,7},{6,4},{7,5},{8,10},{9,11},{10,... | collective-permute-start | bytes 6152 | tf_op jit(solution)/shard_map/ppermute | solution.py:228
  59.7 3.6 %collective-permute-start.19 = (f32[4,128]{1,0:T(4,128)S(1)}, f32[4,128]{1,0:T(4,128)S(1)}, u32[]{:S(2)}, u32[]{:S(2)}) collective-permute-start(f32[4,128]{1,0:T(4,128)S(1)} %get-tuple-element.46), channel_id=1, source_target_pairs={{0,3},{1,2},{2,1},{3,0},{4,7},{5,6},{6,5},{7,4},{8,11},{9,10},{10,... | collective-permute-start | bytes 6152 | tf_op jit(solution)/shard_map/ppermute | solution.py:228

commit v7 on v6

--- a/solution.py
+++ b/solution.py
@@ -21,7 +21,8 @@
 
 
 def dot3(a, b, dims):
-    (ah, al), (bh, bl) = split(a), split(b)
+    ah, al = split(a)
+    bh, bl = split(b) if hasattr(b, "dtype") and b.dtype == F32 else (b[0][...], b[1][...])
     dot = functools.partial(lax.dot_general, dimension_numbers=dims, preferred_element_type=F32)
     return dot(ah, bh) + (dot(ah, bl) + dot(al, bh))
 
@@ -55,30 +56,23 @@
     return panel if devices == 4 and off == 3 and panel % 128 == 0 else order - 2 * panel
 
 
-def far_copies(devices, start, matrix, far):
-    steps, panel, order = matrix.shape
-    s = lax.axis_index("state")
-    for off, piece in enumerate(far, 2):
-        w = width(devices, panel, order, off)
-        column = 2 * panel if w == order - 2 * panel else pl.multiple_of(s * panel, panel)
-        mine = pl.ds(((s ^ off) % 2) * (steps // 2), steps // 2)
-        start(matrix.at[mine, :, pl.ds(column, w)], piece)
-
-
-def pack_kernel(devices, cov, prec, trans, means, terminal, *refs):
-    far, (trans_half, first, near, own, own_means, vector, sems) = refs[: 2 * devices - 4], refs[2 * devices - 4 :]
-    count, panel = cov.shape[0] // 2, cov.shape[1]
+def pack_kernel(devices, cov, prec, trans, terminal, *refs):
+    far, (trans_half, first, near, vector, sems) = refs[: devices - 2], refs[devices - 2 :]
+    count, panel, order = cov.shape[0] // 2, *cov.shape[1:]
     b, s = lax.axis_index("tm"), lax.axis_index("state")
     start, copies = starter(sems)
     start(terminal, vector)
     start(trans.at[pl.ds(pl.multiple_of((b % 2) * (panel // 2), panel // 2), panel // 2), :], trans_half)
-    far_copies(devices, start, cov, far[: devices - 2])
-    far_copies(devices, start, prec, far[devices - 2 :])
-    for target, half in ((near, 1 - s % 2), (own, s % 2)):
-        start(cov.at[pl.ds(half * count, count)], target.at[pl.ds(0, count)])
-        start(prec.at[pl.ds(half * count, count)], target.at[pl.ds(count, count)])
-        start(trans, target.at[2 * count])
-    start(means, own_means)
+    for off, piece in enumerate(far, 2):
+        w = width(devices, panel, order, off)
+        column = 2 * panel if w == order - 2 * panel else pl.multiple_of(s * panel, panel)
+        theirs = pl.ds(((s ^ off) % 2) * count, count)
+        for k, matrix in enumerate((cov, prec)):
+            start(matrix.at[theirs, :, pl.ds(column, w)], piece.at[pl.ds(k * count, count)])
+    theirs = pl.ds((1 - s % 2) * count, count)
+    start(cov.at[theirs], near.at[pl.ds(0, count)])
+    start(prec.at[theirs], near.at[pl.ds(count, count)])
+    start(trans, near.at[2 * count])
     copies[0].wait()
     first[...] = jnp.where(b == lax.axis_size("tm") - 1, vector[...], 0.0)
     for copy in copies[1:]:
@@ -97,56 +91,51 @@
         copy.wait()
 
 
-def cov_kernel(means, own, near, joined, joined_near, *refs):
-    far, (gains, late, info, pf, af, lf, sems) = refs[:-7], refs[-7:]
-    _, panel, order = own.shape
-    count, known = far[0].shape[0], 2 * panel
-    steps = means.shape[0]
-    e = lax.axis_index("state") % 2
+def early_kernel(cov, prec, trans, means, near, joined, joined_near, *refs):
+    info, a_far, l_known, c_known, c_far, g_known, pf, af, lf, sems = refs
+    steps, panel, order = cov.shape
+    count, known = steps // 2, 2 * panel
+    s = lax.axis_index("state")
+    e = s % 2
     start, copies = starter(sems)
     for k in range(count):
-        full = pf.at[pl.ds(k * order, order), :]
-        start(own.at[k], full.at[rows(e, panel), :])
-        start(near.at[k], full.at[rows(1 - e, panel), :])
-        start(own.at[count + k], lf.at[k, rows(e, panel), :])
+        step = e * count + k
+        start(cov.at[step], pf.at[pl.ds(pl.multiple_of(k * known + e * panel, panel), panel), :])
+        start(near.at[k], pf.at[pl.ds(pl.multiple_of(k * known + (1 - e) * panel, panel), panel), :])
+        start(prec.at[step], lf.at[k, rows(e, panel), :])
         start(near.at[count + k], lf.at[k, rows(1 - e, panel), :])
-        for off, piece in enumerate(far, 2):
-            i = e ^ off
-            w = piece.shape[2]
-            column = known if w == order - known else pl.multiple_of(i * panel, panel)
-            start(piece.at[k], full.at[rows(i, panel), pl.ds(column, w)])
-    for j in range(order // (2 * panel)):
-        mine, theirs = (own.at[2 * count], near.at[2 * count]) if j == 0 else (joined.at[j - 1], joined_near.at[j - 1])
-        start(mine, af.at[rows(e ^ (2 * j), panel), :])
-        start(theirs, af.at[rows(e ^ (2 * j) ^ 1, panel), :])
-    pf[count * order :, :] = jnp.concatenate([means[...], jnp.zeros((16 - steps, order), F32)], axis=0)
+    start(trans, af.at[rows(e, panel), :])
+    start(near.at[2 * count], af.at[rows(1 - e, panel), :])
+    for j in range(1, order // known):
+        start(joined.at[j - 1], af.at[rows(e ^ (2 * j), panel), :])
+        start(joined_near.at[j - 1], af.at[rows(e ^ (2 * j) ^ 1, panel), :])
+    pf[count * known :, :] = jnp.concatenate([means[...], jnp.zeros((16 - steps, order), F32)], axis=0)
     for copy in copies:
         copy.wait()
+    product = dot3(pf[...], af[...], NT)
+    info[:8] = pf[count * known : count * known + 8, :]
+    info[8:] = product[count * known : count * known + 8]
+    for half, x in enumerate(split(af[:, known:])):
+        a_far[half] = x
+    across = jnp.concatenate([pf[k * known : (k + 1) * known, known:].T for k in range(count)], axis=0)
+    rest = dot3(across, af[:, :known], NT)
     for k in range(count):
-        full = pf.at[pl.ds(k * order, order), :]
-        full[known:order, :known] = full[:known, known:order].T
-        if far[-1].shape[2] < order - known:
-            i, j = e ^ 3, e ^ 2
-            full[rows(i, panel), rows(j, panel)] = full[rows(j, panel), rows(i, panel)].T
-    product = dot3(pf[...], af[...], NT)
-    info[:8] = pf[count * order : count * order + 8, :]
-    info[8:] = product[count * order : count * order + 8]
-    late[...] = product[: count * order, known:]
-    for k in range(count):
-        part = product[k * order : (k + 1) * order]
+        part = product[k * known : (k + 1) * known]
+        for half, x in enumerate(split(lf[k])):
+            l_known[k, half] = x
         partial = dot3(part[:, :known], lf[k], NN)
-        gains[k, :, :known] = partial[:, :known] + dot3(part[:, known:], lf[k, :, known:], NT)
-        gains[k, :, known:] = partial[:, known:]
-
-
-def gain_kernel(info, gains, late, *refs):
+        g_known[k, :, :known] = partial[:, :known] + dot3(part[:, known:], lf[k, :, known:], NT)
+        g_known[k, :, known:] = partial[:, known:]
+        c_known[k] = part[:, known:]
+        c_far[k] = rest[k * (order - known) : (k + 1) * (order - known)]
+
+
+def late_kernel(info, a_far, l_known, c_known, c_far, g_known, *refs):
     far, (map_ref, gain_ref, ff) = refs[:-3], refs[-3:]
-    count, panel, _ = far[0].shape
-    order = gains.shape[1]
-    known = 2 * panel
-    s = lax.axis_index("state")
-    e = s % 2
-    for k in range(count):
+    count, known, order = g_known.shape
+    panel = known // 2
+    e = lax.axis_index("state") % 2
+    for k in range(2 * count):
         for off, piece in enumerate(far, 2):
             i = (e ^ off) - 2
             if piece.shape[2] == order - known:
@@ -158,8 +147,13 @@
             ff[k, rows(i, panel), rows(j, panel)] = ff[k, rows(j, panel), rows(i, panel)].T
 
     def complete(k):
-        rest = gains[k, :, known:] + dot3(late[k * order : (k + 1) * order, :], ff[k], NN)
-        return jnp.concatenate([gains[k, :, :known], rest], axis=1)
+        c = c_far[k] + dot3(ff[k], a_far, NT)
+        known_rows = (l_known.at[k, 0], l_known.at[k, 1])
+        share = dot3(jnp.concatenate([c_known[k], c[:, known:]], axis=0), ff[count + k], NN)
+        low = dot3(c[:, :known], known_rows, NN)
+        left = low[:, :known] + dot3(c[:, known:], [x[:, known:] for x in known_rows], NT)
+        top = jnp.concatenate([g_known[k, :, :known], g_known[k, :, known:] + share[:known]], axis=1)
+        return jnp.concatenate([top, jnp.concatenate([left, low[:, known:] + share[known:]], axis=1)], axis=0)
 
     ga, gb = complete(0), complete(1)
     gain_ref[...] = gb
@@ -206,7 +200,7 @@
 
 
 def out_kernel(*refs):
-    given, out_ref = refs[:-1], refs[-1]
+    given, out_ref = [refs[0], *refs[-2:0:-1]], refs[-1]
     off = lax.axis_index("state") ^ 1
     x = given[0][...]
     for k, ref in enumerate(given[1:], 1):
@@ -248,19 +242,18 @@
     semaphores = pltpu.SemaphoreType.DMA((8 * devices,))
     square = shape(order, order)
 
-    far = [shape(count, panel, width(devices, panel, order, off)) for off in range(2, devices)]
-    panels = shape(2 * count + 1, panel, order)
-    *far, trans_half, first, near, own, own_means = call(
+    far = [shape(2 * count, panel, width(devices, panel, order, off)) for off in range(2, devices)]
+    *far, trans_half, first, near = call(
         functools.partial(pack_kernel, devices),
         "pack",
-        4,
-        far + far + [shape(panel // 2, order), shape(1, order), panels, panels, shape(steps, order)],
-        [HBM] * 5,
+        6,
+        far + [shape(panel // 2, order), shape(1, order), shape(2 * count + 1, panel, order)],
+        [HBM] * 4,
         [pltpu.VMEM((1, order), F32), semaphores],
-        (cov, prec, trans, means, terminal),
+        (cov, prec, trans, terminal),
     )
     across = [swap(trans_half, off) for off in range(2, devices, 2)]
-    cov_far, prec_far = ([swap(x, off) for off, x in enumerate(part, 2)] for part in (far[: devices - 2], far[devices - 2 :]))
+    far = [swap(x, off) for off, x in enumerate(far, 2)]
     near = swap(near, 1)
     moved = [y for x in across for y in (x, swap(x, 0, 1))]
     (joined,) = call(
@@ -268,30 +261,39 @@
     )
     joined_near = swap(joined, 1)
 
-    gains, late, info = call(
-        cov_kernel,
-        "cov",
-        28,
-        [shape(count, order, order), shape(count * order, order - 2 * panel), shape(16, order)],
-        [VMEM] + [ANY] * (devices + 2),
+    known = 2 * panel
+    parts = call(
+        early_kernel,
+        "early",
+        24,
         [
-            pltpu.VMEM((count * order + 16, order), F32),
+            shape(16, order),
+            jax.ShapeDtypeStruct((2, order, order - known), BF16),
+            jax.ShapeDtypeStruct((count, 2, known, order), BF16),
+            shape(count, known, order - known),
+            shape(count, order - known, order),
+            shape(count, known, order),
+        ],
+        [HBM] * 3 + [VMEM] + [ANY] * 3,
+        [
+            pltpu.VMEM((count * known + 16, order), F32),
             pltpu.VMEM((order, order), F32),
-            pltpu.VMEM((count, 2 * panel, order), F32),
+            pltpu.VMEM((count, known, order), F32),
             semaphores,
         ],
-        (own_means, own, near, joined, joined_near, *cov_far),
+        (cov, prec, trans, means, near, joined, joined_near),
     )
     late_map, g3 = call(
-        gain_kernel,
-        "gain",
-        20,
+        late_kernel,
+        "late",
+        24,
         [shape(order + 8, order), square],
-        [VMEM] * (1 + devices),
-        [pltpu.VMEM((count, order - 2 * panel, order - 2 * panel), F32)],
-        (info, gains, late, *prec_far),
+        [VMEM] * (6 + len(far)),
+        [pltpu.VMEM((2 * count, order - known, order - known), F32)],
+        (*parts, *far),
     )
     early_map = swap(late_map, 1)
+    g1 = swap(lax.optimization_barrier((g3, early_map))[0], 1)
     m, vec = call(block_kernel, "block", 12, [square, shape(8, order)], [VMEM] * 2, [], (late_map, early_map))
 
     incoming = [first]
@@ -302,7 +304,6 @@
         else:
             x = lax.ppermute(x, ("tm", "state"), [(block * devices + 1, (block - 1) * devices + 1)])
         incoming.append(x)
-    g1 = swap(lax.optimization_barrier((g3, incoming[1]))[0], 1)
 
     given = list(call(
         functools.partial(last_kernel, devices),
@@ -315,6 +316,7 @@
     ))
     for off in range(devices - 1, 0, -1):
         given[off] = swap(given[off], off)
+    given = [given[0], *given[:0:-1]]
     (out,) = call(out_kernel, "out", 4, [shape(steps, panel)], [VMEM] * devices, [], given)
     return out
 

time: 64.1 us -> 60.3 us (0.941)
  waiting for transfers between devices: 26.9 us -> 22.7 us
  Pallas kernels: 12.4 us -> 13.4 us
  starting transfers between devices: 24.4 us -> 23.7 us
    ppermute x17 -> x15, waiting for transfers between devices: 26.9 us -> 22.7 us  [swap(): return lax.ppermute(x, ('tm', 'state'), pairs)]
    pallas_call x14, Pallas kernels: 12.4 us -> 13.4 us  [call(): pl.pallas_call(kernel, out_shape=outs, in_specs=in_specs, out_specs=[VMEM...]
    ppermute x17 -> x15, starting transfers between devices: 22.4 us -> 21.8 us  [swap(): return lax.ppermute(x, ('tm', 'state'), pairs)]
  transfers between devices with their start and end apart: 20 -> 18, of which waited for: 10 -> 9; matrix products, arithmetic and copies ran while one was open for 0% -> 0% of each run, Pallas kernels for 10% -> 12%
where the time goes in v7:
time: 60.3 us; the launch traced here: 60 us
  starting transfers between devices  23.7 us (39%)
  waiting for transfers between devices  22.7 us (38%)
  Pallas kernels  13.4 us (22%)
    ppermute x15, waiting for transfers between devices, swap(): return lax.ppermute(x, ('tm', 'state'), pairs)  22.7 us
    ppermute x15, starting transfers between devices, swap(): return lax.ppermute(x, ('tm', 'state'), pairs)  21.8 us
    pallas_call x14, Pallas kernels, call(): pl.pallas_call(kernel, out_shape=outs, in_specs=in_specs, out_specs=[VMEM...  13.4 us
    ppermute x3, starting transfers between devices, local(): lax.ppermute(x, ('tm', 'state'), [(block * devices + 1, (block - 1) * dev...  1.98 us
  transfers between devices with their start and end apart: 18, of which 9 were waited for; matrix products, arithmetic and copies ran while one was open for 0% of the time, Pallas kernels for 12%

profile of v7, /device:TPU:0, one launch (start us, length us, event | category | flops | bytes accessed | tf_op | source)
XLA Modules:
  0.0 60.0 jit_solution(2307951247046377782)
XLA Ops:
  0.0 1.9 %pack.1 = (f32[4,128,256]{2,1,0:T(8,128)S(1)}, f32[4,128,128]{2,1,0:T(8,128)S(1)}, f32[64,512]{1,0:T(8,128)S(1)}, f32[1,512]{1,0:T(1,128)S(1)}, f32[5,128,512]{2,1,0:T(8,128)S(1)}) custom-call(f32[4,128,512]{2,1,0:T(8,128)} %cov.3, f32[4,128,512]{2,1,0:T(8,128)} %prec.3, f32[128,512]{1,0:T(8,128)} %trans.3, f32[1,512]{1,0:T(1,128)} %bitcast.1), custom_call_target="tpu_custom_call" | custom-call | tf_op jit(solution)/shard_map/pack/pallas_call | solution.py:228
  1.9 0.5 collective-permute-start
  2.4 2.6 %collective-permute-start.1 = (f32[64,512]{1,0:T(8,128)S(1)}, f32[64,512]{1,0:T(8,128)S(1)}, u32[]{:S(2)}, u32[]{:S(2)}) collective-permute-start(f32[64,512]{1,0:T(8,128)S(1)} %get-tuple-element.27), channel_id=1, source_target_pairs={{0,2},{1,3},{2,0},{3,1},{4,6},{5,7},{6,4},{7,5},{8,10},{9,11},{10,... | collective-permute-start | bytes 393224 | tf_op jit(solution)/shard_map/ppermute | solution.py:222
  5.1 4.3 %collective-permute-done.1.refs_0_ = f32[64,512]{1,0:T(8,128)S(1)} collective-permute-done((f32[64,512]{1,0:T(8,128)S(1)}, f32[64,512]{1,0:T(8,128)S(1)}, u32[]{:S(2)}, u32[]{:S(2)}) %collective-permute-start.1) | collective-permute-done | bytes 131104 | tf_op jit(solution)/shard_map/ppermute | solution.py:222
  9.3 2.0 %collective-permute-start.2 = (f32[64,512]{1,0:T(8,128)S(1)}, f32[64,512]{1,0:T(8,128)S(1)}, u32[]{:S(2)}, u32[]{:S(2)}) collective-permute-start(f32[64,512]{1,0:T(8,128)S(1)} %collective-permute-done.1.refs_0_), channel_id=1, source_target_pairs={{0,4},{1,5},{2,6},{3,7},{4,0},{5,1},{6,2},{7,3},{8,12},{9,13},{10,... | collective-permute-start | bytes 393224 | tf_op jit(solution)/shard_map/ppermute | solution.py:222
  11.3 3.0 %collective-permute-done.2.refs_1_ = f32[64,512]{1,0:T(8,128)S(1)} collective-permute-done((f32[64,512]{1,0:T(8,128)S(1)}, f32[64,512]{1,0:T(8,128)S(1)}, u32[]{:S(2)}, u32[]{:S(2)}) %collective-permute-start.2) | collective-permute-done | bytes 131104 | tf_op jit(solution)/shard_map/ppermute | solution.py:222
  14.3 0.6 join.1.joined
  15.0 2.0 %collective-permute-start.5 = (f32[4,128,128]{2,1,0:T(8,128)S(1)}, f32[4,128,128]{2,1,0:T(8,128)S(1)}, u32[]{:S(2)}, u32[]{:S(2)}) collective-permute-start(f32[4,128,128]{2,1,0:T(8,128)S(1)} %get-tuple-element.35), channel_id=1, source_target_pairs={{0,3},{1,2},{2,1},{3,0},{4,7},{5,6},{6,5},{7,4},{8,11},{9,10},{10,... | collective-permute-start | bytes 786440 | tf_op jit(solution)/shard_map/ppermute | solution.py:222
  17.0 4.8 %early.1 = (f32[16,512]{1,0:T(8,128)S(1)}, bf16[2,512,256]{2,1,0:T(8,128)(2,1)S(1)}, bf16[2,2,256,512]{3,2,1,0:T(8,128)(2,1)S(1)}, f32[2,256,256]{2,1,0:T(8,128)...) custom-call(f32[4,128,512]{2,1,0:T(8,128)} %cov.3, f32[4,128,512]{2,1,0:T(8,128)} %prec.3, ...), custom_call_target="tpu_custom_call" | custom-call | tf_op jit(solution)/shard_map/early/pallas_call | solution.py:228
  21.8 3.8 %collective-permute-done.5.refs_1_ = f32[4,128,128]{2,1,0:T(8,128)S(1)} collective-permute-done((f32[4,128,128]{2,1,0:T(8,128)S(1)}, f32[4,128,128]{2,1,0:T(8,128)S(1)}, u32[]{:S(2)}, u32[]{:S(2)}) %collective-permute-start.5) | collective-permute-done | bytes 262176 | tf_op jit(solution)/shard_map/ppermute | solution.py:222
  25.7 3.1 %late.1 = (f32[520,512]{1,0:T(8,128)S(1)}, f32[512,512]{1,0:T(8,128)S(1)}) custom-call(f32[16,512]{1,0:T(8,128)S(1)} %get-tuple-element.28.info, bf16[2,512,256]{2,1,0:T(8,128)(2,1)S(1)} %get-tuple-element.29.a_far, bf16[2,2,256,512]{3,2,1,0:T(8,128)(2,1)S(1)} %get-tuple-element.30.l_known, f32[2,256,256]{2,1,0:T(8,128)S(1)} %get-tuple-element.31.c_known, ...), custom_call_target="tpu_custom_call" | custom-call | tf_op jit(solution)/shard_map/late/pallas_call | solution.py:228
  28.8 0.2 collective-permute-start.6
  29.0 2.6 %collective-permute-done.6.early.refs_12_ = f32[520,512]{1,0:T(8,128)S(1)} collective-permute-done((f32[520,512]{1,0:T(8,128)S(1)}, f32[520,512]{1,0:T(8,128)S(1)}, u32[]{:S(2)}, u32[]{:S(2)}) %collective-permute-start.6) | collective-permute-done | bytes 1064992 | tf_op jit(solution)/shard_map/ppermute | solution.py:222
  31.7 1.0 %block.1 = (f32[512,512]{1,0:T(8,128)S(1)}, f32[8,512]{1,0:T(8,128)S(1)}) custom-call(f32[520,512]{1,0:T(8,128)S(1)} %get-tuple-element.36.late.refs_10_, f32[520,512]{1,0:T(8,128)S(1)} %collective-permute-done.6.early.refs_12_), custom_call_target="tpu_custom_call" | custom-call | tf_op jit(solution)/shard_map/block/pallas_call | solution.py:228
  32.7 0.2 hop.7
  32.8 1.8 %collective-permute-start.7 = (f32[1,512]{1,0:T(1,128)S(1)}, f32[1,512]{1,0:T(1,128)S(1)}, u32[]{:S(2)}, u32[]{:S(2)}) collective-permute-start(f32[1,512]{1,0:T(1,128)S(1)} %hop.7), channel_id=1, source_target_pairs={{0,4},{1,5},{2,6},{3,7},{4,0},{5,1},{6,2},{7,3},{8,12},{9,13},{10,... | collective-permute-start | bytes 6152 | tf_op jit(solution)/shard_map/ppermute | solution.py:222
  34.6 1.9 %collective-permute-done.7.x.refs_1_ = f32[1,512]{1,0:T(1,128)S(1)} collective-permute-done((f32[1,512]{1,0:T(1,128)S(1)}, f32[1,512]{1,0:T(1,128)S(1)}, u32[]{:S(2)}, u32[]{:S(2)}) %collective-permute-start.7) | collective-permute-done | bytes 2080 | tf_op jit(solution)/shard_map/ppermute | solution.py:222
  36.6 0.7 %collective-permute-start.8 = (f32[1,512]{1,0:T(1,128)S(1)}, f32[1,512]{1,0:T(1,128)S(1)}, u32[]{:S(2)}, u32[]{:S(2)}) collective-permute-start(f32[1,512]{1,0:T(1,128)S(1)} %hop.8), channel_id=1, source_target_pairs={{25,21}} | collective-permute-start | bytes 6152 | tf_op jit(solution)/shard_map/ppermute | solution.py:305
  37.3 0.2 hop.9
  37.5 1.8 %collective-permute-start.9 = (f32[1,512]{1,0:T(1,128)S(1)}, f32[1,512]{1,0:T(1,128)S(1)}, u32[]{:S(2)}, u32[]{:S(2)}) collective-permute-start(f32[1,512]{1,0:T(1,128)S(1)} %hop.9), channel_id=1, source_target_pairs={{0,4},{1,5},{2,6},{3,7},{4,0},{5,1},{6,2},{7,3},{8,12},{9,13},{10,... | collective-permute-start | bytes 6152 | tf_op jit(solution)/shard_map/ppermute | solution.py:222
  39.3 1.9 %collective-permute-done.9.x.refs_3_ = f32[1,512]{1,0:T(1,128)S(1)} collective-permute-done((f32[1,512]{1,0:T(1,128)S(1)}, f32[1,512]{1,0:T(1,128)S(1)}, u32[]{:S(2)}, u32[]{:S(2)}) %collective-permute-start.9) | collective-permute-done | bytes 2080 | tf_op jit(solution)/shard_map/ppermute | solution.py:222
  41.3 0.7 %collective-permute-start.10 = (f32[1,512]{1,0:T(1,128)S(1)}, f32[1,512]{1,0:T(1,128)S(1)}, u32[]{:S(2)}, u32[]{:S(2)}) collective-permute-start(f32[1,512]{1,0:T(1,128)S(1)} %hop.10), channel_id=1, source_target_pairs={{17,13}} | collective-permute-start | bytes 6152 | tf_op jit(solution)/shard_map/ppermute | solution.py:305
  42.0 0.2 hop.11
  42.1 1.8 %collective-permute-start.11 = (f32[1,512]{1,0:T(1,128)S(1)}, f32[1,512]{1,0:T(1,128)S(1)}, u32[]{:S(2)}, u32[]{:S(2)}) collective-permute-start(f32[1,512]{1,0:T(1,128)S(1)} %hop.11), channel_id=1, source_target_pairs={{0,4},{1,5},{2,6},{3,7},{4,0},{5,1},{6,2},{7,3},{8,12},{9,13},{10,... | collective-permute-start | bytes 6152 | tf_op jit(solution)/shard_map/ppermute | solution.py:222
  43.9 1.9 %collective-permute-done.11.x.refs_5_ = f32[1,512]{1,0:T(1,128)S(1)} collective-permute-done((f32[1,512]{1,0:T(1,128)S(1)}, f32[1,512]{1,0:T(1,128)S(1)}, u32[]{:S(2)}, u32[]{:S(2)}) %collective-permute-start.11) | collective-permute-done | bytes 2080 | tf_op jit(solution)/shard_map/ppermute | solution.py:222
  45.9 0.7 %collective-permute-start.12 = (f32[1,512]{1,0:T(1,128)S(1)}, f32[1,512]{1,0:T(1,128)S(1)}, u32[]{:S(2)}, u32[]{:S(2)}) collective-permute-start(f32[1,512]{1,0:T(1,128)S(1)} %hop.12), channel_id=1, source_target_pairs={{9,5}} | collective-permute-start | bytes 6152 | tf_op jit(solution)/shard_map/ppermute | solution.py:305
  46.8 1.8 %collective-permute-start.13 = (f32[1,512]{1,0:T(1,128)S(1)}, f32[1,512]{1,0:T(1,128)S(1)}, u32[]{:S(2)}, u32[]{:S(2)}) collective-permute-start(f32[1,512]{1,0:T(1,128)S(1)} %hop.13), channel_id=1, source_target_pairs={{0,4},{1,5},{2,6},{3,7},{4,0},{5,1},{6,2},{7,3},{8,12},{9,13},{10,... | collective-permute-start | bytes 6152 | tf_op jit(solution)/shard_map/ppermute | solution.py:222
  48.5 1.9 %collective-permute-done.13.refs_7_ = f32[1,512]{1,0:T(1,128)S(1)} collective-permute-done((f32[1,512]{1,0:T(1,128)S(1)}, f32[1,512]{1,0:T(1,128)S(1)}, u32[]{:S(2)}, u32[]{:S(2)}) %collective-permute-start.13) | collective-permute-done | bytes 2080 | tf_op jit(solution)/shard_map/ppermute | solution.py:222
  50.4 0.4 last.1
  50.9 7.0 %collective-permute-start.16 = (f32[4,128]{1,0:T(4,128)S(1)}, f32[4,128]{1,0:T(4,128)S(1)}, u32[]{:S(2)}, u32[]{:S(2)}) collective-permute-start(f32[4,128]{1,0:T(4,128)S(1)} %get-tuple-element.43), channel_id=1, source_target_pairs={{0,2},{1,3},{2,0},{3,1},{4,6},{5,7},{6,4},{7,5},{8,10},{9,11},{10,... | collective-permute-start | bytes 6152 | tf_op jit(solution)/shard_map/ppermute | solution.py:222
  57.9 1.6 %collective-permute-done.16.refs_2_ = f32[4,128]{1,0:T(4,128)S(1)} collective-permute-done((f32[4,128]{1,0:T(4,128)S(1)}, f32[4,128]{1,0:T(4,128)S(1)}, u32[]{:S(2)}, u32[]{:S(2)}) %collective-permute-start.16) | collective-permute-done | bytes 2080 | tf_op jit(solution)/shard_map/ppermute | solution.py:222
  59.4 0.6 out.1
  (18 shorter events, 1.0 us)
Async XLA Ops:
  1.9 15.2 %collective-permute-start = (f32[5,128,512]{2,1,0:T(8,128)S(1)}, f32[5,128,512]{2,1,0:T(8,128)S(1)}, u32[]{:S(2)}, u32[]{:S(2)}) collective-permute-start(f32[5,128,512]{2,1,0:T(8,128)S(1)} %get-tuple-element.26), channel_id=1, source_target_pairs={{0,1},{1,0},{2,3},{3,2},{4,5},{5,4},{6,7},{7,6},{8,9},{9,8},{10,11... | collective-permute-start | bytes 3932168 | tf_op jit(solution)/shard_map/ppermute | solution.py:222
  2.4 6.9 %collective-permute-start.1 = (f32[64,512]{1,0:T(8,128)S(1)}, f32[64,512]{1,0:T(8,128)S(1)}, u32[]{:S(2)}, u32[]{:S(2)}) collective-permute-start(f32[64,512]{1,0:T(8,128)S(1)} %get-tuple-element.27), channel_id=1, source_target_pairs={{0,2},{1,3},{2,0},{3,1},{4,6},{5,7},{6,4},{7,5},{8,10},{9,11},{10,... | collective-permute-start | bytes 393224 | tf_op jit(solution)/shard_map/ppermute | solution.py:222
  5.0 20.7 %collective-permute-start.4 = (f32[4,128,256]{2,1,0:T(8,128)S(1)}, f32[4,128,256]{2,1,0:T(8,128)S(1)}, u32[]{:S(2)}, u32[]{:S(2)}) collective-permute-start(f32[4,128,256]{2,1,0:T(8,128)S(1)} %get-tuple-element.34), channel_id=1, source_target_pairs={{0,2},{1,3},{2,0},{3,1},{4,6},{5,7},{6,4},{7,5},{8,10},{9,11},{10,... | collective-permute-start | bytes 1572872 | tf_op jit(solution)/shard_map/ppermute | solution.py:222
  9.3 5.0 %collective-permute-start.2 = (f32[64,512]{1,0:T(8,128)S(1)}, f32[64,512]{1,0:T(8,128)S(1)}, u32[]{:S(2)}, u32[]{:S(2)}) collective-permute-start(f32[64,512]{1,0:T(8,128)S(1)} %collective-permute-done.1.refs_0_), channel_id=1, source_target_pairs={{0,4},{1,5},{2,6},{3,7},{4,0},{5,1},{6,2},{7,3},{8,12},{9,13},{10,... | collective-permute-start | bytes 393224 | tf_op jit(solution)/shard_map/ppermute | solution.py:222
  14.9 2.1 %collective-permute-start.3 = (f32[1,128,512]{2,1,0:T(8,128)S(1)}, f32[1,128,512]{2,1,0:T(8,128)S(1)}, u32[]{:S(2)}, u32[]{:S(2)}) collective-permute-start(f32[1,128,512]{2,1,0:T(8,128)S(1)} %join.1.joined), channel_id=1, source_target_pairs={{0,1},{1,0},{2,3},{3,2},{4,5},{5,4},{6,7},{7,6},{8,9},{9,8},{10,11... | collective-permute-start | bytes 786440 | tf_op jit(solution)/shard_map/ppermute | solution.py:222
  15.0 10.7 %collective-permute-start.5 = (f32[4,128,128]{2,1,0:T(8,128)S(1)}, f32[4,128,128]{2,1,0:T(8,128)S(1)}, u32[]{:S(2)}, u32[]{:S(2)}) collective-permute-start(f32[4,128,128]{2,1,0:T(8,128)S(1)} %get-tuple-element.35), channel_id=1, source_target_pairs={{0,3},{1,2},{2,1},{3,0},{4,7},{5,6},{6,5},{7,4},{8,11},{9,10},{10,... | collective-permute-start | bytes 786440 | tf_op jit(solution)/shard_map/ppermute | solution.py:222
  28.8 2.7 %collective-permute-start.6 = (f32[520,512]{1,0:T(8,128)S(1)}, f32[520,512]{1,0:T(8,128)S(1)}, u32[]{:S(2)}, u32[]{:S(2)}) collective-permute-start(f32[520,512]{1,0:T(8,128)S(1)} %get-tuple-element.36.late.refs_10_), channel_id=1, source_target_pairs={{0,1},{1,0},{2,3},{3,2},{4,5},{5,4},{6,7},{7,6},{8,9},{9,8},{10,11... | collective-permute-start | bytes 3194888 | tf_op jit(solution)/shard_map/ppermute | solution.py:222
  31.5 18.9 %collective-permute-start.14 = (f32[512,512]{1,0:T(8,128)S(1)}, f32[512,512]{1,0:T(8,128)S(1)}, u32[]{:S(2)}, u32[]{:S(2)}) collective-permute-start(f32[512,512]{1,0:T(8,128)S(1)} %get-tuple-element.40.refs_11_), channel_id=1, source_target_pairs={{0,1},{1,0},{2,3},{3,2},{4,5},{5,4},{6,7},{7,6},{8,9},{9,8},{10,11... | collective-permute-start | bytes 3145736 | tf_op jit(solution)/shard_map/ppermute | solution.py:222
  32.8 3.7 %collective-permute-start.7 = (f32[1,512]{1,0:T(1,128)S(1)}, f32[1,512]{1,0:T(1,128)S(1)}, u32[]{:S(2)}, u32[]{:S(2)}) collective-permute-start(f32[1,512]{1,0:T(1,128)S(1)} %hop.7), channel_id=1, source_target_pairs={{0,4},{1,5},{2,6},{3,7},{4,0},{5,1},{6,2},{7,3},{8,12},{9,13},{10,... | collective-permute-start | bytes 6152 | tf_op jit(solution)/shard_map/ppermute | solution.py:222
  36.6 0.7 %collective-permute-start.8 = (f32[1,512]{1,0:T(1,128)S(1)}, f32[1,512]{1,0:T(1,128)S(1)}, u32[]{:S(2)}, u32[]{:S(2)}) collective-permute-start(f32[1,512]{1,0:T(1,128)S(1)} %hop.8), channel_id=1, source_target_pairs={{25,21}} | collective-permute-start | bytes 6152 | tf_op jit(solution)/shard_map/ppermute | solution.py:305
  37.5 3.7 %collective-permute-start.9 = (f32[1,512]{1,0:T(1,128)S(1)}, f32[1,512]{1,0:T(1,128)S(1)}, u32[]{:S(2)}, u32[]{:S(2)}) collective-permute-start(f32[1,512]{1,0:T(1,128)S(1)} %hop.9), channel_id=1, source_target_pairs={{0,4},{1,5},{2,6},{3,7},{4,0},{5,1},{6,2},{7,3},{8,12},{9,13},{10,... | collective-permute-start | bytes 6152 | tf_op jit(solution)/shard_map/ppermute | solution.py:222
  41.3 0.7 %collective-permute-start.10 = (f32[1,512]{1,0:T(1,128)S(1)}, f32[1,512]{1,0:T(1,128)S(1)}, u32[]{:S(2)}, u32[]{:S(2)}) collective-permute-start(f32[1,512]{1,0:T(1,128)S(1)} %hop.10), channel_id=1, source_target_pairs={{17,13}} | collective-permute-start | bytes 6152 | tf_op jit(solution)/shard_map/ppermute | solution.py:305
  42.1 3.7 %collective-permute-start.11 = (f32[1,512]{1,0:T(1,128)S(1)}, f32[1,512]{1,0:T(1,128)S(1)}, u32[]{:S(2)}, u32[]{:S(2)}) collective-permute-start(f32[1,512]{1,0:T(1,128)S(1)} %hop.11), channel_id=1, source_target_pairs={{0,4},{1,5},{2,6},{3,7},{4,0},{5,1},{6,2},{7,3},{8,12},{9,13},{10,... | collective-permute-start | bytes 6152 | tf_op jit(solution)/shard_map/ppermute | solution.py:222
  45.9 0.7 %collective-permute-start.12 = (f32[1,512]{1,0:T(1,128)S(1)}, f32[1,512]{1,0:T(1,128)S(1)}, u32[]{:S(2)}, u32[]{:S(2)}) collective-permute-start(f32[1,512]{1,0:T(1,128)S(1)} %hop.12), channel_id=1, source_target_pairs={{9,5}} | collective-permute-start | bytes 6152 | tf_op jit(solution)/shard_map/ppermute | solution.py:305
  46.8 3.7 %collective-permute-start.13 = (f32[1,512]{1,0:T(1,128)S(1)}, f32[1,512]{1,0:T(1,128)S(1)}, u32[]{:S(2)}, u32[]{:S(2)}) collective-permute-start(f32[1,512]{1,0:T(1,128)S(1)} %hop.13), channel_id=1, source_target_pairs={{0,4},{1,5},{2,6},{3,7},{4,0},{5,1},{6,2},{7,3},{8,12},{9,13},{10,... | collective-permute-start | bytes 6152 | tf_op jit(solution)/shard_map/ppermute | solution.py:222
  50.8 7.0 %collective-permute-start.15 = (f32[4,128]{1,0:T(4,128)S(1)}, f32[4,128]{1,0:T(4,128)S(1)}, u32[]{:S(2)}, u32[]{:S(2)}) collective-permute-start(f32[4,128]{1,0:T(4,128)S(1)} %get-tuple-element.42), channel_id=1, source_target_pairs={{0,3},{1,2},{2,1},{3,0},{4,7},{5,6},{6,5},{7,4},{8,11},{9,10},{10,... | collective-permute-start | bytes 6152 | tf_op jit(solution)/shard_map/ppermute | solution.py:222
  50.9 8.5 %collective-permute-start.16 = (f32[4,128]{1,0:T(4,128)S(1)}, f32[4,128]{1,0:T(4,128)S(1)}, u32[]{:S(2)}, u32[]{:S(2)}) collective-permute-start(f32[4,128]{1,0:T(4,128)S(1)} %get-tuple-element.43), channel_id=1, source_target_pairs={{0,2},{1,3},{2,0},{3,1},{4,6},{5,7},{6,4},{7,5},{8,10},{9,11},{10,... | collective-permute-start | bytes 6152 | tf_op jit(solution)/shard_map/ppermute | solution.py:222
  57.9 1.6 %collective-permute-start.17 = (f32[4,128]{1,0:T(4,128)S(1)}, f32[4,128]{1,0:T(4,128)S(1)}, u32[]{:S(2)}, u32[]{:S(2)}) collective-permute-start(f32[4,128]{1,0:T(4,128)S(1)} %get-tuple-element.44), channel_id=1, source_target_pairs={{0,1},{1,0},{2,3},{3,2},{4,5},{5,4},{6,7},{7,6},{8,9},{9,8},{10,11... | collective-permute-start | bytes 6152 | tf_op jit(solution)/shard_map/ppermute | solution.py:222

commit v8 on v7

--- a/solution.py
+++ b/solution.py
@@ -50,25 +50,48 @@
     return start, copies
 
 
-def width(devices, panel, order, off):
-    if off < 2:
-        return order
-    return panel if devices == 4 and off == 3 and panel % 128 == 0 else order - 2 * panel
+def trimmed(devices, panel):
+    return devices == 4 and panel == 128
+
+
+def far_shape(devices, count, panel, order, off):
+    if trimmed(devices, panel):
+        return (2 * count, panel * 3 // 4 + (panel if off == 2 else 0), panel)
+    return (2 * count, panel, order - 2 * panel)
+
+
+def fold(block):
+    lane = lax.broadcasted_iota(jnp.int32, (32, 128), 1)
+    return jnp.concatenate([block[:64], jnp.where(lane < 64, pltpu.roll(block[64:96], 64, 1), block[96:])], axis=0)
+
+
+def unfold(folded):
+    top, right = folded[:64], folded[64:]
+    lane = lax.broadcasted_iota(jnp.int32, (64, 128), 1)
+    mirrored = jnp.concatenate([top, top], axis=0).T[64:]
+    lower = jnp.where(lane < 64, mirrored, jnp.concatenate([pltpu.roll(right, 64, 1), right], axis=0))
+    return jnp.concatenate([top, lower], axis=0)
 
 
 def pack_kernel(devices, cov, prec, trans, terminal, *refs):
-    far, (trans_half, first, near, vector, sems) = refs[: devices - 2], refs[devices - 2 :]
+    far, (trans_half, first, near, vector, diagonal, sems) = refs[: devices - 2], refs[devices - 2 :]
     count, panel, order = cov.shape[0] // 2, *cov.shape[1:]
     b, s = lax.axis_index("tm"), lax.axis_index("state")
     start, copies = starter(sems)
     start(terminal, vector)
     start(trans.at[pl.ds(pl.multiple_of((b % 2) * (panel // 2), panel // 2), panel // 2), :], trans_half)
+    trim = trimmed(devices, panel)
+    if trim:
+        for k, matrix in enumerate((cov, prec)):
+            start(matrix.at[:, :, rows(s, panel)], diagonal.at[k])
     for off, piece in enumerate(far, 2):
-        w = width(devices, panel, order, off)
-        column = 2 * panel if w == order - 2 * panel else pl.multiple_of(s * panel, panel)
         theirs = pl.ds(((s ^ off) % 2) * count, count)
         for k, matrix in enumerate((cov, prec)):
-            start(matrix.at[theirs, :, pl.ds(column, w)], piece.at[pl.ds(k * count, count)])
+            target = piece.at[pl.ds(k * count, count)]
+            if not trim:
+                start(matrix.at[theirs, :, 2 * panel :], target)
+            elif off == 2:
+                start(matrix.at[theirs, :, rows(s ^ 1, panel)], target.at[:, :panel])
     theirs = pl.ds((1 - s % 2) * count, count)
     start(cov.at[theirs], near.at[pl.ds(0, count)])
     start(prec.at[theirs], near.at[pl.ds(count, count)])
@@ -77,6 +100,11 @@
     first[...] = jnp.where(b == lax.axis_size("tm") - 1, vector[...], 0.0)
     for copy in copies[1:]:
         copy.wait()
+    if trim:
+        for off, piece in enumerate(far, 2):
+            for k in range(2 * count):
+                block = diagonal[k // count, ((s ^ off) % 2) * count + k % count]
+                piece[k, piece.shape[1] - panel * 3 // 4 :, :] = fold(block)
 
 
 def join_kernel(*refs):
@@ -136,15 +164,16 @@
     panel = known // 2
     e = lax.axis_index("state") % 2
     for k in range(2 * count):
-        for off, piece in enumerate(far, 2):
-            i = (e ^ off) - 2
-            if piece.shape[2] == order - known:
-                ff[k, rows(i, panel), :] = piece[k]
-            else:
-                ff[k, rows(i, panel), rows(i, panel)] = piece[k]
-        if far[-1].shape[2] < order - known:
-            i, j = (e ^ 3) - 2, (e ^ 2) - 2
-            ff[k, rows(i, panel), rows(j, panel)] = ff[k, rows(j, panel), rows(i, panel)].T
+        if not trimmed(len(far) + 2, panel):
+            for off, piece in enumerate(far, 2):
+                ff[k, rows((e ^ off) - 2, panel), :] = piece[k]
+            continue
+        i, j = (e ^ 2) - 2, (e ^ 3) - 2
+        beside, folded = far[0][k, :panel], far[0][k, panel:]
+        ff[k, rows(i, panel), rows(i, panel)] = unfold(folded)
+        ff[k, rows(j, panel), rows(j, panel)] = unfold(far[1][k])
+        ff[k, rows(i, panel), rows(j, panel)] = beside
+        ff[k, rows(j, panel), rows(i, panel)] = beside.T
 
     def complete(k):
         c = c_far[k] + dot3(ff[k], a_far, NT)
@@ -173,6 +202,12 @@
     )
     vec_ref[...] = jnp.concatenate([late[order + 2 : order + 3, :], shift, jnp.zeros((6, order), F32)], axis=0)
     m_ref[...] = dot3(early[:order, :], late[:order, :], NN)
+
+
+def pair_hop_kernel(x, late, early, out_ref):
+    order = x.shape[1]
+    y = late[order : order + 1, :] + matvec(late[:order, :], x[...] - late[order + 2 : order + 3, :])
+    out_ref[...] = early[order : order + 1, :] + matvec(early[:order, :], y - early[order + 2 : order + 3, :])
 
 
 def hop_kernel(x, m, vec, out_ref):
@@ -242,14 +277,14 @@
     semaphores = pltpu.SemaphoreType.DMA((8 * devices,))
     square = shape(order, order)
 
-    far = [shape(2 * count, panel, width(devices, panel, order, off)) for off in range(2, devices)]
+    far = [shape(*far_shape(devices, count, panel, order, off)) for off in range(2, devices)]
     *far, trans_half, first, near = call(
         functools.partial(pack_kernel, devices),
         "pack",
         6,
         far + [shape(panel // 2, order), shape(1, order), shape(2 * count + 1, panel, order)],
         [HBM] * 4,
-        [pltpu.VMEM((1, order), F32), semaphores],
+        [pltpu.VMEM((1, order), F32), pltpu.VMEM((2, steps, panel, panel), F32), semaphores],
         (cov, prec, trans, terminal),
     )
     across = [swap(trans_half, off) for off in range(2, devices, 2)]
@@ -293,14 +328,14 @@
         (*parts, *far),
     )
     early_map = swap(late_map, 1)
-    g1 = swap(lax.optimization_barrier((g3, early_map))[0], 1)
+    (x,) = call(pair_hop_kernel, "pair_hop", 4, [shape(1, order)], [VMEM] * 3, [], (first, late_map, early_map))
+    g1 = swap(lax.optimization_barrier((g3, x))[0], 1)
+    incoming = [first, swap(x, 0, 1)]
     m, vec = call(block_kernel, "block", 12, [square, shape(8, order)], [VMEM] * 2, [], (late_map, early_map))
-
-    incoming = [first]
-    for block in range(blocks - 1, 0, -1):
+    for block in range(blocks - 2, 0, -1):
         (x,) = call(hop_kernel, "hop", 4, [shape(1, order)], [VMEM] * 3, [], (incoming[-1], m, vec))
-        if block % 2:
-            x = swap(x, 0, 1)
+        if block % 2 or block == 2:
+            x = swap(x, 0, block ^ (block - 1))
         else:
             x = lax.ppermute(x, ("tm", "state"), [(block * devices + 1, (block - 1) * devices + 1)])
         incoming.append(x)

time: 60.3 us -> 56.9 us (0.944)
  waiting for transfers between devices: 22.7 us -> 20.7 us
  starting transfers between devices: 23.7 us -> 22.2 us
    ppermute x15 -> x16, waiting for transfers between devices: 22.7 us -> 20.7 us  [swap(): return lax.ppermute(x, ('tm', 'state'), pairs)]
    ppermute x15 -> x16, starting transfers between devices: 21.8 us -> 20.9 us  [swap(): return lax.ppermute(x, ('tm', 'state'), pairs)]
    ppermute x3 -> x2, starting transfers between devices: 1.98 us -> 1.32 us  [local(): lax.ppermute(x, ('tm', 'state'), [(block * devices + 1, (block - 1) * dev...]
  transfers between devices with their start and end apart: 18 -> 18, of which waited for: 9 -> 10; matrix products, arithmetic and copies ran while one was open for 0% -> 0% of each run, Pallas kernels for 12% -> 13%
where the time goes in v8:
time: 56.9 us; the launch traced here: 56.6 us
  starting transfers between devices  22.2 us (39%)
  waiting for transfers between devices  20.7 us (36%)
  Pallas kernels  13.5 us (24%)
    ppermute x16, starting transfers between devices, swap(): return lax.ppermute(x, ('tm', 'state'), pairs)  20.9 us
    ppermute x16, waiting for transfers between devices, swap(): return lax.ppermute(x, ('tm', 'state'), pairs)  20.7 us
    pallas_call x14, Pallas kernels, call(): pl.pallas_call(kernel, out_shape=outs, in_specs=in_specs, out_specs=[VMEM...  13.5 us
    ppermute x2, starting transfers between devices, local(): lax.ppermute(x, ('tm', 'state'), [(block * devices + 1, (block - 1) * dev...  1.32 us
  transfers between devices with their start and end apart: 18, of which 10 were waited for; matrix products, arithmetic and copies ran while one was open for 0% of the time, Pallas kernels for 13%

profile of v8, /device:TPU:0, one launch (start us, length us, event | category | flops | bytes accessed | tf_op | source)
XLA Modules:
  0.0 56.6 jit_solution(9431014195157255061)
XLA Ops:
  0.0 2.0 %pack.1 = (f32[4,224,128]{2,1,0:T(8,128)S(1)}, f32[4,96,128]{2,1,0:T(8,128)S(1)}, f32[64,512]{1,0:T(8,128)S(1)}, f32[1,512]{1,0:T(1,128)S(1)}, f32[5,128,512]{2,1,0:T(8,128)S(1)}) custom-call(f32[4,128,512]{2,1,0:T(8,128)} %cov.3, f32[4,128,512]{2,1,0:T(8,128)} %prec.3, f32[128,512]{1,0:T(8,128)} %trans.3, f32[1,512]{1,0:T(1,128)} %bitcast.1), custom_call_target="tpu_custom_call" | custom-call | tf_op jit(solution)/shard_map/pack/pallas_call | solution.py:263
  2.0 0.5 collective-permute-start
  2.5 2.6 %collective-permute-start.1 = (f32[64,512]{1,0:T(8,128)S(1)}, f32[64,512]{1,0:T(8,128)S(1)}, u32[]{:S(2)}, u32[]{:S(2)}) collective-permute-start(f32[64,512]{1,0:T(8,128)S(1)} %get-tuple-element.27), channel_id=1, source_target_pairs={{0,2},{1,3},{2,0},{3,1},{4,6},{5,7},{6,4},{7,5},{8,10},{9,11},{10,... | collective-permute-start | bytes 393224 | tf_op jit(solution)/shard_map/ppermute | solution.py:257
  5.2 4.3 %collective-permute-done.1.refs_0_ = f32[64,512]{1,0:T(8,128)S(1)} collective-permute-done((f32[64,512]{1,0:T(8,128)S(1)}, f32[64,512]{1,0:T(8,128)S(1)}, u32[]{:S(2)}, u32[]{:S(2)}) %collective-permute-start.1) | collective-permute-done | bytes 131104 | tf_op jit(solution)/shard_map/ppermute | solution.py:257
  9.4 2.0 %collective-permute-start.2 = (f32[64,512]{1,0:T(8,128)S(1)}, f32[64,512]{1,0:T(8,128)S(1)}, u32[]{:S(2)}, u32[]{:S(2)}) collective-permute-start(f32[64,512]{1,0:T(8,128)S(1)} %collective-permute-done.1.refs_0_), channel_id=1, source_target_pairs={{0,4},{1,5},{2,6},{3,7},{4,0},{5,1},{6,2},{7,3},{8,12},{9,13},{10,... | collective-permute-start | bytes 393224 | tf_op jit(solution)/shard_map/ppermute | solution.py:257
  11.4 3.0 %collective-permute-done.2.refs_1_ = f32[64,512]{1,0:T(8,128)S(1)} collective-permute-done((f32[64,512]{1,0:T(8,128)S(1)}, f32[64,512]{1,0:T(8,128)S(1)}, u32[]{:S(2)}, u32[]{:S(2)}) %collective-permute-start.2) | collective-permute-done | bytes 131104 | tf_op jit(solution)/shard_map/ppermute | solution.py:257
  14.4 0.6 %join.1.joined = f32[1,128,512]{2,1,0:T(8,128)S(1)} custom-call(f32[64,512]{1,0:T(8,128)S(1)} %collective-permute-done.1.refs_0_, f32[64,512]{1,0:T(8,128)S(1)} %collective-permute-done.2.refs_1_), custom_call_target="tpu_custom_call" | custom-call | tf_op jit(solution)/shard_map/join/pallas_call | solution.py:263
  15.1 2.0 %collective-permute-start.5 = (f32[4,96,128]{2,1,0:T(8,128)S(1)}, f32[4,96,128]{2,1,0:T(8,128)S(1)}, u32[]{:S(2)}, u32[]{:S(2)}) collective-permute-start(f32[4,96,128]{2,1,0:T(8,128)S(1)} %get-tuple-element.35), channel_id=1, source_target_pairs={{0,3},{1,2},{2,1},{3,0},{4,7},{5,6},{6,5},{7,4},{8,11},{9,10},{10,... | collective-permute-start | bytes 589832 | tf_op jit(solution)/shard_map/ppermute | solution.py:257
  17.2 4.8 %early.1 = (f32[16,512]{1,0:T(8,128)S(1)}, bf16[2,512,256]{2,1,0:T(8,128)(2,1)S(1)}, bf16[2,2,256,512]{3,2,1,0:T(8,128)(2,1)S(1)}, f32[2,256,256]{2,1,0:T(8,128)...) custom-call(f32[4,128,512]{2,1,0:T(8,128)} %cov.3, f32[4,128,512]{2,1,0:T(8,128)} %prec.3, ...), custom_call_target="tpu_custom_call" | custom-call | tf_op jit(solution)/shard_map/early/pallas_call | solution.py:263
  21.9 1.0 %collective-permute-done.5.refs_1_ = f32[4,96,128]{2,1,0:T(8,128)S(1)} collective-permute-done((f32[4,96,128]{2,1,0:T(8,128)S(1)}, f32[4,96,128]{2,1,0:T(8,128)S(1)}, u32[]{:S(2)}, u32[]{:S(2)}) %collective-permute-start.5) | collective-permute-done | bytes 196640 | tf_op jit(solution)/shard_map/ppermute | solution.py:257
  23.0 3.0 %late.1 = (f32[520,512]{1,0:T(8,128)S(1)}, f32[512,512]{1,0:T(8,128)S(1)}) custom-call(f32[16,512]{1,0:T(8,128)S(1)} %get-tuple-element.28.info, bf16[2,512,256]{2,1,0:T(8,128)(2,1)S(1)} %get-tuple-element.29.a_far, bf16[2,2,256,512]{3,2,1,0:T(8,128)(2,1)S(1)} %get-tuple-element.30.l_known, f32[2,256,256]{2,1,0:T(8,128)S(1)} %get-tuple-element.31.c_known, ...), custom_call_target="tpu_custom_call" | custom-call | tf_op jit(solution)/shard_map/late/pallas_call | solution.py:263
  26.0 0.2 collective-permute-start.6
  26.1 2.6 %collective-permute-done.6.early.refs_12_ = f32[520,512]{1,0:T(8,128)S(1)} collective-permute-done((f32[520,512]{1,0:T(8,128)S(1)}, f32[520,512]{1,0:T(8,128)S(1)}, u32[]{:S(2)}, u32[]{:S(2)}) %collective-permute-start.6) | collective-permute-done | bytes 1064992 | tf_op jit(solution)/shard_map/ppermute | solution.py:257
  28.7 0.3 pair_hop.1
  29.0 0.2 collective-permute-start.14
  29.2 1.7 %collective-permute-start.7 = (f32[1,512]{1,0:T(1,128)S(1)}, f32[1,512]{1,0:T(1,128)S(1)}, u32[]{:S(2)}, u32[]{:S(2)}) collective-permute-start(f32[1,512]{1,0:T(1,128)S(1)} %pair_hop.1), channel_id=1, source_target_pairs={{0,4},{1,5},{2,6},{3,7},{4,0},{5,1},{6,2},{7,3},{8,12},{9,13},{10,... | collective-permute-start | bytes 6152 | tf_op jit(solution)/shard_map/ppermute | solution.py:257
  31.0 1.0 %block.1 = (f32[512,512]{1,0:T(8,128)S(1)}, f32[8,512]{1,0:T(8,128)S(1)}) custom-call(f32[520,512]{1,0:T(8,128)S(1)} %get-tuple-element.36.late.refs_10_, f32[520,512]{1,0:T(8,128)S(1)} %collective-permute-done.6.early.refs_12_), custom_call_target="tpu_custom_call" | custom-call | tf_op jit(solution)/shard_map/block/pallas_call | solution.py:263
  31.9 0.9 %collective-permute-done.7.x.refs_1_ = f32[1,512]{1,0:T(1,128)S(1)} collective-permute-done((f32[1,512]{1,0:T(1,128)S(1)}, f32[1,512]{1,0:T(1,128)S(1)}, u32[]{:S(2)}, u32[]{:S(2)}) %collective-permute-start.7) | collective-permute-done | bytes 2080 | tf_op jit(solution)/shard_map/ppermute | solution.py:257
  33.0 0.7 %collective-permute-start.8 = (f32[1,512]{1,0:T(1,128)S(1)}, f32[1,512]{1,0:T(1,128)S(1)}, u32[]{:S(2)}, u32[]{:S(2)}) collective-permute-start(f32[1,512]{1,0:T(1,128)S(1)} %hop.6), channel_id=1, source_target_pairs={{25,21}} | collective-permute-start | bytes 6152 | tf_op jit(solution)/shard_map/ppermute | solution.py:340
  33.8 1.8 %collective-permute-start.9 = (f32[1,512]{1,0:T(1,128)S(1)}, f32[1,512]{1,0:T(1,128)S(1)}, u32[]{:S(2)}, u32[]{:S(2)}) collective-permute-start(f32[1,512]{1,0:T(1,128)S(1)} %hop.7), channel_id=1, source_target_pairs={{0,4},{1,5},{2,6},{3,7},{4,0},{5,1},{6,2},{7,3},{8,12},{9,13},{10,... | collective-permute-start | bytes 6152 | tf_op jit(solution)/shard_map/ppermute | solution.py:257
  35.6 1.9 %collective-permute-done.9.x.refs_3_ = f32[1,512]{1,0:T(1,128)S(1)} collective-permute-done((f32[1,512]{1,0:T(1,128)S(1)}, f32[1,512]{1,0:T(1,128)S(1)}, u32[]{:S(2)}, u32[]{:S(2)}) %collective-permute-start.9) | collective-permute-done | bytes 2080 | tf_op jit(solution)/shard_map/ppermute | solution.py:257
  37.6 0.7 %collective-permute-start.10 = (f32[1,512]{1,0:T(1,128)S(1)}, f32[1,512]{1,0:T(1,128)S(1)}, u32[]{:S(2)}, u32[]{:S(2)}) collective-permute-start(f32[1,512]{1,0:T(1,128)S(1)} %hop.8), channel_id=1, source_target_pairs={{17,13}} | collective-permute-start | bytes 6152 | tf_op jit(solution)/shard_map/ppermute | solution.py:340
  38.5 1.8 %collective-permute-start.11 = (f32[1,512]{1,0:T(1,128)S(1)}, f32[1,512]{1,0:T(1,128)S(1)}, u32[]{:S(2)}, u32[]{:S(2)}) collective-permute-start(f32[1,512]{1,0:T(1,128)S(1)} %hop.9), channel_id=1, source_target_pairs={{0,4},{1,5},{2,6},{3,7},{4,0},{5,1},{6,2},{7,3},{8,12},{9,13},{10,... | collective-permute-start | bytes 6152 | tf_op jit(solution)/shard_map/ppermute | solution.py:257
  40.2 1.9 %collective-permute-done.11.x.refs_5_ = f32[1,512]{1,0:T(1,128)S(1)} collective-permute-done((f32[1,512]{1,0:T(1,128)S(1)}, f32[1,512]{1,0:T(1,128)S(1)}, u32[]{:S(2)}, u32[]{:S(2)}) %collective-permute-start.11) | collective-permute-done | bytes 2080 | tf_op jit(solution)/shard_map/ppermute | solution.py:257
  42.3 2.8 %collective-permute-start.12 = (f32[1,512]{1,0:T(1,128)S(1)}, f32[1,512]{1,0:T(1,128)S(1)}, u32[]{:S(2)}, u32[]{:S(2)}) collective-permute-start(f32[1,512]{1,0:T(1,128)S(1)} %hop.10), channel_id=1, source_target_pairs={{0,12},{1,13},{2,14},{3,15},{4,8},{5,9},{6,10},{7,11},{8,4},{9,5},... | collective-permute-start | bytes 6152 | tf_op jit(solution)/shard_map/ppermute | solution.py:257
  45.1 1.8 %collective-permute-done.12.x.refs_6_ = f32[1,512]{1,0:T(1,128)S(1)} collective-permute-done((f32[1,512]{1,0:T(1,128)S(1)}, f32[1,512]{1,0:T(1,128)S(1)}, u32[]{:S(2)}, u32[]{:S(2)}) %collective-permute-start.12) | collective-permute-done | bytes 2080 | tf_op jit(solution)/shard_map/ppermute | solution.py:257
  47.0 1.8 %collective-permute-start.13 = (f32[1,512]{1,0:T(1,128)S(1)}, f32[1,512]{1,0:T(1,128)S(1)}, u32[]{:S(2)}, u32[]{:S(2)}) collective-permute-start(f32[1,512]{1,0:T(1,128)S(1)} %hop.11), channel_id=1, source_target_pairs={{0,4},{1,5},{2,6},{3,7},{4,0},{5,1},{6,2},{7,3},{8,12},{9,13},{10,... | collective-permute-start | bytes 6152 | tf_op jit(solution)/shard_map/ppermute | solution.py:257
  48.8 1.9 %collective-permute-done.13.refs_7_ = f32[1,512]{1,0:T(1,128)S(1)} collective-permute-done((f32[1,512]{1,0:T(1,128)S(1)}, f32[1,512]{1,0:T(1,128)S(1)}, u32[]{:S(2)}, u32[]{:S(2)}) %collective-permute-start.13) | collective-permute-done | bytes 2080 | tf_op jit(solution)/shard_map/ppermute | solution.py:257
  50.6 0.4 last.1
  51.1 3.3 %collective-permute-start.16 = (f32[4,128]{1,0:T(4,128)S(1)}, f32[4,128]{1,0:T(4,128)S(1)}, u32[]{:S(2)}, u32[]{:S(2)}) collective-permute-start(f32[4,128]{1,0:T(4,128)S(1)} %get-tuple-element.43), channel_id=1, source_target_pairs={{0,2},{1,3},{2,0},{3,1},{4,6},{5,7},{6,4},{7,5},{8,10},{9,11},{10,... | collective-permute-start | bytes 6152 | tf_op jit(solution)/shard_map/ppermute | solution.py:257
  54.5 1.6 %collective-permute-done.16.refs_2_ = f32[4,128]{1,0:T(4,128)S(1)} collective-permute-done((f32[4,128]{1,0:T(4,128)S(1)}, f32[4,128]{1,0:T(4,128)S(1)}, u32[]{:S(2)}, u32[]{:S(2)}) %collective-permute-start.16) | collective-permute-done | bytes 2080 | tf_op jit(solution)/shard_map/ppermute | solution.py:257
  56.0 0.6 %out.1 = f32[4,128]{1,0:T(4,128)} custom-call(f32[4,128]{1,0:T(4,128)S(1)} %get-tuple-element.41.refs_0_, f32[4,128]{1,0:T(4,128)S(1)} %collective-permute-done.15.refs_1_, f32[4,128]{1,0:T(4,128)S(1)} %collective-permute-done.16.refs_2_, f32[4,128]{1,0:T(4,128)S(1)} %collective-permute-done.17.refs_3_), custom_call_target="tpu_custom_call" | custom-call | tf_op jit(solution)/shard_map/out/pallas_call | solution.py:263
  (18 shorter events, 1.2 us)
Async XLA Ops:
  2.0 15.2 %collective-permute-start = (f32[5,128,512]{2,1,0:T(8,128)S(1)}, f32[5,128,512]{2,1,0:T(8,128)S(1)}, u32[]{:S(2)}, u32[]{:S(2)}) collective-permute-start(f32[5,128,512]{2,1,0:T(8,128)S(1)} %get-tuple-element.26), channel_id=1, source_target_pairs={{0,1},{1,0},{2,3},{3,2},{4,5},{5,4},{6,7},{7,6},{8,9},{9,8},{10,11... | collective-permute-start | bytes 3932168 | tf_op jit(solution)/shard_map/ppermute | solution.py:257
  2.5 6.9 %collective-permute-start.1 = (f32[64,512]{1,0:T(8,128)S(1)}, f32[64,512]{1,0:T(8,128)S(1)}, u32[]{:S(2)}, u32[]{:S(2)}) collective-permute-start(f32[64,512]{1,0:T(8,128)S(1)} %get-tuple-element.27), channel_id=1, source_target_pairs={{0,2},{1,3},{2,0},{3,1},{4,6},{5,7},{6,4},{7,5},{8,10},{9,11},{10,... | collective-permute-start | bytes 393224 | tf_op jit(solution)/shard_map/ppermute | solution.py:257
  5.1 17.9 %collective-permute-start.4 = (f32[4,224,128]{2,1,0:T(8,128)S(1)}, f32[4,224,128]{2,1,0:T(8,128)S(1)}, u32[]{:S(2)}, u32[]{:S(2)}) collective-permute-start(f32[4,224,128]{2,1,0:T(8,128)S(1)} %get-tuple-element.34), channel_id=1, source_target_pairs={{0,2},{1,3},{2,0},{3,1},{4,6},{5,7},{6,4},{7,5},{8,10},{9,11},{10,... | collective-permute-start | bytes 1376264 | tf_op jit(solution)/shard_map/ppermute | solution.py:257
  9.4 5.0 %collective-permute-start.2 = (f32[64,512]{1,0:T(8,128)S(1)}, f32[64,512]{1,0:T(8,128)S(1)}, u32[]{:S(2)}, u32[]{:S(2)}) collective-permute-start(f32[64,512]{1,0:T(8,128)S(1)} %collective-permute-done.1.refs_0_), channel_id=1, source_target_pairs={{0,4},{1,5},{2,6},{3,7},{4,0},{5,1},{6,2},{7,3},{8,12},{9,13},{10,... | collective-permute-start | bytes 393224 | tf_op jit(solution)/shard_map/ppermute | solution.py:257
  15.0 2.1 %collective-permute-start.3 = (f32[1,128,512]{2,1,0:T(8,128)S(1)}, f32[1,128,512]{2,1,0:T(8,128)S(1)}, u32[]{:S(2)}, u32[]{:S(2)}) collective-permute-start(f32[1,128,512]{2,1,0:T(8,128)S(1)} %join.1.joined), channel_id=1, source_target_pairs={{0,1},{1,0},{2,3},{3,2},{4,5},{5,4},{6,7},{7,6},{8,9},{9,8},{10,11... | collective-permute-start | bytes 786440 | tf_op jit(solution)/shard_map/ppermute | solution.py:257
  15.1 7.8 %collective-permute-start.5 = (f32[4,96,128]{2,1,0:T(8,128)S(1)}, f32[4,96,128]{2,1,0:T(8,128)S(1)}, u32[]{:S(2)}, u32[]{:S(2)}) collective-permute-start(f32[4,96,128]{2,1,0:T(8,128)S(1)} %get-tuple-element.35), channel_id=1, source_target_pairs={{0,3},{1,2},{2,1},{3,0},{4,7},{5,6},{6,5},{7,4},{8,11},{9,10},{10,... | collective-permute-start | bytes 589832 | tf_op jit(solution)/shard_map/ppermute | solution.py:257
  26.0 2.7 %collective-permute-start.6 = (f32[520,512]{1,0:T(8,128)S(1)}, f32[520,512]{1,0:T(8,128)S(1)}, u32[]{:S(2)}, u32[]{:S(2)}) collective-permute-start(f32[520,512]{1,0:T(8,128)S(1)} %get-tuple-element.36.late.refs_10_), channel_id=1, source_target_pairs={{0,1},{1,0},{2,3},{3,2},{4,5},{5,4},{6,7},{7,6},{8,9},{9,8},{10,11... | collective-permute-start | bytes 3194888 | tf_op jit(solution)/shard_map/ppermute | solution.py:257
  29.0 21.6 %collective-permute-start.14 = (f32[512,512]{1,0:T(8,128)S(1)}, f32[512,512]{1,0:T(8,128)S(1)}, u32[]{:S(2)}, u32[]{:S(2)}) collective-permute-start(f32[512,512]{1,0:T(8,128)S(1)} %get-tuple-element.40.refs_11_), channel_id=1, source_target_pairs={{0,1},{1,0},{2,3},{3,2},{4,5},{5,4},{6,7},{7,6},{8,9},{9,8},{10,11... | collective-permute-start | bytes 3145736 | tf_op jit(solution)/shard_map/ppermute | solution.py:257
  29.2 3.6 %collective-permute-start.7 = (f32[1,512]{1,0:T(1,128)S(1)}, f32[1,512]{1,0:T(1,128)S(1)}, u32[]{:S(2)}, u32[]{:S(2)}) collective-permute-start(f32[1,512]{1,0:T(1,128)S(1)} %pair_hop.1), channel_id=1, source_target_pairs={{0,4},{1,5},{2,6},{3,7},{4,0},{5,1},{6,2},{7,3},{8,12},{9,13},{10,... | collective-permute-start | bytes 6152 | tf_op jit(solution)/shard_map/ppermute | solution.py:257
  33.0 0.7 %collective-permute-start.8 = (f32[1,512]{1,0:T(1,128)S(1)}, f32[1,512]{1,0:T(1,128)S(1)}, u32[]{:S(2)}, u32[]{:S(2)}) collective-permute-start(f32[1,512]{1,0:T(1,128)S(1)} %hop.6), channel_id=1, source_target_pairs={{25,21}} | collective-permute-start | bytes 6152 | tf_op jit(solution)/shard_map/ppermute | solution.py:340
  33.8 3.7 %collective-permute-start.9 = (f32[1,512]{1,0:T(1,128)S(1)}, f32[1,512]{1,0:T(1,128)S(1)}, u32[]{:S(2)}, u32[]{:S(2)}) collective-permute-start(f32[1,512]{1,0:T(1,128)S(1)} %hop.7), channel_id=1, source_target_pairs={{0,4},{1,5},{2,6},{3,7},{4,0},{5,1},{6,2},{7,3},{8,12},{9,13},{10,... | collective-permute-start | bytes 6152 | tf_op jit(solution)/shard_map/ppermute | solution.py:257
  37.6 0.7 %collective-permute-start.10 = (f32[1,512]{1,0:T(1,128)S(1)}, f32[1,512]{1,0:T(1,128)S(1)}, u32[]{:S(2)}, u32[]{:S(2)}) collective-permute-start(f32[1,512]{1,0:T(1,128)S(1)} %hop.8), channel_id=1, source_target_pairs={{17,13}} | collective-permute-start | bytes 6152 | tf_op jit(solution)/shard_map/ppermute | solution.py:340
  38.5 3.7 %collective-permute-start.11 = (f32[1,512]{1,0:T(1,128)S(1)}, f32[1,512]{1,0:T(1,128)S(1)}, u32[]{:S(2)}, u32[]{:S(2)}) collective-permute-start(f32[1,512]{1,0:T(1,128)S(1)} %hop.9), channel_id=1, source_target_pairs={{0,4},{1,5},{2,6},{3,7},{4,0},{5,1},{6,2},{7,3},{8,12},{9,13},{10,... | collective-permute-start | bytes 6152 | tf_op jit(solution)/shard_map/ppermute | solution.py:257
  42.3 4.5 %collective-permute-start.12 = (f32[1,512]{1,0:T(1,128)S(1)}, f32[1,512]{1,0:T(1,128)S(1)}, u32[]{:S(2)}, u32[]{:S(2)}) collective-permute-start(f32[1,512]{1,0:T(1,128)S(1)} %hop.10), channel_id=1, source_target_pairs={{0,12},{1,13},{2,14},{3,15},{4,8},{5,9},{6,10},{7,11},{8,4},{9,5},... | collective-permute-start | bytes 6152 | tf_op jit(solution)/shard_map/ppermute | solution.py:257
  47.0 3.7 %collective-permute-start.13 = (f32[1,512]{1,0:T(1,128)S(1)}, f32[1,512]{1,0:T(1,128)S(1)}, u32[]{:S(2)}, u32[]{:S(2)}) collective-permute-start(f32[1,512]{1,0:T(1,128)S(1)} %hop.11), channel_id=1, source_target_pairs={{0,4},{1,5},{2,6},{3,7},{4,0},{5,1},{6,2},{7,3},{8,12},{9,13},{10,... | collective-permute-start | bytes 6152 | tf_op jit(solution)/shard_map/ppermute | solution.py:257
  51.0 3.4 %collective-permute-start.15 = (f32[4,128]{1,0:T(4,128)S(1)}, f32[4,128]{1,0:T(4,128)S(1)}, u32[]{:S(2)}, u32[]{:S(2)}) collective-permute-start(f32[4,128]{1,0:T(4,128)S(1)} %get-tuple-element.42), channel_id=1, source_target_pairs={{0,3},{1,2},{2,1},{3,0},{4,7},{5,6},{6,5},{7,4},{8,11},{9,10},{10,... | collective-permute-start | bytes 6152 | tf_op jit(solution)/shard_map/ppermute | solution.py:257
  51.1 4.9 %collective-permute-start.16 = (f32[4,128]{1,0:T(4,128)S(1)}, f32[4,128]{1,0:T(4,128)S(1)}, u32[]{:S(2)}, u32[]{:S(2)}) collective-permute-start(f32[4,128]{1,0:T(4,128)S(1)} %get-tuple-element.43), channel_id=1, source_target_pairs={{0,2},{1,3},{2,0},{3,1},{4,6},{5,7},{6,4},{7,5},{8,10},{9,11},{10,... | collective-permute-start | bytes 6152 | tf_op jit(solution)/shard_map/ppermute | solution.py:257
  54.5 1.6 %collective-permute-start.17 = (f32[4,128]{1,0:T(4,128)S(1)}, f32[4,128]{1,0:T(4,128)S(1)}, u32[]{:S(2)}, u32[]{:S(2)}) collective-permute-start(f32[4,128]{1,0:T(4,128)S(1)} %get-tuple-element.44), channel_id=1, source_target_pairs={{0,1},{1,0},{2,3},{3,2},{4,5},{5,4},{6,7},{7,6},{8,9},{9,8},{10,11... | collective-permute-start | bytes 6152 | tf_op jit(solution)/shard_map/ppermute | solution.py:257

commit v9 on v8

--- a/solution.py
+++ b/solution.py
@@ -74,7 +74,7 @@
 
 
 def pack_kernel(devices, cov, prec, trans, terminal, *refs):
-    far, (trans_half, first, near, vector, diagonal, sems) = refs[: devices - 2], refs[devices - 2 :]
+    far, (trans_half, first, vector, diagonal, sems) = refs[: devices - 2], refs[devices - 2 :]
     count, panel, order = cov.shape[0] // 2, *cov.shape[1:]
     b, s = lax.axis_index("tm"), lax.axis_index("state")
     start, copies = starter(sems)
@@ -92,10 +92,6 @@
                 start(matrix.at[theirs, :, 2 * panel :], target)
             elif off == 2:
                 start(matrix.at[theirs, :, rows(s ^ 1, panel)], target.at[:, :panel])
-    theirs = pl.ds((1 - s % 2) * count, count)
-    start(cov.at[theirs], near.at[pl.ds(0, count)])
-    start(prec.at[theirs], near.at[pl.ds(count, count)])
-    start(trans, near.at[2 * count])
     copies[0].wait()
     first[...] = jnp.where(b == lax.axis_size("tm") - 1, vector[...], 0.0)
     for copy in copies[1:]:
@@ -105,6 +101,17 @@
             for k in range(2 * count):
                 block = diagonal[k // count, ((s ^ off) % 2) * count + k % count]
                 piece[k, piece.shape[1] - panel * 3 // 4 :, :] = fold(block)
+
+
+def near_kernel(cov, prec, trans, after, near_cov, near_prec, near_trans, sems):
+    count = cov.shape[0] // 2
+    theirs = pl.ds((1 - lax.axis_index("state") % 2) * count, count)
+    start, copies = starter(sems)
+    start(cov.at[theirs], near_cov)
+    start(prec.at[theirs], near_prec)
+    start(trans, near_trans)
+    for copy in copies:
+        copy.wait()
 
 
 def join_kernel(*refs):
@@ -119,7 +126,7 @@
         copy.wait()
 
 
-def early_kernel(cov, prec, trans, means, near, joined, joined_near, *refs):
+def early_kernel(cov, prec, trans, means, near_cov, near_prec, near_trans, joined, joined_near, *refs):
     info, a_far, l_known, c_known, c_far, g_known, pf, af, lf, sems = refs
     steps, panel, order = cov.shape
     count, known = steps // 2, 2 * panel
@@ -129,11 +136,11 @@
     for k in range(count):
         step = e * count + k
         start(cov.at[step], pf.at[pl.ds(pl.multiple_of(k * known + e * panel, panel), panel), :])
-        start(near.at[k], pf.at[pl.ds(pl.multiple_of(k * known + (1 - e) * panel, panel), panel), :])
+        start(near_cov.at[k], pf.at[pl.ds(pl.multiple_of(k * known + (1 - e) * panel, panel), panel), :])
         start(prec.at[step], lf.at[k, rows(e, panel), :])
-        start(near.at[count + k], lf.at[k, rows(1 - e, panel), :])
+        start(near_prec.at[k], lf.at[k, rows(1 - e, panel), :])
     start(trans, af.at[rows(e, panel), :])
-    start(near.at[2 * count], af.at[rows(1 - e, panel), :])
+    start(near_trans, af.at[rows(1 - e, panel), :])
     for j in range(1, order // known):
         start(joined.at[j - 1], af.at[rows(e ^ (2 * j), panel), :])
         start(joined_near.at[j - 1], af.at[rows(e ^ (2 * j) ^ 1, panel), :])
@@ -158,8 +165,13 @@
         c_far[k] = rest[k * (order - known) : (k + 1) * (order - known)]
 
 
-def late_kernel(info, a_far, l_known, c_known, c_far, g_known, *refs):
-    far, (map_ref, gain_ref, ff) = refs[:-3], refs[-3:]
+def steps_of(info, count):
+    a = (lax.axis_index("state") % 2) * count
+    return [info[pl.ds(a + shift, 1), :] for shift in (0, 1, 8, 9)]
+
+
+def late_kernel(first, info, a_far, l_known, c_known, c_far, g_known, *refs):
+    far, (ga_ref, gb_ref, mean_ref, ff) = refs[:-4], refs[-4:]
     count, known, order = g_known.shape
     panel = known // 2
     e = lax.axis_index("state") % 2
@@ -185,14 +197,24 @@
         return jnp.concatenate([top, jnp.concatenate([left, low[:, known:] + share[known:]], axis=1)], axis=0)
 
     ga, gb = complete(0), complete(1)
-    gain_ref[...] = gb
-    a = e * count
-    mean_a, mean_b = info[pl.ds(a, 1), :], info[pl.ds(a + 1, 1), :]
-    pred_a, pred_b = info[pl.ds(a + 8, 1), :], info[pl.ds(a + 9, 1), :]
+    ga_ref[...] = ga
+    gb_ref[...] = gb
+    mean_a, mean_b, pred_a, pred_b = steps_of(info, count)
+    mean_ref[...] = mean_a + matvec(ga, mean_b + matvec(gb, first[...] - pred_b) - pred_a)
+
+
+def two_kernel(x, info, ga, gb, out_ref):
+    mean_a, mean_b, pred_a, pred_b = steps_of(info, 2)
+    out_ref[...] = mean_a + matvec(ga[...], mean_b + matvec(gb[...], x[...] - pred_b) - pred_a)
+
+
+def pair_kernel(info, ga, gb, map_ref):
+    order = ga.shape[1]
+    mean_a, mean_b, pred_a, pred_b = steps_of(info, 2)
     map_ref[order:, :] = jnp.concatenate(
-        [mean_a + matvec(ga, mean_b - pred_a), mean_b, pred_b, jnp.zeros((5, order), F32)], axis=0
-    )
-    map_ref[:order, :] = dot3(ga, gb, NN)
+        [mean_a + matvec(ga[...], mean_b - pred_a), mean_b, pred_b, jnp.zeros((5, order), F32)], axis=0
+    )
+    map_ref[:order, :] = dot3(ga[...], gb[...], NN)
 
 
 def block_kernel(late, early, m_ref, vec_ref):
@@ -202,12 +224,6 @@
     )
     vec_ref[...] = jnp.concatenate([late[order + 2 : order + 3, :], shift, jnp.zeros((6, order), F32)], axis=0)
     m_ref[...] = dot3(early[:order, :], late[:order, :], NN)
-
-
-def pair_hop_kernel(x, late, early, out_ref):
-    order = x.shape[1]
-    y = late[order : order + 1, :] + matvec(late[:order, :], x[...] - late[order + 2 : order + 3, :])
-    out_ref[...] = early[order : order + 1, :] + matvec(early[:order, :], y - early[order + 2 : order + 3, :])
 
 
 def hop_kernel(x, m, vec, out_ref):
@@ -278,18 +294,27 @@
     square = shape(order, order)
 
     far = [shape(*far_shape(devices, count, panel, order, off)) for off in range(2, devices)]
-    *far, trans_half, first, near = call(
+    *far, trans_half, first = call(
         functools.partial(pack_kernel, devices),
         "pack",
         6,
-        far + [shape(panel // 2, order), shape(1, order), shape(2 * count + 1, panel, order)],
+        far + [shape(panel // 2, order), shape(1, order)],
         [HBM] * 4,
         [pltpu.VMEM((1, order), F32), pltpu.VMEM((2, steps, panel, panel), F32), semaphores],
         (cov, prec, trans, terminal),
     )
     across = [swap(trans_half, off) for off in range(2, devices, 2)]
     far = [swap(x, off) for off, x in enumerate(far, 2)]
-    near = swap(near, 1)
+    near = call(
+        near_kernel,
+        "near",
+        4,
+        [shape(count, panel, order), shape(count, panel, order), shape(panel, order)],
+        [HBM] * 3 + [ANY],
+        [semaphores],
+        (cov, prec, trans, first),
+    )
+    near = [swap(x, 1) for x in near]
     moved = [y for x in across for y in (x, swap(x, 0, 1))]
     (joined,) = call(
         join_kernel, "join", 4, [shape(devices // 2 - 1, panel, order)], [ANY] * len(moved), [semaphores], moved
@@ -309,36 +334,40 @@
             shape(count, order - known, order),
             shape(count, known, order),
         ],
-        [HBM] * 3 + [VMEM] + [ANY] * 3,
+        [HBM] * 3 + [VMEM] + [ANY] * 5,
         [
             pltpu.VMEM((count * known + 16, order), F32),
             pltpu.VMEM((order, order), F32),
             pltpu.VMEM((count, known, order), F32),
             semaphores,
         ],
-        (cov, prec, trans, means, near, joined, joined_near),
-    )
-    late_map, g3 = call(
+        (cov, prec, trans, means, *near, joined, joined_near),
+    )
+    info = parts[0]
+    ga, gb, mean = call(
         late_kernel,
         "late",
         24,
-        [shape(order + 8, order), square],
-        [VMEM] * (6 + len(far)),
+        [square, square, shape(1, order)],
+        [VMEM] * (7 + len(far)),
         [pltpu.VMEM((2 * count, order - known, order - known), F32)],
-        (*parts, *far),
-    )
-    early_map = swap(late_map, 1)
-    (x,) = call(pair_hop_kernel, "pair_hop", 4, [shape(1, order)], [VMEM] * 3, [], (first, late_map, early_map))
-    g1 = swap(lax.optimization_barrier((g3, x))[0], 1)
-    incoming = [first, swap(x, 0, 1)]
+        (first, *parts, *far),
+    )
+    mean = swap(mean, 1)
+    (late_map,) = call(pair_kernel, "pair", 12, [shape(order + 8, order)], [VMEM] * 3, [], (info, ga, gb))
+    early_map = swap(lax.optimization_barrier((late_map, mean))[0], 1)
+    (mean,) = call(two_kernel, "two", 6, [shape(1, order)], [VMEM] * 4, [], (mean, info, ga, gb))
+
+    incoming = [first, swap(mean, 1, 1)]
     m, vec = call(block_kernel, "block", 12, [square, shape(8, order)], [VMEM] * 2, [], (late_map, early_map))
     for block in range(blocks - 2, 0, -1):
         (x,) = call(hop_kernel, "hop", 4, [shape(1, order)], [VMEM] * 3, [], (incoming[-1], m, vec))
-        if block % 2 or block == 2:
-            x = swap(x, 0, block ^ (block - 1))
+        if block % 2:
+            x = swap(x, 0, 1)
         else:
             x = lax.ppermute(x, ("tm", "state"), [(block * devices + 1, (block - 1) * devices + 1)])
         incoming.append(x)
+    g1 = swap(lax.optimization_barrier((gb, incoming[2]))[0], 1)
 
     given = list(call(
         functools.partial(last_kernel, devices),
@@ -347,7 +376,7 @@
         [shape(steps, panel)] * devices,
         [VMEM] * (blocks + 6),
         [pltpu.VMEM((devices, steps, panel), F32)],
-        (*incoming, m, vec, late_map, g3, early_map, g1),
+        (*incoming, m, vec, late_map, gb, early_map, g1),
     ))
     for off in range(devices - 1, 0, -1):
         given[off] = swap(given[off], off)

time: 56.9 us -> 56.1 us (0.986)
  waiting for transfers between devices: 20.7 us -> 16 us
  starting transfers between devices: 22.2 us -> 24.4 us
  Pallas kernels: 13.5 us -> 15.2 us
    ppermute x16 -> x18, waiting for transfers between devices: 20.7 us -> 16 us  [swap(): return lax.ppermute(x, ('tm', 'state'), pairs)]
    pallas_call x14 -> x16, Pallas kernels: 13.5 us -> 15.2 us  [call(): pl.pallas_call(kernel, out_shape=outs, in_specs=in_specs, out_specs=[VMEM...]
    ppermute x16 -> x18, starting transfers between devices: 20.9 us -> 22.4 us  [swap(): return lax.ppermute(x, ('tm', 'state'), pairs)]
    ppermute x2 -> x3, starting transfers between devices: 1.32 us -> 1.98 us  [local(): lax.ppermute(x, ('tm', 'state'), [(block * devices + 1, (block - 1) * dev...]
  transfers between devices with their start and end apart: 18 -> 21, of which waited for: 10 -> 8; matrix products, arithmetic and copies ran while one was open for 0% -> 0% of each run, Pallas kernels for 13% -> 18%
where the time goes in v9:
time: 56.1 us; the launch traced here: 55.8 us
  starting transfers between devices  24.4 us (43%)
  waiting for transfers between devices  16 us (29%)
  Pallas kernels  15.2 us (27%)
    ppermute x18, starting transfers between devices, swap(): return lax.ppermute(x, ('tm', 'state'), pairs)  22.4 us
    ppermute x18, waiting for transfers between devices, swap(): return lax.ppermute(x, ('tm', 'state'), pairs)  16 us
    pallas_call x16, Pallas kernels, call(): pl.pallas_call(kernel, out_shape=outs, in_specs=in_specs, out_specs=[VMEM...  15.2 us
    ppermute x3, starting transfers between devices, local(): lax.ppermute(x, ('tm', 'state'), [(block * devices + 1, (block - 1) * dev...  1.98 us
  transfers between devices with their start and end apart: 21, of which 8 were waited for; matrix products, arithmetic and copies ran while one was open for 0% of the time, Pallas kernels for 18%

profile of v9, /device:TPU:0, one launch (start us, length us, event | category | flops | bytes accessed | tf_op | source)
XLA Modules:
  0.0 55.8 jit_solution(16770267104476490181)
XLA Ops:
  0.0 1.6 %pack.1 = (f32[4,224,128]{2,1,0:T(8,128)S(1)}, f32[4,96,128]{2,1,0:T(8,128)S(1)}, f32[64,512]{1,0:T(8,128)S(1)}, f32[1,512]{1,0:T(1,128)S(1)}) custom-call(f32[4,128,512]{2,1,0:T(8,128)} %cov.5, f32[4,128,512]{2,1,0:T(8,128)} %prec.5, f32[128,512]{1,0:T(8,128)} %trans.5, f32[1,512]{1,0:T(1,128)} %bitcast.1), custom_call_target="tpu_custom_call" | custom-call | tf_op jit(solution)/shard_map/pack/pallas_call | solution.py:279
  1.6 3.0 %collective-permute-start.3 = (f32[64,512]{1,0:T(8,128)S(1)}, f32[64,512]{1,0:T(8,128)S(1)}, u32[]{:S(2)}, u32[]{:S(2)}) collective-permute-start(f32[64,512]{1,0:T(8,128)S(1)} %get-tuple-element.33), channel_id=1, source_target_pairs={{0,2},{1,3},{2,0},{3,1},{4,6},{5,7},{6,4},{7,5},{8,10},{9,11},{10,... | collective-permute-start | bytes 393224 | tf_op jit(solution)/shard_map/ppermute | solution.py:273
  4.6 1.5 %near.1 = (f32[2,128,512]{2,1,0:T(8,128)S(1)}, f32[2,128,512]{2,1,0:T(8,128)S(1)}, f32[128,512]{1,0:T(8,128)S(1)}) custom-call(f32[4,128,512]{2,1,0:T(8,128)} %cov.5, f32[4,128,512]{2,1,0:T(8,128)} %prec.5, f32[128,512]{1,0:T(8,128)} %trans.5, f32[1,512]{1,0:T(1,128)S(1)} %get-tuple-element.29.after.first.refs_0_), custom_call_target="tpu_custom_call" | custom-call | tf_op jit(solution)/shard_map/near/pallas_call | solution.py:279
  6.2 0.5 collective-permute-start.1
  6.9 1.3 %collective-permute-done.3.refs_0_ = f32[64,512]{1,0:T(8,128)S(1)} collective-permute-done((f32[64,512]{1,0:T(8,128)S(1)}, f32[64,512]{1,0:T(8,128)S(1)}, u32[]{:S(2)}, u32[]{:S(2)}) %collective-permute-start.3) | collective-permute-done | bytes 131104 | tf_op jit(solution)/shard_map/ppermute | solution.py:273
  8.1 1.8 %collective-permute-start.4 = (f32[64,512]{1,0:T(8,128)S(1)}, f32[64,512]{1,0:T(8,128)S(1)}, u32[]{:S(2)}, u32[]{:S(2)}) collective-permute-start(f32[64,512]{1,0:T(8,128)S(1)} %collective-permute-done.3.refs_0_), channel_id=1, source_target_pairs={{0,4},{1,5},{2,6},{3,7},{4,0},{5,1},{6,2},{7,3},{8,12},{9,13},{10,... | collective-permute-start | bytes 393224 | tf_op jit(solution)/shard_map/ppermute | solution.py:273
  9.9 3.2 %collective-permute-done.4.refs_1_ = f32[64,512]{1,0:T(8,128)S(1)} collective-permute-done((f32[64,512]{1,0:T(8,128)S(1)}, f32[64,512]{1,0:T(8,128)S(1)}, u32[]{:S(2)}, u32[]{:S(2)}) %collective-permute-start.4) | collective-permute-done | bytes 131104 | tf_op jit(solution)/shard_map/ppermute | solution.py:273
  13.1 0.6 %join.1.joined = f32[1,128,512]{2,1,0:T(8,128)S(1)} custom-call(f32[64,512]{1,0:T(8,128)S(1)} %collective-permute-done.3.refs_0_, f32[64,512]{1,0:T(8,128)S(1)} %collective-permute-done.4.refs_1_), custom_call_target="tpu_custom_call" | custom-call | tf_op jit(solution)/shard_map/join/pallas_call | solution.py:279
  13.8 1.8 %collective-permute-start.7 = (f32[4,96,128]{2,1,0:T(8,128)S(1)}, f32[4,96,128]{2,1,0:T(8,128)S(1)}, u32[]{:S(2)}, u32[]{:S(2)}) collective-permute-start(f32[4,96,128]{2,1,0:T(8,128)S(1)} %get-tuple-element.41), channel_id=1, source_target_pairs={{0,3},{1,2},{2,1},{3,0},{4,7},{5,6},{6,5},{7,4},{8,11},{9,10},{10,... | collective-permute-start | bytes 589832 | tf_op jit(solution)/shard_map/ppermute | solution.py:273
  15.6 4.8 %early.1 = (f32[16,512]{1,0:T(8,128)S(1)}, bf16[2,512,256]{2,1,0:T(8,128)(2,1)S(1)}, bf16[2,2,256,512]{3,2,1,0:T(8,128)(2,1)S(1)}, f32[2,256,256]{2,1,0:T(8,128)...) custom-call(f32[4,128,512]{2,1,0:T(8,128)} %cov.5, f32[4,128,512]{2,1,0:T(8,128)} %prec.5, ...), custom_call_target="tpu_custom_call" | custom-call | tf_op jit(solution)/shard_map/early/pallas_call | solution.py:279
  20.4 3.0 %collective-permute-done.7.refs_1_ = f32[4,96,128]{2,1,0:T(8,128)S(1)} collective-permute-done((f32[4,96,128]{2,1,0:T(8,128)S(1)}, f32[4,96,128]{2,1,0:T(8,128)S(1)}, u32[]{:S(2)}, u32[]{:S(2)}) %collective-permute-start.7) | collective-permute-done | bytes 196640 | tf_op jit(solution)/shard_map/ppermute | solution.py:273
  23.5 2.5 %late.1 = (f32[512,512]{1,0:T(8,128)S(1)}, f32[512,512]{1,0:T(8,128)S(1)}, f32[1,512]{1,0:T(1,128)S(1)}) custom-call(f32[1,512]{1,0:T(1,128)S(1)} %get-tuple-element.29.after.first.refs_0_, f32[16,512]{1,0:T(8,128)S(1)} %get-tuple-element.34.info, bf16[2,512,256]{2,1,0:T(8,128)(2,1)S(1)} %get-tuple-element.35.a_far, ...), custom_call_target="tpu_custom_call" | custom-call | tf_op jit(solution)/shard_map/late/pallas_call | solution.py:279
  26.0 0.3 collective-permute-start.8
  26.3 1.0 %pair.1.late.refs_10_ = f32[520,512]{1,0:T(8,128)S(1)} custom-call(f32[16,512]{1,0:T(8,128)S(1)} %get-tuple-element.34.info, f32[512,512]{1,0:T(8,128)S(1)} %get-tuple-element.43.ga, f32[512,512]{1,0:T(8,128)S(1)} %get-tuple-element.48.gb.refs_11_), custom_call_target="tpu_custom_call" | custom-call | tf_op jit(solution)/shard_map/pair/pallas_call | solution.py:279
  27.7 0.3 two.1
  28.0 1.5 %collective-permute-start.9 = (f32[1,512]{1,0:T(1,128)S(1)}, f32[1,512]{1,0:T(1,128)S(1)}, u32[]{:S(2)}, u32[]{:S(2)}) collective-permute-start(f32[1,512]{1,0:T(1,128)S(1)} %two.1), channel_id=1, source_target_pairs={{0,5},{1,4},{2,7},{3,6},{4,1},{5,0},{6,3},{7,2},{8,13},{9,12},{10,... | collective-permute-start | bytes 6152 | tf_op jit(solution)/shard_map/ppermute | solution.py:273
  29.4 0.7 %collective-permute-done.10.early.refs_12_ = f32[520,512]{1,0:T(8,128)S(1)} collective-permute-done((f32[520,512]{1,0:T(8,128)S(1)}, f32[520,512]{1,0:T(8,128)S(1)}, u32[]{:S(2)}, u32[]{:S(2)}) %collective-permute-start.10) | collective-permute-done | bytes 1064992 | tf_op jit(solution)/shard_map/ppermute | solution.py:273
  30.1 1.0 %block.1 = (f32[512,512]{1,0:T(8,128)S(1)}, f32[8,512]{1,0:T(8,128)S(1)}) custom-call(f32[520,512]{1,0:T(8,128)S(1)} %pair.1.late.refs_10_, f32[520,512]{1,0:T(8,128)S(1)} %collective-permute-done.10.early.refs_12_), custom_call_target="tpu_custom_call" | custom-call | tf_op jit(solution)/shard_map/block/pallas_call | solution.py:279
  31.3 0.7 %collective-permute-start.11 = (f32[1,512]{1,0:T(1,128)S(1)}, f32[1,512]{1,0:T(1,128)S(1)}, u32[]{:S(2)}, u32[]{:S(2)}) collective-permute-start(f32[1,512]{1,0:T(1,128)S(1)} %hop.6), channel_id=1, source_target_pairs={{25,21}} | collective-permute-start | bytes 6152 | tf_op jit(solution)/shard_map/ppermute | solution.py:368
  32.0 0.3 collective-permute-start.17
  32.4 1.6 %collective-permute-start.12 = (f32[1,512]{1,0:T(1,128)S(1)}, f32[1,512]{1,0:T(1,128)S(1)}, u32[]{:S(2)}, u32[]{:S(2)}) collective-permute-start(f32[1,512]{1,0:T(1,128)S(1)} %hop.7), channel_id=1, source_target_pairs={{0,4},{1,5},{2,6},{3,7},{4,0},{5,1},{6,2},{7,3},{8,12},{9,13},{10,... | collective-permute-start | bytes 6152 | tf_op jit(solution)/shard_map/ppermute | solution.py:273
  34.0 2.1 %collective-permute-done.12.x.refs_3_ = f32[1,512]{1,0:T(1,128)S(1)} collective-permute-done((f32[1,512]{1,0:T(1,128)S(1)}, f32[1,512]{1,0:T(1,128)S(1)}, u32[]{:S(2)}, u32[]{:S(2)}) %collective-permute-start.12) | collective-permute-done | bytes 2080 | tf_op jit(solution)/shard_map/ppermute | solution.py:273
  36.2 0.7 %collective-permute-start.13 = (f32[1,512]{1,0:T(1,128)S(1)}, f32[1,512]{1,0:T(1,128)S(1)}, u32[]{:S(2)}, u32[]{:S(2)}) collective-permute-start(f32[1,512]{1,0:T(1,128)S(1)} %hop.8), channel_id=1, source_target_pairs={{17,13}} | collective-permute-start | bytes 6152 | tf_op jit(solution)/shard_map/ppermute | solution.py:368
  37.1 1.6 %collective-permute-start.14 = (f32[1,512]{1,0:T(1,128)S(1)}, f32[1,512]{1,0:T(1,128)S(1)}, u32[]{:S(2)}, u32[]{:S(2)}) collective-permute-start(f32[1,512]{1,0:T(1,128)S(1)} %hop.9), channel_id=1, source_target_pairs={{0,4},{1,5},{2,6},{3,7},{4,0},{5,1},{6,2},{7,3},{8,12},{9,13},{10,... | collective-permute-start | bytes 6152 | tf_op jit(solution)/shard_map/ppermute | solution.py:273
  38.6 2.1 %collective-permute-done.14.x.refs_5_ = f32[1,512]{1,0:T(1,128)S(1)} collective-permute-done((f32[1,512]{1,0:T(1,128)S(1)}, f32[1,512]{1,0:T(1,128)S(1)}, u32[]{:S(2)}, u32[]{:S(2)}) %collective-permute-start.14) | collective-permute-done | bytes 2080 | tf_op jit(solution)/shard_map/ppermute | solution.py:273
  40.9 0.7 %collective-permute-start.15 = (f32[1,512]{1,0:T(1,128)S(1)}, f32[1,512]{1,0:T(1,128)S(1)}, u32[]{:S(2)}, u32[]{:S(2)}) collective-permute-start(f32[1,512]{1,0:T(1,128)S(1)} %hop.10), channel_id=1, source_target_pairs={{9,5}} | collective-permute-start | bytes 6152 | tf_op jit(solution)/shard_map/ppermute | solution.py:368
  41.7 1.6 %collective-permute-start.16 = (f32[1,512]{1,0:T(1,128)S(1)}, f32[1,512]{1,0:T(1,128)S(1)}, u32[]{:S(2)}, u32[]{:S(2)}) collective-permute-start(f32[1,512]{1,0:T(1,128)S(1)} %hop.11), channel_id=1, source_target_pairs={{0,4},{1,5},{2,6},{3,7},{4,0},{5,1},{6,2},{7,3},{8,12},{9,13},{10,... | collective-permute-start | bytes 6152 | tf_op jit(solution)/shard_map/ppermute | solution.py:273
  43.3 2.1 %collective-permute-done.16.refs_7_ = f32[1,512]{1,0:T(1,128)S(1)} collective-permute-done((f32[1,512]{1,0:T(1,128)S(1)}, f32[1,512]{1,0:T(1,128)S(1)}, u32[]{:S(2)}, u32[]{:S(2)}) %collective-permute-start.16) | collective-permute-done | bytes 2080 | tf_op jit(solution)/shard_map/ppermute | solution.py:273
  45.4 0.4 last.1
  45.8 7.8 %collective-permute-start.19 = (f32[4,128]{1,0:T(4,128)S(1)}, f32[4,128]{1,0:T(4,128)S(1)}, u32[]{:S(2)}, u32[]{:S(2)}) collective-permute-start(f32[4,128]{1,0:T(4,128)S(1)} %get-tuple-element.51), channel_id=1, source_target_pairs={{0,2},{1,3},{2,0},{3,1},{4,6},{5,7},{6,4},{7,5},{8,10},{9,11},{10,... | collective-permute-start | bytes 6152 | tf_op jit(solution)/shard_map/ppermute | solution.py:273
  53.7 1.6 %collective-permute-done.19.refs_2_ = f32[4,128]{1,0:T(4,128)S(1)} collective-permute-done((f32[4,128]{1,0:T(4,128)S(1)}, f32[4,128]{1,0:T(4,128)S(1)}, u32[]{:S(2)}, u32[]{:S(2)}) %collective-permute-start.19) | collective-permute-done | bytes 2080 | tf_op jit(solution)/shard_map/ppermute | solution.py:273
  55.2 0.6 %out.1 = f32[4,128]{1,0:T(4,128)} custom-call(f32[4,128]{1,0:T(4,128)S(1)} %get-tuple-element.49.refs_0_, f32[4,128]{1,0:T(4,128)S(1)} %collective-permute-done.18.refs_1_, f32[4,128]{1,0:T(4,128)S(1)} %collective-permute-done.19.refs_2_, f32[4,128]{1,0:T(4,128)S(1)} %collective-permute-done.20.refs_3_), custom_call_target="tpu_custom_call" | custom-call | tf_op jit(solution)/shard_map/out/pallas_call | solution.py:279
  (26 shorter events, 1.6 us)
Async XLA Ops:
  1.6 6.5 %collective-permute-start.3 = (f32[64,512]{1,0:T(8,128)S(1)}, f32[64,512]{1,0:T(8,128)S(1)}, u32[]{:S(2)}, u32[]{:S(2)}) collective-permute-start(f32[64,512]{1,0:T(8,128)S(1)} %get-tuple-element.33), channel_id=1, source_target_pairs={{0,2},{1,3},{2,0},{3,1},{4,6},{5,7},{6,4},{7,5},{8,10},{9,11},{10,... | collective-permute-start | bytes 393224 | tf_op jit(solution)/shard_map/ppermute | solution.py:273
  6.2 9.5 %collective-permute-start = (f32[2,128,512]{2,1,0:T(8,128)S(1)}, f32[2,128,512]{2,1,0:T(8,128)S(1)}, u32[]{:S(2)}, u32[]{:S(2)}) collective-permute-start(f32[2,128,512]{2,1,0:T(8,128)S(1)} %get-tuple-element.30), channel_id=1, source_target_pairs={{0,1},{1,0},{2,3},{3,2},{4,5},{5,4},{6,7},{7,6},{8,9},{9,8},{10,11... | collective-permute-start | bytes 1572872 | tf_op jit(solution)/shard_map/ppermute | solution.py:273
  6.2 9.4 %collective-permute-start.1 = (f32[2,128,512]{2,1,0:T(8,128)S(1)}, f32[2,128,512]{2,1,0:T(8,128)S(1)}, u32[]{:S(2)}, u32[]{:S(2)}) collective-permute-start(f32[2,128,512]{2,1,0:T(8,128)S(1)} %get-tuple-element.31), channel_id=1, source_target_pairs={{0,1},{1,0},{2,3},{3,2},{4,5},{5,4},{6,7},{7,6},{8,9},{9,8},{10,11... | collective-permute-start | bytes 1572872 | tf_op jit(solution)/shard_map/ppermute | solution.py:273
  6.7 7.0 %collective-permute-start.2 = (f32[128,512]{1,0:T(8,128)S(1)}, f32[128,512]{1,0:T(8,128)S(1)}, u32[]{:S(2)}, u32[]{:S(2)}) collective-permute-start(f32[128,512]{1,0:T(8,128)S(1)} %get-tuple-element.32), channel_id=1, source_target_pairs={{0,1},{1,0},{2,3},{3,2},{4,5},{5,4},{6,7},{7,6},{8,9},{9,8},{10,11... | collective-permute-start | bytes 786440 | tf_op jit(solution)/shard_map/ppermute | solution.py:273
  6.8 16.6 %collective-permute-start.6 = (f32[4,224,128]{2,1,0:T(8,128)S(1)}, f32[4,224,128]{2,1,0:T(8,128)S(1)}, u32[]{:S(2)}, u32[]{:S(2)}) collective-permute-start(f32[4,224,128]{2,1,0:T(8,128)S(1)} %get-tuple-element.40), channel_id=1, source_target_pairs={{0,2},{1,3},{2,0},{3,1},{4,6},{5,7},{6,4},{7,5},{8,10},{9,11},{10,... | collective-permute-start | bytes 1376264 | tf_op jit(solution)/shard_map/ppermute | solution.py:273
  8.1 5.0 %collective-permute-start.4 = (f32[64,512]{1,0:T(8,128)S(1)}, f32[64,512]{1,0:T(8,128)S(1)}, u32[]{:S(2)}, u32[]{:S(2)}) collective-permute-start(f32[64,512]{1,0:T(8,128)S(1)} %collective-permute-done.3.refs_0_), channel_id=1, source_target_pairs={{0,4},{1,5},{2,6},{3,7},{4,0},{5,1},{6,2},{7,3},{8,12},{9,13},{10,... | collective-permute-start | bytes 393224 | tf_op jit(solution)/shard_map/ppermute | solution.py:273
  13.7 1.9 %collective-permute-start.5 = (f32[1,128,512]{2,1,0:T(8,128)S(1)}, f32[1,128,512]{2,1,0:T(8,128)S(1)}, u32[]{:S(2)}, u32[]{:S(2)}) collective-permute-start(f32[1,128,512]{2,1,0:T(8,128)S(1)} %join.1.joined), channel_id=1, source_target_pairs={{0,1},{1,0},{2,3},{3,2},{4,5},{5,4},{6,7},{7,6},{8,9},{9,8},{10,11... | collective-permute-start | bytes 786440 | tf_op jit(solution)/shard_map/ppermute | solution.py:273
  13.8 9.7 %collective-permute-start.7 = (f32[4,96,128]{2,1,0:T(8,128)S(1)}, f32[4,96,128]{2,1,0:T(8,128)S(1)}, u32[]{:S(2)}, u32[]{:S(2)}) collective-permute-start(f32[4,96,128]{2,1,0:T(8,128)S(1)} %get-tuple-element.41), channel_id=1, source_target_pairs={{0,3},{1,2},{2,1},{3,0},{4,7},{5,6},{6,5},{7,4},{8,11},{9,10},{10,... | collective-permute-start | bytes 589832 | tf_op jit(solution)/shard_map/ppermute | solution.py:273
  26.0 1.4 %collective-permute-start.8 = (f32[1,512]{1,0:T(1,128)S(1)}, f32[1,512]{1,0:T(1,128)S(1)}, u32[]{:S(2)}, u32[]{:S(2)}) collective-permute-start(f32[1,512]{1,0:T(1,128)S(1)} %get-tuple-element.42), channel_id=1, source_target_pairs={{0,1},{1,0},{2,3},{3,2},{4,5},{5,4},{6,7},{7,6},{8,9},{9,8},{10,11... | collective-permute-start | bytes 6152 | tf_op jit(solution)/shard_map/ppermute | solution.py:273
  27.4 2.7 %collective-permute-start.10 = (f32[520,512]{1,0:T(8,128)S(1)}, f32[520,512]{1,0:T(8,128)S(1)}, u32[]{:S(2)}, u32[]{:S(2)}) collective-permute-start(f32[520,512]{1,0:T(8,128)S(1)} %pair.1.late.refs_10_), channel_id=1, source_target_pairs={{0,1},{1,0},{2,3},{3,2},{4,5},{5,4},{6,7},{7,6},{8,9},{9,8},{10,11... | collective-permute-start | bytes 3194888 | tf_op jit(solution)/shard_map/ppermute | solution.py:273
  28.0 3.1 %collective-permute-start.9 = (f32[1,512]{1,0:T(1,128)S(1)}, f32[1,512]{1,0:T(1,128)S(1)}, u32[]{:S(2)}, u32[]{:S(2)}) collective-permute-start(f32[1,512]{1,0:T(1,128)S(1)} %two.1), channel_id=1, source_target_pairs={{0,5},{1,4},{2,7},{3,6},{4,1},{5,0},{6,3},{7,2},{8,13},{9,12},{10,... | collective-permute-start | bytes 6152 | tf_op jit(solution)/shard_map/ppermute | solution.py:273
  31.3 0.7 %collective-permute-start.11 = (f32[1,512]{1,0:T(1,128)S(1)}, f32[1,512]{1,0:T(1,128)S(1)}, u32[]{:S(2)}, u32[]{:S(2)}) collective-permute-start(f32[1,512]{1,0:T(1,128)S(1)} %hop.6), channel_id=1, source_target_pairs={{25,21}} | collective-permute-start | bytes 6152 | tf_op jit(solution)/shard_map/ppermute | solution.py:368
  32.0 13.4 %collective-permute-start.17 = (f32[512,512]{1,0:T(8,128)S(1)}, f32[512,512]{1,0:T(8,128)S(1)}, u32[]{:S(2)}, u32[]{:S(2)}) collective-permute-start(f32[512,512]{1,0:T(8,128)S(1)} %get-tuple-element.48.gb.refs_11_), channel_id=1, source_target_pairs={{0,1},{1,0},{2,3},{3,2},{4,5},{5,4},{6,7},{7,6},{8,9},{9,8},{10,11... | collective-permute-start | bytes 3145736 | tf_op jit(solution)/shard_map/ppermute | solution.py:273
  32.4 3.7 %collective-permute-start.12 = (f32[1,512]{1,0:T(1,128)S(1)}, f32[1,512]{1,0:T(1,128)S(1)}, u32[]{:S(2)}, u32[]{:S(2)}) collective-permute-start(f32[1,512]{1,0:T(1,128)S(1)} %hop.7), channel_id=1, source_target_pairs={{0,4},{1,5},{2,6},{3,7},{4,0},{5,1},{6,2},{7,3},{8,12},{9,13},{10,... | collective-permute-start | bytes 6152 | tf_op jit(solution)/shard_map/ppermute | solution.py:273
  36.2 0.7 %collective-permute-start.13 = (f32[1,512]{1,0:T(1,128)S(1)}, f32[1,512]{1,0:T(1,128)S(1)}, u32[]{:S(2)}, u32[]{:S(2)}) collective-permute-start(f32[1,512]{1,0:T(1,128)S(1)} %hop.8), channel_id=1, source_target_pairs={{17,13}} | collective-permute-start | bytes 6152 | tf_op jit(solution)/shard_map/ppermute | solution.py:368
  37.1 3.7 %collective-permute-start.14 = (f32[1,512]{1,0:T(1,128)S(1)}, f32[1,512]{1,0:T(1,128)S(1)}, u32[]{:S(2)}, u32[]{:S(2)}) collective-permute-start(f32[1,512]{1,0:T(1,128)S(1)} %hop.9), channel_id=1, source_target_pairs={{0,4},{1,5},{2,6},{3,7},{4,0},{5,1},{6,2},{7,3},{8,12},{9,13},{10,... | collective-permute-start | bytes 6152 | tf_op jit(solution)/shard_map/ppermute | solution.py:273
  40.9 0.7 %collective-permute-start.15 = (f32[1,512]{1,0:T(1,128)S(1)}, f32[1,512]{1,0:T(1,128)S(1)}, u32[]{:S(2)}, u32[]{:S(2)}) collective-permute-start(f32[1,512]{1,0:T(1,128)S(1)} %hop.10), channel_id=1, source_target_pairs={{9,5}} | collective-permute-start | bytes 6152 | tf_op jit(solution)/shard_map/ppermute | solution.py:368
  41.7 3.7 %collective-permute-start.16 = (f32[1,512]{1,0:T(1,128)S(1)}, f32[1,512]{1,0:T(1,128)S(1)}, u32[]{:S(2)}, u32[]{:S(2)}) collective-permute-start(f32[1,512]{1,0:T(1,128)S(1)} %hop.11), channel_id=1, source_target_pairs={{0,4},{1,5},{2,6},{3,7},{4,0},{5,1},{6,2},{7,3},{8,12},{9,13},{10,... | collective-permute-start | bytes 6152 | tf_op jit(solution)/shard_map/ppermute | solution.py:273
  45.8 7.9 %collective-permute-start.18 = (f32[4,128]{1,0:T(4,128)S(1)}, f32[4,128]{1,0:T(4,128)S(1)}, u32[]{:S(2)}, u32[]{:S(2)}) collective-permute-start(f32[4,128]{1,0:T(4,128)S(1)} %get-tuple-element.50), channel_id=1, source_target_pairs={{0,3},{1,2},{2,1},{3,0},{4,7},{5,6},{6,5},{7,4},{8,11},{9,10},{10,... | collective-permute-start | bytes 6152 | tf_op jit(solution)/shard_map/ppermute | solution.py:273
  45.8 9.4 %collective-permute-start.19 = (f32[4,128]{1,0:T(4,128)S(1)}, f32[4,128]{1,0:T(4,128)S(1)}, u32[]{:S(2)}, u32[]{:S(2)}) collective-permute-start(f32[4,128]{1,0:T(4,128)S(1)} %get-tuple-element.51), channel_id=1, source_target_pairs={{0,2},{1,3},{2,0},{3,1},{4,6},{5,7},{6,4},{7,5},{8,10},{9,11},{10,... | collective-permute-start | bytes 6152 | tf_op jit(solution)/shard_map/ppermute | solution.py:273
  53.6 1.6 %collective-permute-start.20 = (f32[4,128]{1,0:T(4,128)S(1)}, f32[4,128]{1,0:T(4,128)S(1)}, u32[]{:S(2)}, u32[]{:S(2)}) collective-permute-start(f32[4,128]{1,0:T(4,128)S(1)} %get-tuple-element.52), channel_id=1, source_target_pairs={{0,1},{1,0},{2,3},{3,2},{4,5},{5,4},{6,7},{7,6},{8,9},{9,8},{10,11... | collective-permute-start | bytes 6152 | tf_op jit(solution)/shard_map/ppermute | solution.py:273

commit v10 on v9

--- a/solution.py
+++ b/solution.py
@@ -21,8 +21,7 @@
 
 
 def dot3(a, b, dims):
-    ah, al = split(a)
-    bh, bl = split(b) if hasattr(b, "dtype") and b.dtype == F32 else (b[0][...], b[1][...])
+    (ah, al), (bh, bl) = (split(x) if getattr(x, "dtype", None) == F32 else (x[0][...], x[1][...]) for x in (a, b))
     dot = functools.partial(lax.dot_general, dimension_numbers=dims, preferred_element_type=F32)
     return dot(ah, bh) + (dot(ah, bl) + dot(al, bh))
 
@@ -114,7 +113,42 @@
         copy.wait()
 
 
-def join_kernel(*refs):
+def near_kernel(cov, prec, after, *refs):
+    pieces, sems = refs[:-1], refs[-1]
+    count, panel = cov.shape[0] // 2, cov.shape[1]
+    first = (1 - lax.axis_index("state") % 2) * count
+    start, copies = starter(sems)
+    for k in range(2 * count):
+        matrix = (cov, prec)[k // count]
+        for piece, at, source, size in spans(pieces, k, panel):
+            start(matrix.at[first + k % count, pl.ds(source, size), :], pieces[piece].at[pl.ds(at, size), :])
+    for copy in copies:
+        copy.wait()
+
+
+def spans(pieces, k, panel):
+    found, base = [], 0
+    for i, piece in enumerate(pieces):
+        low, high = max(base, k * panel), min(base + piece.shape[0], (k + 1) * panel)
+        if low < high:
+            found.append((i, low - base, low - k * panel, high - low))
+        base += piece.shape[0]
+    return found
+
+
+def own_kernel(cov, prec, trans, means, after, own, own_trans, own_means, sems):
+    count = cov.shape[0] // 2
+    mine = pl.ds((lax.axis_index("state") % 2) * count, count)
+    start, copies = starter(sems)
+    start(cov.at[mine], own.at[pl.ds(0, count)])
+    start(prec.at[mine], own.at[pl.ds(count, count)])
+    start(trans, own_trans)
+    start(means, own_means)
+    for copy in copies:
+        copy.wait()
+
+
+def join_kernel(after, *refs):
     moved, (joined, sems) = refs[:-2], refs[-2:]
     half = moved[0].shape[0]
     b = lax.axis_index("tm")
@@ -126,31 +160,30 @@
         copy.wait()
 
 
-def early_kernel(cov, prec, trans, means, near_cov, near_prec, near_trans, joined, joined_near, *refs):
-    info, a_far, l_known, c_known, c_far, g_known, pf, af, lf, sems = refs
-    steps, panel, order = cov.shape
-    count, known = steps // 2, 2 * panel
-    s = lax.axis_index("state")
-    e = s % 2
-    start, copies = starter(sems)
-    for k in range(count):
-        step = e * count + k
-        start(cov.at[step], pf.at[pl.ds(pl.multiple_of(k * known + e * panel, panel), panel), :])
-        start(near_cov.at[k], pf.at[pl.ds(pl.multiple_of(k * known + (1 - e) * panel, panel), panel), :])
-        start(prec.at[step], lf.at[k, rows(e, panel), :])
-        start(near_prec.at[k], lf.at[k, rows(1 - e, panel), :])
-    start(trans, af.at[rows(e, panel), :])
-    start(near_trans, af.at[rows(1 - e, panel), :])
-    for j in range(1, order // known):
-        start(joined.at[j - 1], af.at[rows(e ^ (2 * j), panel), :])
-        start(joined_near.at[j - 1], af.at[rows(e ^ (2 * j) ^ 1, panel), :])
+def early_kernel(own, means, trans, trans_near, joined, joined_near, *refs):
+    near, (info, a_far, l_known, c_known, c_far, g_known, pf, af, lf, sems) = refs[:-10], refs[-10:]
+    panel, order = own.shape[1:]
+    count, known = own.shape[0] // 2, 2 * panel
+    steps = means.shape[0]
+    e = lax.axis_index("state") % 2
+    start, copies = starter(sems)
+    for k in range(2 * count):
+        target, base = (pf, k * known) if k < count else (lf.at[k - count], 0)
+        start(own.at[k], target.at[pl.ds(pl.multiple_of(base + e * panel, panel), panel), :])
+        for piece, at, row, size in spans(near, k, panel):
+            to = pl.multiple_of(base + (1 - e) * panel + row, 8)
+            start(near[piece].at[pl.ds(at, size), :], target.at[pl.ds(to, size), :])
+    for j in range(order // known):
+        mine, theirs = (joined.at[j - 1], joined_near.at[j - 1]) if j else (trans, trans_near)
+        start(mine, af.at[rows(e ^ (2 * j), panel), :])
+        start(theirs, af.at[rows(e ^ (2 * j) ^ 1, panel), :])
     pf[count * known :, :] = jnp.concatenate([means[...], jnp.zeros((16 - steps, order), F32)], axis=0)
     for copy in copies:
         copy.wait()
     product = dot3(pf[...], af[...], NT)
     info[:8] = pf[count * known : count * known + 8, :]
     info[8:] = product[count * known : count * known + 8]
-    for half, x in enumerate(split(af[:, known:])):
+    for half, x in enumerate(split(af[:, known:].T)):
         a_far[half] = x
     across = jnp.concatenate([pf[k * known : (k + 1) * known, known:].T for k in range(count)], axis=0)
     rest = dot3(across, af[:, :known], NT)
@@ -170,37 +203,68 @@
     return [info[pl.ds(a + shift, 1), :] for shift in (0, 1, 8, 9)]
 
 
-def late_kernel(first, info, a_far, l_known, c_known, c_far, g_known, *refs):
-    far, (ga_ref, gb_ref, mean_ref, ff) = refs[:-4], refs[-4:]
+def far_row(j, panel):
+    return pl.ds(pl.multiple_of(j * panel, panel), panel)
+
+
+def middle_kernel(a_far, l_known, c_known, c_far, g_known, *refs):
+    far, (ga_ref, gb_ref, col_ref, h_ref, ff) = refs[:-5], refs[-5:]
     count, known, order = g_known.shape
     panel = known // 2
     e = lax.axis_index("state") % 2
+    i, j = e, 1 - e
     for k in range(2 * count):
-        if not trimmed(len(far) + 2, panel):
+        if len(far) > 1:
             for off, piece in enumerate(far, 2):
                 ff[k, rows((e ^ off) - 2, panel), :] = piece[k]
             continue
-        i, j = (e ^ 2) - 2, (e ^ 3) - 2
         beside, folded = far[0][k, :panel], far[0][k, panel:]
         ff[k, rows(i, panel), rows(i, panel)] = unfold(folded)
-        ff[k, rows(j, panel), rows(j, panel)] = unfold(far[1][k])
+        ff[k, rows(j, panel), rows(j, panel)] = jnp.zeros((panel, panel), F32)
         ff[k, rows(i, panel), rows(j, panel)] = beside
         ff[k, rows(j, panel), rows(i, panel)] = beside.T
 
-    def complete(k):
-        c = c_far[k] + dot3(ff[k], a_far, NT)
+    for k, out in enumerate((ga_ref, gb_ref)):
+        c = c_far[k] + dot3(ff[k], a_far, NN)
         known_rows = (l_known.at[k, 0], l_known.at[k, 1])
-        share = dot3(jnp.concatenate([c_known[k], c[:, known:]], axis=0), ff[count + k], NN)
+        known_far = [x[:, known:] for x in known_rows]
+        l_far = split(ff[count + k])
+        column = jnp.concatenate([c_known[k], c[:, known:]], axis=0)
+        share = dot3(column, l_far, NN)
         low = dot3(c[:, :known], known_rows, NN)
-        left = low[:, :known] + dot3(c[:, known:], [x[:, known:] for x in known_rows], NT)
-        top = jnp.concatenate([g_known[k, :, :known], g_known[k, :, known:] + share[:known]], axis=1)
-        return jnp.concatenate([top, jnp.concatenate([left, low[:, known:] + share[known:]], axis=1)], axis=0)
-
-    ga, gb = complete(0), complete(1)
-    ga_ref[...] = ga
-    gb_ref[...] = gb
+        out[:known, :known] = g_known[k, :, :known]
+        out[:known, known:] = g_known[k, :, known:] + share[:known]
+        out[known:, :known] = low[:, :known] + dot3(c[:, known:], known_far, NT)
+        out[known:, known:] = low[:, known:] + share[known:]
+        if len(far) == 1:
+            col_ref[k] = jnp.where(j == 0, column[:, :panel], column[:, panel:])
+            halves = a_far[0, far_row(j, panel), :], a_far[1, far_row(j, panel), :]
+            head, tail = [x[:, :known] for x in halves], [x[:, known:] for x in halves]
+            h = dot3(head, known_rows, NN)
+            h_ref[k, :, :known] = h[:, :known] + dot3(tail, known_far, NT)
+            h_ref[k, :, known:] = h[:, known:] + dot3(tail, l_far, NN)
+
+
+def steps_of(info, count):
+    a = (lax.axis_index("state") % 2) * count
+    return [info[pl.ds(a + shift, 1), :] for shift in (0, 1, 8, 9)]
+
+
+def late_kernel(first, info, a_far, ga, gb, col, h, *refs):
+    far, (ga_ref, gb_ref, mean_ref) = refs[:-3], refs[-3:]
+    count, panel, order = h.shape
+    j = 1 - lax.axis_index("state") % 2
+    for k, (gain, out) in enumerate(((ga, ga_ref), (gb, gb_ref))):
+        out[...] = gain[...]
+        if far:
+            at = far_row(2 + j, panel)
+            p_last, l_last = unfold(far[0][k]), unfold(far[0][count + k])
+            corner = [a_far[half, far_row(j, panel), at] for half in range(2)]
+            out[at, :] += dot3(p_last, h[k], NN)
+            out[:, at] += dot3(col[k], l_last, NN)
+            out[at, at] += dot3(dot3(p_last, corner, NN), l_last, NN)
     mean_a, mean_b, pred_a, pred_b = steps_of(info, count)
-    mean_ref[...] = mean_a + matvec(ga, mean_b + matvec(gb, first[...] - pred_b) - pred_a)
+    mean_ref[...] = mean_a + matvec(ga_ref[...], mean_b + matvec(gb_ref[...], first[...] - pred_b) - pred_a)
 
 
 def two_kernel(x, info, ga, gb, out_ref):
@@ -305,21 +369,37 @@
     )
     across = [swap(trans_half, off) for off in range(2, devices, 2)]
     far = [swap(x, off) for off, x in enumerate(far, 2)]
+    moved = [y for x in across for y in (x, swap(x, 0, 1))]
     near = call(
         near_kernel,
         "near",
         4,
-        [shape(count, panel, order), shape(count, panel, order), shape(panel, order)],
-        [HBM] * 3 + [ANY],
+        [shape(count * panel, order)] * 2,
+        [HBM] * 2 + [ANY],
         [semaphores],
-        (cov, prec, trans, first),
+        (cov, prec, first),
     )
     near = [swap(x, 1) for x in near]
-    moved = [y for x in across for y in (x, swap(x, 0, 1))]
+    own, own_trans, own_means = call(
+        own_kernel,
+        "own",
+        4,
+        [shape(2 * count, panel, order), shape(panel, order), shape(steps, order)],
+        [HBM] * 4 + [ANY],
+        [semaphores],
+        (cov, prec, trans, means, across[0]),
+    )
     (joined,) = call(
-        join_kernel, "join", 4, [shape(devices // 2 - 1, panel, order)], [ANY] * len(moved), [semaphores], moved
+        join_kernel,
+        "join",
+        4,
+        [shape(devices // 2 - 1, panel, order)],
+        [ANY] * (1 + len(moved)),
+        [semaphores],
+        (own_trans, *moved),
     )
     joined_near = swap(joined, 1)
+    trans_near = swap(transition, 1)
 
     known = 2 * panel
     parts = call(
@@ -328,30 +408,40 @@
         24,
         [
             shape(16, order),
-            jax.ShapeDtypeStruct((2, order, order - known), BF16),
+            jax.ShapeDtypeStruct((2, order - known, order), BF16),
             jax.ShapeDtypeStruct((count, 2, known, order), BF16),
             shape(count, known, order - known),
             shape(count, order - known, order),
             shape(count, known, order),
         ],
-        [HBM] * 3 + [VMEM] + [ANY] * 5,
+        [ANY, VMEM] + [ANY] * 2 + [ANY] * 4,
         [
             pltpu.VMEM((count * known + 16, order), F32),
             pltpu.VMEM((order, order), F32),
             pltpu.VMEM((count, known, order), F32),
             semaphores,
         ],
-        (cov, prec, trans, means, *near, joined, joined_near),
-    )
-    info = parts[0]
+        (own, own_means, own_trans, trans_near, joined, joined_near, *near),
+    )
+    info, a_far = parts[:2]
+    last = far[1:] if trimmed(devices, panel) else []
+    ga, gb, col, h = call(
+        middle_kernel,
+        "middle",
+        24,
+        [square, square, shape(count, order, panel), shape(count, panel, order)],
+        [VMEM] * (5 + len(far) - len(last)),
+        [pltpu.VMEM((2 * count, order - known, order - known), F32)],
+        (*parts[1:], *far[: len(far) - len(last)]),
+    )
     ga, gb, mean = call(
         late_kernel,
         "late",
-        24,
+        12,
         [square, square, shape(1, order)],
-        [VMEM] * (7 + len(far)),
-        [pltpu.VMEM((2 * count, order - known, order - known), F32)],
-        (first, *parts, *far),
+        [VMEM] * (7 + len(last)),
+        [],
+        (first, info, a_far, ga, gb, col, h, *last),
     )
     mean = swap(mean, 1)
     (late_map,) = call(pair_kernel, "pair", 12, [shape(order + 8, order)], [VMEM] * 3, [], (info, ga, gb))

time: 56.1 us -> 54.3 us (0.968)
  waiting for transfers between devices: 16 us -> 12.8 us
  Pallas kernels: 15.2 us -> 16.2 us
    ppermute x18, waiting for transfers between devices: 16 us -> 12.8 us  [swap(): return lax.ppermute(x, ('tm', 'state'), pairs)]
    pallas_call x16 -> x18, Pallas kernels: 15.2 us -> 16.2 us  [call(): pl.pallas_call(kernel, out_shape=outs, in_specs=in_specs, out_specs=[VMEM...]
  transfers between devices with their start and end apart: 21 -> 21, of which waited for: 8 -> 8; matrix products, arithmetic and copies ran while one was open for 0% -> 0% of each run, Pallas kernels for 18% -> 22%
where the time goes in v10:
time: 54.3 us; the launch traced here: 54 us
  starting transfers between devices  24.9 us (46%)
  Pallas kernels  16.2 us (30%)
  waiting for transfers between devices  12.8 us (24%)
    ppermute x18, starting transfers between devices, swap(): return lax.ppermute(x, ('tm', 'state'), pairs)  22.9 us
    pallas_call x18, Pallas kernels, call(): pl.pallas_call(kernel, out_shape=outs, in_specs=in_specs, out_specs=[VMEM...  16.2 us
    ppermute x18, waiting for transfers between devices, swap(): return lax.ppermute(x, ('tm', 'state'), pairs)  12.8 us
    ppermute x3, starting transfers between devices, local(): lax.ppermute(x, ('tm', 'state'), [(block * devices + 1, (block - 1) * dev...  1.98 us
  transfers between devices with their start and end apart: 21, of which 8 were waited for; matrix products, arithmetic and copies ran while one was open for 0% of the time, Pallas kernels for 22%

profile of v10, /device:TPU:0, one launch (start us, length us, event | category | flops | bytes accessed | tf_op | source)
XLA Modules:
  0.0 54.0 jit_solution(8234355354711125769)
XLA Ops:
  0.0 1.6 %pack.1 = (f32[4,224,128]{2,1,0:T(8,128)S(1)}, f32[4,96,128]{2,1,0:T(8,128)S(1)}, f32[64,512]{1,0:T(8,128)S(1)}, f32[1,512]{1,0:T(1,128)S(1)}) custom-call(f32[4,128,512]{2,1,0:T(8,128)} %cov.5, f32[4,128,512]{2,1,0:T(8,128)} %prec.5, f32[128,512]{1,0:T(8,128)} %trans.3, f32[1,512]{1,0:T(1,128)} %bitcast.1), custom_call_target="tpu_custom_call" | custom-call | tf_op jit(solution)/shard_map/pack/pallas_call | solution.py:343
  1.6 3.0 %collective-permute-start = (f32[64,512]{1,0:T(8,128)S(1)}, f32[64,512]{1,0:T(8,128)S(1)}, u32[]{:S(2)}, u32[]{:S(2)}) collective-permute-start(f32[64,512]{1,0:T(8,128)S(1)} %get-tuple-element.36), channel_id=1, source_target_pairs={{0,2},{1,3},{2,0},{3,1},{4,6},{5,7},{6,4},{7,5},{8,10},{9,11},{10,... | collective-permute-start | bytes 393224 | tf_op jit(solution)/shard_map/ppermute | solution.py:337
  4.6 1.5 %near.1 = (f32[256,512]{1,0:T(8,128)S(1)}, f32[256,512]{1,0:T(8,128)S(1)}) custom-call(f32[4,128,512]{2,1,0:T(8,128)} %cov.5, f32[4,128,512]{2,1,0:T(8,128)} %prec.5, f32[1,512]{1,0:T(1,128)S(1)} %get-tuple-element.35.after.first.refs_0_), custom_call_target="tpu_custom_call" | custom-call | tf_op jit(solution)/shard_map/near/pallas_call | solution.py:343
  6.2 0.5 collective-permute-start.5
  6.8 1.4 %collective-permute-done.after.refs_0_ = f32[64,512]{1,0:T(8,128)S(1)} collective-permute-done((f32[64,512]{1,0:T(8,128)S(1)}, f32[64,512]{1,0:T(8,128)S(1)}, u32[]{:S(2)}, u32[]{:S(2)}) %collective-permute-start) | collective-permute-done | bytes 131104 | tf_op jit(solution)/shard_map/ppermute | solution.py:337
  8.1 1.8 %collective-permute-start.2 = (f32[64,512]{1,0:T(8,128)S(1)}, f32[64,512]{1,0:T(8,128)S(1)}, u32[]{:S(2)}, u32[]{:S(2)}) collective-permute-start(f32[64,512]{1,0:T(8,128)S(1)} %collective-permute-done.after.refs_0_), channel_id=1, source_target_pairs={{0,4},{1,5},{2,6},{3,7},{4,0},{5,1},{6,2},{7,3},{8,12},{9,13},{10,... | collective-permute-start | bytes 393224 | tf_op jit(solution)/shard_map/ppermute | solution.py:337
  9.9 1.6 %own.1 = (f32[4,128,512]{2,1,0:T(8,128)S(1)}, f32[128,512]{1,0:T(8,128)S(1)}, f32[4,512]{1,0:T(4,128)S(1)}) custom-call(f32[4,128,512]{2,1,0:T(8,128)} %cov.5, f32[4,128,512]{2,1,0:T(8,128)} %prec.5, f32[128,512]{1,0:T(8,128)} %trans.3, f32[4,512]{1,0:T(4,128)} %means.1, f32[64,512]{1,0:T(8,128)S(1)} %collective-permute-done.after.refs_0_), custom_call_target="tpu_custom_call" | custom-call | tf_op jit(solution)/shard_map/own/pallas_call | solution.py:343
  11.4 1.6 %collective-permute-done.2.refs_1_ = f32[64,512]{1,0:T(8,128)S(1)} collective-permute-done((f32[64,512]{1,0:T(8,128)S(1)}, f32[64,512]{1,0:T(8,128)S(1)}, u32[]{:S(2)}, u32[]{:S(2)}) %collective-permute-start.2) | collective-permute-done | bytes 131104 | tf_op jit(solution)/shard_map/ppermute | solution.py:337
  13.1 0.6 %join.1.joined = f32[1,128,512]{2,1,0:T(8,128)S(1)} custom-call(f32[128,512]{1,0:T(8,128)S(1)} %get-tuple-element.39.after.trans, f32[64,512]{1,0:T(8,128)S(1)} %collective-permute-done.after.refs_0_, f32[64,512]{1,0:T(8,128)S(1)} %collective-permute-done.2.refs_1_), custom_call_target="tpu_custom_call" | custom-call | tf_op jit(solution)/shard_map/join/pallas_call | solution.py:343
  13.8 2.0 %collective-permute-start.7 = (f32[4,96,128]{2,1,0:T(8,128)S(1)}, f32[4,96,128]{2,1,0:T(8,128)S(1)}, u32[]{:S(2)}, u32[]{:S(2)}) collective-permute-start(f32[4,96,128]{2,1,0:T(8,128)S(1)} %get-tuple-element.53), channel_id=1, source_target_pairs={{0,3},{1,2},{2,1},{3,0},{4,7},{5,6},{6,5},{7,4},{8,11},{9,10},{10,... | collective-permute-start | bytes 589832 | tf_op jit(solution)/shard_map/ppermute | solution.py:337
  15.8 2.9 %early.1 = (f32[16,512]{1,0:T(8,128)S(1)}, bf16[2,256,512]{2,1,0:T(8,128)(2,1)S(1)}, bf16[2,2,256,512]{3,2,1,0:T(8,128)(2,1)S(1)}, f32[2,256,256]{2,1,0:T(8,128)...) custom-call(f32[4,128,512]{2,1,0:T(8,128)S(1)} %get-tuple-element.37.own, ...), custom_call_target="tpu_custom_call" | custom-call | tf_op jit(solution)/shard_map/early/pallas_call | solution.py:343
  18.7 1.3 %collective-permute-done.6.refs_0_ = f32[4,224,128]{2,1,0:T(8,128)S(1)} collective-permute-done((f32[4,224,128]{2,1,0:T(8,128)S(1)}, f32[4,224,128]{2,1,0:T(8,128)S(1)}, u32[]{:S(2)}, u32[]{:S(2)}) %collective-permute-start.6) | collective-permute-done | bytes 458784 | tf_op jit(solution)/shard_map/ppermute | solution.py:337
  20.1 2.5 %middle.1 = (f32[512,512]{1,0:T(8,128)S(1)}, f32[512,512]{1,0:T(8,128)S(1)}, f32[2,512,128]{2,1,0:T(8,128)S(1)}, f32[2,128,512]{2,1,0:T(8,128)S(1)}) custom-call(bf16[2,256,512]{2,1,0:T(8,128)(2,1)S(1)} %get-tuple-element.43.a_far, bf16[2,2,256,512]{3,2,1,0:T(8,128)(2,1)S(1)} %get-tuple-element.44.l_known, f32[2,256,256]{2,1,0:T(8,128)S(1)} %get-tuple-element.45.c_known, ...), custom_call_target="tpu_custom_call" | custom-call | tf_op jit(solution)/shard_map/middle/pallas_call | solution.py:343
  22.6 1.3 %late.1 = (f32[512,512]{1,0:T(8,128)S(1)}, f32[512,512]{1,0:T(8,128)S(1)}, f32[1,512]{1,0:T(1,128)S(1)}) custom-call(f32[1,512]{1,0:T(1,128)S(1)} %get-tuple-element.35.after.first.refs_0_, f32[16,512]{1,0:T(8,128)S(1)} %get-tuple-element.42.info, bf16[2,256,512]{2,1,0:T(8,128)(2,1)S(1)} %get-tuple-element.43.a_far, f32[512,512]{1,0:T(8,128)S(1)} %get-tuple-element.49.ga, ...), custom_call_target="tpu_custom_call" | custom-call | tf_op jit(solution)/shard_map/late/pallas_call | solution.py:343
  23.9 0.7 %collective-permute-start.8 = (f32[1,512]{1,0:T(1,128)S(1)}, f32[1,512]{1,0:T(1,128)S(1)}, u32[]{:S(2)}, u32[]{:S(2)}) collective-permute-start(f32[1,512]{1,0:T(1,128)S(1)} %get-tuple-element.54), channel_id=1, source_target_pairs={{0,1},{1,0},{2,3},{3,2},{4,5},{5,4},{6,7},{7,6},{8,9},{9,8},{10,11... | collective-permute-start | bytes 6152 | tf_op jit(solution)/shard_map/ppermute | solution.py:337
  24.6 1.0 %pair.1.late.refs_10_ = f32[520,512]{1,0:T(8,128)S(1)} custom-call(f32[16,512]{1,0:T(8,128)S(1)} %get-tuple-element.42.info, f32[512,512]{1,0:T(8,128)S(1)} %get-tuple-element.55.ga, f32[512,512]{1,0:T(8,128)S(1)} %get-tuple-element.60.gb.refs_11_), custom_call_target="tpu_custom_call" | custom-call | tf_op jit(solution)/shard_map/pair/pallas_call | solution.py:343
  26.1 1.6 %collective-permute-start.9 = (f32[1,512]{1,0:T(1,128)S(1)}, f32[1,512]{1,0:T(1,128)S(1)}, u32[]{:S(2)}, u32[]{:S(2)}) collective-permute-start(f32[1,512]{1,0:T(1,128)S(1)} %two.1), channel_id=1, source_target_pairs={{0,5},{1,4},{2,7},{3,6},{4,1},{5,0},{6,3},{7,2},{8,13},{9,12},{10,... | collective-permute-start | bytes 6152 | tf_op jit(solution)/shard_map/ppermute | solution.py:337
  27.7 0.7 %collective-permute-done.10.early.refs_12_ = f32[520,512]{1,0:T(8,128)S(1)} collective-permute-done((f32[520,512]{1,0:T(8,128)S(1)}, f32[520,512]{1,0:T(8,128)S(1)}, u32[]{:S(2)}, u32[]{:S(2)}) %collective-permute-start.10) | collective-permute-done | bytes 1064992 | tf_op jit(solution)/shard_map/ppermute | solution.py:337
  28.4 1.0 %block.1 = (f32[512,512]{1,0:T(8,128)S(1)}, f32[8,512]{1,0:T(8,128)S(1)}) custom-call(f32[520,512]{1,0:T(8,128)S(1)} %pair.1.late.refs_10_, f32[520,512]{1,0:T(8,128)S(1)} %collective-permute-done.10.early.refs_12_), custom_call_target="tpu_custom_call" | custom-call | tf_op jit(solution)/shard_map/block/pallas_call | solution.py:343
  29.6 0.7 %collective-permute-start.11 = (f32[1,512]{1,0:T(1,128)S(1)}, f32[1,512]{1,0:T(1,128)S(1)}, u32[]{:S(2)}, u32[]{:S(2)}) collective-permute-start(f32[1,512]{1,0:T(1,128)S(1)} %hop.6), channel_id=1, source_target_pairs={{25,21}} | collective-permute-start | bytes 6152 | tf_op jit(solution)/shard_map/ppermute | solution.py:458
  30.6 1.6 %collective-permute-start.12 = (f32[1,512]{1,0:T(1,128)S(1)}, f32[1,512]{1,0:T(1,128)S(1)}, u32[]{:S(2)}, u32[]{:S(2)}) collective-permute-start(f32[1,512]{1,0:T(1,128)S(1)} %hop.7), channel_id=1, source_target_pairs={{0,4},{1,5},{2,6},{3,7},{4,0},{5,1},{6,2},{7,3},{8,12},{9,13},{10,... | collective-permute-start | bytes 6152 | tf_op jit(solution)/shard_map/ppermute | solution.py:337
  32.2 2.1 %collective-permute-done.12.x.refs_3_ = f32[1,512]{1,0:T(1,128)S(1)} collective-permute-done((f32[1,512]{1,0:T(1,128)S(1)}, f32[1,512]{1,0:T(1,128)S(1)}, u32[]{:S(2)}, u32[]{:S(2)}) %collective-permute-start.12) | collective-permute-done | bytes 2080 | tf_op jit(solution)/shard_map/ppermute | solution.py:337
  34.4 0.7 %collective-permute-start.13 = (f32[1,512]{1,0:T(1,128)S(1)}, f32[1,512]{1,0:T(1,128)S(1)}, u32[]{:S(2)}, u32[]{:S(2)}) collective-permute-start(f32[1,512]{1,0:T(1,128)S(1)} %hop.8), channel_id=1, source_target_pairs={{17,13}} | collective-permute-start | bytes 6152 | tf_op jit(solution)/shard_map/ppermute | solution.py:458
  35.3 1.6 %collective-permute-start.14 = (f32[1,512]{1,0:T(1,128)S(1)}, f32[1,512]{1,0:T(1,128)S(1)}, u32[]{:S(2)}, u32[]{:S(2)}) collective-permute-start(f32[1,512]{1,0:T(1,128)S(1)} %hop.9), channel_id=1, source_target_pairs={{0,4},{1,5},{2,6},{3,7},{4,0},{5,1},{6,2},{7,3},{8,12},{9,13},{10,... | collective-permute-start | bytes 6152 | tf_op jit(solution)/shard_map/ppermute | solution.py:337
  36.9 2.1 %collective-permute-done.14.x.refs_5_ = f32[1,512]{1,0:T(1,128)S(1)} collective-permute-done((f32[1,512]{1,0:T(1,128)S(1)}, f32[1,512]{1,0:T(1,128)S(1)}, u32[]{:S(2)}, u32[]{:S(2)}) %collective-permute-start.14) | collective-permute-done | bytes 2080 | tf_op jit(solution)/shard_map/ppermute | solution.py:337
  39.1 0.7 %collective-permute-start.15 = (f32[1,512]{1,0:T(1,128)S(1)}, f32[1,512]{1,0:T(1,128)S(1)}, u32[]{:S(2)}, u32[]{:S(2)}) collective-permute-start(f32[1,512]{1,0:T(1,128)S(1)} %hop.10), channel_id=1, source_target_pairs={{9,5}} | collective-permute-start | bytes 6152 | tf_op jit(solution)/shard_map/ppermute | solution.py:458
  39.9 1.6 %collective-permute-start.16 = (f32[1,512]{1,0:T(1,128)S(1)}, f32[1,512]{1,0:T(1,128)S(1)}, u32[]{:S(2)}, u32[]{:S(2)}) collective-permute-start(f32[1,512]{1,0:T(1,128)S(1)} %hop.11), channel_id=1, source_target_pairs={{0,4},{1,5},{2,6},{3,7},{4,0},{5,1},{6,2},{7,3},{8,12},{9,13},{10,... | collective-permute-start | bytes 6152 | tf_op jit(solution)/shard_map/ppermute | solution.py:337
  41.5 2.1 %collective-permute-done.16.refs_7_ = f32[1,512]{1,0:T(1,128)S(1)} collective-permute-done((f32[1,512]{1,0:T(1,128)S(1)}, f32[1,512]{1,0:T(1,128)S(1)}, u32[]{:S(2)}, u32[]{:S(2)}) %collective-permute-start.16) | collective-permute-done | bytes 2080 | tf_op jit(solution)/shard_map/ppermute | solution.py:337
  43.6 0.4 last.1
  44.1 7.8 %collective-permute-start.19 = (f32[4,128]{1,0:T(4,128)S(1)}, f32[4,128]{1,0:T(4,128)S(1)}, u32[]{:S(2)}, u32[]{:S(2)}) collective-permute-start(f32[4,128]{1,0:T(4,128)S(1)} %get-tuple-element.63), channel_id=1, source_target_pairs={{0,2},{1,3},{2,0},{3,1},{4,6},{5,7},{6,4},{7,5},{8,10},{9,11},{10,... | collective-permute-start | bytes 6152 | tf_op jit(solution)/shard_map/ppermute | solution.py:337
  51.9 1.6 %collective-permute-done.19.refs_2_ = f32[4,128]{1,0:T(4,128)S(1)} collective-permute-done((f32[4,128]{1,0:T(4,128)S(1)}, f32[4,128]{1,0:T(4,128)S(1)}, u32[]{:S(2)}, u32[]{:S(2)}) %collective-permute-start.19) | collective-permute-done | bytes 2080 | tf_op jit(solution)/shard_map/ppermute | solution.py:337
  53.5 0.6 %out.1 = f32[4,128]{1,0:T(4,128)} custom-call(f32[4,128]{1,0:T(4,128)S(1)} %get-tuple-element.61.refs_0_, f32[4,128]{1,0:T(4,128)S(1)} %collective-permute-done.18.refs_1_, f32[4,128]{1,0:T(4,128)S(1)} %collective-permute-done.19.refs_2_, f32[4,128]{1,0:T(4,128)S(1)} %collective-permute-done.20.refs_3_), custom_call_target="tpu_custom_call" | custom-call | tf_op jit(solution)/shard_map/out/pallas_call | solution.py:343
  (30 shorter events, 1.9 us)
Async XLA Ops:
  1.6 5.1 %copy-start = (f32[128,512]{1,0:T(8,128)S(1)}, f32[128,512]{1,0:T(8,128)}, u32[]{:S(2)}) copy-start(f32[128,512]{1,0:T(8,128)} %trans.3) | copy-start | bytes 786436
  1.6 6.5 %collective-permute-start = (f32[64,512]{1,0:T(8,128)S(1)}, f32[64,512]{1,0:T(8,128)S(1)}, u32[]{:S(2)}, u32[]{:S(2)}) collective-permute-start(f32[64,512]{1,0:T(8,128)S(1)} %get-tuple-element.36), channel_id=1, source_target_pairs={{0,2},{1,3},{2,0},{3,1},{4,6},{5,7},{6,4},{7,5},{8,10},{9,11},{10,... | collective-permute-start | bytes 393224 | tf_op jit(solution)/shard_map/ppermute | solution.py:337
  6.1 9.7 %collective-permute-start.4 = (f32[256,512]{1,0:T(8,128)S(1)}, f32[256,512]{1,0:T(8,128)S(1)}, u32[]{:S(2)}, u32[]{:S(2)}) collective-permute-start(f32[256,512]{1,0:T(8,128)S(1)} %get-tuple-element.40), channel_id=1, source_target_pairs={{0,1},{1,0},{2,3},{3,2},{4,5},{5,4},{6,7},{7,6},{8,9},{9,8},{10,11... | collective-permute-start | bytes 1572872 | tf_op jit(solution)/shard_map/ppermute | solution.py:337
  6.2 9.6 %collective-permute-start.5 = (f32[256,512]{1,0:T(8,128)S(1)}, f32[256,512]{1,0:T(8,128)S(1)}, u32[]{:S(2)}, u32[]{:S(2)}) collective-permute-start(f32[256,512]{1,0:T(8,128)S(1)} %get-tuple-element.41), channel_id=1, source_target_pairs={{0,1},{1,0},{2,3},{3,2},{4,5},{5,4},{6,7},{7,6},{8,9},{9,8},{10,11... | collective-permute-start | bytes 1572872 | tf_op jit(solution)/shard_map/ppermute | solution.py:337
  6.7 13.4 %collective-permute-start.6 = (f32[4,224,128]{2,1,0:T(8,128)S(1)}, f32[4,224,128]{2,1,0:T(8,128)S(1)}, u32[]{:S(2)}, u32[]{:S(2)}) collective-permute-start(f32[4,224,128]{2,1,0:T(8,128)S(1)} %get-tuple-element.48), channel_id=1, source_target_pairs={{0,2},{1,3},{2,0},{3,1},{4,6},{5,7},{6,4},{7,5},{8,10},{9,11},{10,... | collective-permute-start | bytes 1376264 | tf_op jit(solution)/shard_map/ppermute | solution.py:337
  6.7 7.1 %collective-permute-start.1 = (f32[128,512]{1,0:T(8,128)S(1)}, f32[128,512]{1,0:T(8,128)S(1)}, u32[]{:S(2)}, u32[]{:S(2)}) collective-permute-start(f32[128,512]{1,0:T(8,128)S(1)} %copy-done), channel_id=1, source_target_pairs={{0,1},{1,0},{2,3},{3,2},{4,5},{5,4},{6,7},{7,6},{8,9},{9,8},{10,11... | collective-permute-start | bytes 786440 | tf_op jit(solution)/shard_map/ppermute | solution.py:337
  8.1 5.0 %collective-permute-start.2 = (f32[64,512]{1,0:T(8,128)S(1)}, f32[64,512]{1,0:T(8,128)S(1)}, u32[]{:S(2)}, u32[]{:S(2)}) collective-permute-start(f32[64,512]{1,0:T(8,128)S(1)} %collective-permute-done.after.refs_0_), channel_id=1, source_target_pairs={{0,4},{1,5},{2,6},{3,7},{4,0},{5,1},{6,2},{7,3},{8,12},{9,13},{10,... | collective-permute-start | bytes 393224 | tf_op jit(solution)/shard_map/ppermute | solution.py:337
  13.7 2.1 %collective-permute-start.3 = (f32[1,128,512]{2,1,0:T(8,128)S(1)}, f32[1,128,512]{2,1,0:T(8,128)S(1)}, u32[]{:S(2)}, u32[]{:S(2)}) collective-permute-start(f32[1,128,512]{2,1,0:T(8,128)S(1)} %join.1.joined), channel_id=1, source_target_pairs={{0,1},{1,0},{2,3},{3,2},{4,5},{5,4},{6,7},{7,6},{8,9},{9,8},{10,11... | collective-permute-start | bytes 786440 | tf_op jit(solution)/shard_map/ppermute | solution.py:337
  13.8 8.8 %collective-permute-start.7 = (f32[4,96,128]{2,1,0:T(8,128)S(1)}, f32[4,96,128]{2,1,0:T(8,128)S(1)}, u32[]{:S(2)}, u32[]{:S(2)}) collective-permute-start(f32[4,96,128]{2,1,0:T(8,128)S(1)} %get-tuple-element.53), channel_id=1, source_target_pairs={{0,3},{1,2},{2,1},{3,0},{4,7},{5,6},{6,5},{7,4},{8,11},{9,10},{10,... | collective-permute-start | bytes 589832 | tf_op jit(solution)/shard_map/ppermute | solution.py:337
  23.9 1.7 %collective-permute-start.8 = (f32[1,512]{1,0:T(1,128)S(1)}, f32[1,512]{1,0:T(1,128)S(1)}, u32[]{:S(2)}, u32[]{:S(2)}) collective-permute-start(f32[1,512]{1,0:T(1,128)S(1)} %get-tuple-element.54), channel_id=1, source_target_pairs={{0,1},{1,0},{2,3},{3,2},{4,5},{5,4},{6,7},{7,6},{8,9},{9,8},{10,11... | collective-permute-start | bytes 6152 | tf_op jit(solution)/shard_map/ppermute | solution.py:337
  25.6 2.7 %collective-permute-start.10 = (f32[520,512]{1,0:T(8,128)S(1)}, f32[520,512]{1,0:T(8,128)S(1)}, u32[]{:S(2)}, u32[]{:S(2)}) collective-permute-start(f32[520,512]{1,0:T(8,128)S(1)} %pair.1.late.refs_10_), channel_id=1, source_target_pairs={{0,1},{1,0},{2,3},{3,2},{4,5},{5,4},{6,7},{7,6},{8,9},{9,8},{10,11... | collective-permute-start | bytes 3194888 | tf_op jit(solution)/shard_map/ppermute | solution.py:337
  26.1 3.3 %collective-permute-start.9 = (f32[1,512]{1,0:T(1,128)S(1)}, f32[1,512]{1,0:T(1,128)S(1)}, u32[]{:S(2)}, u32[]{:S(2)}) collective-permute-start(f32[1,512]{1,0:T(1,128)S(1)} %two.1), channel_id=1, source_target_pairs={{0,5},{1,4},{2,7},{3,6},{4,1},{5,0},{6,3},{7,2},{8,13},{9,12},{10,... | collective-permute-start | bytes 6152 | tf_op jit(solution)/shard_map/ppermute | solution.py:337
  29.6 0.7 %collective-permute-start.11 = (f32[1,512]{1,0:T(1,128)S(1)}, f32[1,512]{1,0:T(1,128)S(1)}, u32[]{:S(2)}, u32[]{:S(2)}) collective-permute-start(f32[1,512]{1,0:T(1,128)S(1)} %hop.6), channel_id=1, source_target_pairs={{25,21}} | collective-permute-start | bytes 6152 | tf_op jit(solution)/shard_map/ppermute | solution.py:458
  30.2 13.4 %collective-permute-start.17 = (f32[512,512]{1,0:T(8,128)S(1)}, f32[512,512]{1,0:T(8,128)S(1)}, u32[]{:S(2)}, u32[]{:S(2)}) collective-permute-start(f32[512,512]{1,0:T(8,128)S(1)} %get-tuple-element.60.gb.refs_11_), channel_id=1, source_target_pairs={{0,1},{1,0},{2,3},{3,2},{4,5},{5,4},{6,7},{7,6},{8,9},{9,8},{10,11... | collective-permute-start | bytes 3145736 | tf_op jit(solution)/shard_map/ppermute | solution.py:337
  30.6 3.7 %collective-permute-start.12 = (f32[1,512]{1,0:T(1,128)S(1)}, f32[1,512]{1,0:T(1,128)S(1)}, u32[]{:S(2)}, u32[]{:S(2)}) collective-permute-start(f32[1,512]{1,0:T(1,128)S(1)} %hop.7), channel_id=1, source_target_pairs={{0,4},{1,5},{2,6},{3,7},{4,0},{5,1},{6,2},{7,3},{8,12},{9,13},{10,... | collective-permute-start | bytes 6152 | tf_op jit(solution)/shard_map/ppermute | solution.py:337
  34.4 0.7 %collective-permute-start.13 = (f32[1,512]{1,0:T(1,128)S(1)}, f32[1,512]{1,0:T(1,128)S(1)}, u32[]{:S(2)}, u32[]{:S(2)}) collective-permute-start(f32[1,512]{1,0:T(1,128)S(1)} %hop.8), channel_id=1, source_target_pairs={{17,13}} | collective-permute-start | bytes 6152 | tf_op jit(solution)/shard_map/ppermute | solution.py:458
  35.3 3.7 %collective-permute-start.14 = (f32[1,512]{1,0:T(1,128)S(1)}, f32[1,512]{1,0:T(1,128)S(1)}, u32[]{:S(2)}, u32[]{:S(2)}) collective-permute-start(f32[1,512]{1,0:T(1,128)S(1)} %hop.9), channel_id=1, source_target_pairs={{0,4},{1,5},{2,6},{3,7},{4,0},{5,1},{6,2},{7,3},{8,12},{9,13},{10,... | collective-permute-start | bytes 6152 | tf_op jit(solution)/shard_map/ppermute | solution.py:337
  39.1 0.7 %collective-permute-start.15 = (f32[1,512]{1,0:T(1,128)S(1)}, f32[1,512]{1,0:T(1,128)S(1)}, u32[]{:S(2)}, u32[]{:S(2)}) collective-permute-start(f32[1,512]{1,0:T(1,128)S(1)} %hop.10), channel_id=1, source_target_pairs={{9,5}} | collective-permute-start | bytes 6152 | tf_op jit(solution)/shard_map/ppermute | solution.py:458
  39.9 3.7 %collective-permute-start.16 = (f32[1,512]{1,0:T(1,128)S(1)}, f32[1,512]{1,0:T(1,128)S(1)}, u32[]{:S(2)}, u32[]{:S(2)}) collective-permute-start(f32[1,512]{1,0:T(1,128)S(1)} %hop.11), channel_id=1, source_target_pairs={{0,4},{1,5},{2,6},{3,7},{4,0},{5,1},{6,2},{7,3},{8,12},{9,13},{10,... | collective-permute-start | bytes 6152 | tf_op jit(solution)/shard_map/ppermute | solution.py:337
  44.0 7.9 %collective-permute-start.18 = (f32[4,128]{1,0:T(4,128)S(1)}, f32[4,128]{1,0:T(4,128)S(1)}, u32[]{:S(2)}, u32[]{:S(2)}) collective-permute-start(f32[4,128]{1,0:T(4,128)S(1)} %get-tuple-element.62), channel_id=1, source_target_pairs={{0,3},{1,2},{2,1},{3,0},{4,7},{5,6},{6,5},{7,4},{8,11},{9,10},{10,... | collective-permute-start | bytes 6152 | tf_op jit(solution)/shard_map/ppermute | solution.py:337
  44.1 9.4 %collective-permute-start.19 = (f32[4,128]{1,0:T(4,128)S(1)}, f32[4,128]{1,0:T(4,128)S(1)}, u32[]{:S(2)}, u32[]{:S(2)}) collective-permute-start(f32[4,128]{1,0:T(4,128)S(1)} %get-tuple-element.63), channel_id=1, source_target_pairs={{0,2},{1,3},{2,0},{3,1},{4,6},{5,7},{6,4},{7,5},{8,10},{9,11},{10,... | collective-permute-start | bytes 6152 | tf_op jit(solution)/shard_map/ppermute | solution.py:337
  51.9 1.6 %collective-permute-start.20 = (f32[4,128]{1,0:T(4,128)S(1)}, f32[4,128]{1,0:T(4,128)S(1)}, u32[]{:S(2)}, u32[]{:S(2)}) collective-permute-start(f32[4,128]{1,0:T(4,128)S(1)} %get-tuple-element.64), channel_id=1, source_target_pairs={{0,1},{1,0},{2,3},{3,2},{4,5},{5,4},{6,7},{7,6},{8,9},{9,8},{10,11... | collective-permute-start | bytes 6152 | tf_op jit(solution)/shard_map/ppermute | solution.py:337

commit v11 on v10

--- a/solution.py
+++ b/solution.py
@@ -452,10 +452,8 @@
     m, vec = call(block_kernel, "block", 12, [square, shape(8, order)], [VMEM] * 2, [], (late_map, early_map))
     for block in range(blocks - 2, 0, -1):
         (x,) = call(hop_kernel, "hop", 4, [shape(1, order)], [VMEM] * 3, [], (incoming[-1], m, vec))
-        if block % 2:
-            x = swap(x, 0, 1)
-        else:
-            x = lax.ppermute(x, ("tm", "state"), [(block * devices + 1, (block - 1) * devices + 1)])
+        partner = {at * devices + i: to * devices + i for at, to in ((block, block - 1), (block - 1, block)) for i in range(2)}
+        x = lax.ppermute(x, ("tm", "state"), [(i, partner.get(i, i ^ 1)) for i in range(blocks * devices)])
         incoming.append(x)
     g1 = swap(lax.optimization_barrier((gb, incoming[2]))[0], 1)
 

time: 54.3 us -> 55.5 us (1.022)
  waiting for transfers between devices: 12.8 us -> 14.2 us
    ppermute x18 -> x15, starting transfers between devices: 22.9 us -> 12.1 us  [swap(): return lax.ppermute(x, ('tm', 'state'), pairs)]
    ppermute x3 -> x6, starting transfers between devices: 1.98 us -> 12.8 us  [local(): lax.ppermute(x, ('tm', 'state'), [(i, partner.get(i, i ^ 1)) for i in ran...]
    ppermute x3 -> x6, waiting for transfers between devices: 0.01 us -> 7.36 us  [local(): lax.ppermute(x, ('tm', 'state'), [(i, partner.get(i, i ^ 1)) for i in ran...]
    ppermute x18 -> x15, waiting for transfers between devices: 12.8 us -> 6.82 us  [swap(): return lax.ppermute(x, ('tm', 'state'), pairs)]
  transfers between devices with their start and end apart: 21 -> 21, of which waited for: 8 -> 12; matrix products, arithmetic and copies ran while one was open for 0% -> 0% of each run, Pallas kernels for 22% -> 22%
where the time goes in v11:
time: 55.5 us; the launch traced here: 55.4 us
  starting transfers between devices  24.8 us (45%)
  Pallas kernels  16.2 us (29%)
  waiting for transfers between devices  14.2 us (26%)
    pallas_call x18, Pallas kernels, call(): pl.pallas_call(kernel, out_shape=outs, in_specs=in_specs, out_specs=[VMEM...  16.2 us
    ppermute x6, starting transfers between devices, local(): lax.ppermute(x, ('tm', 'state'), [(i, partner.get(i, i ^ 1)) for i in ran...  12.8 us
    ppermute x15, starting transfers between devices, swap(): return lax.ppermute(x, ('tm', 'state'), pairs)  12.1 us
    ppermute x6, waiting for transfers between devices, local(): lax.ppermute(x, ('tm', 'state'), [(i, partner.get(i, i ^ 1)) for i in ran...  7.36 us
    ppermute x15, waiting for transfers between devices, swap(): return lax.ppermute(x, ('tm', 'state'), pairs)  6.82 us
  transfers between devices with their start and end apart: 21, of which 12 were waited for; matrix products, arithmetic and copies ran while one was open for 0% of the time, Pallas kernels for 22%

profile of v11, /device:TPU:0, one launch (start us, length us, event | category | flops | bytes accessed | tf_op | source)
XLA Modules:
  0.0 55.4 jit_solution(2641450254222638501)
XLA Ops:
  0.0 1.6 %pack.1 = (f32[4,224,128]{2,1,0:T(8,128)S(1)}, f32[4,96,128]{2,1,0:T(8,128)S(1)}, f32[64,512]{1,0:T(8,128)S(1)}, f32[1,512]{1,0:T(1,128)S(1)}) custom-call(f32[4,128,512]{2,1,0:T(8,128)} %cov.5, f32[4,128,512]{2,1,0:T(8,128)} %prec.5, f32[128,512]{1,0:T(8,128)} %trans.3, f32[1,512]{1,0:T(1,128)} %bitcast.1), custom_call_target="tpu_custom_call" | custom-call | tf_op jit(solution)/shard_map/pack/pallas_call | solution.py:343
  1.6 3.0 %collective-permute-start = (f32[64,512]{1,0:T(8,128)S(1)}, f32[64,512]{1,0:T(8,128)S(1)}, u32[]{:S(2)}, u32[]{:S(2)}) collective-permute-start(f32[64,512]{1,0:T(8,128)S(1)} %get-tuple-element.36), channel_id=1, source_target_pairs={{0,2},{1,3},{2,0},{3,1},{4,6},{5,7},{6,4},{7,5},{8,10},{9,11},{10,... | collective-permute-start | bytes 393224 | tf_op jit(solution)/shard_map/ppermute | solution.py:337
  4.6 1.5 %near.1 = (f32[256,512]{1,0:T(8,128)S(1)}, f32[256,512]{1,0:T(8,128)S(1)}) custom-call(f32[4,128,512]{2,1,0:T(8,128)} %cov.5, f32[4,128,512]{2,1,0:T(8,128)} %prec.5, f32[1,512]{1,0:T(1,128)S(1)} %get-tuple-element.35.after.first.refs_0_), custom_call_target="tpu_custom_call" | custom-call | tf_op jit(solution)/shard_map/near/pallas_call | solution.py:343
  6.2 0.5 collective-permute-start.5
  6.8 1.4 %collective-permute-done.after.refs_0_ = f32[64,512]{1,0:T(8,128)S(1)} collective-permute-done((f32[64,512]{1,0:T(8,128)S(1)}, f32[64,512]{1,0:T(8,128)S(1)}, u32[]{:S(2)}, u32[]{:S(2)}) %collective-permute-start) | collective-permute-done | bytes 131104 | tf_op jit(solution)/shard_map/ppermute | solution.py:337
  8.1 1.8 %collective-permute-start.2 = (f32[64,512]{1,0:T(8,128)S(1)}, f32[64,512]{1,0:T(8,128)S(1)}, u32[]{:S(2)}, u32[]{:S(2)}) collective-permute-start(f32[64,512]{1,0:T(8,128)S(1)} %collective-permute-done.after.refs_0_), channel_id=1, source_target_pairs={{0,4},{1,5},{2,6},{3,7},{4,0},{5,1},{6,2},{7,3},{8,12},{9,13},{10,... | collective-permute-start | bytes 393224 | tf_op jit(solution)/shard_map/ppermute | solution.py:337
  9.9 1.6 %own.1 = (f32[4,128,512]{2,1,0:T(8,128)S(1)}, f32[128,512]{1,0:T(8,128)S(1)}, f32[4,512]{1,0:T(4,128)S(1)}) custom-call(f32[4,128,512]{2,1,0:T(8,128)} %cov.5, f32[4,128,512]{2,1,0:T(8,128)} %prec.5, f32[128,512]{1,0:T(8,128)} %trans.3, f32[4,512]{1,0:T(4,128)} %means.1, f32[64,512]{1,0:T(8,128)S(1)} %collective-permute-done.after.refs_0_), custom_call_target="tpu_custom_call" | custom-call | tf_op jit(solution)/shard_map/own/pallas_call | solution.py:343
  11.4 1.6 %collective-permute-done.2.refs_1_ = f32[64,512]{1,0:T(8,128)S(1)} collective-permute-done((f32[64,512]{1,0:T(8,128)S(1)}, f32[64,512]{1,0:T(8,128)S(1)}, u32[]{:S(2)}, u32[]{:S(2)}) %collective-permute-start.2) | collective-permute-done | bytes 131104 | tf_op jit(solution)/shard_map/ppermute | solution.py:337
  13.1 0.6 %join.1.joined = f32[1,128,512]{2,1,0:T(8,128)S(1)} custom-call(f32[128,512]{1,0:T(8,128)S(1)} %get-tuple-element.39.after.trans, f32[64,512]{1,0:T(8,128)S(1)} %collective-permute-done.after.refs_0_, f32[64,512]{1,0:T(8,128)S(1)} %collective-permute-done.2.refs_1_), custom_call_target="tpu_custom_call" | custom-call | tf_op jit(solution)/shard_map/join/pallas_call | solution.py:343
  13.8 2.0 %collective-permute-start.7 = (f32[4,96,128]{2,1,0:T(8,128)S(1)}, f32[4,96,128]{2,1,0:T(8,128)S(1)}, u32[]{:S(2)}, u32[]{:S(2)}) collective-permute-start(f32[4,96,128]{2,1,0:T(8,128)S(1)} %get-tuple-element.53), channel_id=1, source_target_pairs={{0,3},{1,2},{2,1},{3,0},{4,7},{5,6},{6,5},{7,4},{8,11},{9,10},{10,... | collective-permute-start | bytes 589832 | tf_op jit(solution)/shard_map/ppermute | solution.py:337
  15.8 2.9 %early.1 = (f32[16,512]{1,0:T(8,128)S(1)}, bf16[2,256,512]{2,1,0:T(8,128)(2,1)S(1)}, bf16[2,2,256,512]{3,2,1,0:T(8,128)(2,1)S(1)}, f32[2,256,256]{2,1,0:T(8,128)...) custom-call(f32[4,128,512]{2,1,0:T(8,128)S(1)} %get-tuple-element.37.own, ...), custom_call_target="tpu_custom_call" | custom-call | tf_op jit(solution)/shard_map/early/pallas_call | solution.py:343
  18.7 1.3 %collective-permute-done.6.refs_0_ = f32[4,224,128]{2,1,0:T(8,128)S(1)} collective-permute-done((f32[4,224,128]{2,1,0:T(8,128)S(1)}, f32[4,224,128]{2,1,0:T(8,128)S(1)}, u32[]{:S(2)}, u32[]{:S(2)}) %collective-permute-start.6) | collective-permute-done | bytes 458784 | tf_op jit(solution)/shard_map/ppermute | solution.py:337
  20.1 2.5 %middle.1 = (f32[512,512]{1,0:T(8,128)S(1)}, f32[512,512]{1,0:T(8,128)S(1)}, f32[2,512,128]{2,1,0:T(8,128)S(1)}, f32[2,128,512]{2,1,0:T(8,128)S(1)}) custom-call(bf16[2,256,512]{2,1,0:T(8,128)(2,1)S(1)} %get-tuple-element.43.a_far, bf16[2,2,256,512]{3,2,1,0:T(8,128)(2,1)S(1)} %get-tuple-element.44.l_known, f32[2,256,256]{2,1,0:T(8,128)S(1)} %get-tuple-element.45.c_known, ...), custom_call_target="tpu_custom_call" | custom-call | tf_op jit(solution)/shard_map/middle/pallas_call | solution.py:343
  22.6 1.3 %late.1 = (f32[512,512]{1,0:T(8,128)S(1)}, f32[512,512]{1,0:T(8,128)S(1)}, f32[1,512]{1,0:T(1,128)S(1)}) custom-call(f32[1,512]{1,0:T(1,128)S(1)} %get-tuple-element.35.after.first.refs_0_, f32[16,512]{1,0:T(8,128)S(1)} %get-tuple-element.42.info, bf16[2,256,512]{2,1,0:T(8,128)(2,1)S(1)} %get-tuple-element.43.a_far, f32[512,512]{1,0:T(8,128)S(1)} %get-tuple-element.49.ga, ...), custom_call_target="tpu_custom_call" | custom-call | tf_op jit(solution)/shard_map/late/pallas_call | solution.py:343
  23.9 0.7 %collective-permute-start.8 = (f32[1,512]{1,0:T(1,128)S(1)}, f32[1,512]{1,0:T(1,128)S(1)}, u32[]{:S(2)}, u32[]{:S(2)}) collective-permute-start(f32[1,512]{1,0:T(1,128)S(1)} %get-tuple-element.54), channel_id=1, source_target_pairs={{0,1},{1,0},{2,3},{3,2},{4,5},{5,4},{6,7},{7,6},{8,9},{9,8},{10,11... | collective-permute-start | bytes 6152 | tf_op jit(solution)/shard_map/ppermute | solution.py:337
  24.6 1.0 %pair.1.late.refs_10_ = f32[520,512]{1,0:T(8,128)S(1)} custom-call(f32[16,512]{1,0:T(8,128)S(1)} %get-tuple-element.42.info, f32[512,512]{1,0:T(8,128)S(1)} %get-tuple-element.55.ga, f32[512,512]{1,0:T(8,128)S(1)} %get-tuple-element.60.gb.refs_11_), custom_call_target="tpu_custom_call" | custom-call | tf_op jit(solution)/shard_map/pair/pallas_call | solution.py:343
  26.1 1.6 %collective-permute-start.9 = (f32[1,512]{1,0:T(1,128)S(1)}, f32[1,512]{1,0:T(1,128)S(1)}, u32[]{:S(2)}, u32[]{:S(2)}) collective-permute-start(f32[1,512]{1,0:T(1,128)S(1)} %two.1), channel_id=1, source_target_pairs={{0,5},{1,4},{2,7},{3,6},{4,1},{5,0},{6,3},{7,2},{8,13},{9,12},{10,... | collective-permute-start | bytes 6152 | tf_op jit(solution)/shard_map/ppermute | solution.py:337
  27.7 0.7 %collective-permute-done.10.early.refs_12_ = f32[520,512]{1,0:T(8,128)S(1)} collective-permute-done((f32[520,512]{1,0:T(8,128)S(1)}, f32[520,512]{1,0:T(8,128)S(1)}, u32[]{:S(2)}, u32[]{:S(2)}) %collective-permute-start.10) | collective-permute-done | bytes 1064992 | tf_op jit(solution)/shard_map/ppermute | solution.py:337
  28.4 1.0 %block.1 = (f32[512,512]{1,0:T(8,128)S(1)}, f32[8,512]{1,0:T(8,128)S(1)}) custom-call(f32[520,512]{1,0:T(8,128)S(1)} %pair.1.late.refs_10_, f32[520,512]{1,0:T(8,128)S(1)} %collective-permute-done.10.early.refs_12_), custom_call_target="tpu_custom_call" | custom-call | tf_op jit(solution)/shard_map/block/pallas_call | solution.py:343
  29.8 1.0 %collective-permute-done.11.x.refs_2_ = f32[1,512]{1,0:T(1,128)S(1)} collective-permute-done((f32[1,512]{1,0:T(1,128)S(1)}, f32[1,512]{1,0:T(1,128)S(1)}, u32[]{:S(2)}, u32[]{:S(2)}) %collective-permute-start.11) | collective-permute-done | bytes 2080 | tf_op jit(solution)/shard_map/ppermute | solution.py:456
  31.1 0.4 collective-permute-start.12
  31.5 1.9 %collective-permute-done.12.x.refs_3_ = f32[1,512]{1,0:T(1,128)S(1)} collective-permute-done((f32[1,512]{1,0:T(1,128)S(1)}, f32[1,512]{1,0:T(1,128)S(1)}, u32[]{:S(2)}, u32[]{:S(2)}) %collective-permute-start.12) | collective-permute-done | bytes 2080 | tf_op jit(solution)/shard_map/ppermute | solution.py:456
  33.8 1.0 %collective-permute-done.13.x.refs_4_ = f32[1,512]{1,0:T(1,128)S(1)} collective-permute-done((f32[1,512]{1,0:T(1,128)S(1)}, f32[1,512]{1,0:T(1,128)S(1)}, u32[]{:S(2)}, u32[]{:S(2)}) %collective-permute-start.13) | collective-permute-done | bytes 2080 | tf_op jit(solution)/shard_map/ppermute | solution.py:456
  35.2 1.0 %collective-permute-done.14.x.refs_5_ = f32[1,512]{1,0:T(1,128)S(1)} collective-permute-done((f32[1,512]{1,0:T(1,128)S(1)}, f32[1,512]{1,0:T(1,128)S(1)}, u32[]{:S(2)}, u32[]{:S(2)}) %collective-permute-start.14) | collective-permute-done | bytes 2080 | tf_op jit(solution)/shard_map/ppermute | solution.py:456
  36.6 1.0 %collective-permute-done.15.x.refs_6_ = f32[1,512]{1,0:T(1,128)S(1)} collective-permute-done((f32[1,512]{1,0:T(1,128)S(1)}, f32[1,512]{1,0:T(1,128)S(1)}, u32[]{:S(2)}, u32[]{:S(2)}) %collective-permute-start.15) | collective-permute-done | bytes 2080 | tf_op jit(solution)/shard_map/ppermute | solution.py:456
  37.7 11.3 %collective-permute-start.16 = (f32[1,512]{1,0:T(1,128)S(1)}, f32[1,512]{1,0:T(1,128)S(1)}, u32[]{:S(2)}, u32[]{:S(2)}) collective-permute-start(f32[1,512]{1,0:T(1,128)S(1)} %hop.11), channel_id=1, source_target_pairs={{0,4},{1,5},{2,3},{3,2},{4,0},{5,1},{6,7},{7,6},{8,9},{9,8},{10,11... | collective-permute-start | bytes 6152 | tf_op jit(solution)/shard_map/ppermute | solution.py:456
  49.1 1.6 %collective-permute-done.16.refs_7_ = f32[1,512]{1,0:T(1,128)S(1)} collective-permute-done((f32[1,512]{1,0:T(1,128)S(1)}, f32[1,512]{1,0:T(1,128)S(1)}, u32[]{:S(2)}, u32[]{:S(2)}) %collective-permute-start.16) | collective-permute-done | bytes 2080 | tf_op jit(solution)/shard_map/ppermute | solution.py:456
  50.6 0.4 last.1
  51.2 1.8 %collective-permute-start.20 = (f32[4,128]{1,0:T(4,128)S(1)}, f32[4,128]{1,0:T(4,128)S(1)}, u32[]{:S(2)}, u32[]{:S(2)}) collective-permute-start(f32[4,128]{1,0:T(4,128)S(1)} %get-tuple-element.64), channel_id=1, source_target_pairs={{0,1},{1,0},{2,3},{3,2},{4,5},{5,4},{6,7},{7,6},{8,9},{9,8},{10,11... | collective-permute-start | bytes 6152 | tf_op jit(solution)/shard_map/ppermute | solution.py:337
  53.0 1.1 %collective-permute-done.18.refs_1_ = f32[4,128]{1,0:T(4,128)S(1)} collective-permute-done((f32[4,128]{1,0:T(4,128)S(1)}, f32[4,128]{1,0:T(4,128)S(1)}, u32[]{:S(2)}, u32[]{:S(2)}) %collective-permute-start.18) | collective-permute-done | bytes 2080 | tf_op jit(solution)/shard_map/ppermute | solution.py:337
  54.1 0.7 %collective-permute-done.19.refs_2_ = f32[4,128]{1,0:T(4,128)S(1)} collective-permute-done((f32[4,128]{1,0:T(4,128)S(1)}, f32[4,128]{1,0:T(4,128)S(1)}, u32[]{:S(2)}, u32[]{:S(2)}) %collective-permute-start.19) | collective-permute-done | bytes 2080 | tf_op jit(solution)/shard_map/ppermute | solution.py:337
  54.8 0.6 %out.1 = f32[4,128]{1,0:T(4,128)} custom-call(f32[4,128]{1,0:T(4,128)S(1)} %get-tuple-element.61.refs_0_, f32[4,128]{1,0:T(4,128)S(1)} %collective-permute-done.18.refs_1_, f32[4,128]{1,0:T(4,128)S(1)} %collective-permute-done.19.refs_2_, f32[4,128]{1,0:T(4,128)S(1)} %collective-permute-done.20.refs_3_), custom_call_target="tpu_custom_call" | custom-call | tf_op jit(solution)/shard_map/out/pallas_call | solution.py:343
  (30 shorter events, 3.0 us)
Async XLA Ops:
  1.6 5.1 %copy-start = (f32[128,512]{1,0:T(8,128)S(1)}, f32[128,512]{1,0:T(8,128)}, u32[]{:S(2)}) copy-start(f32[128,512]{1,0:T(8,128)} %trans.3) | copy-start | bytes 786436
  1.6 6.5 %collective-permute-start = (f32[64,512]{1,0:T(8,128)S(1)}, f32[64,512]{1,0:T(8,128)S(1)}, u32[]{:S(2)}, u32[]{:S(2)}) collective-permute-start(f32[64,512]{1,0:T(8,128)S(1)} %get-tuple-element.36), channel_id=1, source_target_pairs={{0,2},{1,3},{2,0},{3,1},{4,6},{5,7},{6,4},{7,5},{8,10},{9,11},{10,... | collective-permute-start | bytes 393224 | tf_op jit(solution)/shard_map/ppermute | solution.py:337
  6.1 9.7 %collective-permute-start.4 = (f32[256,512]{1,0:T(8,128)S(1)}, f32[256,512]{1,0:T(8,128)S(1)}, u32[]{:S(2)}, u32[]{:S(2)}) collective-permute-start(f32[256,512]{1,0:T(8,128)S(1)} %get-tuple-element.40), channel_id=1, source_target_pairs={{0,1},{1,0},{2,3},{3,2},{4,5},{5,4},{6,7},{7,6},{8,9},{9,8},{10,11... | collective-permute-start | bytes 1572872 | tf_op jit(solution)/shard_map/ppermute | solution.py:337
  6.2 9.6 %collective-permute-start.5 = (f32[256,512]{1,0:T(8,128)S(1)}, f32[256,512]{1,0:T(8,128)S(1)}, u32[]{:S(2)}, u32[]{:S(2)}) collective-permute-start(f32[256,512]{1,0:T(8,128)S(1)} %get-tuple-element.41), channel_id=1, source_target_pairs={{0,1},{1,0},{2,3},{3,2},{4,5},{5,4},{6,7},{7,6},{8,9},{9,8},{10,11... | collective-permute-start | bytes 1572872 | tf_op jit(solution)/shard_map/ppermute | solution.py:337
  6.7 13.4 %collective-permute-start.6 = (f32[4,224,128]{2,1,0:T(8,128)S(1)}, f32[4,224,128]{2,1,0:T(8,128)S(1)}, u32[]{:S(2)}, u32[]{:S(2)}) collective-permute-start(f32[4,224,128]{2,1,0:T(8,128)S(1)} %get-tuple-element.48), channel_id=1, source_target_pairs={{0,2},{1,3},{2,0},{3,1},{4,6},{5,7},{6,4},{7,5},{8,10},{9,11},{10,... | collective-permute-start | bytes 1376264 | tf_op jit(solution)/shard_map/ppermute | solution.py:337
  6.7 7.1 %collective-permute-start.1 = (f32[128,512]{1,0:T(8,128)S(1)}, f32[128,512]{1,0:T(8,128)S(1)}, u32[]{:S(2)}, u32[]{:S(2)}) collective-permute-start(f32[128,512]{1,0:T(8,128)S(1)} %copy-done), channel_id=1, source_target_pairs={{0,1},{1,0},{2,3},{3,2},{4,5},{5,4},{6,7},{7,6},{8,9},{9,8},{10,11... | collective-permute-start | bytes 786440 | tf_op jit(solution)/shard_map/ppermute | solution.py:337
  8.1 5.0 %collective-permute-start.2 = (f32[64,512]{1,0:T(8,128)S(1)}, f32[64,512]{1,0:T(8,128)S(1)}, u32[]{:S(2)}, u32[]{:S(2)}) collective-permute-start(f32[64,512]{1,0:T(8,128)S(1)} %collective-permute-done.after.refs_0_), channel_id=1, source_target_pairs={{0,4},{1,5},{2,6},{3,7},{4,0},{5,1},{6,2},{7,3},{8,12},{9,13},{10,... | collective-permute-start | bytes 393224 | tf_op jit(solution)/shard_map/ppermute | solution.py:337
  13.7 2.1 %collective-permute-start.3 = (f32[1,128,512]{2,1,0:T(8,128)S(1)}, f32[1,128,512]{2,1,0:T(8,128)S(1)}, u32[]{:S(2)}, u32[]{:S(2)}) collective-permute-start(f32[1,128,512]{2,1,0:T(8,128)S(1)} %join.1.joined), channel_id=1, source_target_pairs={{0,1},{1,0},{2,3},{3,2},{4,5},{5,4},{6,7},{7,6},{8,9},{9,8},{10,11... | collective-permute-start | bytes 786440 | tf_op jit(solution)/shard_map/ppermute | solution.py:337
  13.8 8.8 %collective-permute-start.7 = (f32[4,96,128]{2,1,0:T(8,128)S(1)}, f32[4,96,128]{2,1,0:T(8,128)S(1)}, u32[]{:S(2)}, u32[]{:S(2)}) collective-permute-start(f32[4,96,128]{2,1,0:T(8,128)S(1)} %get-tuple-element.53), channel_id=1, source_target_pairs={{0,3},{1,2},{2,1},{3,0},{4,7},{5,6},{6,5},{7,4},{8,11},{9,10},{10,... | collective-permute-start | bytes 589832 | tf_op jit(solution)/shard_map/ppermute | solution.py:337
  23.9 1.7 %collective-permute-start.8 = (f32[1,512]{1,0:T(1,128)S(1)}, f32[1,512]{1,0:T(1,128)S(1)}, u32[]{:S(2)}, u32[]{:S(2)}) collective-permute-start(f32[1,512]{1,0:T(1,128)S(1)} %get-tuple-element.54), channel_id=1, source_target_pairs={{0,1},{1,0},{2,3},{3,2},{4,5},{5,4},{6,7},{7,6},{8,9},{9,8},{10,11... | collective-permute-start | bytes 6152 | tf_op jit(solution)/shard_map/ppermute | solution.py:337
  25.6 2.7 %collective-permute-start.10 = (f32[520,512]{1,0:T(8,128)S(1)}, f32[520,512]{1,0:T(8,128)S(1)}, u32[]{:S(2)}, u32[]{:S(2)}) collective-permute-start(f32[520,512]{1,0:T(8,128)S(1)} %pair.1.late.refs_10_), channel_id=1, source_target_pairs={{0,1},{1,0},{2,3},{3,2},{4,5},{5,4},{6,7},{7,6},{8,9},{9,8},{10,11... | collective-permute-start | bytes 3194888 | tf_op jit(solution)/shard_map/ppermute | solution.py:337
  26.1 3.3 %collective-permute-start.9 = (f32[1,512]{1,0:T(1,128)S(1)}, f32[1,512]{1,0:T(1,128)S(1)}, u32[]{:S(2)}, u32[]{:S(2)}) collective-permute-start(f32[1,512]{1,0:T(1,128)S(1)} %two.1), channel_id=1, source_target_pairs={{0,5},{1,4},{2,7},{3,6},{4,1},{5,0},{6,3},{7,2},{8,13},{9,12},{10,... | collective-permute-start | bytes 6152 | tf_op jit(solution)/shard_map/ppermute | solution.py:337
  29.6 1.2 %collective-permute-start.11 = (f32[1,512]{1,0:T(1,128)S(1)}, f32[1,512]{1,0:T(1,128)S(1)}, u32[]{:S(2)}, u32[]{:S(2)}) collective-permute-start(f32[1,512]{1,0:T(1,128)S(1)} %hop.6), channel_id=1, source_target_pairs={{0,1},{1,0},{2,3},{3,2},{4,5},{5,4},{6,7},{7,6},{8,9},{9,8},{10,11... | collective-permute-start | bytes 6152 | tf_op jit(solution)/shard_map/ppermute | solution.py:456
  30.8 19.9 %collective-permute-start.17 = (f32[512,512]{1,0:T(8,128)S(1)}, f32[512,512]{1,0:T(8,128)S(1)}, u32[]{:S(2)}, u32[]{:S(2)}) collective-permute-start(f32[512,512]{1,0:T(8,128)S(1)} %get-tuple-element.60.gb.refs_11_), channel_id=1, source_target_pairs={{0,1},{1,0},{2,3},{3,2},{4,5},{5,4},{6,7},{7,6},{8,9},{9,8},{10,11... | collective-permute-start | bytes 3145736 | tf_op jit(solution)/shard_map/ppermute | solution.py:337
  31.1 2.3 %collective-permute-start.12 = (f32[1,512]{1,0:T(1,128)S(1)}, f32[1,512]{1,0:T(1,128)S(1)}, u32[]{:S(2)}, u32[]{:S(2)}) collective-permute-start(f32[1,512]{1,0:T(1,128)S(1)} %hop.7), channel_id=1, source_target_pairs={{0,1},{1,0},{2,3},{3,2},{4,5},{5,4},{6,7},{7,6},{8,9},{9,8},{10,11... | collective-permute-start | bytes 6152 | tf_op jit(solution)/shard_map/ppermute | solution.py:456
  33.6 1.2 %collective-permute-start.13 = (f32[1,512]{1,0:T(1,128)S(1)}, f32[1,512]{1,0:T(1,128)S(1)}, u32[]{:S(2)}, u32[]{:S(2)}) collective-permute-start(f32[1,512]{1,0:T(1,128)S(1)} %hop.8), channel_id=1, source_target_pairs={{0,1},{1,0},{2,3},{3,2},{4,5},{5,4},{6,7},{7,6},{8,9},{9,8},{10,11... | collective-permute-start | bytes 6152 | tf_op jit(solution)/shard_map/ppermute | solution.py:456
  35.0 1.2 %collective-permute-start.14 = (f32[1,512]{1,0:T(1,128)S(1)}, f32[1,512]{1,0:T(1,128)S(1)}, u32[]{:S(2)}, u32[]{:S(2)}) collective-permute-start(f32[1,512]{1,0:T(1,128)S(1)} %hop.9), channel_id=1, source_target_pairs={{0,1},{1,0},{2,3},{3,2},{4,5},{5,4},{6,7},{7,6},{8,12},{9,13},{10,... | collective-permute-start | bytes 6152 | tf_op jit(solution)/shard_map/ppermute | solution.py:456
  36.3 1.2 %collective-permute-start.15 = (f32[1,512]{1,0:T(1,128)S(1)}, f32[1,512]{1,0:T(1,128)S(1)}, u32[]{:S(2)}, u32[]{:S(2)}) collective-permute-start(f32[1,512]{1,0:T(1,128)S(1)} %hop.10), channel_id=1, source_target_pairs={{0,1},{1,0},{2,3},{3,2},{4,8},{5,9},{6,7},{7,6},{8,4},{9,5},{10,11... | collective-permute-start | bytes 6152 | tf_op jit(solution)/shard_map/ppermute | solution.py:456
  37.7 12.9 %collective-permute-start.16 = (f32[1,512]{1,0:T(1,128)S(1)}, f32[1,512]{1,0:T(1,128)S(1)}, u32[]{:S(2)}, u32[]{:S(2)}) collective-permute-start(f32[1,512]{1,0:T(1,128)S(1)} %hop.11), channel_id=1, source_target_pairs={{0,4},{1,5},{2,3},{3,2},{4,0},{5,1},{6,7},{7,6},{8,9},{9,8},{10,11... | collective-permute-start | bytes 6152 | tf_op jit(solution)/shard_map/ppermute | solution.py:456
  51.0 3.1 %collective-permute-start.18 = (f32[4,128]{1,0:T(4,128)S(1)}, f32[4,128]{1,0:T(4,128)S(1)}, u32[]{:S(2)}, u32[]{:S(2)}) collective-permute-start(f32[4,128]{1,0:T(4,128)S(1)} %get-tuple-element.62), channel_id=1, source_target_pairs={{0,3},{1,2},{2,1},{3,0},{4,7},{5,6},{6,5},{7,4},{8,11},{9,10},{10,... | collective-permute-start | bytes 6152 | tf_op jit(solution)/shard_map/ppermute | solution.py:337
  51.1 3.7 %collective-permute-start.19 = (f32[4,128]{1,0:T(4,128)S(1)}, f32[4,128]{1,0:T(4,128)S(1)}, u32[]{:S(2)}, u32[]{:S(2)}) collective-permute-start(f32[4,128]{1,0:T(4,128)S(1)} %get-tuple-element.63), channel_id=1, source_target_pairs={{0,2},{1,3},{2,0},{3,1},{4,6},{5,7},{6,4},{7,5},{8,10},{9,11},{10,... | collective-permute-start | bytes 6152 | tf_op jit(solution)/shard_map/ppermute | solution.py:337
  51.2 3.6 %collective-permute-start.20 = (f32[4,128]{1,0:T(4,128)S(1)}, f32[4,128]{1,0:T(4,128)S(1)}, u32[]{:S(2)}, u32[]{:S(2)}) collective-permute-start(f32[4,128]{1,0:T(4,128)S(1)} %get-tuple-element.64), channel_id=1, source_target_pairs={{0,1},{1,0},{2,3},{3,2},{4,5},{5,4},{6,7},{7,6},{8,9},{9,8},{10,11... | collective-permute-start | bytes 6152 | tf_op jit(solution)/shard_map/ppermute | solution.py:337

commit v12 on v11

--- a/solution.py
+++ b/solution.py
@@ -452,8 +452,11 @@
     m, vec = call(block_kernel, "block", 12, [square, shape(8, order)], [VMEM] * 2, [], (late_map, early_map))
     for block in range(blocks - 2, 0, -1):
         (x,) = call(hop_kernel, "hop", 4, [shape(1, order)], [VMEM] * 3, [], (incoming[-1], m, vec))
-        partner = {at * devices + i: to * devices + i for at, to in ((block, block - 1), (block - 1, block)) for i in range(2)}
-        x = lax.ppermute(x, ("tm", "state"), [(i, partner.get(i, i ^ 1)) for i in range(blocks * devices)])
+        target = {i: i ^ 1 for i in range(blocks * devices)}
+        for at, to in ((block, block - 1), (block - 1, block)):
+            target[at * devices + 1] = to * devices + 1
+            target.update({at * devices + i: at * devices + j for i, j in ((0, 2), (2, 3), (3, 0))})
+        x = lax.ppermute(x, ("tm", "state"), list(target.items()))
         incoming.append(x)
     g1 = swap(lax.optimization_barrier((gb, incoming[2]))[0], 1)
 

time: 55.5 us -> 49.8 us (0.90)
  starting transfers between devices: 24.8 us -> 18.4 us
  waiting for transfers between devices: 14.2 us -> 14.9 us
    ppermute x6, starting transfers between devices: 12.8 us -> 1.96 us  [local(): x = lax.ppermute(x, ('tm', 'state'), list(target.items()))]
    ppermute x15, starting transfers between devices: 12.1 us -> 16.4 us  [swap(): return lax.ppermute(x, ('tm', 'state'), pairs)]
    ppermute x6, waiting for transfers between devices: 7.36 us -> 8.31 us  [local(): x = lax.ppermute(x, ('tm', 'state'), list(target.items()))]
  transfers between devices with their start and end apart: 21 -> 21, of which waited for: 12 -> 11; matrix products, arithmetic and copies ran while one was open for 0% -> 0% of each run, Pallas kernels for 22% -> 24%
where the time goes in v12:
time: 49.8 us; the launch traced here: 49.6 us
  starting transfers between devices  18.4 us (37%)
  Pallas kernels  16.2 us (33%)
  waiting for transfers between devices  14.9 us (30%)
    ppermute x15, starting transfers between devices, swap(): return lax.ppermute(x, ('tm', 'state'), pairs)  16.4 us
    pallas_call x18, Pallas kernels, call(): pl.pallas_call(kernel, out_shape=outs, in_specs=in_specs, out_specs=[VMEM...  16.2 us
    ppermute x6, waiting for transfers between devices, local(): x = lax.ppermute(x, ('tm', 'state'), list(target.items()))  8.31 us
    ppermute x15, waiting for transfers between devices, swap(): return lax.ppermute(x, ('tm', 'state'), pairs)  6.59 us
    ppermute x6, starting transfers between devices, local(): x = lax.ppermute(x, ('tm', 'state'), list(target.items()))  1.96 us
  transfers between devices with their start and end apart: 21, of which 11 were waited for; matrix products, arithmetic and copies ran while one was open for 0% of the time, Pallas kernels for 24%

profile of v12, /device:TPU:0, one launch (start us, length us, event | category | flops | bytes accessed | tf_op | source)
XLA Modules:
  0.0 49.6 jit_solution(17382912832818068038)
XLA Ops:
  0.0 1.6 %pack.1 = (f32[4,224,128]{2,1,0:T(8,128)S(1)}, f32[4,96,128]{2,1,0:T(8,128)S(1)}, f32[64,512]{1,0:T(8,128)S(1)}, f32[1,512]{1,0:T(1,128)S(1)}) custom-call(f32[4,128,512]{2,1,0:T(8,128)} %cov.5, f32[4,128,512]{2,1,0:T(8,128)} %prec.5, f32[128,512]{1,0:T(8,128)} %trans.3, f32[1,512]{1,0:T(1,128)} %bitcast.1), custom_call_target="tpu_custom_call" | custom-call | tf_op jit(solution)/shard_map/pack/pallas_call | solution.py:343
  1.6 3.0 %collective-permute-start = (f32[64,512]{1,0:T(8,128)S(1)}, f32[64,512]{1,0:T(8,128)S(1)}, u32[]{:S(2)}, u32[]{:S(2)}) collective-permute-start(f32[64,512]{1,0:T(8,128)S(1)} %get-tuple-element.36), channel_id=1, source_target_pairs={{0,2},{1,3},{2,0},{3,1},{4,6},{5,7},{6,4},{7,5},{8,10},{9,11},{10,... | collective-permute-start | bytes 393224 | tf_op jit(solution)/shard_map/ppermute | solution.py:337
  4.6 1.5 %near.1 = (f32[256,512]{1,0:T(8,128)S(1)}, f32[256,512]{1,0:T(8,128)S(1)}) custom-call(f32[4,128,512]{2,1,0:T(8,128)} %cov.5, f32[4,128,512]{2,1,0:T(8,128)} %prec.5, f32[1,512]{1,0:T(1,128)S(1)} %get-tuple-element.35.after.first.refs_0_), custom_call_target="tpu_custom_call" | custom-call | tf_op jit(solution)/shard_map/near/pallas_call | solution.py:343
  6.2 0.5 %collective-permute-start.5 = (f32[256,512]{1,0:T(8,128)S(1)}, f32[256,512]{1,0:T(8,128)S(1)}, u32[]{:S(2)}, u32[]{:S(2)}) collective-permute-start(f32[256,512]{1,0:T(8,128)S(1)} %get-tuple-element.41), channel_id=1, source_target_pairs={{0,1},{1,0},{2,3},{3,2},{4,5},{5,4},{6,7},{7,6},{8,9},{9,8},{10,11... | collective-permute-start | bytes 1572872 | tf_op jit(solution)/shard_map/ppermute | solution.py:337
  6.8 1.4 %collective-permute-done.after.refs_0_ = f32[64,512]{1,0:T(8,128)S(1)} collective-permute-done((f32[64,512]{1,0:T(8,128)S(1)}, f32[64,512]{1,0:T(8,128)S(1)}, u32[]{:S(2)}, u32[]{:S(2)}) %collective-permute-start) | collective-permute-done | bytes 131104 | tf_op jit(solution)/shard_map/ppermute | solution.py:337
  8.1 1.8 %collective-permute-start.2 = (f32[64,512]{1,0:T(8,128)S(1)}, f32[64,512]{1,0:T(8,128)S(1)}, u32[]{:S(2)}, u32[]{:S(2)}) collective-permute-start(f32[64,512]{1,0:T(8,128)S(1)} %collective-permute-done.after.refs_0_), channel_id=1, source_target_pairs={{0,4},{1,5},{2,6},{3,7},{4,0},{5,1},{6,2},{7,3},{8,12},{9,13},{10,... | collective-permute-start | bytes 393224 | tf_op jit(solution)/shard_map/ppermute | solution.py:337
  9.9 1.6 %own.1 = (f32[4,128,512]{2,1,0:T(8,128)S(1)}, f32[128,512]{1,0:T(8,128)S(1)}, f32[4,512]{1,0:T(4,128)S(1)}) custom-call(f32[4,128,512]{2,1,0:T(8,128)} %cov.5, f32[4,128,512]{2,1,0:T(8,128)} %prec.5, f32[128,512]{1,0:T(8,128)} %trans.3, f32[4,512]{1,0:T(4,128)} %means.1, f32[64,512]{1,0:T(8,128)S(1)} %collective-permute-done.after.refs_0_), custom_call_target="tpu_custom_call" | custom-call | tf_op jit(solution)/shard_map/own/pallas_call | solution.py:343
  11.4 1.6 %collective-permute-done.2.refs_1_ = f32[64,512]{1,0:T(8,128)S(1)} collective-permute-done((f32[64,512]{1,0:T(8,128)S(1)}, f32[64,512]{1,0:T(8,128)S(1)}, u32[]{:S(2)}, u32[]{:S(2)}) %collective-permute-start.2) | collective-permute-done | bytes 131104 | tf_op jit(solution)/shard_map/ppermute | solution.py:337
  13.1 0.6 %join.1.joined = f32[1,128,512]{2,1,0:T(8,128)S(1)} custom-call(f32[128,512]{1,0:T(8,128)S(1)} %get-tuple-element.39.after.trans, f32[64,512]{1,0:T(8,128)S(1)} %collective-permute-done.after.refs_0_, f32[64,512]{1,0:T(8,128)S(1)} %collective-permute-done.2.refs_1_), custom_call_target="tpu_custom_call" | custom-call | tf_op jit(solution)/shard_map/join/pallas_call | solution.py:343
  13.8 2.0 %collective-permute-start.7 = (f32[4,96,128]{2,1,0:T(8,128)S(1)}, f32[4,96,128]{2,1,0:T(8,128)S(1)}, u32[]{:S(2)}, u32[]{:S(2)}) collective-permute-start(f32[4,96,128]{2,1,0:T(8,128)S(1)} %get-tuple-element.53), channel_id=1, source_target_pairs={{0,3},{1,2},{2,1},{3,0},{4,7},{5,6},{6,5},{7,4},{8,11},{9,10},{10,... | collective-permute-start | bytes 589832 | tf_op jit(solution)/shard_map/ppermute | solution.py:337
  15.8 2.9 %early.1 = (f32[16,512]{1,0:T(8,128)S(1)}, bf16[2,256,512]{2,1,0:T(8,128)(2,1)S(1)}, bf16[2,2,256,512]{3,2,1,0:T(8,128)(2,1)S(1)}, f32[2,256,256]{2,1,0:T(8,128)...) custom-call(f32[4,128,512]{2,1,0:T(8,128)S(1)} %get-tuple-element.37.own, ...), custom_call_target="tpu_custom_call" | custom-call | tf_op jit(solution)/shard_map/early/pallas_call | solution.py:343
  18.7 1.3 %collective-permute-done.6.refs_0_ = f32[4,224,128]{2,1,0:T(8,128)S(1)} collective-permute-done((f32[4,224,128]{2,1,0:T(8,128)S(1)}, f32[4,224,128]{2,1,0:T(8,128)S(1)}, u32[]{:S(2)}, u32[]{:S(2)}) %collective-permute-start.6) | collective-permute-done | bytes 458784 | tf_op jit(solution)/shard_map/ppermute | solution.py:337
  20.1 2.5 %middle.1 = (f32[512,512]{1,0:T(8,128)S(1)}, f32[512,512]{1,0:T(8,128)S(1)}, f32[2,512,128]{2,1,0:T(8,128)S(1)}, f32[2,128,512]{2,1,0:T(8,128)S(1)}) custom-call(bf16[2,256,512]{2,1,0:T(8,128)(2,1)S(1)} %get-tuple-element.43.a_far, bf16[2,2,256,512]{3,2,1,0:T(8,128)(2,1)S(1)} %get-tuple-element.44.l_known, f32[2,256,256]{2,1,0:T(8,128)S(1)} %get-tuple-element.45.c_known, ...), custom_call_target="tpu_custom_call" | custom-call | tf_op jit(solution)/shard_map/middle/pallas_call | solution.py:343
  22.6 1.3 %late.1 = (f32[512,512]{1,0:T(8,128)S(1)}, f32[512,512]{1,0:T(8,128)S(1)}, f32[1,512]{1,0:T(1,128)S(1)}) custom-call(f32[1,512]{1,0:T(1,128)S(1)} %get-tuple-element.35.after.first.refs_0_, f32[16,512]{1,0:T(8,128)S(1)} %get-tuple-element.42.info, bf16[2,256,512]{2,1,0:T(8,128)(2,1)S(1)} %get-tuple-element.43.a_far, f32[512,512]{1,0:T(8,128)S(1)} %get-tuple-element.49.ga, ...), custom_call_target="tpu_custom_call" | custom-call | tf_op jit(solution)/shard_map/late/pallas_call | solution.py:343
  23.9 0.7 %collective-permute-start.8 = (f32[1,512]{1,0:T(1,128)S(1)}, f32[1,512]{1,0:T(1,128)S(1)}, u32[]{:S(2)}, u32[]{:S(2)}) collective-permute-start(f32[1,512]{1,0:T(1,128)S(1)} %get-tuple-element.54), channel_id=1, source_target_pairs={{0,1},{1,0},{2,3},{3,2},{4,5},{5,4},{6,7},{7,6},{8,9},{9,8},{10,11... | collective-permute-start | bytes 6152 | tf_op jit(solution)/shard_map/ppermute | solution.py:337
  24.6 1.0 %pair.1.late.refs_10_ = f32[520,512]{1,0:T(8,128)S(1)} custom-call(f32[16,512]{1,0:T(8,128)S(1)} %get-tuple-element.42.info, f32[512,512]{1,0:T(8,128)S(1)} %get-tuple-element.55.ga, f32[512,512]{1,0:T(8,128)S(1)} %get-tuple-element.60.gb.refs_11_), custom_call_target="tpu_custom_call" | custom-call | tf_op jit(solution)/shard_map/pair/pallas_call | solution.py:343
  25.8 0.3 two.1
  26.1 1.6 %collective-permute-start.9 = (f32[1,512]{1,0:T(1,128)S(1)}, f32[1,512]{1,0:T(1,128)S(1)}, u32[]{:S(2)}, u32[]{:S(2)}) collective-permute-start(f32[1,512]{1,0:T(1,128)S(1)} %two.1), channel_id=1, source_target_pairs={{0,5},{1,4},{2,7},{3,6},{4,1},{5,0},{6,3},{7,2},{8,13},{9,12},{10,... | collective-permute-start | bytes 6152 | tf_op jit(solution)/shard_map/ppermute | solution.py:337
  27.7 0.7 %collective-permute-done.10.early.refs_12_ = f32[520,512]{1,0:T(8,128)S(1)} collective-permute-done((f32[520,512]{1,0:T(8,128)S(1)}, f32[520,512]{1,0:T(8,128)S(1)}, u32[]{:S(2)}, u32[]{:S(2)}) %collective-permute-start.10) | collective-permute-done | bytes 1064992 | tf_op jit(solution)/shard_map/ppermute | solution.py:337
  28.4 1.0 %block.1 = (f32[512,512]{1,0:T(8,128)S(1)}, f32[8,512]{1,0:T(8,128)S(1)}) custom-call(f32[520,512]{1,0:T(8,128)S(1)} %pair.1.late.refs_10_, f32[520,512]{1,0:T(8,128)S(1)} %collective-permute-done.10.early.refs_12_), custom_call_target="tpu_custom_call" | custom-call | tf_op jit(solution)/shard_map/block/pallas_call | solution.py:343
  29.8 1.0 %collective-permute-done.11.x.refs_2_ = f32[1,512]{1,0:T(1,128)S(1)} collective-permute-done((f32[1,512]{1,0:T(1,128)S(1)}, f32[1,512]{1,0:T(1,128)S(1)}, u32[]{:S(2)}, u32[]{:S(2)}) %collective-permute-start.11) | collective-permute-done | bytes 2080 | tf_op jit(solution)/shard_map/ppermute | solution.py:459
  31.1 0.4 collective-permute-start.12
  31.4 2.0 %collective-permute-done.12.x.refs_3_ = f32[1,512]{1,0:T(1,128)S(1)} collective-permute-done((f32[1,512]{1,0:T(1,128)S(1)}, f32[1,512]{1,0:T(1,128)S(1)}, u32[]{:S(2)}, u32[]{:S(2)}) %collective-permute-start.12) | collective-permute-done | bytes 2080 | tf_op jit(solution)/shard_map/ppermute | solution.py:459
  33.8 1.0 %collective-permute-done.13.x.refs_4_ = f32[1,512]{1,0:T(1,128)S(1)} collective-permute-done((f32[1,512]{1,0:T(1,128)S(1)}, f32[1,512]{1,0:T(1,128)S(1)}, u32[]{:S(2)}, u32[]{:S(2)}) %collective-permute-start.13) | collective-permute-done | bytes 2080 | tf_op jit(solution)/shard_map/ppermute | solution.py:459
  35.2 1.0 %collective-permute-done.14.x.refs_5_ = f32[1,512]{1,0:T(1,128)S(1)} collective-permute-done((f32[1,512]{1,0:T(1,128)S(1)}, f32[1,512]{1,0:T(1,128)S(1)}, u32[]{:S(2)}, u32[]{:S(2)}) %collective-permute-start.14) | collective-permute-done | bytes 2080 | tf_op jit(solution)/shard_map/ppermute | solution.py:459
  36.6 1.0 %collective-permute-done.15.x.refs_6_ = f32[1,512]{1,0:T(1,128)S(1)} collective-permute-done((f32[1,512]{1,0:T(1,128)S(1)}, f32[1,512]{1,0:T(1,128)S(1)}, u32[]{:S(2)}, u32[]{:S(2)}) %collective-permute-start.15) | collective-permute-done | bytes 2080 | tf_op jit(solution)/shard_map/ppermute | solution.py:459
  37.7 0.6 %collective-permute-start.16 = (f32[1,512]{1,0:T(1,128)S(1)}, f32[1,512]{1,0:T(1,128)S(1)}, u32[]{:S(2)}, u32[]{:S(2)}) collective-permute-start(f32[1,512]{1,0:T(1,128)S(1)} %hop.11), channel_id=1, source_target_pairs={{0,2},{1,5},{2,3},{3,0},{4,6},{5,1},{6,7},{7,4},{8,9},{9,8},{10,11... | collective-permute-start | bytes 6152 | tf_op jit(solution)/shard_map/ppermute | solution.py:459
  38.3 2.5 %collective-permute-done.16.refs_7_ = f32[1,512]{1,0:T(1,128)S(1)} collective-permute-done((f32[1,512]{1,0:T(1,128)S(1)}, f32[1,512]{1,0:T(1,128)S(1)}, u32[]{:S(2)}, u32[]{:S(2)}) %collective-permute-start.16) | collective-permute-done | bytes 2080 | tf_op jit(solution)/shard_map/ppermute | solution.py:459
  40.8 0.4 last.1
  41.3 6.2 %collective-permute-start.19 = (f32[4,128]{1,0:T(4,128)S(1)}, f32[4,128]{1,0:T(4,128)S(1)}, u32[]{:S(2)}, u32[]{:S(2)}) collective-permute-start(f32[4,128]{1,0:T(4,128)S(1)} %get-tuple-element.63), channel_id=1, source_target_pairs={{0,2},{1,3},{2,0},{3,1},{4,6},{5,7},{6,4},{7,5},{8,10},{9,11},{10,... | collective-permute-start | bytes 6152 | tf_op jit(solution)/shard_map/ppermute | solution.py:337
  47.5 1.6 %collective-permute-done.19.refs_2_ = f32[4,128]{1,0:T(4,128)S(1)} collective-permute-done((f32[4,128]{1,0:T(4,128)S(1)}, f32[4,128]{1,0:T(4,128)S(1)}, u32[]{:S(2)}, u32[]{:S(2)}) %collective-permute-start.19) | collective-permute-done | bytes 2080 | tf_op jit(solution)/shard_map/ppermute | solution.py:337
  49.1 0.6 %out.1 = f32[4,128]{1,0:T(4,128)} custom-call(f32[4,128]{1,0:T(4,128)S(1)} %get-tuple-element.61.refs_0_, f32[4,128]{1,0:T(4,128)S(1)} %collective-permute-done.18.refs_1_, f32[4,128]{1,0:T(4,128)S(1)} %collective-permute-done.19.refs_2_, f32[4,128]{1,0:T(4,128)S(1)} %collective-permute-done.20.refs_3_), custom_call_target="tpu_custom_call" | custom-call | tf_op jit(solution)/shard_map/out/pallas_call | solution.py:343
  (30 shorter events, 2.6 us)
Async XLA Ops:
  1.6 5.1 %copy-start = (f32[128,512]{1,0:T(8,128)S(1)}, f32[128,512]{1,0:T(8,128)}, u32[]{:S(2)}) copy-start(f32[128,512]{1,0:T(8,128)} %trans.3) | copy-start | bytes 786436
  1.6 6.5 %collective-permute-start = (f32[64,512]{1,0:T(8,128)S(1)}, f32[64,512]{1,0:T(8,128)S(1)}, u32[]{:S(2)}, u32[]{:S(2)}) collective-permute-start(f32[64,512]{1,0:T(8,128)S(1)} %get-tuple-element.36), channel_id=1, source_target_pairs={{0,2},{1,3},{2,0},{3,1},{4,6},{5,7},{6,4},{7,5},{8,10},{9,11},{10,... | collective-permute-start | bytes 393224 | tf_op jit(solution)/shard_map/ppermute | solution.py:337
  6.1 9.7 %collective-permute-start.4 = (f32[256,512]{1,0:T(8,128)S(1)}, f32[256,512]{1,0:T(8,128)S(1)}, u32[]{:S(2)}, u32[]{:S(2)}) collective-permute-start(f32[256,512]{1,0:T(8,128)S(1)} %get-tuple-element.40), channel_id=1, source_target_pairs={{0,1},{1,0},{2,3},{3,2},{4,5},{5,4},{6,7},{7,6},{8,9},{9,8},{10,11... | collective-permute-start | bytes 1572872 | tf_op jit(solution)/shard_map/ppermute | solution.py:337
  6.2 9.6 %collective-permute-start.5 = (f32[256,512]{1,0:T(8,128)S(1)}, f32[256,512]{1,0:T(8,128)S(1)}, u32[]{:S(2)}, u32[]{:S(2)}) collective-permute-start(f32[256,512]{1,0:T(8,128)S(1)} %get-tuple-element.41), channel_id=1, source_target_pairs={{0,1},{1,0},{2,3},{3,2},{4,5},{5,4},{6,7},{7,6},{8,9},{9,8},{10,11... | collective-permute-start | bytes 1572872 | tf_op jit(solution)/shard_map/ppermute | solution.py:337
  6.7 13.4 %collective-permute-start.6 = (f32[4,224,128]{2,1,0:T(8,128)S(1)}, f32[4,224,128]{2,1,0:T(8,128)S(1)}, u32[]{:S(2)}, u32[]{:S(2)}) collective-permute-start(f32[4,224,128]{2,1,0:T(8,128)S(1)} %get-tuple-element.48), channel_id=1, source_target_pairs={{0,2},{1,3},{2,0},{3,1},{4,6},{5,7},{6,4},{7,5},{8,10},{9,11},{10,... | collective-permute-start | bytes 1376264 | tf_op jit(solution)/shard_map/ppermute | solution.py:337
  6.7 7.1 %collective-permute-start.1 = (f32[128,512]{1,0:T(8,128)S(1)}, f32[128,512]{1,0:T(8,128)S(1)}, u32[]{:S(2)}, u32[]{:S(2)}) collective-permute-start(f32[128,512]{1,0:T(8,128)S(1)} %copy-done), channel_id=1, source_target_pairs={{0,1},{1,0},{2,3},{3,2},{4,5},{5,4},{6,7},{7,6},{8,9},{9,8},{10,11... | collective-permute-start | bytes 786440 | tf_op jit(solution)/shard_map/ppermute | solution.py:337
  8.1 5.0 %collective-permute-start.2 = (f32[64,512]{1,0:T(8,128)S(1)}, f32[64,512]{1,0:T(8,128)S(1)}, u32[]{:S(2)}, u32[]{:S(2)}) collective-permute-start(f32[64,512]{1,0:T(8,128)S(1)} %collective-permute-done.after.refs_0_), channel_id=1, source_target_pairs={{0,4},{1,5},{2,6},{3,7},{4,0},{5,1},{6,2},{7,3},{8,12},{9,13},{10,... | collective-permute-start | bytes 393224 | tf_op jit(solution)/shard_map/ppermute | solution.py:337
  13.7 2.1 %collective-permute-start.3 = (f32[1,128,512]{2,1,0:T(8,128)S(1)}, f32[1,128,512]{2,1,0:T(8,128)S(1)}, u32[]{:S(2)}, u32[]{:S(2)}) collective-permute-start(f32[1,128,512]{2,1,0:T(8,128)S(1)} %join.1.joined), channel_id=1, source_target_pairs={{0,1},{1,0},{2,3},{3,2},{4,5},{5,4},{6,7},{7,6},{8,9},{9,8},{10,11... | collective-permute-start | bytes 786440 | tf_op jit(solution)/shard_map/ppermute | solution.py:337
  13.8 8.8 %collective-permute-start.7 = (f32[4,96,128]{2,1,0:T(8,128)S(1)}, f32[4,96,128]{2,1,0:T(8,128)S(1)}, u32[]{:S(2)}, u32[]{:S(2)}) collective-permute-start(f32[4,96,128]{2,1,0:T(8,128)S(1)} %get-tuple-element.53), channel_id=1, source_target_pairs={{0,3},{1,2},{2,1},{3,0},{4,7},{5,6},{6,5},{7,4},{8,11},{9,10},{10,... | collective-permute-start | bytes 589832 | tf_op jit(solution)/shard_map/ppermute | solution.py:337
  23.9 1.7 %collective-permute-start.8 = (f32[1,512]{1,0:T(1,128)S(1)}, f32[1,512]{1,0:T(1,128)S(1)}, u32[]{:S(2)}, u32[]{:S(2)}) collective-permute-start(f32[1,512]{1,0:T(1,128)S(1)} %get-tuple-element.54), channel_id=1, source_target_pairs={{0,1},{1,0},{2,3},{3,2},{4,5},{5,4},{6,7},{7,6},{8,9},{9,8},{10,11... | collective-permute-start | bytes 6152 | tf_op jit(solution)/shard_map/ppermute | solution.py:337
  25.6 2.7 %collective-permute-start.10 = (f32[520,512]{1,0:T(8,128)S(1)}, f32[520,512]{1,0:T(8,128)S(1)}, u32[]{:S(2)}, u32[]{:S(2)}) collective-permute-start(f32[520,512]{1,0:T(8,128)S(1)} %pair.1.late.refs_10_), channel_id=1, source_target_pairs={{0,1},{1,0},{2,3},{3,2},{4,5},{5,4},{6,7},{7,6},{8,9},{9,8},{10,11... | collective-permute-start | bytes 3194888 | tf_op jit(solution)/shard_map/ppermute | solution.py:337
  26.1 3.3 %collective-permute-start.9 = (f32[1,512]{1,0:T(1,128)S(1)}, f32[1,512]{1,0:T(1,128)S(1)}, u32[]{:S(2)}, u32[]{:S(2)}) collective-permute-start(f32[1,512]{1,0:T(1,128)S(1)} %two.1), channel_id=1, source_target_pairs={{0,5},{1,4},{2,7},{3,6},{4,1},{5,0},{6,3},{7,2},{8,13},{9,12},{10,... | collective-permute-start | bytes 6152 | tf_op jit(solution)/shard_map/ppermute | solution.py:337
  29.6 1.2 %collective-permute-start.11 = (f32[1,512]{1,0:T(1,128)S(1)}, f32[1,512]{1,0:T(1,128)S(1)}, u32[]{:S(2)}, u32[]{:S(2)}) collective-permute-start(f32[1,512]{1,0:T(1,128)S(1)} %hop.6), channel_id=1, source_target_pairs={{0,1},{1,0},{2,3},{3,2},{4,5},{5,4},{6,7},{7,6},{8,9},{9,8},{10,11... | collective-permute-start | bytes 6152 | tf_op jit(solution)/shard_map/ppermute | solution.py:459
  30.7 10.1 %collective-permute-start.17 = (f32[512,512]{1,0:T(8,128)S(1)}, f32[512,512]{1,0:T(8,128)S(1)}, u32[]{:S(2)}, u32[]{:S(2)}) collective-permute-start(f32[512,512]{1,0:T(8,128)S(1)} %get-tuple-element.60.gb.refs_11_), channel_id=1, source_target_pairs={{0,1},{1,0},{2,3},{3,2},{4,5},{5,4},{6,7},{7,6},{8,9},{9,8},{10,11... | collective-permute-start | bytes 3145736 | tf_op jit(solution)/shard_map/ppermute | solution.py:337
  31.1 2.3 %collective-permute-start.12 = (f32[1,512]{1,0:T(1,128)S(1)}, f32[1,512]{1,0:T(1,128)S(1)}, u32[]{:S(2)}, u32[]{:S(2)}) collective-permute-start(f32[1,512]{1,0:T(1,128)S(1)} %hop.7), channel_id=1, source_target_pairs={{0,1},{1,0},{2,3},{3,2},{4,5},{5,4},{6,7},{7,6},{8,9},{9,8},{10,11... | collective-permute-start | bytes 6152 | tf_op jit(solution)/shard_map/ppermute | solution.py:459
  33.6 1.2 %collective-permute-start.13 = (f32[1,512]{1,0:T(1,128)S(1)}, f32[1,512]{1,0:T(1,128)S(1)}, u32[]{:S(2)}, u32[]{:S(2)}) collective-permute-start(f32[1,512]{1,0:T(1,128)S(1)} %hop.8), channel_id=1, source_target_pairs={{0,1},{1,0},{2,3},{3,2},{4,5},{5,4},{6,7},{7,6},{8,9},{9,8},{10,11... | collective-permute-start | bytes 6152 | tf_op jit(solution)/shard_map/ppermute | solution.py:459
  34.9 1.2 %collective-permute-start.14 = (f32[1,512]{1,0:T(1,128)S(1)}, f32[1,512]{1,0:T(1,128)S(1)}, u32[]{:S(2)}, u32[]{:S(2)}) collective-permute-start(f32[1,512]{1,0:T(1,128)S(1)} %hop.9), channel_id=1, source_target_pairs={{0,1},{1,0},{2,3},{3,2},{4,5},{5,4},{6,7},{7,6},{8,10},{9,13},{10,... | collective-permute-start | bytes 6152 | tf_op jit(solution)/shard_map/ppermute | solution.py:459
  36.3 1.2 %collective-permute-start.15 = (f32[1,512]{1,0:T(1,128)S(1)}, f32[1,512]{1,0:T(1,128)S(1)}, u32[]{:S(2)}, u32[]{:S(2)}) collective-permute-start(f32[1,512]{1,0:T(1,128)S(1)} %hop.10), channel_id=1, source_target_pairs={{0,1},{1,0},{2,3},{3,2},{4,6},{5,9},{6,7},{7,4},{8,10},{9,5},{10,1... | collective-permute-start | bytes 6152 | tf_op jit(solution)/shard_map/ppermute | solution.py:459
  37.7 3.1 %collective-permute-start.16 = (f32[1,512]{1,0:T(1,128)S(1)}, f32[1,512]{1,0:T(1,128)S(1)}, u32[]{:S(2)}, u32[]{:S(2)}) collective-permute-start(f32[1,512]{1,0:T(1,128)S(1)} %hop.11), channel_id=1, source_target_pairs={{0,2},{1,5},{2,3},{3,0},{4,6},{5,1},{6,7},{7,4},{8,9},{9,8},{10,11... | collective-permute-start | bytes 6152 | tf_op jit(solution)/shard_map/ppermute | solution.py:459
  41.2 6.3 %collective-permute-start.18 = (f32[4,128]{1,0:T(4,128)S(1)}, f32[4,128]{1,0:T(4,128)S(1)}, u32[]{:S(2)}, u32[]{:S(2)}) collective-permute-start(f32[4,128]{1,0:T(4,128)S(1)} %get-tuple-element.62), channel_id=1, source_target_pairs={{0,3},{1,2},{2,1},{3,0},{4,7},{5,6},{6,5},{7,4},{8,11},{9,10},{10,... | collective-permute-start | bytes 6152 | tf_op jit(solution)/shard_map/ppermute | solution.py:337
  41.3 7.8 %collective-permute-start.19 = (f32[4,128]{1,0:T(4,128)S(1)}, f32[4,128]{1,0:T(4,128)S(1)}, u32[]{:S(2)}, u32[]{:S(2)}) collective-permute-start(f32[4,128]{1,0:T(4,128)S(1)} %get-tuple-element.63), channel_id=1, source_target_pairs={{0,2},{1,3},{2,0},{3,1},{4,6},{5,7},{6,4},{7,5},{8,10},{9,11},{10,... | collective-permute-start | bytes 6152 | tf_op jit(solution)/shard_map/ppermute | solution.py:337
  47.5 1.6 %collective-permute-start.20 = (f32[4,128]{1,0:T(4,128)S(1)}, f32[4,128]{1,0:T(4,128)S(1)}, u32[]{:S(2)}, u32[]{:S(2)}) collective-permute-start(f32[4,128]{1,0:T(4,128)S(1)} %get-tuple-element.64), channel_id=1, source_target_pairs={{0,1},{1,0},{2,3},{3,2},{4,5},{5,4},{6,7},{7,6},{8,9},{9,8},{10,11... | collective-permute-start | bytes 6152 | tf_op jit(solution)/shard_map/ppermute | solution.py:337

commit v13 on v12

--- a/solution.py
+++ b/solution.py
@@ -55,21 +55,31 @@
 
 def far_shape(devices, count, panel, order, off):
     if trimmed(devices, panel):
-        return (2 * count, panel * 3 // 4 + (panel if off == 2 else 0), panel)
+        return (2 * count, panel * 5 // 8 + (panel if off == 2 else 0), panel)
     return (2 * count, panel, order - 2 * panel)
 
 
+def lanes(rows):
+    return lax.broadcasted_iota(jnp.int32, (rows, 128), 1)
+
+
 def fold(block):
-    lane = lax.broadcasted_iota(jnp.int32, (32, 128), 1)
-    return jnp.concatenate([block[:64], jnp.where(lane < 64, pltpu.roll(block[64:96], 64, 1), block[96:])], axis=0)
+    corner = jnp.where(lanes(32) < 32, pltpu.roll(block[96:], 32, 1), block[32:64])
+    third = jnp.where(lanes(16) < 64, pltpu.roll(block[64:80], 64, 1), block[80:96])
+    return jnp.concatenate([block[:32], corner, third], axis=0)
 
 
 def unfold(folded):
-    top, right = folded[:64], folded[64:]
-    lane = lax.broadcasted_iota(jnp.int32, (64, 128), 1)
-    mirrored = jnp.concatenate([top, top], axis=0).T[64:]
-    lower = jnp.where(lane < 64, mirrored, jnp.concatenate([pltpu.roll(right, 64, 1), right], axis=0))
-    return jnp.concatenate([top, lower], axis=0)
+    corner, third = folded[32:64], folded[64:]
+    upper = jnp.concatenate(
+        [folded[:64], pltpu.roll(third, 64, 1), third, pltpu.roll(corner, 96, 1)], axis=0
+    )
+    row = lax.broadcasted_iota(jnp.int32, (128, 128), 0)
+    return jnp.where(row // 32 <= lanes(128) // 32, upper, upper.T)
+
+
+def base(device, count):
+    return (1 - device % 2) * count
 
 
 def pack_kernel(devices, cov, prec, trans, terminal, *refs):
@@ -84,7 +94,7 @@
         for k, matrix in enumerate((cov, prec)):
             start(matrix.at[:, :, rows(s, panel)], diagonal.at[k])
     for off, piece in enumerate(far, 2):
-        theirs = pl.ds(((s ^ off) % 2) * count, count)
+        theirs = pl.ds(base(s ^ off, count), count)
         for k, matrix in enumerate((cov, prec)):
             target = piece.at[pl.ds(k * count, count)]
             if not trim:
@@ -98,8 +108,8 @@
     if trim:
         for off, piece in enumerate(far, 2):
             for k in range(2 * count):
-                block = diagonal[k // count, ((s ^ off) % 2) * count + k % count]
-                piece[k, piece.shape[1] - panel * 3 // 4 :, :] = fold(block)
+                block = diagonal[k // count, base(s ^ off, count) + k % count]
+                piece[k, piece.shape[1] - panel * 5 // 8 :, :] = fold(block)
 
 
 def near_kernel(cov, prec, trans, after, near_cov, near_prec, near_trans, sems):
@@ -116,7 +126,7 @@
 def near_kernel(cov, prec, after, *refs):
     pieces, sems = refs[:-1], refs[-1]
     count, panel = cov.shape[0] // 2, cov.shape[1]
-    first = (1 - lax.axis_index("state") % 2) * count
+    first = base(lax.axis_index("state") ^ 1, count)
     start, copies = starter(sems)
     for k in range(2 * count):
         matrix = (cov, prec)[k // count]
@@ -127,18 +137,18 @@
 
 
 def spans(pieces, k, panel):
-    found, base = [], 0
+    found, at = [], 0
     for i, piece in enumerate(pieces):
-        low, high = max(base, k * panel), min(base + piece.shape[0], (k + 1) * panel)
+        low, high = max(at, k * panel), min(at + piece.shape[0], (k + 1) * panel)
         if low < high:
-            found.append((i, low - base, low - k * panel, high - low))
-        base += piece.shape[0]
+            found.append((i, low - at, low - k * panel, high - low))
+        at += piece.shape[0]
     return found
 
 
 def own_kernel(cov, prec, trans, means, after, own, own_trans, own_means, sems):
     count = cov.shape[0] // 2
-    mine = pl.ds((lax.axis_index("state") % 2) * count, count)
+    mine = pl.ds(base(lax.axis_index("state"), count), count)
     start, copies = starter(sems)
     start(cov.at[mine], own.at[pl.ds(0, count)])
     start(prec.at[mine], own.at[pl.ds(count, count)])
@@ -168,10 +178,10 @@
     e = lax.axis_index("state") % 2
     start, copies = starter(sems)
     for k in range(2 * count):
-        target, base = (pf, k * known) if k < count else (lf.at[k - count], 0)
-        start(own.at[k], target.at[pl.ds(pl.multiple_of(base + e * panel, panel), panel), :])
+        target, top = (pf, k * known) if k < count else (lf.at[k - count], 0)
+        start(own.at[k], target.at[pl.ds(pl.multiple_of(top + e * panel, panel), panel), :])
         for piece, at, row, size in spans(near, k, panel):
-            to = pl.multiple_of(base + (1 - e) * panel + row, 8)
+            to = pl.multiple_of(top + (1 - e) * panel + row, 8)
             start(near[piece].at[pl.ds(at, size), :], target.at[pl.ds(to, size), :])
     for j in range(order // known):
         mine, theirs = (joined.at[j - 1], joined_near.at[j - 1]) if j else (trans, trans_near)
@@ -199,7 +209,7 @@
 
 
 def steps_of(info, count):
-    a = (lax.axis_index("state") % 2) * count
+    a = base(lax.axis_index("state"), count)
     return [info[pl.ds(a + shift, 1), :] for shift in (0, 1, 8, 9)]
 
 
@@ -246,7 +256,7 @@
 
 
 def steps_of(info, count):
-    a = (lax.axis_index("state") % 2) * count
+    a = base(lax.axis_index("state"), count)
     return [info[pl.ds(a + shift, 1), :] for shift in (0, 1, 8, 9)]
 
 
@@ -288,6 +298,12 @@
     )
     vec_ref[...] = jnp.concatenate([late[order + 2 : order + 3, :], shift, jnp.zeros((6, order), F32)], axis=0)
     m_ref[...] = dot3(early[:order, :], late[:order, :], NN)
+
+
+def pair_hop_kernel(x, late, early, out_ref):
+    order = x.shape[1]
+    y = late[order : order + 1, :] + matvec(late[:order, :], x[...] - late[order + 2 : order + 3, :])
+    out_ref[...] = early[order : order + 1, :] + matvec(early[:order, :], y - early[order + 2 : order + 3, :])
 
 
 def hop_kernel(x, m, vec, out_ref):
@@ -444,21 +460,23 @@
         (first, info, a_far, ga, gb, col, h, *last),
     )
     mean = swap(mean, 1)
-    (late_map,) = call(pair_kernel, "pair", 12, [shape(order + 8, order)], [VMEM] * 3, [], (info, ga, gb))
-    early_map = swap(lax.optimization_barrier((late_map, mean))[0], 1)
+    (early_map,) = call(pair_kernel, "pair", 12, [shape(order + 8, order)], [VMEM] * 3, [], (info, ga, gb))
+    late_map = swap(lax.optimization_barrier((early_map, mean))[0], 1)
     (mean,) = call(two_kernel, "two", 6, [shape(1, order)], [VMEM] * 4, [], (mean, info, ga, gb))
 
-    incoming = [first, swap(mean, 1, 1)]
+    incoming = [first, swap(mean, 0, 1)]
+    (x,) = call(pair_hop_kernel, "pair_hop", 4, [shape(1, order)], [VMEM] * 3, [], (incoming[-1], late_map, early_map))
     m, vec = call(block_kernel, "block", 12, [square, shape(8, order)], [VMEM] * 2, [], (late_map, early_map))
     for block in range(blocks - 2, 0, -1):
-        (x,) = call(hop_kernel, "hop", 4, [shape(1, order)], [VMEM] * 3, [], (incoming[-1], m, vec))
+        if block < blocks - 2:
+            (x,) = call(hop_kernel, "hop", 4, [shape(1, order)], [VMEM] * 3, [], (incoming[-1], m, vec))
         target = {i: i ^ 1 for i in range(blocks * devices)}
         for at, to in ((block, block - 1), (block - 1, block)):
             target[at * devices + 1] = to * devices + 1
             target.update({at * devices + i: at * devices + j for i, j in ((0, 2), (2, 3), (3, 0))})
         x = lax.ppermute(x, ("tm", "state"), list(target.items()))
         incoming.append(x)
-    g1 = swap(lax.optimization_barrier((gb, incoming[2]))[0], 1)
+    g3 = swap(lax.optimization_barrier((gb, incoming[3]))[0], 1)
 
     given = list(call(
         functools.partial(last_kernel, devices),
@@ -467,7 +485,7 @@
         [shape(steps, panel)] * devices,
         [VMEM] * (blocks + 6),
         [pltpu.VMEM((devices, steps, panel), F32)],
-        (*incoming, m, vec, late_map, gb, early_map, g1),
+        (*incoming, m, vec, late_map, g3, early_map, gb),
     ))
     for off in range(devices - 1, 0, -1):
         given[off] = swap(given[off], off)

time: 49.8 us -> 48.5 us (0.974)
  starting transfers between devices: 18.4 us -> 17.5 us
  waiting for transfers between devices: 14.9 us -> 14.2 us
    ppermute x6, waiting for transfers between devices: 8.31 us -> 6.83 us  [local(): x = lax.ppermute(x, ('tm', 'state'), list(target.items()))]
    ppermute x15, starting transfers between devices: 16.4 us -> 15.2 us  [swap(): return lax.ppermute(x, ('tm', 'state'), pairs)]
    ppermute x15, waiting for transfers between devices: 6.59 us -> 7.41 us  [swap(): return lax.ppermute(x, ('tm', 'state'), pairs)]
  transfers between devices with their start and end apart: 21 -> 21, of which waited for: 11 -> 12; matrix products, arithmetic and copies ran while one was open for 0% -> 0% of each run, Pallas kernels for 24% -> 25%
where the time goes in v13:
time: 48.5 us; the launch traced here: 48.3 us
  starting transfers between devices  17.5 us (36%)
  Pallas kernels  16.3 us (34%)
  waiting for transfers between devices  14.2 us (29%)
    pallas_call x18, Pallas kernels, call(): pl.pallas_call(kernel, out_shape=outs, in_specs=in_specs, out_specs=[VMEM...  16.3 us
    ppermute x15, starting transfers between devices, swap(): return lax.ppermute(x, ('tm', 'state'), pairs)  15.2 us
    ppermute x15, waiting for transfers between devices, swap(): return lax.ppermute(x, ('tm', 'state'), pairs)  7.41 us
    ppermute x6, waiting for transfers between devices, local(): x = lax.ppermute(x, ('tm', 'state'), list(target.items()))  6.83 us
    ppermute x6, starting transfers between devices, local(): x = lax.ppermute(x, ('tm', 'state'), list(target.items()))  2.3 us
  transfers between devices with their start and end apart: 21, of which 12 were waited for; matrix products, arithmetic and copies ran while one was open for 0% of the time, Pallas kernels for 25%

profile of v13, /device:TPU:0, one launch (start us, length us, event | category | flops | bytes accessed | tf_op | source)
XLA Modules:
  0.0 48.3 jit_solution(17912553483774292930)
XLA Ops:
  0.0 1.6 %pack.1 = (f32[4,208,128]{2,1,0:T(8,128)S(1)}, f32[4,80,128]{2,1,0:T(8,128)S(1)}, f32[64,512]{1,0:T(8,128)S(1)}, f32[1,512]{1,0:T(1,128)S(1)}) custom-call(f32[4,128,512]{2,1,0:T(8,128)} %cov.5, f32[4,128,512]{2,1,0:T(8,128)} %prec.5, f32[128,512]{1,0:T(8,128)} %trans.3, f32[1,512]{1,0:T(1,128)} %bitcast.1), custom_call_target="tpu_custom_call" | custom-call | tf_op jit(solution)/shard_map/pack/pallas_call | solution.py:359
  1.6 3.0 %collective-permute-start = (f32[64,512]{1,0:T(8,128)S(1)}, f32[64,512]{1,0:T(8,128)S(1)}, u32[]{:S(2)}, u32[]{:S(2)}) collective-permute-start(f32[64,512]{1,0:T(8,128)S(1)} %get-tuple-element.36), channel_id=1, source_target_pairs={{0,2},{1,3},{2,0},{3,1},{4,6},{5,7},{6,4},{7,5},{8,10},{9,11},{10,... | collective-permute-start | bytes 393224 | tf_op jit(solution)/shard_map/ppermute | solution.py:353
  4.6 1.5 %near.1 = (f32[256,512]{1,0:T(8,128)S(1)}, f32[256,512]{1,0:T(8,128)S(1)}) custom-call(f32[4,128,512]{2,1,0:T(8,128)} %cov.5, f32[4,128,512]{2,1,0:T(8,128)} %prec.5, f32[1,512]{1,0:T(1,128)S(1)} %get-tuple-element.35.after.first.refs_0_), custom_call_target="tpu_custom_call" | custom-call | tf_op jit(solution)/shard_map/near/pallas_call | solution.py:359
  6.2 0.5 %collective-permute-start.5 = (f32[256,512]{1,0:T(8,128)S(1)}, f32[256,512]{1,0:T(8,128)S(1)}, u32[]{:S(2)}, u32[]{:S(2)}) collective-permute-start(f32[256,512]{1,0:T(8,128)S(1)} %get-tuple-element.41), channel_id=1, source_target_pairs={{0,1},{1,0},{2,3},{3,2},{4,5},{5,4},{6,7},{7,6},{8,9},{9,8},{10,11... | collective-permute-start | bytes 1572872 | tf_op jit(solution)/shard_map/ppermute | solution.py:353
  6.8 1.4 %collective-permute-done.after.refs_0_ = f32[64,512]{1,0:T(8,128)S(1)} collective-permute-done((f32[64,512]{1,0:T(8,128)S(1)}, f32[64,512]{1,0:T(8,128)S(1)}, u32[]{:S(2)}, u32[]{:S(2)}) %collective-permute-start) | collective-permute-done | bytes 131104 | tf_op jit(solution)/shard_map/ppermute | solution.py:353
  8.1 1.8 %collective-permute-start.2 = (f32[64,512]{1,0:T(8,128)S(1)}, f32[64,512]{1,0:T(8,128)S(1)}, u32[]{:S(2)}, u32[]{:S(2)}) collective-permute-start(f32[64,512]{1,0:T(8,128)S(1)} %collective-permute-done.after.refs_0_), channel_id=1, source_target_pairs={{0,4},{1,5},{2,6},{3,7},{4,0},{5,1},{6,2},{7,3},{8,12},{9,13},{10,... | collective-permute-start | bytes 393224 | tf_op jit(solution)/shard_map/ppermute | solution.py:353
  9.9 1.6 %own.1 = (f32[4,128,512]{2,1,0:T(8,128)S(1)}, f32[128,512]{1,0:T(8,128)S(1)}, f32[4,512]{1,0:T(4,128)S(1)}) custom-call(f32[4,128,512]{2,1,0:T(8,128)} %cov.5, f32[4,128,512]{2,1,0:T(8,128)} %prec.5, f32[128,512]{1,0:T(8,128)} %trans.3, f32[4,512]{1,0:T(4,128)} %means.1, f32[64,512]{1,0:T(8,128)S(1)} %collective-permute-done.after.refs_0_), custom_call_target="tpu_custom_call" | custom-call | tf_op jit(solution)/shard_map/own/pallas_call | solution.py:359
  11.5 1.6 %collective-permute-done.2.refs_1_ = f32[64,512]{1,0:T(8,128)S(1)} collective-permute-done((f32[64,512]{1,0:T(8,128)S(1)}, f32[64,512]{1,0:T(8,128)S(1)}, u32[]{:S(2)}, u32[]{:S(2)}) %collective-permute-start.2) | collective-permute-done | bytes 131104 | tf_op jit(solution)/shard_map/ppermute | solution.py:353
  13.1 0.6 %join.1.joined = f32[1,128,512]{2,1,0:T(8,128)S(1)} custom-call(f32[128,512]{1,0:T(8,128)S(1)} %get-tuple-element.39.after.trans, f32[64,512]{1,0:T(8,128)S(1)} %collective-permute-done.after.refs_0_, f32[64,512]{1,0:T(8,128)S(1)} %collective-permute-done.2.refs_1_), custom_call_target="tpu_custom_call" | custom-call | tf_op jit(solution)/shard_map/join/pallas_call | solution.py:359
  13.8 2.0 %collective-permute-start.7 = (f32[4,80,128]{2,1,0:T(8,128)S(1)}, f32[4,80,128]{2,1,0:T(8,128)S(1)}, u32[]{:S(2)}, u32[]{:S(2)}) collective-permute-start(f32[4,80,128]{2,1,0:T(8,128)S(1)} %get-tuple-element.53), channel_id=1, source_target_pairs={{0,3},{1,2},{2,1},{3,0},{4,7},{5,6},{6,5},{7,4},{8,11},{9,10},{10,... | collective-permute-start | bytes 491528 | tf_op jit(solution)/shard_map/ppermute | solution.py:353
  15.8 2.9 %early.1 = (f32[16,512]{1,0:T(8,128)S(1)}, bf16[2,256,512]{2,1,0:T(8,128)(2,1)S(1)}, bf16[2,2,256,512]{3,2,1,0:T(8,128)(2,1)S(1)}, f32[2,256,256]{2,1,0:T(8,128)...) custom-call(f32[4,128,512]{2,1,0:T(8,128)S(1)} %get-tuple-element.37.own, ...), custom_call_target="tpu_custom_call" | custom-call | tf_op jit(solution)/shard_map/early/pallas_call | solution.py:359
  18.7 0.6 %collective-permute-done.6.refs_0_ = f32[4,208,128]{2,1,0:T(8,128)S(1)} collective-permute-done((f32[4,208,128]{2,1,0:T(8,128)S(1)}, f32[4,208,128]{2,1,0:T(8,128)S(1)}, u32[]{:S(2)}, u32[]{:S(2)}) %collective-permute-start.6) | collective-permute-done | bytes 426016 | tf_op jit(solution)/shard_map/ppermute | solution.py:353
  19.4 2.5 %middle.1 = (f32[512,512]{1,0:T(8,128)S(1)}, f32[512,512]{1,0:T(8,128)S(1)}, f32[2,512,128]{2,1,0:T(8,128)S(1)}, f32[2,128,512]{2,1,0:T(8,128)S(1)}) custom-call(bf16[2,256,512]{2,1,0:T(8,128)(2,1)S(1)} %get-tuple-element.43.a_far, bf16[2,2,256,512]{3,2,1,0:T(8,128)(2,1)S(1)} %get-tuple-element.44.l_known, f32[2,256,256]{2,1,0:T(8,128)S(1)} %get-tuple-element.45.c_known, ...), custom_call_target="tpu_custom_call" | custom-call | tf_op jit(solution)/shard_map/middle/pallas_call | solution.py:359
  21.9 1.3 %late.1 = (f32[512,512]{1,0:T(8,128)S(1)}, f32[512,512]{1,0:T(8,128)S(1)}, f32[1,512]{1,0:T(1,128)S(1)}) custom-call(f32[1,512]{1,0:T(1,128)S(1)} %get-tuple-element.35.after.first.refs_0_, f32[16,512]{1,0:T(8,128)S(1)} %get-tuple-element.42.info, bf16[2,256,512]{2,1,0:T(8,128)(2,1)S(1)} %get-tuple-element.43.a_far, f32[512,512]{1,0:T(8,128)S(1)} %get-tuple-element.49.ga, ...), custom_call_target="tpu_custom_call" | custom-call | tf_op jit(solution)/shard_map/late/pallas_call | solution.py:359
  23.3 1.0 %pair.1.early.refs_12_ = f32[520,512]{1,0:T(8,128)S(1)} custom-call(f32[16,512]{1,0:T(8,128)S(1)} %get-tuple-element.42.info, f32[512,512]{1,0:T(8,128)S(1)} %get-tuple-element.55.ga, f32[512,512]{1,0:T(8,128)S(1)} %get-tuple-element.60.gb.refs_13_), custom_call_target="tpu_custom_call" | custom-call | tf_op jit(solution)/shard_map/pair/pallas_call | solution.py:359
  24.5 0.4 collective-permute-start.10
  25.2 1.6 %collective-permute-start.9 = (f32[1,512]{1,0:T(1,128)S(1)}, f32[1,512]{1,0:T(1,128)S(1)}, u32[]{:S(2)}, u32[]{:S(2)}) collective-permute-start(f32[1,512]{1,0:T(1,128)S(1)} %two.1), channel_id=1, source_target_pairs={{0,4},{1,5},{2,6},{3,7},{4,0},{5,1},{6,2},{7,3},{8,12},{9,13},{10,... | collective-permute-start | bytes 6152 | tf_op jit(solution)/shard_map/ppermute | solution.py:353
  26.8 2.1 %collective-permute-done.9.x.refs_1_ = f32[1,512]{1,0:T(1,128)S(1)} collective-permute-done((f32[1,512]{1,0:T(1,128)S(1)}, f32[1,512]{1,0:T(1,128)S(1)}, u32[]{:S(2)}, u32[]{:S(2)}) %collective-permute-start.9) | collective-permute-done | bytes 2080 | tf_op jit(solution)/shard_map/ppermute | solution.py:353
  29.2 1.0 %block.1 = (f32[512,512]{1,0:T(8,128)S(1)}, f32[8,512]{1,0:T(8,128)S(1)}) custom-call(f32[520,512]{1,0:T(8,128)S(1)} %collective-permute-done.10.late.refs_10_, f32[520,512]{1,0:T(8,128)S(1)} %pair.1.early.refs_12_), custom_call_target="tpu_custom_call" | custom-call | tf_op jit(solution)/shard_map/block/pallas_call | solution.py:359
  30.5 0.4 collective-permute-start.12
  30.9 0.8 %collective-permute-done.12.x.refs_3_ = f32[1,512]{1,0:T(1,128)S(1)} collective-permute-done((f32[1,512]{1,0:T(1,128)S(1)}, f32[1,512]{1,0:T(1,128)S(1)}, u32[]{:S(2)}, u32[]{:S(2)}) %collective-permute-start.12) | collective-permute-done | bytes 2080 | tf_op jit(solution)/shard_map/ppermute | solution.py:477
  32.4 1.9 %collective-permute-done.13.x.refs_4_ = f32[1,512]{1,0:T(1,128)S(1)} collective-permute-done((f32[1,512]{1,0:T(1,128)S(1)}, f32[1,512]{1,0:T(1,128)S(1)}, u32[]{:S(2)}, u32[]{:S(2)}) %collective-permute-start.13) | collective-permute-done | bytes 2080 | tf_op jit(solution)/shard_map/ppermute | solution.py:477
  34.5 0.4 collective-permute-start.14
  35.0 0.8 %collective-permute-done.14.x.refs_5_ = f32[1,512]{1,0:T(1,128)S(1)} collective-permute-done((f32[1,512]{1,0:T(1,128)S(1)}, f32[1,512]{1,0:T(1,128)S(1)}, u32[]{:S(2)}, u32[]{:S(2)}) %collective-permute-start.14) | collective-permute-done | bytes 2080 | tf_op jit(solution)/shard_map/ppermute | solution.py:477
  35.9 0.4 collective-permute-start.15
  36.4 0.8 %collective-permute-done.15.x.refs_6_ = f32[1,512]{1,0:T(1,128)S(1)} collective-permute-done((f32[1,512]{1,0:T(1,128)S(1)}, f32[1,512]{1,0:T(1,128)S(1)}, u32[]{:S(2)}, u32[]{:S(2)}) %collective-permute-start.15) | collective-permute-done | bytes 2080 | tf_op jit(solution)/shard_map/ppermute | solution.py:477
  37.3 0.8 %collective-permute-start.16 = (f32[1,512]{1,0:T(1,128)S(1)}, f32[1,512]{1,0:T(1,128)S(1)}, u32[]{:S(2)}, u32[]{:S(2)}) collective-permute-start(f32[1,512]{1,0:T(1,128)S(1)} %hop.9), channel_id=1, source_target_pairs={{0,2},{1,5},{2,3},{3,0},{4,6},{5,1},{6,7},{7,4},{8,9},{9,8},{10,11... | collective-permute-start | bytes 6152 | tf_op jit(solution)/shard_map/ppermute | solution.py:477
  38.2 2.3 %collective-permute-done.16.refs_7_ = f32[1,512]{1,0:T(1,128)S(1)} collective-permute-done((f32[1,512]{1,0:T(1,128)S(1)}, f32[1,512]{1,0:T(1,128)S(1)}, u32[]{:S(2)}, u32[]{:S(2)}) %collective-permute-start.16) | collective-permute-done | bytes 2080 | tf_op jit(solution)/shard_map/ppermute | solution.py:477
  40.4 0.4 last.1
  40.9 5.2 %collective-permute-start.19 = (f32[4,128]{1,0:T(4,128)S(1)}, f32[4,128]{1,0:T(4,128)S(1)}, u32[]{:S(2)}, u32[]{:S(2)}) collective-permute-start(f32[4,128]{1,0:T(4,128)S(1)} %get-tuple-element.63), channel_id=1, source_target_pairs={{0,2},{1,3},{2,0},{3,1},{4,6},{5,7},{6,4},{7,5},{8,10},{9,11},{10,... | collective-permute-start | bytes 6152 | tf_op jit(solution)/shard_map/ppermute | solution.py:353
  46.1 1.6 %collective-permute-done.19.refs_2_ = f32[4,128]{1,0:T(4,128)S(1)} collective-permute-done((f32[4,128]{1,0:T(4,128)S(1)}, f32[4,128]{1,0:T(4,128)S(1)}, u32[]{:S(2)}, u32[]{:S(2)}) %collective-permute-start.19) | collective-permute-done | bytes 2080 | tf_op jit(solution)/shard_map/ppermute | solution.py:353
  47.7 0.6 %out.1 = f32[4,128]{1,0:T(4,128)} custom-call(f32[4,128]{1,0:T(4,128)S(1)} %get-tuple-element.61.refs_0_, f32[4,128]{1,0:T(4,128)S(1)} %collective-permute-done.18.refs_1_, f32[4,128]{1,0:T(4,128)S(1)} %collective-permute-done.19.refs_2_, f32[4,128]{1,0:T(4,128)S(1)} %collective-permute-done.20.refs_3_), custom_call_target="tpu_custom_call" | custom-call | tf_op jit(solution)/shard_map/out/pallas_call | solution.py:359
  (30 shorter events, 2.6 us)
Async XLA Ops:
  1.6 5.1 %copy-start = (f32[128,512]{1,0:T(8,128)S(1)}, f32[128,512]{1,0:T(8,128)}, u32[]{:S(2)}) copy-start(f32[128,512]{1,0:T(8,128)} %trans.3) | copy-start | bytes 786436
  1.6 6.5 %collective-permute-start = (f32[64,512]{1,0:T(8,128)S(1)}, f32[64,512]{1,0:T(8,128)S(1)}, u32[]{:S(2)}, u32[]{:S(2)}) collective-permute-start(f32[64,512]{1,0:T(8,128)S(1)} %get-tuple-element.36), channel_id=1, source_target_pairs={{0,2},{1,3},{2,0},{3,1},{4,6},{5,7},{6,4},{7,5},{8,10},{9,11},{10,... | collective-permute-start | bytes 393224 | tf_op jit(solution)/shard_map/ppermute | solution.py:353
  6.1 9.7 %collective-permute-start.4 = (f32[256,512]{1,0:T(8,128)S(1)}, f32[256,512]{1,0:T(8,128)S(1)}, u32[]{:S(2)}, u32[]{:S(2)}) collective-permute-start(f32[256,512]{1,0:T(8,128)S(1)} %get-tuple-element.40), channel_id=1, source_target_pairs={{0,1},{1,0},{2,3},{3,2},{4,5},{5,4},{6,7},{7,6},{8,9},{9,8},{10,11... | collective-permute-start | bytes 1572872 | tf_op jit(solution)/shard_map/ppermute | solution.py:353
  6.2 9.6 %collective-permute-start.5 = (f32[256,512]{1,0:T(8,128)S(1)}, f32[256,512]{1,0:T(8,128)S(1)}, u32[]{:S(2)}, u32[]{:S(2)}) collective-permute-start(f32[256,512]{1,0:T(8,128)S(1)} %get-tuple-element.41), channel_id=1, source_target_pairs={{0,1},{1,0},{2,3},{3,2},{4,5},{5,4},{6,7},{7,6},{8,9},{9,8},{10,11... | collective-permute-start | bytes 1572872 | tf_op jit(solution)/shard_map/ppermute | solution.py:353
  6.7 12.7 %collective-permute-start.6 = (f32[4,208,128]{2,1,0:T(8,128)S(1)}, f32[4,208,128]{2,1,0:T(8,128)S(1)}, u32[]{:S(2)}, u32[]{:S(2)}) collective-permute-start(f32[4,208,128]{2,1,0:T(8,128)S(1)} %get-tuple-element.48), channel_id=1, source_target_pairs={{0,2},{1,3},{2,0},{3,1},{4,6},{5,7},{6,4},{7,5},{8,10},{9,11},{10,... | collective-permute-start | bytes 1277960 | tf_op jit(solution)/shard_map/ppermute | solution.py:353
  6.7 7.1 %collective-permute-start.1 = (f32[128,512]{1,0:T(8,128)S(1)}, f32[128,512]{1,0:T(8,128)S(1)}, u32[]{:S(2)}, u32[]{:S(2)}) collective-permute-start(f32[128,512]{1,0:T(8,128)S(1)} %copy-done), channel_id=1, source_target_pairs={{0,1},{1,0},{2,3},{3,2},{4,5},{5,4},{6,7},{7,6},{8,9},{9,8},{10,11... | collective-permute-start | bytes 786440 | tf_op jit(solution)/shard_map/ppermute | solution.py:353
  8.1 5.0 %collective-permute-start.2 = (f32[64,512]{1,0:T(8,128)S(1)}, f32[64,512]{1,0:T(8,128)S(1)}, u32[]{:S(2)}, u32[]{:S(2)}) collective-permute-start(f32[64,512]{1,0:T(8,128)S(1)} %collective-permute-done.after.refs_0_), channel_id=1, source_target_pairs={{0,4},{1,5},{2,6},{3,7},{4,0},{5,1},{6,2},{7,3},{8,12},{9,13},{10,... | collective-permute-start | bytes 393224 | tf_op jit(solution)/shard_map/ppermute | solution.py:353
  13.7 2.1 %collective-permute-start.3 = (f32[1,128,512]{2,1,0:T(8,128)S(1)}, f32[1,128,512]{2,1,0:T(8,128)S(1)}, u32[]{:S(2)}, u32[]{:S(2)}) collective-permute-start(f32[1,128,512]{2,1,0:T(8,128)S(1)} %join.1.joined), channel_id=1, source_target_pairs={{0,1},{1,0},{2,3},{3,2},{4,5},{5,4},{6,7},{7,6},{8,9},{9,8},{10,11... | collective-permute-start | bytes 786440 | tf_op jit(solution)/shard_map/ppermute | solution.py:353
  13.8 8.1 %collective-permute-start.7 = (f32[4,80,128]{2,1,0:T(8,128)S(1)}, f32[4,80,128]{2,1,0:T(8,128)S(1)}, u32[]{:S(2)}, u32[]{:S(2)}) collective-permute-start(f32[4,80,128]{2,1,0:T(8,128)S(1)} %get-tuple-element.53), channel_id=1, source_target_pairs={{0,3},{1,2},{2,1},{3,0},{4,7},{5,6},{6,5},{7,4},{8,11},{9,10},{10,... | collective-permute-start | bytes 491528 | tf_op jit(solution)/shard_map/ppermute | solution.py:353
  23.2 1.2 %collective-permute-start.8 = (f32[1,512]{1,0:T(1,128)S(1)}, f32[1,512]{1,0:T(1,128)S(1)}, u32[]{:S(2)}, u32[]{:S(2)}) collective-permute-start(f32[1,512]{1,0:T(1,128)S(1)} %get-tuple-element.54), channel_id=1, source_target_pairs={{0,1},{1,0},{2,3},{3,2},{4,5},{5,4},{6,7},{7,6},{8,9},{9,8},{10,11... | collective-permute-start | bytes 6152 | tf_op jit(solution)/shard_map/ppermute | solution.py:353
  24.5 4.4 %collective-permute-start.10 = (f32[520,512]{1,0:T(8,128)S(1)}, f32[520,512]{1,0:T(8,128)S(1)}, u32[]{:S(2)}, u32[]{:S(2)}) collective-permute-start(f32[520,512]{1,0:T(8,128)S(1)} %pair.1.early.refs_12_), channel_id=1, source_target_pairs={{0,1},{1,0},{2,3},{3,2},{4,5},{5,4},{6,7},{7,6},{8,9},{9,8},{10,11... | collective-permute-start | bytes 3194888 | tf_op jit(solution)/shard_map/ppermute | solution.py:353
  25.2 3.7 %collective-permute-start.9 = (f32[1,512]{1,0:T(1,128)S(1)}, f32[1,512]{1,0:T(1,128)S(1)}, u32[]{:S(2)}, u32[]{:S(2)}) collective-permute-start(f32[1,512]{1,0:T(1,128)S(1)} %two.1), channel_id=1, source_target_pairs={{0,4},{1,5},{2,6},{3,7},{4,0},{5,1},{6,2},{7,3},{8,12},{9,13},{10,... | collective-permute-start | bytes 6152 | tf_op jit(solution)/shard_map/ppermute | solution.py:353
  29.2 1.2 %collective-permute-start.11 = (f32[1,512]{1,0:T(1,128)S(1)}, f32[1,512]{1,0:T(1,128)S(1)}, u32[]{:S(2)}, u32[]{:S(2)}) collective-permute-start(f32[1,512]{1,0:T(1,128)S(1)} %pair_hop.1), channel_id=1, source_target_pairs={{0,1},{1,0},{2,3},{3,2},{4,5},{5,4},{6,7},{7,6},{8,9},{9,8},{10,11... | collective-permute-start | bytes 6152 | tf_op jit(solution)/shard_map/ppermute | solution.py:477
  30.5 1.2 %collective-permute-start.12 = (f32[1,512]{1,0:T(1,128)S(1)}, f32[1,512]{1,0:T(1,128)S(1)}, u32[]{:S(2)}, u32[]{:S(2)}) collective-permute-start(f32[1,512]{1,0:T(1,128)S(1)} %hop.5), channel_id=1, source_target_pairs={{0,1},{1,0},{2,3},{3,2},{4,5},{5,4},{6,7},{7,6},{8,9},{9,8},{10,11... | collective-permute-start | bytes 6152 | tf_op jit(solution)/shard_map/ppermute | solution.py:477
  31.7 8.7 %collective-permute-start.17 = (f32[512,512]{1,0:T(8,128)S(1)}, f32[512,512]{1,0:T(8,128)S(1)}, u32[]{:S(2)}, u32[]{:S(2)}) collective-permute-start(f32[512,512]{1,0:T(8,128)S(1)} %get-tuple-element.60.gb.refs_13_), channel_id=1, source_target_pairs={{0,1},{1,0},{2,3},{3,2},{4,5},{5,4},{6,7},{7,6},{8,9},{9,8},{10,11... | collective-permute-start | bytes 3145736 | tf_op jit(solution)/shard_map/ppermute | solution.py:353
  32.2 2.2 %collective-permute-start.13 = (f32[1,512]{1,0:T(1,128)S(1)}, f32[1,512]{1,0:T(1,128)S(1)}, u32[]{:S(2)}, u32[]{:S(2)}) collective-permute-start(f32[1,512]{1,0:T(1,128)S(1)} %hop.6), channel_id=1, source_target_pairs={{0,1},{1,0},{2,3},{3,2},{4,5},{5,4},{6,7},{7,6},{8,9},{9,8},{10,11... | collective-permute-start | bytes 6152 | tf_op jit(solution)/shard_map/ppermute | solution.py:477
  34.5 1.2 %collective-permute-start.14 = (f32[1,512]{1,0:T(1,128)S(1)}, f32[1,512]{1,0:T(1,128)S(1)}, u32[]{:S(2)}, u32[]{:S(2)}) collective-permute-start(f32[1,512]{1,0:T(1,128)S(1)} %hop.7), channel_id=1, source_target_pairs={{0,1},{1,0},{2,3},{3,2},{4,5},{5,4},{6,7},{7,6},{8,10},{9,13},{10,... | collective-permute-start | bytes 6152 | tf_op jit(solution)/shard_map/ppermute | solution.py:477
  35.9 1.2 %collective-permute-start.15 = (f32[1,512]{1,0:T(1,128)S(1)}, f32[1,512]{1,0:T(1,128)S(1)}, u32[]{:S(2)}, u32[]{:S(2)}) collective-permute-start(f32[1,512]{1,0:T(1,128)S(1)} %hop.8), channel_id=1, source_target_pairs={{0,1},{1,0},{2,3},{3,2},{4,6},{5,9},{6,7},{7,4},{8,10},{9,5},{10,1... | collective-permute-start | bytes 6152 | tf_op jit(solution)/shard_map/ppermute | solution.py:477
  37.3 3.1 %collective-permute-start.16 = (f32[1,512]{1,0:T(1,128)S(1)}, f32[1,512]{1,0:T(1,128)S(1)}, u32[]{:S(2)}, u32[]{:S(2)}) collective-permute-start(f32[1,512]{1,0:T(1,128)S(1)} %hop.9), channel_id=1, source_target_pairs={{0,2},{1,5},{2,3},{3,0},{4,6},{5,1},{6,7},{7,4},{8,9},{9,8},{10,11... | collective-permute-start | bytes 6152 | tf_op jit(solution)/shard_map/ppermute | solution.py:477
  40.8 5.3 %collective-permute-start.18 = (f32[4,128]{1,0:T(4,128)S(1)}, f32[4,128]{1,0:T(4,128)S(1)}, u32[]{:S(2)}, u32[]{:S(2)}) collective-permute-start(f32[4,128]{1,0:T(4,128)S(1)} %get-tuple-element.62), channel_id=1, source_target_pairs={{0,3},{1,2},{2,1},{3,0},{4,7},{5,6},{6,5},{7,4},{8,11},{9,10},{10,... | collective-permute-start | bytes 6152 | tf_op jit(solution)/shard_map/ppermute | solution.py:353
  40.9 6.8 %collective-permute-start.19 = (f32[4,128]{1,0:T(4,128)S(1)}, f32[4,128]{1,0:T(4,128)S(1)}, u32[]{:S(2)}, u32[]{:S(2)}) collective-permute-start(f32[4,128]{1,0:T(4,128)S(1)} %get-tuple-element.63), channel_id=1, source_target_pairs={{0,2},{1,3},{2,0},{3,1},{4,6},{5,7},{6,4},{7,5},{8,10},{9,11},{10,... | collective-permute-start | bytes 6152 | tf_op jit(solution)/shard_map/ppermute | solution.py:353
  46.1 1.6 %collective-permute-start.20 = (f32[4,128]{1,0:T(4,128)S(1)}, f32[4,128]{1,0:T(4,128)S(1)}, u32[]{:S(2)}, u32[]{:S(2)}) collective-permute-start(f32[4,128]{1,0:T(4,128)S(1)} %get-tuple-element.64), channel_id=1, source_target_pairs={{0,1},{1,0},{2,3},{3,2},{4,5},{5,4},{6,7},{7,6},{8,9},{9,8},{10,11... | collective-permute-start | bytes 6152 | tf_op jit(solution)/shard_map/ppermute | solution.py:353

commit v14 on v13

--- a/solution.py
+++ b/solution.py
@@ -55,7 +55,7 @@
 
 def far_shape(devices, count, panel, order, off):
     if trimmed(devices, panel):
-        return (2 * count, panel * 5 // 8 + (panel if off == 2 else 0), panel)
+        return (2 * count, panel * 9 // 16 + (panel if off == 2 else 0), panel)
     return (2 * count, panel, order - 2 * panel)
 
 
@@ -64,18 +64,21 @@
 
 
 def fold(block):
-    corner = jnp.where(lanes(32) < 32, pltpu.roll(block[96:], 32, 1), block[32:64])
-    third = jnp.where(lanes(16) < 64, pltpu.roll(block[64:80], 64, 1), block[80:96])
-    return jnp.concatenate([block[:32], corner, third], axis=0)
+    lower = ((112, 16), (96, 32), (80, 48))
+    filled = [
+        jnp.where(lanes(16) < width, pltpu.roll(block[row : row + 16], width, 1), block[width : width + 16])
+        for row, width in lower
+    ]
+    rest = jnp.where(lanes(8) < 64, pltpu.roll(block[64:72], 64, 1), block[72:80])
+    return jnp.concatenate([block[:16], *filled, rest], axis=0)
 
 
 def unfold(folded):
-    corner, third = folded[32:64], folded[64:]
-    upper = jnp.concatenate(
-        [folded[:64], pltpu.roll(third, 64, 1), third, pltpu.roll(corner, 96, 1)], axis=0
-    )
+    rest = folded[64:]
+    moved = [pltpu.roll(folded[width : width + 16], 128 - width, 1) for width in (48, 32, 16)]
+    upper = jnp.concatenate([folded[:64], pltpu.roll(rest, 64, 1), rest, *moved], axis=0)
     row = lax.broadcasted_iota(jnp.int32, (128, 128), 0)
-    return jnp.where(row // 32 <= lanes(128) // 32, upper, upper.T)
+    return jnp.where(row // 16 <= lanes(128) // 16, upper, upper.T)
 
 
 def base(device, count):
@@ -109,7 +112,7 @@
         for off, piece in enumerate(far, 2):
             for k in range(2 * count):
                 block = diagonal[k // count, base(s ^ off, count) + k % count]
-                piece[k, piece.shape[1] - panel * 5 // 8 :, :] = fold(block)
+                piece[k, piece.shape[1] - panel * 9 // 16 :, :] = fold(block)
 
 
 def near_kernel(cov, prec, trans, after, near_cov, near_prec, near_trans, sems):
@@ -265,12 +268,11 @@
     count, panel, order = h.shape
     j = 1 - lax.axis_index("state") % 2
     for k, (gain, out) in enumerate(((ga, ga_ref), (gb, gb_ref))):
-        out[...] = gain[...]
         if far:
             at = far_row(2 + j, panel)
             p_last, l_last = unfold(far[0][k]), unfold(far[0][count + k])
             corner = [a_far[half, far_row(j, panel), at] for half in range(2)]
-            out[at, :] += dot3(p_last, h[k], NN)
+            out[at, :] = gain[at, :] + dot3(p_last, h[k], NN)
             out[:, at] += dot3(col[k], l_last, NN)
             out[at, at] += dot3(dot3(p_last, corner, NN), l_last, NN)
     mean_a, mean_b, pred_a, pred_b = steps_of(info, count)
@@ -355,13 +357,14 @@
     def shape(*dims):
         return jax.ShapeDtypeStruct(dims, F32)
 
-    def call(kernel, name, mebibytes, outs, in_specs, scratch, args):
+    def call(kernel, name, mebibytes, outs, in_specs, scratch, args, aliases={}):
         return pl.pallas_call(
             kernel,
             out_shape=outs,
             in_specs=in_specs,
             out_specs=[VMEM] * len(outs),
             scratch_shapes=scratch,
+            input_output_aliases=aliases,
             compiler_params=params(mebibytes),
             name=name,
         )(*args)
@@ -458,6 +461,7 @@
         [VMEM] * (7 + len(last)),
         [],
         (first, info, a_far, ga, gb, col, h, *last),
+        {3: 0, 4: 1},
     )
     mean = swap(mean, 1)
     (early_map,) = call(pair_kernel, "pair", 12, [shape(order + 8, order)], [VMEM] * 3, [], (info, ga, gb))

time: 48.5 us -> 48.1 us (level)
  waiting for transfers between devices: 14.2 us -> 13.6 us
where the time goes in v14:
time: 48.1 us; the launch traced here: 47.9 us
  starting transfers between devices  17.9 us (37%)
  Pallas kernels  16.3 us (34%)
  waiting for transfers between devices  13.6 us (28%)
    pallas_call x18, Pallas kernels, call(): pl.pallas_call(kernel, out_shape=outs, in_specs=in_specs, out_specs=[VMEM...  16.3 us
    ppermute x15, starting transfers between devices, swap(): return lax.ppermute(x, ('tm', 'state'), pairs)  15.2 us
    ppermute x15, waiting for transfers between devices, swap(): return lax.ppermute(x, ('tm', 'state'), pairs)  7.09 us
    ppermute x6, waiting for transfers between devices, local(): x = lax.ppermute(x, ('tm', 'state'), list(target.items()))  6.46 us
    ppermute x6, starting transfers between devices, local(): x = lax.ppermute(x, ('tm', 'state'), list(target.items()))  2.67 us
  transfers between devices with their start and end apart: 21, of which 12 were waited for; matrix products, arithmetic and copies ran while one was open for 0% of the time, Pallas kernels for 25%

profile of v14, /device:TPU:0, one launch (start us, length us, event | category | flops | bytes accessed | tf_op | source)
XLA Modules:
  0.0 47.9 jit_solution(4648441274796912953)
XLA Ops:
  0.0 1.6 %pack.1 = (f32[4,200,128]{2,1,0:T(8,128)S(1)}, f32[4,72,128]{2,1,0:T(8,128)S(1)}, f32[64,512]{1,0:T(8,128)S(1)}, f32[1,512]{1,0:T(1,128)S(1)}) custom-call(f32[4,128,512]{2,1,0:T(8,128)} %cov.5, f32[4,128,512]{2,1,0:T(8,128)} %prec.5, f32[128,512]{1,0:T(8,128)} %trans.3, f32[1,512]{1,0:T(1,128)} %bitcast.1), custom_call_target="tpu_custom_call" | custom-call | tf_op jit(solution)/shard_map/pack/pallas_call | solution.py:361
  1.6 3.0 %collective-permute-start = (f32[64,512]{1,0:T(8,128)S(1)}, f32[64,512]{1,0:T(8,128)S(1)}, u32[]{:S(2)}, u32[]{:S(2)}) collective-permute-start(f32[64,512]{1,0:T(8,128)S(1)} %get-tuple-element.36), channel_id=1, source_target_pairs={{0,2},{1,3},{2,0},{3,1},{4,6},{5,7},{6,4},{7,5},{8,10},{9,11},{10,... | collective-permute-start | bytes 393224 | tf_op jit(solution)/shard_map/ppermute | solution.py:355
  4.6 1.5 %near.1 = (f32[256,512]{1,0:T(8,128)S(1)}, f32[256,512]{1,0:T(8,128)S(1)}) custom-call(f32[4,128,512]{2,1,0:T(8,128)} %cov.5, f32[4,128,512]{2,1,0:T(8,128)} %prec.5, f32[1,512]{1,0:T(1,128)S(1)} %get-tuple-element.35.after.first.refs_0_), custom_call_target="tpu_custom_call" | custom-call | tf_op jit(solution)/shard_map/near/pallas_call | solution.py:361
  6.2 0.5 %collective-permute-start.5 = (f32[256,512]{1,0:T(8,128)S(1)}, f32[256,512]{1,0:T(8,128)S(1)}, u32[]{:S(2)}, u32[]{:S(2)}) collective-permute-start(f32[256,512]{1,0:T(8,128)S(1)} %get-tuple-element.41), channel_id=1, source_target_pairs={{0,1},{1,0},{2,3},{3,2},{4,5},{5,4},{6,7},{7,6},{8,9},{9,8},{10,11... | collective-permute-start | bytes 1572872 | tf_op jit(solution)/shard_map/ppermute | solution.py:355
  6.8 1.4 %collective-permute-done.after.refs_0_ = f32[64,512]{1,0:T(8,128)S(1)} collective-permute-done((f32[64,512]{1,0:T(8,128)S(1)}, f32[64,512]{1,0:T(8,128)S(1)}, u32[]{:S(2)}, u32[]{:S(2)}) %collective-permute-start) | collective-permute-done | bytes 131104 | tf_op jit(solution)/shard_map/ppermute | solution.py:355
  8.1 1.8 %collective-permute-start.2 = (f32[64,512]{1,0:T(8,128)S(1)}, f32[64,512]{1,0:T(8,128)S(1)}, u32[]{:S(2)}, u32[]{:S(2)}) collective-permute-start(f32[64,512]{1,0:T(8,128)S(1)} %collective-permute-done.after.refs_0_), channel_id=1, source_target_pairs={{0,4},{1,5},{2,6},{3,7},{4,0},{5,1},{6,2},{7,3},{8,12},{9,13},{10,... | collective-permute-start | bytes 393224 | tf_op jit(solution)/shard_map/ppermute | solution.py:355
  9.9 1.6 %own.1 = (f32[4,128,512]{2,1,0:T(8,128)S(1)}, f32[128,512]{1,0:T(8,128)S(1)}, f32[4,512]{1,0:T(4,128)S(1)}) custom-call(f32[4,128,512]{2,1,0:T(8,128)} %cov.5, f32[4,128,512]{2,1,0:T(8,128)} %prec.5, f32[128,512]{1,0:T(8,128)} %trans.3, f32[4,512]{1,0:T(4,128)} %means.1, f32[64,512]{1,0:T(8,128)S(1)} %collective-permute-done.after.refs_0_), custom_call_target="tpu_custom_call" | custom-call | tf_op jit(solution)/shard_map/own/pallas_call | solution.py:361
  11.5 1.6 %collective-permute-done.2.refs_1_ = f32[64,512]{1,0:T(8,128)S(1)} collective-permute-done((f32[64,512]{1,0:T(8,128)S(1)}, f32[64,512]{1,0:T(8,128)S(1)}, u32[]{:S(2)}, u32[]{:S(2)}) %collective-permute-start.2) | collective-permute-done | bytes 131104 | tf_op jit(solution)/shard_map/ppermute | solution.py:355
  13.1 0.6 %join.1.joined = f32[1,128,512]{2,1,0:T(8,128)S(1)} custom-call(f32[128,512]{1,0:T(8,128)S(1)} %get-tuple-element.39.after.trans, f32[64,512]{1,0:T(8,128)S(1)} %collective-permute-done.after.refs_0_, f32[64,512]{1,0:T(8,128)S(1)} %collective-permute-done.2.refs_1_), custom_call_target="tpu_custom_call" | custom-call | tf_op jit(solution)/shard_map/join/pallas_call | solution.py:361
  13.8 2.0 %collective-permute-start.7 = (f32[4,72,128]{2,1,0:T(8,128)S(1)}, f32[4,72,128]{2,1,0:T(8,128)S(1)}, u32[]{:S(2)}, u32[]{:S(2)}) collective-permute-start(f32[4,72,128]{2,1,0:T(8,128)S(1)} %get-tuple-element.53), channel_id=1, source_target_pairs={{0,3},{1,2},{2,1},{3,0},{4,7},{5,6},{6,5},{7,4},{8,11},{9,10},{10,... | collective-permute-start | bytes 442376 | tf_op jit(solution)/shard_map/ppermute | solution.py:355
  15.8 2.9 %early.1 = (f32[16,512]{1,0:T(8,128)S(1)}, bf16[2,256,512]{2,1,0:T(8,128)(2,1)S(1)}, bf16[2,2,256,512]{3,2,1,0:T(8,128)(2,1)S(1)}, f32[2,256,256]{2,1,0:T(8,128)...) custom-call(f32[4,128,512]{2,1,0:T(8,128)S(1)} %get-tuple-element.37.own, ...), custom_call_target="tpu_custom_call" | custom-call | tf_op jit(solution)/shard_map/early/pallas_call | solution.py:361
  19.0 2.5 %middle.1 = (f32[512,512]{1,0:T(8,128)S(1)}, f32[512,512]{1,0:T(8,128)S(1)}, f32[2,512,128]{2,1,0:T(8,128)S(1)}, f32[2,128,512]{2,1,0:T(8,128)S(1)}) custom-call(bf16[2,256,512]{2,1,0:T(8,128)(2,1)S(1)} %get-tuple-element.43.a_far, bf16[2,2,256,512]{3,2,1,0:T(8,128)(2,1)S(1)} %get-tuple-element.44.l_known, f32[2,256,256]{2,1,0:T(8,128)S(1)} %get-tuple-element.45.c_known, ...), custom_call_target="tpu_custom_call" | custom-call | tf_op jit(solution)/shard_map/middle/pallas_call | solution.py:361
  21.6 1.3 %late.1 = (f32[512,512]{1,0:T(8,128)S(1)}, f32[512,512]{1,0:T(8,128)S(1)}, f32[1,512]{1,0:T(1,128)S(1)}) custom-call(f32[1,512]{1,0:T(1,128)S(1)} %get-tuple-element.35.after.first.refs_0_, f32[16,512]{1,0:T(8,128)S(1)} %get-tuple-element.42.info, bf16[2,256,512]{2,1,0:T(8,128)(2,1)S(1)} %get-tuple-element.43.a_far, ...), custom_call_target="tpu_custom_call", output_to_operand_aliasing={{0}: (3, {}), {1}: (4, {})} | custom-call | tf_op jit(solution)/shard_map/late/pallas_call | solution.py:361
  23.0 1.0 %pair.1.early.refs_12_ = f32[520,512]{1,0:T(8,128)S(1)} custom-call(f32[16,512]{1,0:T(8,128)S(1)} %get-tuple-element.42.info, f32[512,512]{1,0:T(8,128)S(1)} %get-tuple-element.55.ga, f32[512,512]{1,0:T(8,128)S(1)} %get-tuple-element.60.gb.refs_13_), custom_call_target="tpu_custom_call" | custom-call | tf_op jit(solution)/shard_map/pair/pallas_call | solution.py:361
  24.1 0.4 collective-permute-start.10
  24.8 1.6 %collective-permute-start.9 = (f32[1,512]{1,0:T(1,128)S(1)}, f32[1,512]{1,0:T(1,128)S(1)}, u32[]{:S(2)}, u32[]{:S(2)}) collective-permute-start(f32[1,512]{1,0:T(1,128)S(1)} %two.1), channel_id=1, source_target_pairs={{0,4},{1,5},{2,6},{3,7},{4,0},{5,1},{6,2},{7,3},{8,12},{9,13},{10,... | collective-permute-start | bytes 6152 | tf_op jit(solution)/shard_map/ppermute | solution.py:355
  26.4 2.1 %collective-permute-done.9.x.refs_1_ = f32[1,512]{1,0:T(1,128)S(1)} collective-permute-done((f32[1,512]{1,0:T(1,128)S(1)}, f32[1,512]{1,0:T(1,128)S(1)}, u32[]{:S(2)}, u32[]{:S(2)}) %collective-permute-start.9) | collective-permute-done | bytes 2080 | tf_op jit(solution)/shard_map/ppermute | solution.py:355
  28.8 1.0 %block.1 = (f32[512,512]{1,0:T(8,128)S(1)}, f32[8,512]{1,0:T(8,128)S(1)}) custom-call(f32[520,512]{1,0:T(8,128)S(1)} %collective-permute-done.10.late.refs_10_, f32[520,512]{1,0:T(8,128)S(1)} %pair.1.early.refs_12_), custom_call_target="tpu_custom_call" | custom-call | tf_op jit(solution)/shard_map/block/pallas_call | solution.py:361
  30.1 0.4 collective-permute-start.12
  30.5 0.8 %collective-permute-done.12.x.refs_3_ = f32[1,512]{1,0:T(1,128)S(1)} collective-permute-done((f32[1,512]{1,0:T(1,128)S(1)}, f32[1,512]{1,0:T(1,128)S(1)}, u32[]{:S(2)}, u32[]{:S(2)}) %collective-permute-start.12) | collective-permute-done | bytes 2080 | tf_op jit(solution)/shard_map/ppermute | solution.py:481
  31.4 0.3 collective-permute-start.17
  32.1 1.9 %collective-permute-done.13.x.refs_4_ = f32[1,512]{1,0:T(1,128)S(1)} collective-permute-done((f32[1,512]{1,0:T(1,128)S(1)}, f32[1,512]{1,0:T(1,128)S(1)}, u32[]{:S(2)}, u32[]{:S(2)}) %collective-permute-start.13) | collective-permute-done | bytes 2080 | tf_op jit(solution)/shard_map/ppermute | solution.py:481
  34.2 0.4 collective-permute-start.14
  34.6 0.8 %collective-permute-done.14.x.refs_5_ = f32[1,512]{1,0:T(1,128)S(1)} collective-permute-done((f32[1,512]{1,0:T(1,128)S(1)}, f32[1,512]{1,0:T(1,128)S(1)}, u32[]{:S(2)}, u32[]{:S(2)}) %collective-permute-start.14) | collective-permute-done | bytes 2080 | tf_op jit(solution)/shard_map/ppermute | solution.py:481
  35.6 0.4 collective-permute-start.15
  36.0 0.8 %collective-permute-done.15.x.refs_6_ = f32[1,512]{1,0:T(1,128)S(1)} collective-permute-done((f32[1,512]{1,0:T(1,128)S(1)}, f32[1,512]{1,0:T(1,128)S(1)}, u32[]{:S(2)}, u32[]{:S(2)}) %collective-permute-start.15) | collective-permute-done | bytes 2080 | tf_op jit(solution)/shard_map/ppermute | solution.py:481
  37.0 1.2 %collective-permute-start.16 = (f32[1,512]{1,0:T(1,128)S(1)}, f32[1,512]{1,0:T(1,128)S(1)}, u32[]{:S(2)}, u32[]{:S(2)}) collective-permute-start(f32[1,512]{1,0:T(1,128)S(1)} %hop.9), channel_id=1, source_target_pairs={{0,2},{1,5},{2,3},{3,0},{4,6},{5,1},{6,7},{7,4},{8,9},{9,8},{10,11... | collective-permute-start | bytes 6152 | tf_op jit(solution)/shard_map/ppermute | solution.py:481
  38.1 1.9 %collective-permute-done.16.refs_7_ = f32[1,512]{1,0:T(1,128)S(1)} collective-permute-done((f32[1,512]{1,0:T(1,128)S(1)}, f32[1,512]{1,0:T(1,128)S(1)}, u32[]{:S(2)}, u32[]{:S(2)}) %collective-permute-start.16) | collective-permute-done | bytes 2080 | tf_op jit(solution)/shard_map/ppermute | solution.py:481
  40.1 0.4 last.1
  40.5 5.2 %collective-permute-start.19 = (f32[4,128]{1,0:T(4,128)S(1)}, f32[4,128]{1,0:T(4,128)S(1)}, u32[]{:S(2)}, u32[]{:S(2)}) collective-permute-start(f32[4,128]{1,0:T(4,128)S(1)} %get-tuple-element.63), channel_id=1, source_target_pairs={{0,2},{1,3},{2,0},{3,1},{4,6},{5,7},{6,4},{7,5},{8,10},{9,11},{10,... | collective-permute-start | bytes 6152 | tf_op jit(solution)/shard_map/ppermute | solution.py:355
  45.7 1.6 %collective-permute-done.19.refs_2_ = f32[4,128]{1,0:T(4,128)S(1)} collective-permute-done((f32[4,128]{1,0:T(4,128)S(1)}, f32[4,128]{1,0:T(4,128)S(1)}, u32[]{:S(2)}, u32[]{:S(2)}) %collective-permute-start.19) | collective-permute-done | bytes 2080 | tf_op jit(solution)/shard_map/ppermute | solution.py:355
  47.3 0.6 %out.1 = f32[4,128]{1,0:T(4,128)} custom-call(f32[4,128]{1,0:T(4,128)S(1)} %get-tuple-element.61.refs_0_, f32[4,128]{1,0:T(4,128)S(1)} %collective-permute-done.18.refs_1_, f32[4,128]{1,0:T(4,128)S(1)} %collective-permute-done.19.refs_2_, f32[4,128]{1,0:T(4,128)S(1)} %collective-permute-done.20.refs_3_), custom_call_target="tpu_custom_call" | custom-call | tf_op jit(solution)/shard_map/out/pallas_call | solution.py:361
  (30 shorter events, 2.6 us)
Async XLA Ops:
  1.6 5.1 %copy-start = (f32[128,512]{1,0:T(8,128)S(1)}, f32[128,512]{1,0:T(8,128)}, u32[]{:S(2)}) copy-start(f32[128,512]{1,0:T(8,128)} %trans.3) | copy-start | bytes 786436
  1.6 6.5 %collective-permute-start = (f32[64,512]{1,0:T(8,128)S(1)}, f32[64,512]{1,0:T(8,128)S(1)}, u32[]{:S(2)}, u32[]{:S(2)}) collective-permute-start(f32[64,512]{1,0:T(8,128)S(1)} %get-tuple-element.36), channel_id=1, source_target_pairs={{0,2},{1,3},{2,0},{3,1},{4,6},{5,7},{6,4},{7,5},{8,10},{9,11},{10,... | collective-permute-start | bytes 393224 | tf_op jit(solution)/shard_map/ppermute | solution.py:355
  6.1 9.7 %collective-permute-start.4 = (f32[256,512]{1,0:T(8,128)S(1)}, f32[256,512]{1,0:T(8,128)S(1)}, u32[]{:S(2)}, u32[]{:S(2)}) collective-permute-start(f32[256,512]{1,0:T(8,128)S(1)} %get-tuple-element.40), channel_id=1, source_target_pairs={{0,1},{1,0},{2,3},{3,2},{4,5},{5,4},{6,7},{7,6},{8,9},{9,8},{10,11... | collective-permute-start | bytes 1572872 | tf_op jit(solution)/shard_map/ppermute | solution.py:355
  6.2 9.6 %collective-permute-start.5 = (f32[256,512]{1,0:T(8,128)S(1)}, f32[256,512]{1,0:T(8,128)S(1)}, u32[]{:S(2)}, u32[]{:S(2)}) collective-permute-start(f32[256,512]{1,0:T(8,128)S(1)} %get-tuple-element.41), channel_id=1, source_target_pairs={{0,1},{1,0},{2,3},{3,2},{4,5},{5,4},{6,7},{7,6},{8,9},{9,8},{10,11... | collective-permute-start | bytes 1572872 | tf_op jit(solution)/shard_map/ppermute | solution.py:355
  6.7 12.3 %collective-permute-start.6 = (f32[4,200,128]{2,1,0:T(8,128)S(1)}, f32[4,200,128]{2,1,0:T(8,128)S(1)}, u32[]{:S(2)}, u32[]{:S(2)}) collective-permute-start(f32[4,200,128]{2,1,0:T(8,128)S(1)} %get-tuple-element.48), channel_id=1, source_target_pairs={{0,2},{1,3},{2,0},{3,1},{4,6},{5,7},{6,4},{7,5},{8,10},{9,11},{10,... | collective-permute-start | bytes 1228808 | tf_op jit(solution)/shard_map/ppermute | solution.py:355
  6.7 7.1 %collective-permute-start.1 = (f32[128,512]{1,0:T(8,128)S(1)}, f32[128,512]{1,0:T(8,128)S(1)}, u32[]{:S(2)}, u32[]{:S(2)}) collective-permute-start(f32[128,512]{1,0:T(8,128)S(1)} %copy-done), channel_id=1, source_target_pairs={{0,1},{1,0},{2,3},{3,2},{4,5},{5,4},{6,7},{7,6},{8,9},{9,8},{10,11... | collective-permute-start | bytes 786440 | tf_op jit(solution)/shard_map/ppermute | solution.py:355
  8.1 5.0 %collective-permute-start.2 = (f32[64,512]{1,0:T(8,128)S(1)}, f32[64,512]{1,0:T(8,128)S(1)}, u32[]{:S(2)}, u32[]{:S(2)}) collective-permute-start(f32[64,512]{1,0:T(8,128)S(1)} %collective-permute-done.after.refs_0_), channel_id=1, source_target_pairs={{0,4},{1,5},{2,6},{3,7},{4,0},{5,1},{6,2},{7,3},{8,12},{9,13},{10,... | collective-permute-start | bytes 393224 | tf_op jit(solution)/shard_map/ppermute | solution.py:355
  13.7 2.1 %collective-permute-start.3 = (f32[1,128,512]{2,1,0:T(8,128)S(1)}, f32[1,128,512]{2,1,0:T(8,128)S(1)}, u32[]{:S(2)}, u32[]{:S(2)}) collective-permute-start(f32[1,128,512]{2,1,0:T(8,128)S(1)} %join.1.joined), channel_id=1, source_target_pairs={{0,1},{1,0},{2,3},{3,2},{4,5},{5,4},{6,7},{7,6},{8,9},{9,8},{10,11... | collective-permute-start | bytes 786440 | tf_op jit(solution)/shard_map/ppermute | solution.py:355
  13.8 7.8 %collective-permute-start.7 = (f32[4,72,128]{2,1,0:T(8,128)S(1)}, f32[4,72,128]{2,1,0:T(8,128)S(1)}, u32[]{:S(2)}, u32[]{:S(2)}) collective-permute-start(f32[4,72,128]{2,1,0:T(8,128)S(1)} %get-tuple-element.53), channel_id=1, source_target_pairs={{0,3},{1,2},{2,1},{3,0},{4,7},{5,6},{6,5},{7,4},{8,11},{9,10},{10,... | collective-permute-start | bytes 442376 | tf_op jit(solution)/shard_map/ppermute | solution.py:355
  22.9 1.2 %collective-permute-start.8 = (f32[1,512]{1,0:T(1,128)S(1)}, f32[1,512]{1,0:T(1,128)S(1)}, u32[]{:S(2)}, u32[]{:S(2)}) collective-permute-start(f32[1,512]{1,0:T(1,128)S(1)} %get-tuple-element.54), channel_id=1, source_target_pairs={{0,1},{1,0},{2,3},{3,2},{4,5},{5,4},{6,7},{7,6},{8,9},{9,8},{10,11... | collective-permute-start | bytes 6152 | tf_op jit(solution)/shard_map/ppermute | solution.py:355
  24.1 4.4 %collective-permute-start.10 = (f32[520,512]{1,0:T(8,128)S(1)}, f32[520,512]{1,0:T(8,128)S(1)}, u32[]{:S(2)}, u32[]{:S(2)}) collective-permute-start(f32[520,512]{1,0:T(8,128)S(1)} %pair.1.early.refs_12_), channel_id=1, source_target_pairs={{0,1},{1,0},{2,3},{3,2},{4,5},{5,4},{6,7},{7,6},{8,9},{9,8},{10,11... | collective-permute-start | bytes 3194888 | tf_op jit(solution)/shard_map/ppermute | solution.py:355
  24.8 3.7 %collective-permute-start.9 = (f32[1,512]{1,0:T(1,128)S(1)}, f32[1,512]{1,0:T(1,128)S(1)}, u32[]{:S(2)}, u32[]{:S(2)}) collective-permute-start(f32[1,512]{1,0:T(1,128)S(1)} %two.1), channel_id=1, source_target_pairs={{0,4},{1,5},{2,6},{3,7},{4,0},{5,1},{6,2},{7,3},{8,12},{9,13},{10,... | collective-permute-start | bytes 6152 | tf_op jit(solution)/shard_map/ppermute | solution.py:355
  28.8 1.2 %collective-permute-start.11 = (f32[1,512]{1,0:T(1,128)S(1)}, f32[1,512]{1,0:T(1,128)S(1)}, u32[]{:S(2)}, u32[]{:S(2)}) collective-permute-start(f32[1,512]{1,0:T(1,128)S(1)} %pair_hop.1), channel_id=1, source_target_pairs={{0,1},{1,0},{2,3},{3,2},{4,5},{5,4},{6,7},{7,6},{8,9},{9,8},{10,11... | collective-permute-start | bytes 6152 | tf_op jit(solution)/shard_map/ppermute | solution.py:481
  30.1 1.2 %collective-permute-start.12 = (f32[1,512]{1,0:T(1,128)S(1)}, f32[1,512]{1,0:T(1,128)S(1)}, u32[]{:S(2)}, u32[]{:S(2)}) collective-permute-start(f32[1,512]{1,0:T(1,128)S(1)} %hop.5), channel_id=1, source_target_pairs={{0,1},{1,0},{2,3},{3,2},{4,5},{5,4},{6,7},{7,6},{8,9},{9,8},{10,11... | collective-permute-start | bytes 6152 | tf_op jit(solution)/shard_map/ppermute | solution.py:481
  31.4 8.7 %collective-permute-start.17 = (f32[512,512]{1,0:T(8,128)S(1)}, f32[512,512]{1,0:T(8,128)S(1)}, u32[]{:S(2)}, u32[]{:S(2)}) collective-permute-start(f32[512,512]{1,0:T(8,128)S(1)} %get-tuple-element.60.gb.refs_13_), channel_id=1, source_target_pairs={{0,1},{1,0},{2,3},{3,2},{4,5},{5,4},{6,7},{7,6},{8,9},{9,8},{10,11... | collective-permute-start | bytes 3145736 | tf_op jit(solution)/shard_map/ppermute | solution.py:355
  31.9 2.2 %collective-permute-start.13 = (f32[1,512]{1,0:T(1,128)S(1)}, f32[1,512]{1,0:T(1,128)S(1)}, u32[]{:S(2)}, u32[]{:S(2)}) collective-permute-start(f32[1,512]{1,0:T(1,128)S(1)} %hop.6), channel_id=1, source_target_pairs={{0,1},{1,0},{2,3},{3,2},{4,5},{5,4},{6,7},{7,6},{8,9},{9,8},{10,11... | collective-permute-start | bytes 6152 | tf_op jit(solution)/shard_map/ppermute | solution.py:481
  34.2 1.2 %collective-permute-start.14 = (f32[1,512]{1,0:T(1,128)S(1)}, f32[1,512]{1,0:T(1,128)S(1)}, u32[]{:S(2)}, u32[]{:S(2)}) collective-permute-start(f32[1,512]{1,0:T(1,128)S(1)} %hop.7), channel_id=1, source_target_pairs={{0,1},{1,0},{2,3},{3,2},{4,5},{5,4},{6,7},{7,6},{8,10},{9,13},{10,... | collective-permute-start | bytes 6152 | tf_op jit(solution)/shard_map/ppermute | solution.py:481
  35.6 1.2 %collective-permute-start.15 = (f32[1,512]{1,0:T(1,128)S(1)}, f32[1,512]{1,0:T(1,128)S(1)}, u32[]{:S(2)}, u32[]{:S(2)}) collective-permute-start(f32[1,512]{1,0:T(1,128)S(1)} %hop.8), channel_id=1, source_target_pairs={{0,1},{1,0},{2,3},{3,2},{4,6},{5,9},{6,7},{7,4},{8,10},{9,5},{10,1... | collective-permute-start | bytes 6152 | tf_op jit(solution)/shard_map/ppermute | solution.py:481
  37.0 3.1 %collective-permute-start.16 = (f32[1,512]{1,0:T(1,128)S(1)}, f32[1,512]{1,0:T(1,128)S(1)}, u32[]{:S(2)}, u32[]{:S(2)}) collective-permute-start(f32[1,512]{1,0:T(1,128)S(1)} %hop.9), channel_id=1, source_target_pairs={{0,2},{1,5},{2,3},{3,0},{4,6},{5,1},{6,7},{7,4},{8,9},{9,8},{10,11... | collective-permute-start | bytes 6152 | tf_op jit(solution)/shard_map/ppermute | solution.py:481
  40.4 5.3 %collective-permute-start.18 = (f32[4,128]{1,0:T(4,128)S(1)}, f32[4,128]{1,0:T(4,128)S(1)}, u32[]{:S(2)}, u32[]{:S(2)}) collective-permute-start(f32[4,128]{1,0:T(4,128)S(1)} %get-tuple-element.62), channel_id=1, source_target_pairs={{0,3},{1,2},{2,1},{3,0},{4,7},{5,6},{6,5},{7,4},{8,11},{9,10},{10,... | collective-permute-start | bytes 6152 | tf_op jit(solution)/shard_map/ppermute | solution.py:355
  40.5 6.8 %collective-permute-start.19 = (f32[4,128]{1,0:T(4,128)S(1)}, f32[4,128]{1,0:T(4,128)S(1)}, u32[]{:S(2)}, u32[]{:S(2)}) collective-permute-start(f32[4,128]{1,0:T(4,128)S(1)} %get-tuple-element.63), channel_id=1, source_target_pairs={{0,2},{1,3},{2,0},{3,1},{4,6},{5,7},{6,4},{7,5},{8,10},{9,11},{10,... | collective-permute-start | bytes 6152 | tf_op jit(solution)/shard_map/ppermute | solution.py:355
  45.7 1.6 %collective-permute-start.20 = (f32[4,128]{1,0:T(4,128)S(1)}, f32[4,128]{1,0:T(4,128)S(1)}, u32[]{:S(2)}, u32[]{:S(2)}) collective-permute-start(f32[4,128]{1,0:T(4,128)S(1)} %get-tuple-element.64), channel_id=1, source_target_pairs={{0,1},{1,0},{2,3},{3,2},{4,5},{5,4},{6,7},{7,6},{8,9},{9,8},{10,11... | collective-permute-start | bytes 6152 | tf_op jit(solution)/shard_map/ppermute | solution.py:355

commit v15 on v14

--- a/solution.py
+++ b/solution.py
@@ -186,10 +186,15 @@
         for piece, at, row, size in spans(near, k, panel):
             to = pl.multiple_of(top + (1 - e) * panel + row, 8)
             start(near[piece].at[pl.ds(at, size), :], target.at[pl.ds(to, size), :])
-    for j in range(order // known):
-        mine, theirs = (joined.at[j - 1], joined_near.at[j - 1]) if j else (trans, trans_near)
-        start(mine, af.at[rows(e ^ (2 * j), panel), :])
-        start(theirs, af.at[rows(e ^ (2 * j) ^ 1, panel), :])
+    start(trans, af.at[rows(e, panel), :])
+    start(trans_near, af.at[rows(1 - e, panel), :])
+    size = panel // 2
+    for j in range(1, order // known):
+        for half in range(2):
+            mine = e ^ (2 * j) ^ ((lax.axis_index("tm") + half) % 2)
+            for i, piece in ((mine, joined), (mine ^ 1, joined_near)):
+                at = pl.multiple_of(i * panel + half * size, size)
+                start(piece.at[j - 1, pl.ds(half * size, size), :], af.at[pl.ds(at, size), :])
     pf[count * known :, :] = jnp.concatenate([means[...], jnp.zeros((16 - steps, order), F32)], axis=0)
     for copy in copies:
         copy.wait()
@@ -388,7 +393,7 @@
     )
     across = [swap(trans_half, off) for off in range(2, devices, 2)]
     far = [swap(x, off) for off, x in enumerate(far, 2)]
-    moved = [y for x in across for y in (x, swap(x, 0, 1))]
+    moved = [y for x in across for y in (x, swap(x, 1, 1))]
     near = call(
         near_kernel,
         "near",
@@ -468,18 +473,20 @@
     late_map = swap(lax.optimization_barrier((early_map, mean))[0], 1)
     (mean,) = call(two_kernel, "two", 6, [shape(1, order)], [VMEM] * 4, [], (mean, info, ga, gb))
 
-    incoming = [first, swap(mean, 0, 1)]
+    def hop(x, block):
+        target = {i: i ^ 1 for i in range(blocks * devices)}
+        for at, to in ((block, block - 1), (block - 1, block)):
+            target[at * devices + 1] = to * devices + 1
+            target.update({at * devices + i: at * devices + j for i, j in ((0, 2), (2, 3), (3, 0))})
+        return lax.ppermute(x, ("tm", "state"), list(target.items()))
+
+    incoming = [first, hop(mean, blocks - 1)]
     (x,) = call(pair_hop_kernel, "pair_hop", 4, [shape(1, order)], [VMEM] * 3, [], (incoming[-1], late_map, early_map))
     m, vec = call(block_kernel, "block", 12, [square, shape(8, order)], [VMEM] * 2, [], (late_map, early_map))
     for block in range(blocks - 2, 0, -1):
         if block < blocks - 2:
             (x,) = call(hop_kernel, "hop", 4, [shape(1, order)], [VMEM] * 3, [], (incoming[-1], m, vec))
-        target = {i: i ^ 1 for i in range(blocks * devices)}
-        for at, to in ((block, block - 1), (block - 1, block)):
-            target[at * devices + 1] = to * devices + 1
-            target.update({at * devices + i: at * devices + j for i, j in ((0, 2), (2, 3), (3, 0))})
-        x = lax.ppermute(x, ("tm", "state"), list(target.items()))
-        incoming.append(x)
+        incoming.append(hop(x, block))
     g3 = swap(lax.optimization_barrier((gb, incoming[3]))[0], 1)
 
     given = list(call(

time: 48.1 us -> 48.2 us (level)
  starting transfers between devices: 17.9 us -> 16.2 us
  waiting for transfers between devices: 13.6 us -> 14.7 us
  Pallas kernels: 16.3 us -> 17 us
    ppermute x15 -> x14, starting transfers between devices: 15.2 us -> 13.2 us  [swap(): return lax.ppermute(x, ('tm', 'state'), pairs)]
    ppermute x6 -> x7, waiting for transfers between devices: 6.46 us -> 8.44 us  [hop(): return lax.ppermute(x, ('tm', 'state'), list(target.items()))]
    ppermute x15 -> x14, waiting for transfers between devices: 7.09 us -> 6.22 us  [swap(): return lax.ppermute(x, ('tm', 'state'), pairs)]
    pallas_call x18, Pallas kernels: 16.3 us -> 17 us  [call(): pl.pallas_call(kernel, out_shape=outs, in_specs=in_specs, out_specs=[VMEM...]
    ppermute x6 -> x7, starting transfers between devices: 2.67 us -> 3.06 us  [hop(): return lax.ppermute(x, ('tm', 'state'), list(target.items()))]
  transfers between devices with their start and end apart: 21 -> 21, of which waited for: 12 -> 10; matrix products, arithmetic and copies ran while one was open for 0% -> 0% of each run, Pallas kernels for 25% -> 26%
where the time goes in v15:
time: 48.2 us; the launch traced here: 48 us
  Pallas kernels  17 us (35%)
  starting transfers between devices  16.2 us (34%)
  waiting for transfers between devices  14.7 us (30%)
    pallas_call x18, Pallas kernels, call(): pl.pallas_call(kernel, out_shape=outs, in_specs=in_specs, out_specs=[VMEM...  17 us
    ppermute x14, starting transfers between devices, swap(): return lax.ppermute(x, ('tm', 'state'), pairs)  13.2 us
    ppermute x7, waiting for transfers between devices, hop(): return lax.ppermute(x, ('tm', 'state'), list(target.items()))  8.44 us
    ppermute x14, waiting for transfers between devices, swap(): return lax.ppermute(x, ('tm', 'state'), pairs)  6.22 us
    ppermute x7, starting transfers between devices, hop(): return lax.ppermute(x, ('tm', 'state'), list(target.items()))  3.06 us
  transfers between devices with their start and end apart: 21, of which 10 were waited for; matrix products, arithmetic and copies ran while one was open for 0% of the time, Pallas kernels for 26%

profile of v15, /device:TPU:0, one launch (start us, length us, event | category | flops | bytes accessed | tf_op | source)
XLA Modules:
  0.0 48.0 jit_solution(17737768711873143273)
XLA Ops:
  0.0 1.6 %pack.1 = (f32[4,200,128]{2,1,0:T(8,128)S(1)}, f32[4,72,128]{2,1,0:T(8,128)S(1)}, f32[64,512]{1,0:T(8,128)S(1)}, f32[1,512]{1,0:T(1,128)S(1)}) custom-call(f32[4,128,512]{2,1,0:T(8,128)} %cov.5, f32[4,128,512]{2,1,0:T(8,128)} %prec.5, f32[128,512]{1,0:T(8,128)} %trans.3, f32[1,512]{1,0:T(1,128)} %bitcast.1), custom_call_target="tpu_custom_call" | custom-call | tf_op jit(solution)/shard_map/pack/pallas_call | solution.py:366
  1.6 3.0 %collective-permute-start = (f32[64,512]{1,0:T(8,128)S(1)}, f32[64,512]{1,0:T(8,128)S(1)}, u32[]{:S(2)}, u32[]{:S(2)}) collective-permute-start(f32[64,512]{1,0:T(8,128)S(1)} %get-tuple-element.36), channel_id=1, source_target_pairs={{0,2},{1,3},{2,0},{3,1},{4,6},{5,7},{6,4},{7,5},{8,10},{9,11},{10,... | collective-permute-start | bytes 393224 | tf_op jit(solution)/shard_map/ppermute | solution.py:360
  4.6 1.5 %near.1 = (f32[256,512]{1,0:T(8,128)S(1)}, f32[256,512]{1,0:T(8,128)S(1)}) custom-call(f32[4,128,512]{2,1,0:T(8,128)} %cov.5, f32[4,128,512]{2,1,0:T(8,128)} %prec.5, f32[1,512]{1,0:T(1,128)S(1)} %get-tuple-element.35.after.first.refs_0_), custom_call_target="tpu_custom_call" | custom-call | tf_op jit(solution)/shard_map/near/pallas_call | solution.py:366
  6.2 0.5 %collective-permute-start.5 = (f32[256,512]{1,0:T(8,128)S(1)}, f32[256,512]{1,0:T(8,128)S(1)}, u32[]{:S(2)}, u32[]{:S(2)}) collective-permute-start(f32[256,512]{1,0:T(8,128)S(1)} %get-tuple-element.41), channel_id=1, source_target_pairs={{0,1},{1,0},{2,3},{3,2},{4,5},{5,4},{6,7},{7,6},{8,9},{9,8},{10,11... | collective-permute-start | bytes 1572872 | tf_op jit(solution)/shard_map/ppermute | solution.py:360
  6.8 1.4 %collective-permute-done.after.refs_0_ = f32[64,512]{1,0:T(8,128)S(1)} collective-permute-done((f32[64,512]{1,0:T(8,128)S(1)}, f32[64,512]{1,0:T(8,128)S(1)}, u32[]{:S(2)}, u32[]{:S(2)}) %collective-permute-start) | collective-permute-done | bytes 131104 | tf_op jit(solution)/shard_map/ppermute | solution.py:360
  8.1 0.7 %collective-permute-start.2 = (f32[64,512]{1,0:T(8,128)S(1)}, f32[64,512]{1,0:T(8,128)S(1)}, u32[]{:S(2)}, u32[]{:S(2)}) collective-permute-start(f32[64,512]{1,0:T(8,128)S(1)} %collective-permute-done.after.refs_0_), channel_id=1, source_target_pairs={{0,5},{1,4},{2,7},{3,6},{4,1},{5,0},{6,3},{7,2},{8,13},{9,12},{10,... | collective-permute-start | bytes 393224 | tf_op jit(solution)/shard_map/ppermute | solution.py:360
  8.9 1.6 %own.1 = (f32[4,128,512]{2,1,0:T(8,128)S(1)}, f32[128,512]{1,0:T(8,128)S(1)}, f32[4,512]{1,0:T(4,128)S(1)}) custom-call(f32[4,128,512]{2,1,0:T(8,128)} %cov.5, f32[4,128,512]{2,1,0:T(8,128)} %prec.5, f32[128,512]{1,0:T(8,128)} %trans.3, f32[4,512]{1,0:T(4,128)} %means.1, f32[64,512]{1,0:T(8,128)S(1)} %collective-permute-done.after.refs_0_), custom_call_target="tpu_custom_call" | custom-call | tf_op jit(solution)/shard_map/own/pallas_call | solution.py:366
  10.4 3.2 %collective-permute-done.2.refs_1_ = f32[64,512]{1,0:T(8,128)S(1)} collective-permute-done((f32[64,512]{1,0:T(8,128)S(1)}, f32[64,512]{1,0:T(8,128)S(1)}, u32[]{:S(2)}, u32[]{:S(2)}) %collective-permute-start.2) | collective-permute-done | bytes 131104 | tf_op jit(solution)/shard_map/ppermute | solution.py:360
  13.6 0.6 %join.1.joined = f32[1,128,512]{2,1,0:T(8,128)S(1)} custom-call(f32[128,512]{1,0:T(8,128)S(1)} %get-tuple-element.39.after.trans, f32[64,512]{1,0:T(8,128)S(1)} %collective-permute-done.after.refs_0_, f32[64,512]{1,0:T(8,128)S(1)} %collective-permute-done.2.refs_1_), custom_call_target="tpu_custom_call" | custom-call | tf_op jit(solution)/shard_map/join/pallas_call | solution.py:366
  14.2 0.5 %collective-permute-start.3 = (f32[1,128,512]{2,1,0:T(8,128)S(1)}, f32[1,128,512]{2,1,0:T(8,128)S(1)}, u32[]{:S(2)}, u32[]{:S(2)}) collective-permute-start(f32[1,128,512]{2,1,0:T(8,128)S(1)} %join.1.joined), channel_id=1, source_target_pairs={{0,1},{1,0},{2,3},{3,2},{4,5},{5,4},{6,7},{7,6},{8,9},{9,8},{10,11... | collective-permute-start | bytes 786440 | tf_op jit(solution)/shard_map/ppermute | solution.py:360
  14.7 1.8 %collective-permute-start.7 = (f32[4,72,128]{2,1,0:T(8,128)S(1)}, f32[4,72,128]{2,1,0:T(8,128)S(1)}, u32[]{:S(2)}, u32[]{:S(2)}) collective-permute-start(f32[4,72,128]{2,1,0:T(8,128)S(1)} %get-tuple-element.53), channel_id=1, source_target_pairs={{0,3},{1,2},{2,1},{3,0},{4,7},{5,6},{6,5},{7,4},{8,11},{9,10},{10,... | collective-permute-start | bytes 442376 | tf_op jit(solution)/shard_map/ppermute | solution.py:360
  16.6 3.6 %early.1 = (f32[16,512]{1,0:T(8,128)S(1)}, bf16[2,256,512]{2,1,0:T(8,128)(2,1)S(1)}, bf16[2,2,256,512]{3,2,1,0:T(8,128)(2,1)S(1)}, f32[2,256,256]{2,1,0:T(8,128)...) custom-call(f32[4,128,512]{2,1,0:T(8,128)S(1)} %get-tuple-element.37.own, ...), custom_call_target="tpu_custom_call" | custom-call | tf_op jit(solution)/shard_map/early/pallas_call | solution.py:366
  20.1 2.5 %middle.1 = (f32[512,512]{1,0:T(8,128)S(1)}, f32[512,512]{1,0:T(8,128)S(1)}, f32[2,512,128]{2,1,0:T(8,128)S(1)}, f32[2,128,512]{2,1,0:T(8,128)S(1)}) custom-call(bf16[2,256,512]{2,1,0:T(8,128)(2,1)S(1)} %get-tuple-element.43.a_far, bf16[2,2,256,512]{3,2,1,0:T(8,128)(2,1)S(1)} %get-tuple-element.44.l_known, f32[2,256,256]{2,1,0:T(8,128)S(1)} %get-tuple-element.45.c_known, ...), custom_call_target="tpu_custom_call" | custom-call | tf_op jit(solution)/shard_map/middle/pallas_call | solution.py:366
  22.7 1.3 %late.1 = (f32[512,512]{1,0:T(8,128)S(1)}, f32[512,512]{1,0:T(8,128)S(1)}, f32[1,512]{1,0:T(1,128)S(1)}) custom-call(f32[1,512]{1,0:T(1,128)S(1)} %get-tuple-element.35.after.first.refs_0_, f32[16,512]{1,0:T(8,128)S(1)} %get-tuple-element.42.info, bf16[2,256,512]{2,1,0:T(8,128)(2,1)S(1)} %get-tuple-element.43.a_far, ...), custom_call_target="tpu_custom_call", output_to_operand_aliasing={{0}: (3, {}), {1}: (4, {})} | custom-call | tf_op jit(solution)/shard_map/late/pallas_call | solution.py:366
  24.2 1.0 %pair.1.early.refs_12_ = f32[520,512]{1,0:T(8,128)S(1)} custom-call(f32[16,512]{1,0:T(8,128)S(1)} %get-tuple-element.42.info, f32[512,512]{1,0:T(8,128)S(1)} %get-tuple-element.55.ga, f32[512,512]{1,0:T(8,128)S(1)} %get-tuple-element.60.gb.refs_13_), custom_call_target="tpu_custom_call" | custom-call | tf_op jit(solution)/shard_map/pair/pallas_call | solution.py:366
  25.2 0.4 collective-permute-start.10
  25.7 0.3 two.1
  26.1 1.9 %collective-permute-done.9.x.refs_1_ = f32[1,512]{1,0:T(1,128)S(1)} collective-permute-done((f32[1,512]{1,0:T(1,128)S(1)}, f32[1,512]{1,0:T(1,128)S(1)}, u32[]{:S(2)}, u32[]{:S(2)}) %collective-permute-start.9) | collective-permute-done | bytes 2080 | tf_op jit(solution)/shard_map/ppermute | solution.py:481
  28.0 0.3 pair_hop.1
  28.3 0.4 collective-permute-start.11
  28.7 1.0 %block.1 = (f32[512,512]{1,0:T(8,128)S(1)}, f32[8,512]{1,0:T(8,128)S(1)}) custom-call(f32[520,512]{1,0:T(8,128)S(1)} %collective-permute-done.10.late.refs_10_, f32[520,512]{1,0:T(8,128)S(1)} %pair.1.early.refs_12_), custom_call_target="tpu_custom_call" | custom-call | tf_op jit(solution)/shard_map/block/pallas_call | solution.py:366
  30.0 1.0 %collective-permute-done.12.x.refs_3_ = f32[1,512]{1,0:T(1,128)S(1)} collective-permute-done((f32[1,512]{1,0:T(1,128)S(1)}, f32[1,512]{1,0:T(1,128)S(1)}, u32[]{:S(2)}, u32[]{:S(2)}) %collective-permute-start.12) | collective-permute-done | bytes 2080 | tf_op jit(solution)/shard_map/ppermute | solution.py:481
  31.4 0.4 collective-permute-start.13
  31.8 1.9 %collective-permute-done.13.x.refs_4_ = f32[1,512]{1,0:T(1,128)S(1)} collective-permute-done((f32[1,512]{1,0:T(1,128)S(1)}, f32[1,512]{1,0:T(1,128)S(1)}, u32[]{:S(2)}, u32[]{:S(2)}) %collective-permute-start.13) | collective-permute-done | bytes 2080 | tf_op jit(solution)/shard_map/ppermute | solution.py:481
  34.1 1.0 %collective-permute-done.14.x.refs_5_ = f32[1,512]{1,0:T(1,128)S(1)} collective-permute-done((f32[1,512]{1,0:T(1,128)S(1)}, f32[1,512]{1,0:T(1,128)S(1)}, u32[]{:S(2)}, u32[]{:S(2)}) %collective-permute-start.14) | collective-permute-done | bytes 2080 | tf_op jit(solution)/shard_map/ppermute | solution.py:481
  35.5 1.0 %collective-permute-done.15.x.refs_6_ = f32[1,512]{1,0:T(1,128)S(1)} collective-permute-done((f32[1,512]{1,0:T(1,128)S(1)}, f32[1,512]{1,0:T(1,128)S(1)}, u32[]{:S(2)}, u32[]{:S(2)}) %collective-permute-start.15) | collective-permute-done | bytes 2080 | tf_op jit(solution)/shard_map/ppermute | solution.py:481
  36.6 1.4 %collective-permute-start.16 = (f32[1,512]{1,0:T(1,128)S(1)}, f32[1,512]{1,0:T(1,128)S(1)}, u32[]{:S(2)}, u32[]{:S(2)}) collective-permute-start(f32[1,512]{1,0:T(1,128)S(1)} %hop.9), channel_id=1, source_target_pairs={{0,2},{1,5},{2,3},{3,0},{4,6},{5,1},{6,7},{7,4},{8,9},{9,8},{10,11... | collective-permute-start | bytes 6152 | tf_op jit(solution)/shard_map/ppermute | solution.py:481
  38.1 1.6 %collective-permute-done.16.refs_7_ = f32[1,512]{1,0:T(1,128)S(1)} collective-permute-done((f32[1,512]{1,0:T(1,128)S(1)}, f32[1,512]{1,0:T(1,128)S(1)}, u32[]{:S(2)}, u32[]{:S(2)}) %collective-permute-start.16) | collective-permute-done | bytes 2080 | tf_op jit(solution)/shard_map/ppermute | solution.py:481
  39.7 0.4 last.1
  40.2 5.6 %collective-permute-start.19 = (f32[4,128]{1,0:T(4,128)S(1)}, f32[4,128]{1,0:T(4,128)S(1)}, u32[]{:S(2)}, u32[]{:S(2)}) collective-permute-start(f32[4,128]{1,0:T(4,128)S(1)} %get-tuple-element.63), channel_id=1, source_target_pairs={{0,2},{1,3},{2,0},{3,1},{4,6},{5,7},{6,4},{7,5},{8,10},{9,11},{10,... | collective-permute-start | bytes 6152 | tf_op jit(solution)/shard_map/ppermute | solution.py:360
  45.9 1.6 %collective-permute-done.19.refs_2_ = f32[4,128]{1,0:T(4,128)S(1)} collective-permute-done((f32[4,128]{1,0:T(4,128)S(1)}, f32[4,128]{1,0:T(4,128)S(1)}, u32[]{:S(2)}, u32[]{:S(2)}) %collective-permute-start.19) | collective-permute-done | bytes 2080 | tf_op jit(solution)/shard_map/ppermute | solution.py:360
  47.4 0.6 %out.1 = f32[4,128]{1,0:T(4,128)} custom-call(f32[4,128]{1,0:T(4,128)S(1)} %get-tuple-element.61.refs_0_, f32[4,128]{1,0:T(4,128)S(1)} %collective-permute-done.18.refs_1_, f32[4,128]{1,0:T(4,128)S(1)} %collective-permute-done.19.refs_2_, f32[4,128]{1,0:T(4,128)S(1)} %collective-permute-done.20.refs_3_), custom_call_target="tpu_custom_call" | custom-call | tf_op jit(solution)/shard_map/out/pallas_call | solution.py:366
  (30 shorter events, 2.2 us)
Async XLA Ops:
  1.6 5.1 %copy-start = (f32[128,512]{1,0:T(8,128)S(1)}, f32[128,512]{1,0:T(8,128)}, u32[]{:S(2)}) copy-start(f32[128,512]{1,0:T(8,128)} %trans.3) | copy-start | bytes 786436
  1.6 6.5 %collective-permute-start = (f32[64,512]{1,0:T(8,128)S(1)}, f32[64,512]{1,0:T(8,128)S(1)}, u32[]{:S(2)}, u32[]{:S(2)}) collective-permute-start(f32[64,512]{1,0:T(8,128)S(1)} %get-tuple-element.36), channel_id=1, source_target_pairs={{0,2},{1,3},{2,0},{3,1},{4,6},{5,7},{6,4},{7,5},{8,10},{9,11},{10,... | collective-permute-start | bytes 393224 | tf_op jit(solution)/shard_map/ppermute | solution.py:360
  6.1 10.4 %collective-permute-start.4 = (f32[256,512]{1,0:T(8,128)S(1)}, f32[256,512]{1,0:T(8,128)S(1)}, u32[]{:S(2)}, u32[]{:S(2)}) collective-permute-start(f32[256,512]{1,0:T(8,128)S(1)} %get-tuple-element.40), channel_id=1, source_target_pairs={{0,1},{1,0},{2,3},{3,2},{4,5},{5,4},{6,7},{7,6},{8,9},{9,8},{10,11... | collective-permute-start | bytes 1572872 | tf_op jit(solution)/shard_map/ppermute | solution.py:360
  6.2 10.4 %collective-permute-start.5 = (f32[256,512]{1,0:T(8,128)S(1)}, f32[256,512]{1,0:T(8,128)S(1)}, u32[]{:S(2)}, u32[]{:S(2)}) collective-permute-start(f32[256,512]{1,0:T(8,128)S(1)} %get-tuple-element.41), channel_id=1, source_target_pairs={{0,1},{1,0},{2,3},{3,2},{4,5},{5,4},{6,7},{7,6},{8,9},{9,8},{10,11... | collective-permute-start | bytes 1572872 | tf_op jit(solution)/shard_map/ppermute | solution.py:360
  6.7 13.4 %collective-permute-start.6 = (f32[4,200,128]{2,1,0:T(8,128)S(1)}, f32[4,200,128]{2,1,0:T(8,128)S(1)}, u32[]{:S(2)}, u32[]{:S(2)}) collective-permute-start(f32[4,200,128]{2,1,0:T(8,128)S(1)} %get-tuple-element.48), channel_id=1, source_target_pairs={{0,2},{1,3},{2,0},{3,1},{4,6},{5,7},{6,4},{7,5},{8,10},{9,11},{10,... | collective-permute-start | bytes 1228808 | tf_op jit(solution)/shard_map/ppermute | solution.py:360
  6.7 8.0 %collective-permute-start.1 = (f32[128,512]{1,0:T(8,128)S(1)}, f32[128,512]{1,0:T(8,128)S(1)}, u32[]{:S(2)}, u32[]{:S(2)}) collective-permute-start(f32[128,512]{1,0:T(8,128)S(1)} %copy-done), channel_id=1, source_target_pairs={{0,1},{1,0},{2,3},{3,2},{4,5},{5,4},{6,7},{7,6},{8,9},{9,8},{10,11... | collective-permute-start | bytes 786440 | tf_op jit(solution)/shard_map/ppermute | solution.py:360
  8.1 5.5 %collective-permute-start.2 = (f32[64,512]{1,0:T(8,128)S(1)}, f32[64,512]{1,0:T(8,128)S(1)}, u32[]{:S(2)}, u32[]{:S(2)}) collective-permute-start(f32[64,512]{1,0:T(8,128)S(1)} %collective-permute-done.after.refs_0_), channel_id=1, source_target_pairs={{0,5},{1,4},{2,7},{3,6},{4,1},{5,0},{6,3},{7,2},{8,13},{9,12},{10,... | collective-permute-start | bytes 393224 | tf_op jit(solution)/shard_map/ppermute | solution.py:360
  14.2 2.3 %collective-permute-start.3 = (f32[1,128,512]{2,1,0:T(8,128)S(1)}, f32[1,128,512]{2,1,0:T(8,128)S(1)}, u32[]{:S(2)}, u32[]{:S(2)}) collective-permute-start(f32[1,128,512]{2,1,0:T(8,128)S(1)} %join.1.joined), channel_id=1, source_target_pairs={{0,1},{1,0},{2,3},{3,2},{4,5},{5,4},{6,7},{7,6},{8,9},{9,8},{10,11... | collective-permute-start | bytes 786440 | tf_op jit(solution)/shard_map/ppermute | solution.py:360
  14.7 8.0 %collective-permute-start.7 = (f32[4,72,128]{2,1,0:T(8,128)S(1)}, f32[4,72,128]{2,1,0:T(8,128)S(1)}, u32[]{:S(2)}, u32[]{:S(2)}) collective-permute-start(f32[4,72,128]{2,1,0:T(8,128)S(1)} %get-tuple-element.53), channel_id=1, source_target_pairs={{0,3},{1,2},{2,1},{3,0},{4,7},{5,6},{6,5},{7,4},{8,11},{9,10},{10,... | collective-permute-start | bytes 442376 | tf_op jit(solution)/shard_map/ppermute | solution.py:360
  24.0 1.2 %collective-permute-start.8 = (f32[1,512]{1,0:T(1,128)S(1)}, f32[1,512]{1,0:T(1,128)S(1)}, u32[]{:S(2)}, u32[]{:S(2)}) collective-permute-start(f32[1,512]{1,0:T(1,128)S(1)} %get-tuple-element.54), channel_id=1, source_target_pairs={{0,1},{1,0},{2,3},{3,2},{4,5},{5,4},{6,7},{7,6},{8,9},{9,8},{10,11... | collective-permute-start | bytes 6152 | tf_op jit(solution)/shard_map/ppermute | solution.py:360
  25.2 2.7 %collective-permute-start.10 = (f32[520,512]{1,0:T(8,128)S(1)}, f32[520,512]{1,0:T(8,128)S(1)}, u32[]{:S(2)}, u32[]{:S(2)}) collective-permute-start(f32[520,512]{1,0:T(8,128)S(1)} %pair.1.early.refs_12_), channel_id=1, source_target_pairs={{0,1},{1,0},{2,3},{3,2},{4,5},{5,4},{6,7},{7,6},{8,9},{9,8},{10,11... | collective-permute-start | bytes 3194888 | tf_op jit(solution)/shard_map/ppermute | solution.py:360
  26.0 2.0 %collective-permute-start.9 = (f32[1,512]{1,0:T(1,128)S(1)}, f32[1,512]{1,0:T(1,128)S(1)}, u32[]{:S(2)}, u32[]{:S(2)}) collective-permute-start(f32[1,512]{1,0:T(1,128)S(1)} %two.1), channel_id=1, source_target_pairs={{0,1},{1,0},{2,3},{3,2},{4,5},{5,4},{6,7},{7,6},{8,9},{9,8},{10,11... | collective-permute-start | bytes 6152 | tf_op jit(solution)/shard_map/ppermute | solution.py:481
  28.3 1.4 %collective-permute-start.11 = (f32[1,512]{1,0:T(1,128)S(1)}, f32[1,512]{1,0:T(1,128)S(1)}, u32[]{:S(2)}, u32[]{:S(2)}) collective-permute-start(f32[1,512]{1,0:T(1,128)S(1)} %pair_hop.1), channel_id=1, source_target_pairs={{0,1},{1,0},{2,3},{3,2},{4,5},{5,4},{6,7},{7,6},{8,9},{9,8},{10,11... | collective-permute-start | bytes 6152 | tf_op jit(solution)/shard_map/ppermute | solution.py:481
  29.8 1.2 %collective-permute-start.12 = (f32[1,512]{1,0:T(1,128)S(1)}, f32[1,512]{1,0:T(1,128)S(1)}, u32[]{:S(2)}, u32[]{:S(2)}) collective-permute-start(f32[1,512]{1,0:T(1,128)S(1)} %hop.5), channel_id=1, source_target_pairs={{0,1},{1,0},{2,3},{3,2},{4,5},{5,4},{6,7},{7,6},{8,9},{9,8},{10,11... | collective-permute-start | bytes 6152 | tf_op jit(solution)/shard_map/ppermute | solution.py:481
  31.0 8.7 %collective-permute-start.17 = (f32[512,512]{1,0:T(8,128)S(1)}, f32[512,512]{1,0:T(8,128)S(1)}, u32[]{:S(2)}, u32[]{:S(2)}) collective-permute-start(f32[512,512]{1,0:T(8,128)S(1)} %get-tuple-element.60.gb.refs_13_), channel_id=1, source_target_pairs={{0,1},{1,0},{2,3},{3,2},{4,5},{5,4},{6,7},{7,6},{8,9},{9,8},{10,11... | collective-permute-start | bytes 3145736 | tf_op jit(solution)/shard_map/ppermute | solution.py:360
  31.4 2.3 %collective-permute-start.13 = (f32[1,512]{1,0:T(1,128)S(1)}, f32[1,512]{1,0:T(1,128)S(1)}, u32[]{:S(2)}, u32[]{:S(2)}) collective-permute-start(f32[1,512]{1,0:T(1,128)S(1)} %hop.6), channel_id=1, source_target_pairs={{0,1},{1,0},{2,3},{3,2},{4,5},{5,4},{6,7},{7,6},{8,9},{9,8},{10,11... | collective-permute-start | bytes 6152 | tf_op jit(solution)/shard_map/ppermute | solution.py:481
  33.9 1.2 %collective-permute-start.14 = (f32[1,512]{1,0:T(1,128)S(1)}, f32[1,512]{1,0:T(1,128)S(1)}, u32[]{:S(2)}, u32[]{:S(2)}) collective-permute-start(f32[1,512]{1,0:T(1,128)S(1)} %hop.7), channel_id=1, source_target_pairs={{0,1},{1,0},{2,3},{3,2},{4,5},{5,4},{6,7},{7,6},{8,10},{9,13},{10,... | collective-permute-start | bytes 6152 | tf_op jit(solution)/shard_map/ppermute | solution.py:481
  35.2 1.2 %collective-permute-start.15 = (f32[1,512]{1,0:T(1,128)S(1)}, f32[1,512]{1,0:T(1,128)S(1)}, u32[]{:S(2)}, u32[]{:S(2)}) collective-permute-start(f32[1,512]{1,0:T(1,128)S(1)} %hop.8), channel_id=1, source_target_pairs={{0,1},{1,0},{2,3},{3,2},{4,6},{5,9},{6,7},{7,4},{8,10},{9,5},{10,1... | collective-permute-start | bytes 6152 | tf_op jit(solution)/shard_map/ppermute | solution.py:481
  36.6 3.1 %collective-permute-start.16 = (f32[1,512]{1,0:T(1,128)S(1)}, f32[1,512]{1,0:T(1,128)S(1)}, u32[]{:S(2)}, u32[]{:S(2)}) collective-permute-start(f32[1,512]{1,0:T(1,128)S(1)} %hop.9), channel_id=1, source_target_pairs={{0,2},{1,5},{2,3},{3,0},{4,6},{5,1},{6,7},{7,4},{8,9},{9,8},{10,11... | collective-permute-start | bytes 6152 | tf_op jit(solution)/shard_map/ppermute | solution.py:481
  40.1 5.7 %collective-permute-start.18 = (f32[4,128]{1,0:T(4,128)S(1)}, f32[4,128]{1,0:T(4,128)S(1)}, u32[]{:S(2)}, u32[]{:S(2)}) collective-permute-start(f32[4,128]{1,0:T(4,128)S(1)} %get-tuple-element.62), channel_id=1, source_target_pairs={{0,3},{1,2},{2,1},{3,0},{4,7},{5,6},{6,5},{7,4},{8,11},{9,10},{10,... | collective-permute-start | bytes 6152 | tf_op jit(solution)/shard_map/ppermute | solution.py:360
  40.2 7.2 %collective-permute-start.19 = (f32[4,128]{1,0:T(4,128)S(1)}, f32[4,128]{1,0:T(4,128)S(1)}, u32[]{:S(2)}, u32[]{:S(2)}) collective-permute-start(f32[4,128]{1,0:T(4,128)S(1)} %get-tuple-element.63), channel_id=1, source_target_pairs={{0,2},{1,3},{2,0},{3,1},{4,6},{5,7},{6,4},{7,5},{8,10},{9,11},{10,... | collective-permute-start | bytes 6152 | tf_op jit(solution)/shard_map/ppermute | solution.py:360
  45.8 1.6 %collective-permute-start.20 = (f32[4,128]{1,0:T(4,128)S(1)}, f32[4,128]{1,0:T(4,128)S(1)}, u32[]{:S(2)}, u32[]{:S(2)}) collective-permute-start(f32[4,128]{1,0:T(4,128)S(1)} %get-tuple-element.64), channel_id=1, source_target_pairs={{0,1},{1,0},{2,3},{3,2},{4,5},{5,4},{6,7},{7,6},{8,9},{9,8},{10,11... | collective-permute-start | bytes 6152 | tf_op jit(solution)/shard_map/ppermute | solution.py:360

commit v16 on v15

--- a/solution.py
+++ b/solution.py
@@ -186,15 +186,10 @@
         for piece, at, row, size in spans(near, k, panel):
             to = pl.multiple_of(top + (1 - e) * panel + row, 8)
             start(near[piece].at[pl.ds(at, size), :], target.at[pl.ds(to, size), :])
-    start(trans, af.at[rows(e, panel), :])
-    start(trans_near, af.at[rows(1 - e, panel), :])
-    size = panel // 2
-    for j in range(1, order // known):
-        for half in range(2):
-            mine = e ^ (2 * j) ^ ((lax.axis_index("tm") + half) % 2)
-            for i, piece in ((mine, joined), (mine ^ 1, joined_near)):
-                at = pl.multiple_of(i * panel + half * size, size)
-                start(piece.at[j - 1, pl.ds(half * size, size), :], af.at[pl.ds(at, size), :])
+    for j in range(order // known):
+        mine, theirs = (joined.at[j - 1], joined_near.at[j - 1]) if j else (trans, trans_near)
+        start(mine, af.at[rows(e ^ (2 * j), panel), :])
+        start(theirs, af.at[rows(e ^ (2 * j) ^ 1, panel), :])
     pf[count * known :, :] = jnp.concatenate([means[...], jnp.zeros((16 - steps, order), F32)], axis=0)
     for copy in copies:
         copy.wait()
@@ -393,7 +388,7 @@
     )
     across = [swap(trans_half, off) for off in range(2, devices, 2)]
     far = [swap(x, off) for off, x in enumerate(far, 2)]
-    moved = [y for x in across for y in (x, swap(x, 1, 1))]
+    moved = [y for x in across for y in (x, swap(x, 0, 1))]
     near = call(
         near_kernel,
         "near",

time: 48.2 us -> 47.6 us (0.988)
  starting transfers between devices: 16.2 us -> 17.2 us
  waiting for transfers between devices: 14.7 us -> 13.7 us
  Pallas kernels: 17 us -> 16.3 us
    ppermute x14, starting transfers between devices: 13.2 us -> 14.4 us  [swap(): return lax.ppermute(x, ('tm', 'state'), pairs)]
    ppermute x14, waiting for transfers between devices: 6.22 us -> 5.02 us  [swap(): return lax.ppermute(x, ('tm', 'state'), pairs)]
    pallas_call x18, Pallas kernels: 17 us -> 16.3 us  [call(): pl.pallas_call(kernel, out_shape=outs, in_specs=in_specs, out_specs=[VMEM...]
  transfers between devices with their start and end apart: 21 -> 21, of which waited for: 10 -> 11; matrix products, arithmetic and copies ran while one was open for 0% -> 0% of each run, Pallas kernels for 26% -> 25%
where the time goes in v16:
time: 47.6 us; the launch traced here: 47.4 us
  starting transfers between devices  17.2 us (36%)
  Pallas kernels  16.3 us (34%)
  waiting for transfers between devices  13.7 us (29%)
    pallas_call x18, Pallas kernels, call(): pl.pallas_call(kernel, out_shape=outs, in_specs=in_specs, out_specs=[VMEM...  16.3 us
    ppermute x14, starting transfers between devices, swap(): return lax.ppermute(x, ('tm', 'state'), pairs)  14.4 us
    ppermute x7, waiting for transfers between devices, hop(): return lax.ppermute(x, ('tm', 'state'), list(target.items()))  8.69 us
    ppermute x14, waiting for transfers between devices, swap(): return lax.ppermute(x, ('tm', 'state'), pairs)  5.02 us
    ppermute x7, starting transfers between devices, hop(): return lax.ppermute(x, ('tm', 'state'), list(target.items()))  2.8 us
  transfers between devices with their start and end apart: 21, of which 11 were waited for; matrix products, arithmetic and copies ran while one was open for 0% of the time, Pallas kernels for 25%

profile of v16, /device:TPU:0, one launch (start us, length us, event | category | flops | bytes accessed | tf_op | source)
XLA Modules:
  0.0 47.4 jit_solution(2109707291983138593)
XLA Ops:
  0.0 1.6 %pack.1 = (f32[4,200,128]{2,1,0:T(8,128)S(1)}, f32[4,72,128]{2,1,0:T(8,128)S(1)}, f32[64,512]{1,0:T(8,128)S(1)}, f32[1,512]{1,0:T(1,128)S(1)}) custom-call(f32[4,128,512]{2,1,0:T(8,128)} %cov.5, f32[4,128,512]{2,1,0:T(8,128)} %prec.5, f32[128,512]{1,0:T(8,128)} %trans.3, f32[1,512]{1,0:T(1,128)} %bitcast.1), custom_call_target="tpu_custom_call" | custom-call | tf_op jit(solution)/shard_map/pack/pallas_call | solution.py:361
  1.6 3.0 %collective-permute-start = (f32[64,512]{1,0:T(8,128)S(1)}, f32[64,512]{1,0:T(8,128)S(1)}, u32[]{:S(2)}, u32[]{:S(2)}) collective-permute-start(f32[64,512]{1,0:T(8,128)S(1)} %get-tuple-element.36), channel_id=1, source_target_pairs={{0,2},{1,3},{2,0},{3,1},{4,6},{5,7},{6,4},{7,5},{8,10},{9,11},{10,... | collective-permute-start | bytes 393224 | tf_op jit(solution)/shard_map/ppermute | solution.py:355
  4.6 1.5 %near.1 = (f32[256,512]{1,0:T(8,128)S(1)}, f32[256,512]{1,0:T(8,128)S(1)}) custom-call(f32[4,128,512]{2,1,0:T(8,128)} %cov.5, f32[4,128,512]{2,1,0:T(8,128)} %prec.5, f32[1,512]{1,0:T(1,128)S(1)} %get-tuple-element.35.after.first.refs_0_), custom_call_target="tpu_custom_call" | custom-call | tf_op jit(solution)/shard_map/near/pallas_call | solution.py:361
  6.2 0.5 %collective-permute-start.5 = (f32[256,512]{1,0:T(8,128)S(1)}, f32[256,512]{1,0:T(8,128)S(1)}, u32[]{:S(2)}, u32[]{:S(2)}) collective-permute-start(f32[256,512]{1,0:T(8,128)S(1)} %get-tuple-element.41), channel_id=1, source_target_pairs={{0,1},{1,0},{2,3},{3,2},{4,5},{5,4},{6,7},{7,6},{8,9},{9,8},{10,11... | collective-permute-start | bytes 1572872 | tf_op jit(solution)/shard_map/ppermute | solution.py:355
  6.8 1.4 %collective-permute-done.after.refs_0_ = f32[64,512]{1,0:T(8,128)S(1)} collective-permute-done((f32[64,512]{1,0:T(8,128)S(1)}, f32[64,512]{1,0:T(8,128)S(1)}, u32[]{:S(2)}, u32[]{:S(2)}) %collective-permute-start) | collective-permute-done | bytes 131104 | tf_op jit(solution)/shard_map/ppermute | solution.py:355
  8.1 1.8 %collective-permute-start.2 = (f32[64,512]{1,0:T(8,128)S(1)}, f32[64,512]{1,0:T(8,128)S(1)}, u32[]{:S(2)}, u32[]{:S(2)}) collective-permute-start(f32[64,512]{1,0:T(8,128)S(1)} %collective-permute-done.after.refs_0_), channel_id=1, source_target_pairs={{0,4},{1,5},{2,6},{3,7},{4,0},{5,1},{6,2},{7,3},{8,12},{9,13},{10,... | collective-permute-start | bytes 393224 | tf_op jit(solution)/shard_map/ppermute | solution.py:355
  9.9 1.6 %own.1 = (f32[4,128,512]{2,1,0:T(8,128)S(1)}, f32[128,512]{1,0:T(8,128)S(1)}, f32[4,512]{1,0:T(4,128)S(1)}) custom-call(f32[4,128,512]{2,1,0:T(8,128)} %cov.5, f32[4,128,512]{2,1,0:T(8,128)} %prec.5, f32[128,512]{1,0:T(8,128)} %trans.3, f32[4,512]{1,0:T(4,128)} %means.1, f32[64,512]{1,0:T(8,128)S(1)} %collective-permute-done.after.refs_0_), custom_call_target="tpu_custom_call" | custom-call | tf_op jit(solution)/shard_map/own/pallas_call | solution.py:361
  11.5 1.6 %collective-permute-done.2.refs_1_ = f32[64,512]{1,0:T(8,128)S(1)} collective-permute-done((f32[64,512]{1,0:T(8,128)S(1)}, f32[64,512]{1,0:T(8,128)S(1)}, u32[]{:S(2)}, u32[]{:S(2)}) %collective-permute-start.2) | collective-permute-done | bytes 131104 | tf_op jit(solution)/shard_map/ppermute | solution.py:355
  13.1 0.6 %join.1.joined = f32[1,128,512]{2,1,0:T(8,128)S(1)} custom-call(f32[128,512]{1,0:T(8,128)S(1)} %get-tuple-element.39.after.trans, f32[64,512]{1,0:T(8,128)S(1)} %collective-permute-done.after.refs_0_, f32[64,512]{1,0:T(8,128)S(1)} %collective-permute-done.2.refs_1_), custom_call_target="tpu_custom_call" | custom-call | tf_op jit(solution)/shard_map/join/pallas_call | solution.py:361
  13.8 2.0 %collective-permute-start.7 = (f32[4,72,128]{2,1,0:T(8,128)S(1)}, f32[4,72,128]{2,1,0:T(8,128)S(1)}, u32[]{:S(2)}, u32[]{:S(2)}) collective-permute-start(f32[4,72,128]{2,1,0:T(8,128)S(1)} %get-tuple-element.53), channel_id=1, source_target_pairs={{0,3},{1,2},{2,1},{3,0},{4,7},{5,6},{6,5},{7,4},{8,11},{9,10},{10,... | collective-permute-start | bytes 442376 | tf_op jit(solution)/shard_map/ppermute | solution.py:355
  15.8 2.9 %early.1 = (f32[16,512]{1,0:T(8,128)S(1)}, bf16[2,256,512]{2,1,0:T(8,128)(2,1)S(1)}, bf16[2,2,256,512]{3,2,1,0:T(8,128)(2,1)S(1)}, f32[2,256,256]{2,1,0:T(8,128)...) custom-call(f32[4,128,512]{2,1,0:T(8,128)S(1)} %get-tuple-element.37.own, ...), custom_call_target="tpu_custom_call" | custom-call | tf_op jit(solution)/shard_map/early/pallas_call | solution.py:361
  18.7 0.3 collective-permute-done.6.refs_0_
  19.0 2.5 %middle.1 = (f32[512,512]{1,0:T(8,128)S(1)}, f32[512,512]{1,0:T(8,128)S(1)}, f32[2,512,128]{2,1,0:T(8,128)S(1)}, f32[2,128,512]{2,1,0:T(8,128)S(1)}) custom-call(bf16[2,256,512]{2,1,0:T(8,128)(2,1)S(1)} %get-tuple-element.43.a_far, bf16[2,2,256,512]{3,2,1,0:T(8,128)(2,1)S(1)} %get-tuple-element.44.l_known, f32[2,256,256]{2,1,0:T(8,128)S(1)} %get-tuple-element.45.c_known, ...), custom_call_target="tpu_custom_call" | custom-call | tf_op jit(solution)/shard_map/middle/pallas_call | solution.py:361
  21.6 1.3 %late.1 = (f32[512,512]{1,0:T(8,128)S(1)}, f32[512,512]{1,0:T(8,128)S(1)}, f32[1,512]{1,0:T(1,128)S(1)}) custom-call(f32[1,512]{1,0:T(1,128)S(1)} %get-tuple-element.35.after.first.refs_0_, f32[16,512]{1,0:T(8,128)S(1)} %get-tuple-element.42.info, bf16[2,256,512]{2,1,0:T(8,128)(2,1)S(1)} %get-tuple-element.43.a_far, ...), custom_call_target="tpu_custom_call", output_to_operand_aliasing={{0}: (3, {}), {1}: (4, {})} | custom-call | tf_op jit(solution)/shard_map/late/pallas_call | solution.py:361
  23.0 1.0 %pair.1.early.refs_12_ = f32[520,512]{1,0:T(8,128)S(1)} custom-call(f32[16,512]{1,0:T(8,128)S(1)} %get-tuple-element.42.info, f32[512,512]{1,0:T(8,128)S(1)} %get-tuple-element.55.ga, f32[512,512]{1,0:T(8,128)S(1)} %get-tuple-element.60.gb.refs_13_), custom_call_target="tpu_custom_call" | custom-call | tf_op jit(solution)/shard_map/pair/pallas_call | solution.py:361
  24.1 0.4 collective-permute-start.10
  24.5 0.3 two.1
  25.0 1.9 %collective-permute-done.9.x.refs_1_ = f32[1,512]{1,0:T(1,128)S(1)} collective-permute-done((f32[1,512]{1,0:T(1,128)S(1)}, f32[1,512]{1,0:T(1,128)S(1)}, u32[]{:S(2)}, u32[]{:S(2)}) %collective-permute-start.9) | collective-permute-done | bytes 2080 | tf_op jit(solution)/shard_map/ppermute | solution.py:476
  26.8 0.3 pair_hop.1
  27.1 0.4 collective-permute-start.11
  27.6 1.0 %block.1 = (f32[512,512]{1,0:T(8,128)S(1)}, f32[8,512]{1,0:T(8,128)S(1)}) custom-call(f32[520,512]{1,0:T(8,128)S(1)} %collective-permute-done.10.late.refs_10_, f32[520,512]{1,0:T(8,128)S(1)} %pair.1.early.refs_12_), custom_call_target="tpu_custom_call" | custom-call | tf_op jit(solution)/shard_map/block/pallas_call | solution.py:361
  28.9 1.0 %collective-permute-done.12.x.refs_3_ = f32[1,512]{1,0:T(1,128)S(1)} collective-permute-done((f32[1,512]{1,0:T(1,128)S(1)}, f32[1,512]{1,0:T(1,128)S(1)}, u32[]{:S(2)}, u32[]{:S(2)}) %collective-permute-start.12) | collective-permute-done | bytes 2080 | tf_op jit(solution)/shard_map/ppermute | solution.py:476
  30.2 0.4 collective-permute-start.13
  30.6 1.9 %collective-permute-done.13.x.refs_4_ = f32[1,512]{1,0:T(1,128)S(1)} collective-permute-done((f32[1,512]{1,0:T(1,128)S(1)}, f32[1,512]{1,0:T(1,128)S(1)}, u32[]{:S(2)}, u32[]{:S(2)}) %collective-permute-start.13) | collective-permute-done | bytes 2080 | tf_op jit(solution)/shard_map/ppermute | solution.py:476
  33.0 1.0 %collective-permute-done.14.x.refs_5_ = f32[1,512]{1,0:T(1,128)S(1)} collective-permute-done((f32[1,512]{1,0:T(1,128)S(1)}, f32[1,512]{1,0:T(1,128)S(1)}, u32[]{:S(2)}, u32[]{:S(2)}) %collective-permute-start.14) | collective-permute-done | bytes 2080 | tf_op jit(solution)/shard_map/ppermute | solution.py:476
  34.4 1.0 %collective-permute-done.15.x.refs_6_ = f32[1,512]{1,0:T(1,128)S(1)} collective-permute-done((f32[1,512]{1,0:T(1,128)S(1)}, f32[1,512]{1,0:T(1,128)S(1)}, u32[]{:S(2)}, u32[]{:S(2)}) %collective-permute-start.15) | collective-permute-done | bytes 2080 | tf_op jit(solution)/shard_map/ppermute | solution.py:476
  35.5 1.2 %collective-permute-start.16 = (f32[1,512]{1,0:T(1,128)S(1)}, f32[1,512]{1,0:T(1,128)S(1)}, u32[]{:S(2)}, u32[]{:S(2)}) collective-permute-start(f32[1,512]{1,0:T(1,128)S(1)} %hop.9), channel_id=1, source_target_pairs={{0,2},{1,5},{2,3},{3,0},{4,6},{5,1},{6,7},{7,4},{8,9},{9,8},{10,11... | collective-permute-start | bytes 6152 | tf_op jit(solution)/shard_map/ppermute | solution.py:476
  36.7 1.9 %collective-permute-done.16.refs_7_ = f32[1,512]{1,0:T(1,128)S(1)} collective-permute-done((f32[1,512]{1,0:T(1,128)S(1)}, f32[1,512]{1,0:T(1,128)S(1)}, u32[]{:S(2)}, u32[]{:S(2)}) %collective-permute-start.16) | collective-permute-done | bytes 2080 | tf_op jit(solution)/shard_map/ppermute | solution.py:476
  38.6 0.4 last.1
  39.1 6.2 %collective-permute-start.19 = (f32[4,128]{1,0:T(4,128)S(1)}, f32[4,128]{1,0:T(4,128)S(1)}, u32[]{:S(2)}, u32[]{:S(2)}) collective-permute-start(f32[4,128]{1,0:T(4,128)S(1)} %get-tuple-element.63), channel_id=1, source_target_pairs={{0,2},{1,3},{2,0},{3,1},{4,6},{5,7},{6,4},{7,5},{8,10},{9,11},{10,... | collective-permute-start | bytes 6152 | tf_op jit(solution)/shard_map/ppermute | solution.py:355
  45.3 1.6 %collective-permute-done.19.refs_2_ = f32[4,128]{1,0:T(4,128)S(1)} collective-permute-done((f32[4,128]{1,0:T(4,128)S(1)}, f32[4,128]{1,0:T(4,128)S(1)}, u32[]{:S(2)}, u32[]{:S(2)}) %collective-permute-start.19) | collective-permute-done | bytes 2080 | tf_op jit(solution)/shard_map/ppermute | solution.py:355
  46.8 0.6 %out.1 = f32[4,128]{1,0:T(4,128)} custom-call(f32[4,128]{1,0:T(4,128)S(1)} %get-tuple-element.61.refs_0_, f32[4,128]{1,0:T(4,128)S(1)} %collective-permute-done.18.refs_1_, f32[4,128]{1,0:T(4,128)S(1)} %collective-permute-done.19.refs_2_, f32[4,128]{1,0:T(4,128)S(1)} %collective-permute-done.20.refs_3_), custom_call_target="tpu_custom_call" | custom-call | tf_op jit(solution)/shard_map/out/pallas_call | solution.py:361
  (30 shorter events, 2.3 us)
Async XLA Ops:
  1.6 5.1 %copy-start = (f32[128,512]{1,0:T(8,128)S(1)}, f32[128,512]{1,0:T(8,128)}, u32[]{:S(2)}) copy-start(f32[128,512]{1,0:T(8,128)} %trans.3) | copy-start | bytes 786436
  1.6 6.5 %collective-permute-start = (f32[64,512]{1,0:T(8,128)S(1)}, f32[64,512]{1,0:T(8,128)S(1)}, u32[]{:S(2)}, u32[]{:S(2)}) collective-permute-start(f32[64,512]{1,0:T(8,128)S(1)} %get-tuple-element.36), channel_id=1, source_target_pairs={{0,2},{1,3},{2,0},{3,1},{4,6},{5,7},{6,4},{7,5},{8,10},{9,11},{10,... | collective-permute-start | bytes 393224 | tf_op jit(solution)/shard_map/ppermute | solution.py:355
  6.1 9.7 %collective-permute-start.4 = (f32[256,512]{1,0:T(8,128)S(1)}, f32[256,512]{1,0:T(8,128)S(1)}, u32[]{:S(2)}, u32[]{:S(2)}) collective-permute-start(f32[256,512]{1,0:T(8,128)S(1)} %get-tuple-element.40), channel_id=1, source_target_pairs={{0,1},{1,0},{2,3},{3,2},{4,5},{5,4},{6,7},{7,6},{8,9},{9,8},{10,11... | collective-permute-start | bytes 1572872 | tf_op jit(solution)/shard_map/ppermute | solution.py:355
  6.2 9.6 %collective-permute-start.5 = (f32[256,512]{1,0:T(8,128)S(1)}, f32[256,512]{1,0:T(8,128)S(1)}, u32[]{:S(2)}, u32[]{:S(2)}) collective-permute-start(f32[256,512]{1,0:T(8,128)S(1)} %get-tuple-element.41), channel_id=1, source_target_pairs={{0,1},{1,0},{2,3},{3,2},{4,5},{5,4},{6,7},{7,6},{8,9},{9,8},{10,11... | collective-permute-start | bytes 1572872 | tf_op jit(solution)/shard_map/ppermute | solution.py:355
  6.7 12.3 %collective-permute-start.6 = (f32[4,200,128]{2,1,0:T(8,128)S(1)}, f32[4,200,128]{2,1,0:T(8,128)S(1)}, u32[]{:S(2)}, u32[]{:S(2)}) collective-permute-start(f32[4,200,128]{2,1,0:T(8,128)S(1)} %get-tuple-element.48), channel_id=1, source_target_pairs={{0,2},{1,3},{2,0},{3,1},{4,6},{5,7},{6,4},{7,5},{8,10},{9,11},{10,... | collective-permute-start | bytes 1228808 | tf_op jit(solution)/shard_map/ppermute | solution.py:355
  6.7 7.1 %collective-permute-start.1 = (f32[128,512]{1,0:T(8,128)S(1)}, f32[128,512]{1,0:T(8,128)S(1)}, u32[]{:S(2)}, u32[]{:S(2)}) collective-permute-start(f32[128,512]{1,0:T(8,128)S(1)} %copy-done), channel_id=1, source_target_pairs={{0,1},{1,0},{2,3},{3,2},{4,5},{5,4},{6,7},{7,6},{8,9},{9,8},{10,11... | collective-permute-start | bytes 786440 | tf_op jit(solution)/shard_map/ppermute | solution.py:355
  8.1 5.0 %collective-permute-start.2 = (f32[64,512]{1,0:T(8,128)S(1)}, f32[64,512]{1,0:T(8,128)S(1)}, u32[]{:S(2)}, u32[]{:S(2)}) collective-permute-start(f32[64,512]{1,0:T(8,128)S(1)} %collective-permute-done.after.refs_0_), channel_id=1, source_target_pairs={{0,4},{1,5},{2,6},{3,7},{4,0},{5,1},{6,2},{7,3},{8,12},{9,13},{10,... | collective-permute-start | bytes 393224 | tf_op jit(solution)/shard_map/ppermute | solution.py:355
  13.7 2.1 %collective-permute-start.3 = (f32[1,128,512]{2,1,0:T(8,128)S(1)}, f32[1,128,512]{2,1,0:T(8,128)S(1)}, u32[]{:S(2)}, u32[]{:S(2)}) collective-permute-start(f32[1,128,512]{2,1,0:T(8,128)S(1)} %join.1.joined), channel_id=1, source_target_pairs={{0,1},{1,0},{2,3},{3,2},{4,5},{5,4},{6,7},{7,6},{8,9},{9,8},{10,11... | collective-permute-start | bytes 786440 | tf_op jit(solution)/shard_map/ppermute | solution.py:355
  13.8 7.8 %collective-permute-start.7 = (f32[4,72,128]{2,1,0:T(8,128)S(1)}, f32[4,72,128]{2,1,0:T(8,128)S(1)}, u32[]{:S(2)}, u32[]{:S(2)}) collective-permute-start(f32[4,72,128]{2,1,0:T(8,128)S(1)} %get-tuple-element.53), channel_id=1, source_target_pairs={{0,3},{1,2},{2,1},{3,0},{4,7},{5,6},{6,5},{7,4},{8,11},{9,10},{10,... | collective-permute-start | bytes 442376 | tf_op jit(solution)/shard_map/ppermute | solution.py:355
  22.9 1.2 %collective-permute-start.8 = (f32[1,512]{1,0:T(1,128)S(1)}, f32[1,512]{1,0:T(1,128)S(1)}, u32[]{:S(2)}, u32[]{:S(2)}) collective-permute-start(f32[1,512]{1,0:T(1,128)S(1)} %get-tuple-element.54), channel_id=1, source_target_pairs={{0,1},{1,0},{2,3},{3,2},{4,5},{5,4},{6,7},{7,6},{8,9},{9,8},{10,11... | collective-permute-start | bytes 6152 | tf_op jit(solution)/shard_map/ppermute | solution.py:355
  24.1 2.7 %collective-permute-start.10 = (f32[520,512]{1,0:T(8,128)S(1)}, f32[520,512]{1,0:T(8,128)S(1)}, u32[]{:S(2)}, u32[]{:S(2)}) collective-permute-start(f32[520,512]{1,0:T(8,128)S(1)} %pair.1.early.refs_12_), channel_id=1, source_target_pairs={{0,1},{1,0},{2,3},{3,2},{4,5},{5,4},{6,7},{7,6},{8,9},{9,8},{10,11... | collective-permute-start | bytes 3194888 | tf_op jit(solution)/shard_map/ppermute | solution.py:355
  24.8 2.0 %collective-permute-start.9 = (f32[1,512]{1,0:T(1,128)S(1)}, f32[1,512]{1,0:T(1,128)S(1)}, u32[]{:S(2)}, u32[]{:S(2)}) collective-permute-start(f32[1,512]{1,0:T(1,128)S(1)} %two.1), channel_id=1, source_target_pairs={{0,1},{1,0},{2,3},{3,2},{4,5},{5,4},{6,7},{7,6},{8,9},{9,8},{10,11... | collective-permute-start | bytes 6152 | tf_op jit(solution)/shard_map/ppermute | solution.py:476
  27.1 1.4 %collective-permute-start.11 = (f32[1,512]{1,0:T(1,128)S(1)}, f32[1,512]{1,0:T(1,128)S(1)}, u32[]{:S(2)}, u32[]{:S(2)}) collective-permute-start(f32[1,512]{1,0:T(1,128)S(1)} %pair_hop.1), channel_id=1, source_target_pairs={{0,1},{1,0},{2,3},{3,2},{4,5},{5,4},{6,7},{7,6},{8,9},{9,8},{10,11... | collective-permute-start | bytes 6152 | tf_op jit(solution)/shard_map/ppermute | solution.py:476
  28.7 1.2 %collective-permute-start.12 = (f32[1,512]{1,0:T(1,128)S(1)}, f32[1,512]{1,0:T(1,128)S(1)}, u32[]{:S(2)}, u32[]{:S(2)}) collective-permute-start(f32[1,512]{1,0:T(1,128)S(1)} %hop.5), channel_id=1, source_target_pairs={{0,1},{1,0},{2,3},{3,2},{4,5},{5,4},{6,7},{7,6},{8,9},{9,8},{10,11... | collective-permute-start | bytes 6152 | tf_op jit(solution)/shard_map/ppermute | solution.py:476
  29.9 8.7 %collective-permute-start.17 = (f32[512,512]{1,0:T(8,128)S(1)}, f32[512,512]{1,0:T(8,128)S(1)}, u32[]{:S(2)}, u32[]{:S(2)}) collective-permute-start(f32[512,512]{1,0:T(8,128)S(1)} %get-tuple-element.60.gb.refs_13_), channel_id=1, source_target_pairs={{0,1},{1,0},{2,3},{3,2},{4,5},{5,4},{6,7},{7,6},{8,9},{9,8},{10,11... | collective-permute-start | bytes 3145736 | tf_op jit(solution)/shard_map/ppermute | solution.py:355
  30.2 2.3 %collective-permute-start.13 = (f32[1,512]{1,0:T(1,128)S(1)}, f32[1,512]{1,0:T(1,128)S(1)}, u32[]{:S(2)}, u32[]{:S(2)}) collective-permute-start(f32[1,512]{1,0:T(1,128)S(1)} %hop.6), channel_id=1, source_target_pairs={{0,1},{1,0},{2,3},{3,2},{4,5},{5,4},{6,7},{7,6},{8,9},{9,8},{10,11... | collective-permute-start | bytes 6152 | tf_op jit(solution)/shard_map/ppermute | solution.py:476
  32.7 1.2 %collective-permute-start.14 = (f32[1,512]{1,0:T(1,128)S(1)}, f32[1,512]{1,0:T(1,128)S(1)}, u32[]{:S(2)}, u32[]{:S(2)}) collective-permute-start(f32[1,512]{1,0:T(1,128)S(1)} %hop.7), channel_id=1, source_target_pairs={{0,1},{1,0},{2,3},{3,2},{4,5},{5,4},{6,7},{7,6},{8,10},{9,13},{10,... | collective-permute-start | bytes 6152 | tf_op jit(solution)/shard_map/ppermute | solution.py:476
  34.1 1.2 %collective-permute-start.15 = (f32[1,512]{1,0:T(1,128)S(1)}, f32[1,512]{1,0:T(1,128)S(1)}, u32[]{:S(2)}, u32[]{:S(2)}) collective-permute-start(f32[1,512]{1,0:T(1,128)S(1)} %hop.8), channel_id=1, source_target_pairs={{0,1},{1,0},{2,3},{3,2},{4,6},{5,9},{6,7},{7,4},{8,10},{9,5},{10,1... | collective-permute-start | bytes 6152 | tf_op jit(solution)/shard_map/ppermute | solution.py:476
  35.5 3.1 %collective-permute-start.16 = (f32[1,512]{1,0:T(1,128)S(1)}, f32[1,512]{1,0:T(1,128)S(1)}, u32[]{:S(2)}, u32[]{:S(2)}) collective-permute-start(f32[1,512]{1,0:T(1,128)S(1)} %hop.9), channel_id=1, source_target_pairs={{0,2},{1,5},{2,3},{3,0},{4,6},{5,1},{6,7},{7,4},{8,9},{9,8},{10,11... | collective-permute-start | bytes 6152 | tf_op jit(solution)/shard_map/ppermute | solution.py:476
  39.0 6.3 %collective-permute-start.18 = (f32[4,128]{1,0:T(4,128)S(1)}, f32[4,128]{1,0:T(4,128)S(1)}, u32[]{:S(2)}, u32[]{:S(2)}) collective-permute-start(f32[4,128]{1,0:T(4,128)S(1)} %get-tuple-element.62), channel_id=1, source_target_pairs={{0,3},{1,2},{2,1},{3,0},{4,7},{5,6},{6,5},{7,4},{8,11},{9,10},{10,... | collective-permute-start | bytes 6152 | tf_op jit(solution)/shard_map/ppermute | solution.py:355
  39.1 7.8 %collective-permute-start.19 = (f32[4,128]{1,0:T(4,128)S(1)}, f32[4,128]{1,0:T(4,128)S(1)}, u32[]{:S(2)}, u32[]{:S(2)}) collective-permute-start(f32[4,128]{1,0:T(4,128)S(1)} %get-tuple-element.63), channel_id=1, source_target_pairs={{0,2},{1,3},{2,0},{3,1},{4,6},{5,7},{6,4},{7,5},{8,10},{9,11},{10,... | collective-permute-start | bytes 6152 | tf_op jit(solution)/shard_map/ppermute | solution.py:355
  45.3 1.6 %collective-permute-start.20 = (f32[4,128]{1,0:T(4,128)S(1)}, f32[4,128]{1,0:T(4,128)S(1)}, u32[]{:S(2)}, u32[]{:S(2)}) collective-permute-start(f32[4,128]{1,0:T(4,128)S(1)} %get-tuple-element.64), channel_id=1, source_target_pairs={{0,1},{1,0},{2,3},{3,2},{4,5},{5,4},{6,7},{7,6},{8,9},{9,8},{10,11... | collective-permute-start | bytes 6152 | tf_op jit(solution)/shard_map/ppermute | solution.py:355

commit v17 on v16

--- a/solution.py
+++ b/solution.py
@@ -241,6 +241,57 @@
         c = c_far[k] + dot3(ff[k], a_far, NN)
         known_rows = (l_known.at[k, 0], l_known.at[k, 1])
         known_far = [x[:, known:] for x in known_rows]
+        column = jnp.concatenate([c_known[k], c[:, known:]], axis=0)
+        low_rows, share_rows = split(c), split(column)
+        if len(far) == 1:
+            halves = a_far[0, far_row(j, panel), :], a_far[1, far_row(j, panel), :]
+            low_rows = [jnp.concatenate([x, y], axis=0) for x, y in zip(low_rows, halves)]
+            share_rows = [jnp.concatenate([x, y[:, known:]], axis=0) for x, y in zip(share_rows, halves)]
+        share = dot3(share_rows, split(ff[count + k]), NN)
+        low = dot3([x[:, :known] for x in low_rows], known_rows, NN)
+        left = low[:, :known] + dot3([x[:, known:] for x in low_rows], known_far, NT)
+        right = low[:, known:] + share[known:]
+        size = order - known
+        out[:known, :known] = g_known[k, :, :known]
+        out[:known, known:] = g_known[k, :, known:] + share[:known]
+        out[known:, :known] = left[:size]
+        out[known:, known:] = right[:size]
+        if len(far) == 1:
+            col_ref[k] = jnp.where(j == 0, column[:, :panel], column[:, panel:])
+            h_ref[k, :, :known] = left[size:]
+            h_ref[k, :, known:] = right[size:]
+
+
+def steps_of(info, count):
+    a = base(lax.axis_index("state"), count)
+    return [info[pl.ds(a + shift, 1), :] for shift in (0, 1, 8, 9)]
+
+
+def far_row(j, panel):
+    return pl.ds(pl.multiple_of(j * panel, panel), panel)
+
+
+def middle_kernel(a_far, l_known, c_known, c_far, g_known, *refs):
+    far, (ga_ref, gb_ref, col_ref, h_ref, ff) = refs[:-5], refs[-5:]
+    count, known, order = g_known.shape
+    panel = known // 2
+    e = lax.axis_index("state") % 2
+    i, j = e, 1 - e
+    for k in range(2 * count):
+        if len(far) > 1:
+            for off, piece in enumerate(far, 2):
+                ff[k, rows((e ^ off) - 2, panel), :] = piece[k]
+            continue
+        beside, folded = far[0][k, :panel], far[0][k, panel:]
+        ff[k, rows(i, panel), rows(i, panel)] = unfold(folded)
+        ff[k, rows(j, panel), rows(j, panel)] = jnp.zeros((panel, panel), F32)
+        ff[k, rows(i, panel), rows(j, panel)] = beside
+        ff[k, rows(j, panel), rows(i, panel)] = beside.T
+
+    for k, out in enumerate((ga_ref, gb_ref)):
+        c = c_far[k] + dot3(ff[k], a_far, NN)
+        known_rows = (l_known.at[k, 0], l_known.at[k, 1])
+        known_far = [x[:, known:] for x in known_rows]
         l_far = split(ff[count + k])
         column = jnp.concatenate([c_known[k], c[:, known:]], axis=0)
         share = dot3(column, l_far, NN)
@@ -271,10 +322,12 @@
         if far:
             at = far_row(2 + j, panel)
             p_last, l_last = unfold(far[0][k]), unfold(far[0][count + k])
-            corner = [a_far[half, far_row(j, panel), at] for half in range(2)]
-            out[at, :] = gain[at, :] + dot3(p_last, h[k], NN)
-            out[:, at] += dot3(col[k], l_last, NN)
-            out[at, at] += dot3(dot3(p_last, corner, NN), l_last, NN)
+            corner = sum(a_far[half, far_row(j, panel), at].astype(F32) for half in range(2))
+            wide = dot3(p_last, jnp.concatenate([h[k], corner], axis=1), NN)
+            tall = dot3(jnp.concatenate([col[k], wide[:, order:]], axis=0), l_last, NN)
+            out[at, :] = gain[at, :] + wide[:, :order]
+            out[:, at] += tall[:order]
+            out[at, at] += tall[order:]
     mean_a, mean_b, pred_a, pred_b = steps_of(info, count)
     mean_ref[...] = mean_a + matvec(ga_ref[...], mean_b + matvec(gb_ref[...], first[...] - pred_b) - pred_a)
 

time: 47.6 us -> 47.7 us (level)
  no operation moved by 1% of the time
where the time goes in v17:
time: 47.7 us; the launch traced here: 47.5 us
  starting transfers between devices  17.2 us (36%)
  Pallas kernels  16.4 us (34%)
  waiting for transfers between devices  13.7 us (29%)
    pallas_call x18, Pallas kernels, call(): pl.pallas_call(kernel, out_shape=outs, in_specs=in_specs, out_specs=[VMEM...  16.4 us
    ppermute x14, starting transfers between devices, swap(): return lax.ppermute(x, ('tm', 'state'), pairs)  14.4 us
    ppermute x7, waiting for transfers between devices, hop(): return lax.ppermute(x, ('tm', 'state'), list(target.items()))  8.7 us
    ppermute x14, waiting for transfers between devices, swap(): return lax.ppermute(x, ('tm', 'state'), pairs)  5.02 us
    ppermute x7, starting transfers between devices, hop(): return lax.ppermute(x, ('tm', 'state'), list(target.items()))  2.8 us
  transfers between devices with their start and end apart: 21, of which 11 were waited for; matrix products, arithmetic and copies ran while one was open for 0% of the time, Pallas kernels for 25%

profile of v17, /device:TPU:0, one launch (start us, length us, event | category | flops | bytes accessed | tf_op | source)
XLA Modules:
  0.0 47.5 jit_solution(13631517223161203356)
XLA Ops:
  0.0 1.6 %pack.1 = (f32[4,200,128]{2,1,0:T(8,128)S(1)}, f32[4,72,128]{2,1,0:T(8,128)S(1)}, f32[64,512]{1,0:T(8,128)S(1)}, f32[1,512]{1,0:T(1,128)S(1)}) custom-call(f32[4,128,512]{2,1,0:T(8,128)} %cov.5, f32[4,128,512]{2,1,0:T(8,128)} %prec.5, f32[128,512]{1,0:T(8,128)} %trans.3, f32[1,512]{1,0:T(1,128)} %bitcast.1), custom_call_target="tpu_custom_call" | custom-call | tf_op jit(solution)/shard_map/pack/pallas_call | solution.py:414
  1.6 3.0 %collective-permute-start = (f32[64,512]{1,0:T(8,128)S(1)}, f32[64,512]{1,0:T(8,128)S(1)}, u32[]{:S(2)}, u32[]{:S(2)}) collective-permute-start(f32[64,512]{1,0:T(8,128)S(1)} %get-tuple-element.36), channel_id=1, source_target_pairs={{0,2},{1,3},{2,0},{3,1},{4,6},{5,7},{6,4},{7,5},{8,10},{9,11},{10,... | collective-permute-start | bytes 393224 | tf_op jit(solution)/shard_map/ppermute | solution.py:408
  4.6 1.5 %near.1 = (f32[256,512]{1,0:T(8,128)S(1)}, f32[256,512]{1,0:T(8,128)S(1)}) custom-call(f32[4,128,512]{2,1,0:T(8,128)} %cov.5, f32[4,128,512]{2,1,0:T(8,128)} %prec.5, f32[1,512]{1,0:T(1,128)S(1)} %get-tuple-element.35.after.first.refs_0_), custom_call_target="tpu_custom_call" | custom-call | tf_op jit(solution)/shard_map/near/pallas_call | solution.py:414
  6.2 0.5 %collective-permute-start.5 = (f32[256,512]{1,0:T(8,128)S(1)}, f32[256,512]{1,0:T(8,128)S(1)}, u32[]{:S(2)}, u32[]{:S(2)}) collective-permute-start(f32[256,512]{1,0:T(8,128)S(1)} %get-tuple-element.41), channel_id=1, source_target_pairs={{0,1},{1,0},{2,3},{3,2},{4,5},{5,4},{6,7},{7,6},{8,9},{9,8},{10,11... | collective-permute-start | bytes 1572872 | tf_op jit(solution)/shard_map/ppermute | solution.py:408
  6.8 1.4 %collective-permute-done.after.refs_0_ = f32[64,512]{1,0:T(8,128)S(1)} collective-permute-done((f32[64,512]{1,0:T(8,128)S(1)}, f32[64,512]{1,0:T(8,128)S(1)}, u32[]{:S(2)}, u32[]{:S(2)}) %collective-permute-start) | collective-permute-done | bytes 131104 | tf_op jit(solution)/shard_map/ppermute | solution.py:408
  8.1 1.8 %collective-permute-start.2 = (f32[64,512]{1,0:T(8,128)S(1)}, f32[64,512]{1,0:T(8,128)S(1)}, u32[]{:S(2)}, u32[]{:S(2)}) collective-permute-start(f32[64,512]{1,0:T(8,128)S(1)} %collective-permute-done.after.refs_0_), channel_id=1, source_target_pairs={{0,4},{1,5},{2,6},{3,7},{4,0},{5,1},{6,2},{7,3},{8,12},{9,13},{10,... | collective-permute-start | bytes 393224 | tf_op jit(solution)/shard_map/ppermute | solution.py:408
  9.9 1.6 %own.1 = (f32[4,128,512]{2,1,0:T(8,128)S(1)}, f32[128,512]{1,0:T(8,128)S(1)}, f32[4,512]{1,0:T(4,128)S(1)}) custom-call(f32[4,128,512]{2,1,0:T(8,128)} %cov.5, f32[4,128,512]{2,1,0:T(8,128)} %prec.5, f32[128,512]{1,0:T(8,128)} %trans.3, f32[4,512]{1,0:T(4,128)} %means.1, f32[64,512]{1,0:T(8,128)S(1)} %collective-permute-done.after.refs_0_), custom_call_target="tpu_custom_call" | custom-call | tf_op jit(solution)/shard_map/own/pallas_call | solution.py:414
  11.5 1.6 %collective-permute-done.2.refs_1_ = f32[64,512]{1,0:T(8,128)S(1)} collective-permute-done((f32[64,512]{1,0:T(8,128)S(1)}, f32[64,512]{1,0:T(8,128)S(1)}, u32[]{:S(2)}, u32[]{:S(2)}) %collective-permute-start.2) | collective-permute-done | bytes 131104 | tf_op jit(solution)/shard_map/ppermute | solution.py:408
  13.1 0.6 %join.1.joined = f32[1,128,512]{2,1,0:T(8,128)S(1)} custom-call(f32[128,512]{1,0:T(8,128)S(1)} %get-tuple-element.39.after.trans, f32[64,512]{1,0:T(8,128)S(1)} %collective-permute-done.after.refs_0_, f32[64,512]{1,0:T(8,128)S(1)} %collective-permute-done.2.refs_1_), custom_call_target="tpu_custom_call" | custom-call | tf_op jit(solution)/shard_map/join/pallas_call | solution.py:414
  13.8 2.0 %collective-permute-start.7 = (f32[4,72,128]{2,1,0:T(8,128)S(1)}, f32[4,72,128]{2,1,0:T(8,128)S(1)}, u32[]{:S(2)}, u32[]{:S(2)}) collective-permute-start(f32[4,72,128]{2,1,0:T(8,128)S(1)} %get-tuple-element.53), channel_id=1, source_target_pairs={{0,3},{1,2},{2,1},{3,0},{4,7},{5,6},{6,5},{7,4},{8,11},{9,10},{10,... | collective-permute-start | bytes 442376 | tf_op jit(solution)/shard_map/ppermute | solution.py:408
  15.8 2.9 %early.1 = (f32[16,512]{1,0:T(8,128)S(1)}, bf16[2,256,512]{2,1,0:T(8,128)(2,1)S(1)}, bf16[2,2,256,512]{3,2,1,0:T(8,128)(2,1)S(1)}, f32[2,256,256]{2,1,0:T(8,128)...) custom-call(f32[4,128,512]{2,1,0:T(8,128)S(1)} %get-tuple-element.37.own, ...), custom_call_target="tpu_custom_call" | custom-call | tf_op jit(solution)/shard_map/early/pallas_call | solution.py:414
  18.7 0.3 collective-permute-done.6.refs_0_
  19.0 2.5 %middle.1 = (f32[512,512]{1,0:T(8,128)S(1)}, f32[512,512]{1,0:T(8,128)S(1)}, f32[2,512,128]{2,1,0:T(8,128)S(1)}, f32[2,128,512]{2,1,0:T(8,128)S(1)}) custom-call(bf16[2,256,512]{2,1,0:T(8,128)(2,1)S(1)} %get-tuple-element.43.a_far, bf16[2,2,256,512]{3,2,1,0:T(8,128)(2,1)S(1)} %get-tuple-element.44.l_known, f32[2,256,256]{2,1,0:T(8,128)S(1)} %get-tuple-element.45.c_known, ...), custom_call_target="tpu_custom_call" | custom-call | tf_op jit(solution)/shard_map/middle/pallas_call | solution.py:414
  21.6 1.4 %late.1 = (f32[512,512]{1,0:T(8,128)S(1)}, f32[512,512]{1,0:T(8,128)S(1)}, f32[1,512]{1,0:T(1,128)S(1)}) custom-call(f32[1,512]{1,0:T(1,128)S(1)} %get-tuple-element.35.after.first.refs_0_, f32[16,512]{1,0:T(8,128)S(1)} %get-tuple-element.42.info, bf16[2,256,512]{2,1,0:T(8,128)(2,1)S(1)} %get-tuple-element.43.a_far, ...), custom_call_target="tpu_custom_call", output_to_operand_aliasing={{0}: (3, {}), {1}: (4, {})} | custom-call | tf_op jit(solution)/shard_map/late/pallas_call | solution.py:414
  23.1 1.0 %pair.1.early.refs_12_ = f32[520,512]{1,0:T(8,128)S(1)} custom-call(f32[16,512]{1,0:T(8,128)S(1)} %get-tuple-element.42.info, f32[512,512]{1,0:T(8,128)S(1)} %get-tuple-element.55.ga, f32[512,512]{1,0:T(8,128)S(1)} %get-tuple-element.60.gb.refs_13_), custom_call_target="tpu_custom_call" | custom-call | tf_op jit(solution)/shard_map/pair/pallas_call | solution.py:414
  24.2 0.4 collective-permute-start.10
  24.6 0.3 two.1
  25.1 1.9 %collective-permute-done.9.x.refs_1_ = f32[1,512]{1,0:T(1,128)S(1)} collective-permute-done((f32[1,512]{1,0:T(1,128)S(1)}, f32[1,512]{1,0:T(1,128)S(1)}, u32[]{:S(2)}, u32[]{:S(2)}) %collective-permute-start.9) | collective-permute-done | bytes 2080 | tf_op jit(solution)/shard_map/ppermute | solution.py:529
  27.0 0.3 pair_hop.1
  27.3 0.4 collective-permute-start.11
  27.7 1.0 %block.1 = (f32[512,512]{1,0:T(8,128)S(1)}, f32[8,512]{1,0:T(8,128)S(1)}) custom-call(f32[520,512]{1,0:T(8,128)S(1)} %collective-permute-done.10.late.refs_10_, f32[520,512]{1,0:T(8,128)S(1)} %pair.1.early.refs_12_), custom_call_target="tpu_custom_call" | custom-call | tf_op jit(solution)/shard_map/block/pallas_call | solution.py:414
  29.0 1.0 %collective-permute-done.12.x.refs_3_ = f32[1,512]{1,0:T(1,128)S(1)} collective-permute-done((f32[1,512]{1,0:T(1,128)S(1)}, f32[1,512]{1,0:T(1,128)S(1)}, u32[]{:S(2)}, u32[]{:S(2)}) %collective-permute-start.12) | collective-permute-done | bytes 2080 | tf_op jit(solution)/shard_map/ppermute | solution.py:529
  30.4 0.4 collective-permute-start.13
  30.7 1.9 %collective-permute-done.13.x.refs_4_ = f32[1,512]{1,0:T(1,128)S(1)} collective-permute-done((f32[1,512]{1,0:T(1,128)S(1)}, f32[1,512]{1,0:T(1,128)S(1)}, u32[]{:S(2)}, u32[]{:S(2)}) %collective-permute-start.13) | collective-permute-done | bytes 2080 | tf_op jit(solution)/shard_map/ppermute | solution.py:529
  33.1 1.0 %collective-permute-done.14.x.refs_5_ = f32[1,512]{1,0:T(1,128)S(1)} collective-permute-done((f32[1,512]{1,0:T(1,128)S(1)}, f32[1,512]{1,0:T(1,128)S(1)}, u32[]{:S(2)}, u32[]{:S(2)}) %collective-permute-start.14) | collective-permute-done | bytes 2080 | tf_op jit(solution)/shard_map/ppermute | solution.py:529
  34.5 1.0 %collective-permute-done.15.x.refs_6_ = f32[1,512]{1,0:T(1,128)S(1)} collective-permute-done((f32[1,512]{1,0:T(1,128)S(1)}, f32[1,512]{1,0:T(1,128)S(1)}, u32[]{:S(2)}, u32[]{:S(2)}) %collective-permute-start.15) | collective-permute-done | bytes 2080 | tf_op jit(solution)/shard_map/ppermute | solution.py:529
  35.6 1.2 %collective-permute-start.16 = (f32[1,512]{1,0:T(1,128)S(1)}, f32[1,512]{1,0:T(1,128)S(1)}, u32[]{:S(2)}, u32[]{:S(2)}) collective-permute-start(f32[1,512]{1,0:T(1,128)S(1)} %hop.9), channel_id=1, source_target_pairs={{0,2},{1,5},{2,3},{3,0},{4,6},{5,1},{6,7},{7,4},{8,9},{9,8},{10,11... | collective-permute-start | bytes 6152 | tf_op jit(solution)/shard_map/ppermute | solution.py:529
  36.8 1.9 %collective-permute-done.16.refs_7_ = f32[1,512]{1,0:T(1,128)S(1)} collective-permute-done((f32[1,512]{1,0:T(1,128)S(1)}, f32[1,512]{1,0:T(1,128)S(1)}, u32[]{:S(2)}, u32[]{:S(2)}) %collective-permute-start.16) | collective-permute-done | bytes 2080 | tf_op jit(solution)/shard_map/ppermute | solution.py:529
  38.7 0.4 last.1
  39.2 6.2 %collective-permute-start.19 = (f32[4,128]{1,0:T(4,128)S(1)}, f32[4,128]{1,0:T(4,128)S(1)}, u32[]{:S(2)}, u32[]{:S(2)}) collective-permute-start(f32[4,128]{1,0:T(4,128)S(1)} %get-tuple-element.63), channel_id=1, source_target_pairs={{0,2},{1,3},{2,0},{3,1},{4,6},{5,7},{6,4},{7,5},{8,10},{9,11},{10,... | collective-permute-start | bytes 6152 | tf_op jit(solution)/shard_map/ppermute | solution.py:408
  45.4 1.6 %collective-permute-done.19.refs_2_ = f32[4,128]{1,0:T(4,128)S(1)} collective-permute-done((f32[4,128]{1,0:T(4,128)S(1)}, f32[4,128]{1,0:T(4,128)S(1)}, u32[]{:S(2)}, u32[]{:S(2)}) %collective-permute-start.19) | collective-permute-done | bytes 2080 | tf_op jit(solution)/shard_map/ppermute | solution.py:408
  47.0 0.6 %out.1 = f32[4,128]{1,0:T(4,128)} custom-call(f32[4,128]{1,0:T(4,128)S(1)} %get-tuple-element.61.refs_0_, f32[4,128]{1,0:T(4,128)S(1)} %collective-permute-done.18.refs_1_, f32[4,128]{1,0:T(4,128)S(1)} %collective-permute-done.19.refs_2_, f32[4,128]{1,0:T(4,128)S(1)} %collective-permute-done.20.refs_3_), custom_call_target="tpu_custom_call" | custom-call | tf_op jit(solution)/shard_map/out/pallas_call | solution.py:414
  (30 shorter events, 2.3 us)
Async XLA Ops:
  1.6 5.1 %copy-start = (f32[128,512]{1,0:T(8,128)S(1)}, f32[128,512]{1,0:T(8,128)}, u32[]{:S(2)}) copy-start(f32[128,512]{1,0:T(8,128)} %trans.3) | copy-start | bytes 786436
  1.6 6.5 %collective-permute-start = (f32[64,512]{1,0:T(8,128)S(1)}, f32[64,512]{1,0:T(8,128)S(1)}, u32[]{:S(2)}, u32[]{:S(2)}) collective-permute-start(f32[64,512]{1,0:T(8,128)S(1)} %get-tuple-element.36), channel_id=1, source_target_pairs={{0,2},{1,3},{2,0},{3,1},{4,6},{5,7},{6,4},{7,5},{8,10},{9,11},{10,... | collective-permute-start | bytes 393224 | tf_op jit(solution)/shard_map/ppermute | solution.py:408
  6.1 9.7 %collective-permute-start.4 = (f32[256,512]{1,0:T(8,128)S(1)}, f32[256,512]{1,0:T(8,128)S(1)}, u32[]{:S(2)}, u32[]{:S(2)}) collective-permute-start(f32[256,512]{1,0:T(8,128)S(1)} %get-tuple-element.40), channel_id=1, source_target_pairs={{0,1},{1,0},{2,3},{3,2},{4,5},{5,4},{6,7},{7,6},{8,9},{9,8},{10,11... | collective-permute-start | bytes 1572872 | tf_op jit(solution)/shard_map/ppermute | solution.py:408
  6.2 9.6 %collective-permute-start.5 = (f32[256,512]{1,0:T(8,128)S(1)}, f32[256,512]{1,0:T(8,128)S(1)}, u32[]{:S(2)}, u32[]{:S(2)}) collective-permute-start(f32[256,512]{1,0:T(8,128)S(1)} %get-tuple-element.41), channel_id=1, source_target_pairs={{0,1},{1,0},{2,3},{3,2},{4,5},{5,4},{6,7},{7,6},{8,9},{9,8},{10,11... | collective-permute-start | bytes 1572872 | tf_op jit(solution)/shard_map/ppermute | solution.py:408
  6.7 12.3 %collective-permute-start.6 = (f32[4,200,128]{2,1,0:T(8,128)S(1)}, f32[4,200,128]{2,1,0:T(8,128)S(1)}, u32[]{:S(2)}, u32[]{:S(2)}) collective-permute-start(f32[4,200,128]{2,1,0:T(8,128)S(1)} %get-tuple-element.48), channel_id=1, source_target_pairs={{0,2},{1,3},{2,0},{3,1},{4,6},{5,7},{6,4},{7,5},{8,10},{9,11},{10,... | collective-permute-start | bytes 1228808 | tf_op jit(solution)/shard_map/ppermute | solution.py:408
  6.7 7.1 %collective-permute-start.1 = (f32[128,512]{1,0:T(8,128)S(1)}, f32[128,512]{1,0:T(8,128)S(1)}, u32[]{:S(2)}, u32[]{:S(2)}) collective-permute-start(f32[128,512]{1,0:T(8,128)S(1)} %copy-done), channel_id=1, source_target_pairs={{0,1},{1,0},{2,3},{3,2},{4,5},{5,4},{6,7},{7,6},{8,9},{9,8},{10,11... | collective-permute-start | bytes 786440 | tf_op jit(solution)/shard_map/ppermute | solution.py:408
  8.1 5.0 %collective-permute-start.2 = (f32[64,512]{1,0:T(8,128)S(1)}, f32[64,512]{1,0:T(8,128)S(1)}, u32[]{:S(2)}, u32[]{:S(2)}) collective-permute-start(f32[64,512]{1,0:T(8,128)S(1)} %collective-permute-done.after.refs_0_), channel_id=1, source_target_pairs={{0,4},{1,5},{2,6},{3,7},{4,0},{5,1},{6,2},{7,3},{8,12},{9,13},{10,... | collective-permute-start | bytes 393224 | tf_op jit(solution)/shard_map/ppermute | solution.py:408
  13.7 2.1 %collective-permute-start.3 = (f32[1,128,512]{2,1,0:T(8,128)S(1)}, f32[1,128,512]{2,1,0:T(8,128)S(1)}, u32[]{:S(2)}, u32[]{:S(2)}) collective-permute-start(f32[1,128,512]{2,1,0:T(8,128)S(1)} %join.1.joined), channel_id=1, source_target_pairs={{0,1},{1,0},{2,3},{3,2},{4,5},{5,4},{6,7},{7,6},{8,9},{9,8},{10,11... | collective-permute-start | bytes 786440 | tf_op jit(solution)/shard_map/ppermute | solution.py:408
  13.8 7.8 %collective-permute-start.7 = (f32[4,72,128]{2,1,0:T(8,128)S(1)}, f32[4,72,128]{2,1,0:T(8,128)S(1)}, u32[]{:S(2)}, u32[]{:S(2)}) collective-permute-start(f32[4,72,128]{2,1,0:T(8,128)S(1)} %get-tuple-element.53), channel_id=1, source_target_pairs={{0,3},{1,2},{2,1},{3,0},{4,7},{5,6},{6,5},{7,4},{8,11},{9,10},{10,... | collective-permute-start | bytes 442376 | tf_op jit(solution)/shard_map/ppermute | solution.py:408
  23.0 1.2 %collective-permute-start.8 = (f32[1,512]{1,0:T(1,128)S(1)}, f32[1,512]{1,0:T(1,128)S(1)}, u32[]{:S(2)}, u32[]{:S(2)}) collective-permute-start(f32[1,512]{1,0:T(1,128)S(1)} %get-tuple-element.54), channel_id=1, source_target_pairs={{0,1},{1,0},{2,3},{3,2},{4,5},{5,4},{6,7},{7,6},{8,9},{9,8},{10,11... | collective-permute-start | bytes 6152 | tf_op jit(solution)/shard_map/ppermute | solution.py:408
  24.2 2.7 %collective-permute-start.10 = (f32[520,512]{1,0:T(8,128)S(1)}, f32[520,512]{1,0:T(8,128)S(1)}, u32[]{:S(2)}, u32[]{:S(2)}) collective-permute-start(f32[520,512]{1,0:T(8,128)S(1)} %pair.1.early.refs_12_), channel_id=1, source_target_pairs={{0,1},{1,0},{2,3},{3,2},{4,5},{5,4},{6,7},{7,6},{8,9},{9,8},{10,11... | collective-permute-start | bytes 3194888 | tf_op jit(solution)/shard_map/ppermute | solution.py:408
  25.0 2.0 %collective-permute-start.9 = (f32[1,512]{1,0:T(1,128)S(1)}, f32[1,512]{1,0:T(1,128)S(1)}, u32[]{:S(2)}, u32[]{:S(2)}) collective-permute-start(f32[1,512]{1,0:T(1,128)S(1)} %two.1), channel_id=1, source_target_pairs={{0,1},{1,0},{2,3},{3,2},{4,5},{5,4},{6,7},{7,6},{8,9},{9,8},{10,11... | collective-permute-start | bytes 6152 | tf_op jit(solution)/shard_map/ppermute | solution.py:529
  27.3 1.4 %collective-permute-start.11 = (f32[1,512]{1,0:T(1,128)S(1)}, f32[1,512]{1,0:T(1,128)S(1)}, u32[]{:S(2)}, u32[]{:S(2)}) collective-permute-start(f32[1,512]{1,0:T(1,128)S(1)} %pair_hop.1), channel_id=1, source_target_pairs={{0,1},{1,0},{2,3},{3,2},{4,5},{5,4},{6,7},{7,6},{8,9},{9,8},{10,11... | collective-permute-start | bytes 6152 | tf_op jit(solution)/shard_map/ppermute | solution.py:529
  28.8 1.2 %collective-permute-start.12 = (f32[1,512]{1,0:T(1,128)S(1)}, f32[1,512]{1,0:T(1,128)S(1)}, u32[]{:S(2)}, u32[]{:S(2)}) collective-permute-start(f32[1,512]{1,0:T(1,128)S(1)} %hop.5), channel_id=1, source_target_pairs={{0,1},{1,0},{2,3},{3,2},{4,5},{5,4},{6,7},{7,6},{8,9},{9,8},{10,11... | collective-permute-start | bytes 6152 | tf_op jit(solution)/shard_map/ppermute | solution.py:529
  30.0 8.7 %collective-permute-start.17 = (f32[512,512]{1,0:T(8,128)S(1)}, f32[512,512]{1,0:T(8,128)S(1)}, u32[]{:S(2)}, u32[]{:S(2)}) collective-permute-start(f32[512,512]{1,0:T(8,128)S(1)} %get-tuple-element.60.gb.refs_13_), channel_id=1, source_target_pairs={{0,1},{1,0},{2,3},{3,2},{4,5},{5,4},{6,7},{7,6},{8,9},{9,8},{10,11... | collective-permute-start | bytes 3145736 | tf_op jit(solution)/shard_map/ppermute | solution.py:408
  30.4 2.3 %collective-permute-start.13 = (f32[1,512]{1,0:T(1,128)S(1)}, f32[1,512]{1,0:T(1,128)S(1)}, u32[]{:S(2)}, u32[]{:S(2)}) collective-permute-start(f32[1,512]{1,0:T(1,128)S(1)} %hop.6), channel_id=1, source_target_pairs={{0,1},{1,0},{2,3},{3,2},{4,5},{5,4},{6,7},{7,6},{8,9},{9,8},{10,11... | collective-permute-start | bytes 6152 | tf_op jit(solution)/shard_map/ppermute | solution.py:529
  32.8 1.2 %collective-permute-start.14 = (f32[1,512]{1,0:T(1,128)S(1)}, f32[1,512]{1,0:T(1,128)S(1)}, u32[]{:S(2)}, u32[]{:S(2)}) collective-permute-start(f32[1,512]{1,0:T(1,128)S(1)} %hop.7), channel_id=1, source_target_pairs={{0,1},{1,0},{2,3},{3,2},{4,5},{5,4},{6,7},{7,6},{8,10},{9,13},{10,... | collective-permute-start | bytes 6152 | tf_op jit(solution)/shard_map/ppermute | solution.py:529
  34.2 1.2 %collective-permute-start.15 = (f32[1,512]{1,0:T(1,128)S(1)}, f32[1,512]{1,0:T(1,128)S(1)}, u32[]{:S(2)}, u32[]{:S(2)}) collective-permute-start(f32[1,512]{1,0:T(1,128)S(1)} %hop.8), channel_id=1, source_target_pairs={{0,1},{1,0},{2,3},{3,2},{4,6},{5,9},{6,7},{7,4},{8,10},{9,5},{10,1... | collective-permute-start | bytes 6152 | tf_op jit(solution)/shard_map/ppermute | solution.py:529
  35.6 3.1 %collective-permute-start.16 = (f32[1,512]{1,0:T(1,128)S(1)}, f32[1,512]{1,0:T(1,128)S(1)}, u32[]{:S(2)}, u32[]{:S(2)}) collective-permute-start(f32[1,512]{1,0:T(1,128)S(1)} %hop.9), channel_id=1, source_target_pairs={{0,2},{1,5},{2,3},{3,0},{4,6},{5,1},{6,7},{7,4},{8,9},{9,8},{10,11... | collective-permute-start | bytes 6152 | tf_op jit(solution)/shard_map/ppermute | solution.py:529
  39.1 6.3 %collective-permute-start.18 = (f32[4,128]{1,0:T(4,128)S(1)}, f32[4,128]{1,0:T(4,128)S(1)}, u32[]{:S(2)}, u32[]{:S(2)}) collective-permute-start(f32[4,128]{1,0:T(4,128)S(1)} %get-tuple-element.62), channel_id=1, source_target_pairs={{0,3},{1,2},{2,1},{3,0},{4,7},{5,6},{6,5},{7,4},{8,11},{9,10},{10,... | collective-permute-start | bytes 6152 | tf_op jit(solution)/shard_map/ppermute | solution.py:408
  39.2 7.8 %collective-permute-start.19 = (f32[4,128]{1,0:T(4,128)S(1)}, f32[4,128]{1,0:T(4,128)S(1)}, u32[]{:S(2)}, u32[]{:S(2)}) collective-permute-start(f32[4,128]{1,0:T(4,128)S(1)} %get-tuple-element.63), channel_id=1, source_target_pairs={{0,2},{1,3},{2,0},{3,1},{4,6},{5,7},{6,4},{7,5},{8,10},{9,11},{10,... | collective-permute-start | bytes 6152 | tf_op jit(solution)/shard_map/ppermute | solution.py:408
  45.4 1.6 %collective-permute-start.20 = (f32[4,128]{1,0:T(4,128)S(1)}, f32[4,128]{1,0:T(4,128)S(1)}, u32[]{:S(2)}, u32[]{:S(2)}) collective-permute-start(f32[4,128]{1,0:T(4,128)S(1)} %get-tuple-element.64), channel_id=1, source_target_pairs={{0,1},{1,0},{2,3},{3,2},{4,5},{5,4},{6,7},{7,6},{8,9},{9,8},{10,11... | collective-permute-start | bytes 6152 | tf_op jit(solution)/shard_map/ppermute | solution.py:408

commit v18 on v16

--- a/solution.py
+++ b/solution.py
@@ -267,7 +267,9 @@
     far, (ga_ref, gb_ref, mean_ref) = refs[:-3], refs[-3:]
     count, panel, order = h.shape
     j = 1 - lax.axis_index("state") % 2
-    for k, (gain, out) in enumerate(((ga, ga_ref), (gb, gb_ref))):
+    mean_a, mean_b, pred_a, pred_b = steps_of(info, count)
+    row = first[...]
+    for k, gain, out, mean, pred in ((1, gb, gb_ref, mean_b, pred_b), (0, ga, ga_ref, mean_a, pred_a)):
         if far:
             at = far_row(2 + j, panel)
             p_last, l_last = unfold(far[0][k]), unfold(far[0][count + k])
@@ -275,8 +277,8 @@
             out[at, :] = gain[at, :] + dot3(p_last, h[k], NN)
             out[:, at] += dot3(col[k], l_last, NN)
             out[at, at] += dot3(dot3(p_last, corner, NN), l_last, NN)
-    mean_a, mean_b, pred_a, pred_b = steps_of(info, count)
-    mean_ref[...] = mean_a + matvec(ga_ref[...], mean_b + matvec(gb_ref[...], first[...] - pred_b) - pred_a)
+        row = mean + matvec(out[...], row - pred)
+    mean_ref[...] = row
 
 
 def two_kernel(x, info, ga, gb, out_ref):
@@ -333,7 +335,7 @@
 
 
 def out_kernel(*refs):
-    given, out_ref = [refs[0], *refs[-2:0:-1]], refs[-1]
+    given, out_ref = [refs[0], refs[-2], *refs[1:-2]], refs[-1]
     off = lax.axis_index("state") ^ 1
     x = given[0][...]
     for k, ref in enumerate(given[1:], 1):
@@ -493,9 +495,15 @@
         [pltpu.VMEM((devices, steps, panel), F32)],
         (*incoming, m, vec, late_map, g3, early_map, gb),
     ))
-    for off in range(devices - 1, 0, -1):
-        given[off] = swap(given[off], off)
-    given = [given[0], *given[:0:-1]]
+    order_of = (*range(2, devices), 1)
+    ring = {1: 2, 2: 0, 0: 3, 3: 1}
+    for off in order_of:
+        if off == 3:
+            pairs = [(i, ring.get(i, i ^ 3)) for i in range(devices)]
+            given[off] = lax.ppermute(given[off], "state", pairs)
+        else:
+            given[off] = swap(given[off], off)
+    given = [given[0], *(given[off] for off in order_of)]
     (out,) = call(out_kernel, "out", 4, [shape(steps, panel)], [VMEM] * devices, [], given)
     return out
 

time: 47.6 us -> 46.9 us (0.985)
    ppermute x14 -> x13, starting transfers between devices: 14.4 us -> 9.92 us  [swap(): return lax.ppermute(x, ('tm', 'state'), pairs)]
    ppermute x0 -> x1, starting transfers between devices: none -> 4.23 us  [local(): given[off] = lax.ppermute(given[off], 'state', pairs)]
    ppermute x14 -> x13, waiting for transfers between devices: 5.02 us -> 3.45 us  [swap(): return lax.ppermute(x, ('tm', 'state'), pairs)]
    ppermute x0 -> x1, waiting for transfers between devices: none -> 1.3 us  [local(): given[off] = lax.ppermute(given[off], 'state', pairs)]
  transfers between devices with their start and end apart: 21 -> 21, of which waited for: 11 -> 11; matrix products, arithmetic and copies ran while one was open for 0% -> 0% of each run, Pallas kernels for 25% -> 26%
where the time goes in v18:
time: 46.9 us; the launch traced here: 46.7 us
  starting transfers between devices  17 us (36%)
  Pallas kernels  16.1 us (34%)
  waiting for transfers between devices  13.4 us (29%)
    pallas_call x18, Pallas kernels, call(): pl.pallas_call(kernel, out_shape=outs, in_specs=in_specs, out_specs=[VMEM...  16.1 us
    ppermute x13, starting transfers between devices, swap(): return lax.ppermute(x, ('tm', 'state'), pairs)  9.92 us
    ppermute x7, waiting for transfers between devices, hop(): return lax.ppermute(x, ('tm', 'state'), list(target.items()))  8.69 us
    ppermute x1, starting transfers between devices, local(): given[off] = lax.ppermute(given[off], 'state', pairs)  4.23 us
    ppermute x13, waiting for transfers between devices, swap(): return lax.ppermute(x, ('tm', 'state'), pairs)  3.45 us
    ppermute x7, starting transfers between devices, hop(): return lax.ppermute(x, ('tm', 'state'), list(target.items()))  2.8 us
    ppermute x1, waiting for transfers between devices, local(): given[off] = lax.ppermute(given[off], 'state', pairs)  1.3 us
  transfers between devices with their start and end apart: 21, of which 11 were waited for; matrix products, arithmetic and copies ran while one was open for 0% of the time, Pallas kernels for 26%

profile of v18, /device:TPU:0, one launch (start us, length us, event | category | flops | bytes accessed | tf_op | source)
XLA Modules:
  0.0 46.7 jit_solution(16381147292289696209)
XLA Ops:
  0.0 1.6 %pack.1 = (f32[4,200,128]{2,1,0:T(8,128)S(1)}, f32[4,72,128]{2,1,0:T(8,128)S(1)}, f32[64,512]{1,0:T(8,128)S(1)}, f32[1,512]{1,0:T(1,128)S(1)}) custom-call(f32[4,128,512]{2,1,0:T(8,128)} %cov.5, f32[4,128,512]{2,1,0:T(8,128)} %prec.5, f32[128,512]{1,0:T(8,128)} %trans.3, f32[1,512]{1,0:T(1,128)} %bitcast.1), custom_call_target="tpu_custom_call" | custom-call | tf_op jit(solution)/shard_map/pack/pallas_call | solution.py:363
  1.6 3.0 %collective-permute-start = (f32[64,512]{1,0:T(8,128)S(1)}, f32[64,512]{1,0:T(8,128)S(1)}, u32[]{:S(2)}, u32[]{:S(2)}) collective-permute-start(f32[64,512]{1,0:T(8,128)S(1)} %get-tuple-element.36), channel_id=1, source_target_pairs={{0,2},{1,3},{2,0},{3,1},{4,6},{5,7},{6,4},{7,5},{8,10},{9,11},{10,... | collective-permute-start | bytes 393224 | tf_op jit(solution)/shard_map/ppermute | solution.py:357
  4.6 1.5 %near.1 = (f32[256,512]{1,0:T(8,128)S(1)}, f32[256,512]{1,0:T(8,128)S(1)}) custom-call(f32[4,128,512]{2,1,0:T(8,128)} %cov.5, f32[4,128,512]{2,1,0:T(8,128)} %prec.5, f32[1,512]{1,0:T(1,128)S(1)} %get-tuple-element.35.after.first.refs_0_), custom_call_target="tpu_custom_call" | custom-call | tf_op jit(solution)/shard_map/near/pallas_call | solution.py:363
  6.2 0.5 %collective-permute-start.5 = (f32[256,512]{1,0:T(8,128)S(1)}, f32[256,512]{1,0:T(8,128)S(1)}, u32[]{:S(2)}, u32[]{:S(2)}) collective-permute-start(f32[256,512]{1,0:T(8,128)S(1)} %get-tuple-element.41), channel_id=1, source_target_pairs={{0,1},{1,0},{2,3},{3,2},{4,5},{5,4},{6,7},{7,6},{8,9},{9,8},{10,11... | collective-permute-start | bytes 1572872 | tf_op jit(solution)/shard_map/ppermute | solution.py:357
  6.8 1.4 %collective-permute-done.after.refs_0_ = f32[64,512]{1,0:T(8,128)S(1)} collective-permute-done((f32[64,512]{1,0:T(8,128)S(1)}, f32[64,512]{1,0:T(8,128)S(1)}, u32[]{:S(2)}, u32[]{:S(2)}) %collective-permute-start) | collective-permute-done | bytes 131104 | tf_op jit(solution)/shard_map/ppermute | solution.py:357
  8.1 1.8 %collective-permute-start.2 = (f32[64,512]{1,0:T(8,128)S(1)}, f32[64,512]{1,0:T(8,128)S(1)}, u32[]{:S(2)}, u32[]{:S(2)}) collective-permute-start(f32[64,512]{1,0:T(8,128)S(1)} %collective-permute-done.after.refs_0_), channel_id=1, source_target_pairs={{0,4},{1,5},{2,6},{3,7},{4,0},{5,1},{6,2},{7,3},{8,12},{9,13},{10,... | collective-permute-start | bytes 393224 | tf_op jit(solution)/shard_map/ppermute | solution.py:357
  9.9 1.6 %own.1 = (f32[4,128,512]{2,1,0:T(8,128)S(1)}, f32[128,512]{1,0:T(8,128)S(1)}, f32[4,512]{1,0:T(4,128)S(1)}) custom-call(f32[4,128,512]{2,1,0:T(8,128)} %cov.5, f32[4,128,512]{2,1,0:T(8,128)} %prec.5, f32[128,512]{1,0:T(8,128)} %trans.3, f32[4,512]{1,0:T(4,128)} %means.1, f32[64,512]{1,0:T(8,128)S(1)} %collective-permute-done.after.refs_0_), custom_call_target="tpu_custom_call" | custom-call | tf_op jit(solution)/shard_map/own/pallas_call | solution.py:363
  11.5 1.6 %collective-permute-done.2.refs_1_ = f32[64,512]{1,0:T(8,128)S(1)} collective-permute-done((f32[64,512]{1,0:T(8,128)S(1)}, f32[64,512]{1,0:T(8,128)S(1)}, u32[]{:S(2)}, u32[]{:S(2)}) %collective-permute-start.2) | collective-permute-done | bytes 131104 | tf_op jit(solution)/shard_map/ppermute | solution.py:357
  13.1 0.6 %join.1.joined = f32[1,128,512]{2,1,0:T(8,128)S(1)} custom-call(f32[128,512]{1,0:T(8,128)S(1)} %get-tuple-element.39.after.trans, f32[64,512]{1,0:T(8,128)S(1)} %collective-permute-done.after.refs_0_, f32[64,512]{1,0:T(8,128)S(1)} %collective-permute-done.2.refs_1_), custom_call_target="tpu_custom_call" | custom-call | tf_op jit(solution)/shard_map/join/pallas_call | solution.py:363
  13.8 2.0 %collective-permute-start.7 = (f32[4,72,128]{2,1,0:T(8,128)S(1)}, f32[4,72,128]{2,1,0:T(8,128)S(1)}, u32[]{:S(2)}, u32[]{:S(2)}) collective-permute-start(f32[4,72,128]{2,1,0:T(8,128)S(1)} %get-tuple-element.53), channel_id=1, source_target_pairs={{0,3},{1,2},{2,1},{3,0},{4,7},{5,6},{6,5},{7,4},{8,11},{9,10},{10,... | collective-permute-start | bytes 442376 | tf_op jit(solution)/shard_map/ppermute | solution.py:357
  15.8 2.9 %early.1 = (f32[16,512]{1,0:T(8,128)S(1)}, bf16[2,256,512]{2,1,0:T(8,128)(2,1)S(1)}, bf16[2,2,256,512]{3,2,1,0:T(8,128)(2,1)S(1)}, f32[2,256,256]{2,1,0:T(8,128)...) custom-call(f32[4,128,512]{2,1,0:T(8,128)S(1)} %get-tuple-element.37.own, ...), custom_call_target="tpu_custom_call" | custom-call | tf_op jit(solution)/shard_map/early/pallas_call | solution.py:363
  19.0 2.5 %middle.1 = (f32[512,512]{1,0:T(8,128)S(1)}, f32[512,512]{1,0:T(8,128)S(1)}, f32[2,512,128]{2,1,0:T(8,128)S(1)}, f32[2,128,512]{2,1,0:T(8,128)S(1)}) custom-call(bf16[2,256,512]{2,1,0:T(8,128)(2,1)S(1)} %get-tuple-element.43.a_far, bf16[2,2,256,512]{3,2,1,0:T(8,128)(2,1)S(1)} %get-tuple-element.44.l_known, f32[2,256,256]{2,1,0:T(8,128)S(1)} %get-tuple-element.45.c_known, ...), custom_call_target="tpu_custom_call" | custom-call | tf_op jit(solution)/shard_map/middle/pallas_call | solution.py:363
  21.6 1.2 %late.1 = (f32[512,512]{1,0:T(8,128)S(1)}, f32[512,512]{1,0:T(8,128)S(1)}, f32[1,512]{1,0:T(1,128)S(1)}) custom-call(f32[1,512]{1,0:T(1,128)S(1)} %get-tuple-element.35.after.first.refs_0_, f32[16,512]{1,0:T(8,128)S(1)} %get-tuple-element.42.info, bf16[2,256,512]{2,1,0:T(8,128)(2,1)S(1)} %get-tuple-element.43.a_far, ...), custom_call_target="tpu_custom_call", output_to_operand_aliasing={{0}: (3, {}), {1}: (4, {})} | custom-call | tf_op jit(solution)/shard_map/late/pallas_call | solution.py:363
  22.8 1.0 %pair.1.early.refs_12_ = f32[520,512]{1,0:T(8,128)S(1)} custom-call(f32[16,512]{1,0:T(8,128)S(1)} %get-tuple-element.42.info, f32[512,512]{1,0:T(8,128)S(1)} %get-tuple-element.55.ga, f32[512,512]{1,0:T(8,128)S(1)} %get-tuple-element.60.gb.refs_13_), custom_call_target="tpu_custom_call" | custom-call | tf_op jit(solution)/shard_map/pair/pallas_call | solution.py:363
  23.9 0.4 collective-permute-start.10
  24.4 0.3 two.1
  24.8 1.9 %collective-permute-done.9.x.refs_1_ = f32[1,512]{1,0:T(1,128)S(1)} collective-permute-done((f32[1,512]{1,0:T(1,128)S(1)}, f32[1,512]{1,0:T(1,128)S(1)}, u32[]{:S(2)}, u32[]{:S(2)}) %collective-permute-start.9) | collective-permute-done | bytes 2080 | tf_op jit(solution)/shard_map/ppermute | solution.py:478
  26.7 0.3 pair_hop.1
  27.0 0.4 collective-permute-start.11
  27.4 1.0 %block.1 = (f32[512,512]{1,0:T(8,128)S(1)}, f32[8,512]{1,0:T(8,128)S(1)}) custom-call(f32[520,512]{1,0:T(8,128)S(1)} %collective-permute-done.10.late.refs_10_, f32[520,512]{1,0:T(8,128)S(1)} %pair.1.early.refs_12_), custom_call_target="tpu_custom_call" | custom-call | tf_op jit(solution)/shard_map/block/pallas_call | solution.py:363
  28.7 1.0 %collective-permute-done.12.x.refs_3_ = f32[1,512]{1,0:T(1,128)S(1)} collective-permute-done((f32[1,512]{1,0:T(1,128)S(1)}, f32[1,512]{1,0:T(1,128)S(1)}, u32[]{:S(2)}, u32[]{:S(2)}) %collective-permute-start.12) | collective-permute-done | bytes 2080 | tf_op jit(solution)/shard_map/ppermute | solution.py:478
  30.1 0.4 collective-permute-start.13
  30.5 1.9 %collective-permute-done.13.x.refs_4_ = f32[1,512]{1,0:T(1,128)S(1)} collective-permute-done((f32[1,512]{1,0:T(1,128)S(1)}, f32[1,512]{1,0:T(1,128)S(1)}, u32[]{:S(2)}, u32[]{:S(2)}) %collective-permute-start.13) | collective-permute-done | bytes 2080 | tf_op jit(solution)/shard_map/ppermute | solution.py:478
  32.8 1.0 %collective-permute-done.14.x.refs_5_ = f32[1,512]{1,0:T(1,128)S(1)} collective-permute-done((f32[1,512]{1,0:T(1,128)S(1)}, f32[1,512]{1,0:T(1,128)S(1)}, u32[]{:S(2)}, u32[]{:S(2)}) %collective-permute-start.14) | collective-permute-done | bytes 2080 | tf_op jit(solution)/shard_map/ppermute | solution.py:478
  34.2 1.0 %collective-permute-done.15.x.refs_6_ = f32[1,512]{1,0:T(1,128)S(1)} collective-permute-done((f32[1,512]{1,0:T(1,128)S(1)}, f32[1,512]{1,0:T(1,128)S(1)}, u32[]{:S(2)}, u32[]{:S(2)}) %collective-permute-start.15) | collective-permute-done | bytes 2080 | tf_op jit(solution)/shard_map/ppermute | solution.py:478
  35.3 1.2 %collective-permute-start.16 = (f32[1,512]{1,0:T(1,128)S(1)}, f32[1,512]{1,0:T(1,128)S(1)}, u32[]{:S(2)}, u32[]{:S(2)}) collective-permute-start(f32[1,512]{1,0:T(1,128)S(1)} %hop.9), channel_id=1, source_target_pairs={{0,2},{1,5},{2,3},{3,0},{4,6},{5,1},{6,7},{7,4},{8,9},{9,8},{10,11... | collective-permute-start | bytes 6152 | tf_op jit(solution)/shard_map/ppermute | solution.py:478
  36.5 1.9 %collective-permute-done.16.refs_7_ = f32[1,512]{1,0:T(1,128)S(1)} collective-permute-done((f32[1,512]{1,0:T(1,128)S(1)}, f32[1,512]{1,0:T(1,128)S(1)}, u32[]{:S(2)}, u32[]{:S(2)}) %collective-permute-start.16) | collective-permute-done | bytes 2080 | tf_op jit(solution)/shard_map/ppermute | solution.py:478
  38.4 0.4 last.1
  38.8 1.7 %collective-permute-start.18 = (f32[4,128]{1,0:T(4,128)S(1)}, f32[4,128]{1,0:T(4,128)S(1)}, u32[]{:S(2)}, u32[]{:S(2)}) collective-permute-start(f32[4,128]{1,0:T(4,128)S(1)} %get-tuple-element.62), channel_id=1, source_target_pairs={{0,2},{1,3},{2,0},{3,1},{4,6},{5,7},{6,4},{7,5},{8,10},{9,11},{10,... | collective-permute-start | bytes 6152 | tf_op jit(solution)/shard_map/ppermute | solution.py:357
  40.6 4.2 %collective-permute-start.19 = (f32[4,128]{1,0:T(4,128)S(1)}, f32[4,128]{1,0:T(4,128)S(1)}, u32[]{:S(2)}, u32[]{:S(2)}) collective-permute-start(f32[4,128]{1,0:T(4,128)S(1)} %get-tuple-element.63), channel_id=1, source_target_pairs={{0,3},{1,2},{2,0},{3,1},{4,7},{5,6},{6,4},{7,5},{8,11},{9,10},{10,... | collective-permute-start | bytes 6152 | tf_op jit(solution)/shard_map/ppermute | solution.py:503
  44.8 1.3 %collective-permute-done.19.refs_2_ = f32[4,128]{1,0:T(4,128)S(1)} collective-permute-done((f32[4,128]{1,0:T(4,128)S(1)}, f32[4,128]{1,0:T(4,128)S(1)}, u32[]{:S(2)}, u32[]{:S(2)}) %collective-permute-start.19) | collective-permute-done | bytes 2080 | tf_op jit(solution)/shard_map/ppermute | solution.py:503
  46.1 0.6 %out.1 = f32[4,128]{1,0:T(4,128)} custom-call(f32[4,128]{1,0:T(4,128)S(1)} %get-tuple-element.61.refs_0_, f32[4,128]{1,0:T(4,128)S(1)} %collective-permute-done.18.refs_1_, f32[4,128]{1,0:T(4,128)S(1)} %collective-permute-done.19.refs_2_, f32[4,128]{1,0:T(4,128)S(1)} %collective-permute-done.20.refs_3_), custom_call_target="tpu_custom_call" | custom-call | tf_op jit(solution)/shard_map/out/pallas_call | solution.py:363
  (30 shorter events, 2.5 us)
Async XLA Ops:
  1.6 5.1 %copy-start = (f32[128,512]{1,0:T(8,128)S(1)}, f32[128,512]{1,0:T(8,128)}, u32[]{:S(2)}) copy-start(f32[128,512]{1,0:T(8,128)} %trans.3) | copy-start | bytes 786436
  1.6 6.5 %collective-permute-start = (f32[64,512]{1,0:T(8,128)S(1)}, f32[64,512]{1,0:T(8,128)S(1)}, u32[]{:S(2)}, u32[]{:S(2)}) collective-permute-start(f32[64,512]{1,0:T(8,128)S(1)} %get-tuple-element.36), channel_id=1, source_target_pairs={{0,2},{1,3},{2,0},{3,1},{4,6},{5,7},{6,4},{7,5},{8,10},{9,11},{10,... | collective-permute-start | bytes 393224 | tf_op jit(solution)/shard_map/ppermute | solution.py:357
  6.1 9.7 %collective-permute-start.4 = (f32[256,512]{1,0:T(8,128)S(1)}, f32[256,512]{1,0:T(8,128)S(1)}, u32[]{:S(2)}, u32[]{:S(2)}) collective-permute-start(f32[256,512]{1,0:T(8,128)S(1)} %get-tuple-element.40), channel_id=1, source_target_pairs={{0,1},{1,0},{2,3},{3,2},{4,5},{5,4},{6,7},{7,6},{8,9},{9,8},{10,11... | collective-permute-start | bytes 1572872 | tf_op jit(solution)/shard_map/ppermute | solution.py:357
  6.2 9.6 %collective-permute-start.5 = (f32[256,512]{1,0:T(8,128)S(1)}, f32[256,512]{1,0:T(8,128)S(1)}, u32[]{:S(2)}, u32[]{:S(2)}) collective-permute-start(f32[256,512]{1,0:T(8,128)S(1)} %get-tuple-element.41), channel_id=1, source_target_pairs={{0,1},{1,0},{2,3},{3,2},{4,5},{5,4},{6,7},{7,6},{8,9},{9,8},{10,11... | collective-permute-start | bytes 1572872 | tf_op jit(solution)/shard_map/ppermute | solution.py:357
  6.7 12.3 %collective-permute-start.6 = (f32[4,200,128]{2,1,0:T(8,128)S(1)}, f32[4,200,128]{2,1,0:T(8,128)S(1)}, u32[]{:S(2)}, u32[]{:S(2)}) collective-permute-start(f32[4,200,128]{2,1,0:T(8,128)S(1)} %get-tuple-element.48), channel_id=1, source_target_pairs={{0,2},{1,3},{2,0},{3,1},{4,6},{5,7},{6,4},{7,5},{8,10},{9,11},{10,... | collective-permute-start | bytes 1228808 | tf_op jit(solution)/shard_map/ppermute | solution.py:357
  6.7 7.1 %collective-permute-start.1 = (f32[128,512]{1,0:T(8,128)S(1)}, f32[128,512]{1,0:T(8,128)S(1)}, u32[]{:S(2)}, u32[]{:S(2)}) collective-permute-start(f32[128,512]{1,0:T(8,128)S(1)} %copy-done), channel_id=1, source_target_pairs={{0,1},{1,0},{2,3},{3,2},{4,5},{5,4},{6,7},{7,6},{8,9},{9,8},{10,11... | collective-permute-start | bytes 786440 | tf_op jit(solution)/shard_map/ppermute | solution.py:357
  8.1 5.0 %collective-permute-start.2 = (f32[64,512]{1,0:T(8,128)S(1)}, f32[64,512]{1,0:T(8,128)S(1)}, u32[]{:S(2)}, u32[]{:S(2)}) collective-permute-start(f32[64,512]{1,0:T(8,128)S(1)} %collective-permute-done.after.refs_0_), channel_id=1, source_target_pairs={{0,4},{1,5},{2,6},{3,7},{4,0},{5,1},{6,2},{7,3},{8,12},{9,13},{10,... | collective-permute-start | bytes 393224 | tf_op jit(solution)/shard_map/ppermute | solution.py:357
  13.7 2.1 %collective-permute-start.3 = (f32[1,128,512]{2,1,0:T(8,128)S(1)}, f32[1,128,512]{2,1,0:T(8,128)S(1)}, u32[]{:S(2)}, u32[]{:S(2)}) collective-permute-start(f32[1,128,512]{2,1,0:T(8,128)S(1)} %join.1.joined), channel_id=1, source_target_pairs={{0,1},{1,0},{2,3},{3,2},{4,5},{5,4},{6,7},{7,6},{8,9},{9,8},{10,11... | collective-permute-start | bytes 786440 | tf_op jit(solution)/shard_map/ppermute | solution.py:357
  13.8 7.8 %collective-permute-start.7 = (f32[4,72,128]{2,1,0:T(8,128)S(1)}, f32[4,72,128]{2,1,0:T(8,128)S(1)}, u32[]{:S(2)}, u32[]{:S(2)}) collective-permute-start(f32[4,72,128]{2,1,0:T(8,128)S(1)} %get-tuple-element.53), channel_id=1, source_target_pairs={{0,3},{1,2},{2,1},{3,0},{4,7},{5,6},{6,5},{7,4},{8,11},{9,10},{10,... | collective-permute-start | bytes 442376 | tf_op jit(solution)/shard_map/ppermute | solution.py:357
  22.7 1.2 %collective-permute-start.8 = (f32[1,512]{1,0:T(1,128)S(1)}, f32[1,512]{1,0:T(1,128)S(1)}, u32[]{:S(2)}, u32[]{:S(2)}) collective-permute-start(f32[1,512]{1,0:T(1,128)S(1)} %get-tuple-element.54), channel_id=1, source_target_pairs={{0,1},{1,0},{2,3},{3,2},{4,5},{5,4},{6,7},{7,6},{8,9},{9,8},{10,11... | collective-permute-start | bytes 6152 | tf_op jit(solution)/shard_map/ppermute | solution.py:357
  23.9 2.7 %collective-permute-start.10 = (f32[520,512]{1,0:T(8,128)S(1)}, f32[520,512]{1,0:T(8,128)S(1)}, u32[]{:S(2)}, u32[]{:S(2)}) collective-permute-start(f32[520,512]{1,0:T(8,128)S(1)} %pair.1.early.refs_12_), channel_id=1, source_target_pairs={{0,1},{1,0},{2,3},{3,2},{4,5},{5,4},{6,7},{7,6},{8,9},{9,8},{10,11... | collective-permute-start | bytes 3194888 | tf_op jit(solution)/shard_map/ppermute | solution.py:357
  24.7 2.0 %collective-permute-start.9 = (f32[1,512]{1,0:T(1,128)S(1)}, f32[1,512]{1,0:T(1,128)S(1)}, u32[]{:S(2)}, u32[]{:S(2)}) collective-permute-start(f32[1,512]{1,0:T(1,128)S(1)} %two.1), channel_id=1, source_target_pairs={{0,1},{1,0},{2,3},{3,2},{4,5},{5,4},{6,7},{7,6},{8,9},{9,8},{10,11... | collective-permute-start | bytes 6152 | tf_op jit(solution)/shard_map/ppermute | solution.py:478
  27.0 1.4 %collective-permute-start.11 = (f32[1,512]{1,0:T(1,128)S(1)}, f32[1,512]{1,0:T(1,128)S(1)}, u32[]{:S(2)}, u32[]{:S(2)}) collective-permute-start(f32[1,512]{1,0:T(1,128)S(1)} %pair_hop.1), channel_id=1, source_target_pairs={{0,1},{1,0},{2,3},{3,2},{4,5},{5,4},{6,7},{7,6},{8,9},{9,8},{10,11... | collective-permute-start | bytes 6152 | tf_op jit(solution)/shard_map/ppermute | solution.py:478
  28.6 1.2 %collective-permute-start.12 = (f32[1,512]{1,0:T(1,128)S(1)}, f32[1,512]{1,0:T(1,128)S(1)}, u32[]{:S(2)}, u32[]{:S(2)}) collective-permute-start(f32[1,512]{1,0:T(1,128)S(1)} %hop.5), channel_id=1, source_target_pairs={{0,1},{1,0},{2,3},{3,2},{4,5},{5,4},{6,7},{7,6},{8,9},{9,8},{10,11... | collective-permute-start | bytes 6152 | tf_op jit(solution)/shard_map/ppermute | solution.py:478
  29.7 8.7 %collective-permute-start.17 = (f32[512,512]{1,0:T(8,128)S(1)}, f32[512,512]{1,0:T(8,128)S(1)}, u32[]{:S(2)}, u32[]{:S(2)}) collective-permute-start(f32[512,512]{1,0:T(8,128)S(1)} %get-tuple-element.60.gb.refs_13_), channel_id=1, source_target_pairs={{0,1},{1,0},{2,3},{3,2},{4,5},{5,4},{6,7},{7,6},{8,9},{9,8},{10,11... | collective-permute-start | bytes 3145736 | tf_op jit(solution)/shard_map/ppermute | solution.py:357
  30.1 2.3 %collective-permute-start.13 = (f32[1,512]{1,0:T(1,128)S(1)}, f32[1,512]{1,0:T(1,128)S(1)}, u32[]{:S(2)}, u32[]{:S(2)}) collective-permute-start(f32[1,512]{1,0:T(1,128)S(1)} %hop.6), channel_id=1, source_target_pairs={{0,1},{1,0},{2,3},{3,2},{4,5},{5,4},{6,7},{7,6},{8,9},{9,8},{10,11... | collective-permute-start | bytes 6152 | tf_op jit(solution)/shard_map/ppermute | solution.py:478
  32.6 1.2 %collective-permute-start.14 = (f32[1,512]{1,0:T(1,128)S(1)}, f32[1,512]{1,0:T(1,128)S(1)}, u32[]{:S(2)}, u32[]{:S(2)}) collective-permute-start(f32[1,512]{1,0:T(1,128)S(1)} %hop.7), channel_id=1, source_target_pairs={{0,1},{1,0},{2,3},{3,2},{4,5},{5,4},{6,7},{7,6},{8,10},{9,13},{10,... | collective-permute-start | bytes 6152 | tf_op jit(solution)/shard_map/ppermute | solution.py:478
  34.0 1.2 %collective-permute-start.15 = (f32[1,512]{1,0:T(1,128)S(1)}, f32[1,512]{1,0:T(1,128)S(1)}, u32[]{:S(2)}, u32[]{:S(2)}) collective-permute-start(f32[1,512]{1,0:T(1,128)S(1)} %hop.8), channel_id=1, source_target_pairs={{0,1},{1,0},{2,3},{3,2},{4,6},{5,9},{6,7},{7,4},{8,10},{9,5},{10,1... | collective-permute-start | bytes 6152 | tf_op jit(solution)/shard_map/ppermute | solution.py:478
  35.3 3.1 %collective-permute-start.16 = (f32[1,512]{1,0:T(1,128)S(1)}, f32[1,512]{1,0:T(1,128)S(1)}, u32[]{:S(2)}, u32[]{:S(2)}) collective-permute-start(f32[1,512]{1,0:T(1,128)S(1)} %hop.9), channel_id=1, source_target_pairs={{0,2},{1,5},{2,3},{3,0},{4,6},{5,1},{6,7},{7,4},{8,9},{9,8},{10,11... | collective-permute-start | bytes 6152 | tf_op jit(solution)/shard_map/ppermute | solution.py:478
  38.8 6.0 %collective-permute-start.18 = (f32[4,128]{1,0:T(4,128)S(1)}, f32[4,128]{1,0:T(4,128)S(1)}, u32[]{:S(2)}, u32[]{:S(2)}) collective-permute-start(f32[4,128]{1,0:T(4,128)S(1)} %get-tuple-element.62), channel_id=1, source_target_pairs={{0,2},{1,3},{2,0},{3,1},{4,6},{5,7},{6,4},{7,5},{8,10},{9,11},{10,... | collective-permute-start | bytes 6152 | tf_op jit(solution)/shard_map/ppermute | solution.py:357
  40.6 5.5 %collective-permute-start.19 = (f32[4,128]{1,0:T(4,128)S(1)}, f32[4,128]{1,0:T(4,128)S(1)}, u32[]{:S(2)}, u32[]{:S(2)}) collective-permute-start(f32[4,128]{1,0:T(4,128)S(1)} %get-tuple-element.63), channel_id=1, source_target_pairs={{0,3},{1,2},{2,0},{3,1},{4,7},{5,6},{6,4},{7,5},{8,11},{9,10},{10,... | collective-permute-start | bytes 6152 | tf_op jit(solution)/shard_map/ppermute | solution.py:503
  44.8 1.3 %collective-permute-start.20 = (f32[4,128]{1,0:T(4,128)S(1)}, f32[4,128]{1,0:T(4,128)S(1)}, u32[]{:S(2)}, u32[]{:S(2)}) collective-permute-start(f32[4,128]{1,0:T(4,128)S(1)} %get-tuple-element.64), channel_id=1, source_target_pairs={{0,1},{1,0},{2,3},{3,2},{4,5},{5,4},{6,7},{7,6},{8,9},{9,8},{10,11... | collective-permute-start | bytes 6152 | tf_op jit(solution)/shard_map/ppermute | solution.py:357

commit v19 on v18

--- a/solution.py
+++ b/solution.py
@@ -288,11 +288,14 @@
 
 def pair_kernel(info, ga, gb, map_ref):
     order = ga.shape[1]
+    left = split(ga[...])
+    for at in range(0, order, order // 2):
+        columns = slice(at, at + order // 2)
+        map_ref[:order, columns] = dot3(left, gb[:, columns], NN)
     mean_a, mean_b, pred_a, pred_b = steps_of(info, 2)
     map_ref[order:, :] = jnp.concatenate(
         [mean_a + matvec(ga[...], mean_b - pred_a), mean_b, pred_b, jnp.zeros((5, order), F32)], axis=0
     )
-    map_ref[:order, :] = dot3(ga[...], gb[...], NN)
 
 
 def block_kernel(late, early, m_ref, vec_ref):

time: 46.9 us -> 46.9 us (level)
  no operation moved by 1% of the time
where the time goes in v19:
time: 46.9 us; the launch traced here: 46.7 us
  starting transfers between devices  17 us (36%)
  Pallas kernels  16.1 us (34%)
  waiting for transfers between devices  13.4 us (29%)
    pallas_call x18, Pallas kernels, call(): pl.pallas_call(kernel, out_shape=outs, in_specs=in_specs, out_specs=[VMEM...  16.1 us
    ppermute x13, starting transfers between devices, swap(): return lax.ppermute(x, ('tm', 'state'), pairs)  9.92 us
    ppermute x7, waiting for transfers between devices, hop(): return lax.ppermute(x, ('tm', 'state'), list(target.items()))  8.69 us
    ppermute x1, starting transfers between devices, local(): given[off] = lax.ppermute(given[off], 'state', pairs)  4.23 us
    ppermute x13, waiting for transfers between devices, swap(): return lax.ppermute(x, ('tm', 'state'), pairs)  3.45 us
    ppermute x7, starting transfers between devices, hop(): return lax.ppermute(x, ('tm', 'state'), list(target.items()))  2.8 us
    ppermute x1, waiting for transfers between devices, local(): given[off] = lax.ppermute(given[off], 'state', pairs)  1.3 us
  transfers between devices with their start and end apart: 21, of which 11 were waited for; matrix products, arithmetic and copies ran while one was open for 0% of the time, Pallas kernels for 26%

profile of v19, /device:TPU:0, one launch (start us, length us, event | category | flops | bytes accessed | tf_op | source)
XLA Modules:
  0.0 46.7 jit_solution(15543313593233609200)
XLA Ops:
  0.0 1.6 %pack.1 = (f32[4,200,128]{2,1,0:T(8,128)S(1)}, f32[4,72,128]{2,1,0:T(8,128)S(1)}, f32[64,512]{1,0:T(8,128)S(1)}, f32[1,512]{1,0:T(1,128)S(1)}) custom-call(f32[4,128,512]{2,1,0:T(8,128)} %cov.5, f32[4,128,512]{2,1,0:T(8,128)} %prec.5, f32[128,512]{1,0:T(8,128)} %trans.3, f32[1,512]{1,0:T(1,128)} %bitcast.1), custom_call_target="tpu_custom_call" | custom-call | tf_op jit(solution)/shard_map/pack/pallas_call | solution.py:366
  1.6 3.0 %collective-permute-start = (f32[64,512]{1,0:T(8,128)S(1)}, f32[64,512]{1,0:T(8,128)S(1)}, u32[]{:S(2)}, u32[]{:S(2)}) collective-permute-start(f32[64,512]{1,0:T(8,128)S(1)} %get-tuple-element.36), channel_id=1, source_target_pairs={{0,2},{1,3},{2,0},{3,1},{4,6},{5,7},{6,4},{7,5},{8,10},{9,11},{10,... | collective-permute-start | bytes 393224 | tf_op jit(solution)/shard_map/ppermute | solution.py:360
  4.6 1.5 %near.1 = (f32[256,512]{1,0:T(8,128)S(1)}, f32[256,512]{1,0:T(8,128)S(1)}) custom-call(f32[4,128,512]{2,1,0:T(8,128)} %cov.5, f32[4,128,512]{2,1,0:T(8,128)} %prec.5, f32[1,512]{1,0:T(1,128)S(1)} %get-tuple-element.35.after.first.refs_0_), custom_call_target="tpu_custom_call" | custom-call | tf_op jit(solution)/shard_map/near/pallas_call | solution.py:366
  6.2 0.5 %collective-permute-start.5 = (f32[256,512]{1,0:T(8,128)S(1)}, f32[256,512]{1,0:T(8,128)S(1)}, u32[]{:S(2)}, u32[]{:S(2)}) collective-permute-start(f32[256,512]{1,0:T(8,128)S(1)} %get-tuple-element.41), channel_id=1, source_target_pairs={{0,1},{1,0},{2,3},{3,2},{4,5},{5,4},{6,7},{7,6},{8,9},{9,8},{10,11... | collective-permute-start | bytes 1572872 | tf_op jit(solution)/shard_map/ppermute | solution.py:360
  6.8 1.4 %collective-permute-done.after.refs_0_ = f32[64,512]{1,0:T(8,128)S(1)} collective-permute-done((f32[64,512]{1,0:T(8,128)S(1)}, f32[64,512]{1,0:T(8,128)S(1)}, u32[]{:S(2)}, u32[]{:S(2)}) %collective-permute-start) | collective-permute-done | bytes 131104 | tf_op jit(solution)/shard_map/ppermute | solution.py:360
  8.1 1.8 %collective-permute-start.2 = (f32[64,512]{1,0:T(8,128)S(1)}, f32[64,512]{1,0:T(8,128)S(1)}, u32[]{:S(2)}, u32[]{:S(2)}) collective-permute-start(f32[64,512]{1,0:T(8,128)S(1)} %collective-permute-done.after.refs_0_), channel_id=1, source_target_pairs={{0,4},{1,5},{2,6},{3,7},{4,0},{5,1},{6,2},{7,3},{8,12},{9,13},{10,... | collective-permute-start | bytes 393224 | tf_op jit(solution)/shard_map/ppermute | solution.py:360
  9.9 1.6 %own.1 = (f32[4,128,512]{2,1,0:T(8,128)S(1)}, f32[128,512]{1,0:T(8,128)S(1)}, f32[4,512]{1,0:T(4,128)S(1)}) custom-call(f32[4,128,512]{2,1,0:T(8,128)} %cov.5, f32[4,128,512]{2,1,0:T(8,128)} %prec.5, f32[128,512]{1,0:T(8,128)} %trans.3, f32[4,512]{1,0:T(4,128)} %means.1, f32[64,512]{1,0:T(8,128)S(1)} %collective-permute-done.after.refs_0_), custom_call_target="tpu_custom_call" | custom-call | tf_op jit(solution)/shard_map/own/pallas_call | solution.py:366
  11.5 1.6 %collective-permute-done.2.refs_1_ = f32[64,512]{1,0:T(8,128)S(1)} collective-permute-done((f32[64,512]{1,0:T(8,128)S(1)}, f32[64,512]{1,0:T(8,128)S(1)}, u32[]{:S(2)}, u32[]{:S(2)}) %collective-permute-start.2) | collective-permute-done | bytes 131104 | tf_op jit(solution)/shard_map/ppermute | solution.py:360
  13.1 0.6 %join.1.joined = f32[1,128,512]{2,1,0:T(8,128)S(1)} custom-call(f32[128,512]{1,0:T(8,128)S(1)} %get-tuple-element.39.after.trans, f32[64,512]{1,0:T(8,128)S(1)} %collective-permute-done.after.refs_0_, f32[64,512]{1,0:T(8,128)S(1)} %collective-permute-done.2.refs_1_), custom_call_target="tpu_custom_call" | custom-call | tf_op jit(solution)/shard_map/join/pallas_call | solution.py:366
  13.8 2.0 %collective-permute-start.7 = (f32[4,72,128]{2,1,0:T(8,128)S(1)}, f32[4,72,128]{2,1,0:T(8,128)S(1)}, u32[]{:S(2)}, u32[]{:S(2)}) collective-permute-start(f32[4,72,128]{2,1,0:T(8,128)S(1)} %get-tuple-element.53), channel_id=1, source_target_pairs={{0,3},{1,2},{2,1},{3,0},{4,7},{5,6},{6,5},{7,4},{8,11},{9,10},{10,... | collective-permute-start | bytes 442376 | tf_op jit(solution)/shard_map/ppermute | solution.py:360
  15.8 2.9 %early.1 = (f32[16,512]{1,0:T(8,128)S(1)}, bf16[2,256,512]{2,1,0:T(8,128)(2,1)S(1)}, bf16[2,2,256,512]{3,2,1,0:T(8,128)(2,1)S(1)}, f32[2,256,256]{2,1,0:T(8,128)...) custom-call(f32[4,128,512]{2,1,0:T(8,128)S(1)} %get-tuple-element.37.own, ...), custom_call_target="tpu_custom_call" | custom-call | tf_op jit(solution)/shard_map/early/pallas_call | solution.py:366
  19.0 2.5 %middle.1 = (f32[512,512]{1,0:T(8,128)S(1)}, f32[512,512]{1,0:T(8,128)S(1)}, f32[2,512,128]{2,1,0:T(8,128)S(1)}, f32[2,128,512]{2,1,0:T(8,128)S(1)}) custom-call(bf16[2,256,512]{2,1,0:T(8,128)(2,1)S(1)} %get-tuple-element.43.a_far, bf16[2,2,256,512]{3,2,1,0:T(8,128)(2,1)S(1)} %get-tuple-element.44.l_known, f32[2,256,256]{2,1,0:T(8,128)S(1)} %get-tuple-element.45.c_known, ...), custom_call_target="tpu_custom_call" | custom-call | tf_op jit(solution)/shard_map/middle/pallas_call | solution.py:366
  21.6 1.2 %late.1 = (f32[512,512]{1,0:T(8,128)S(1)}, f32[512,512]{1,0:T(8,128)S(1)}, f32[1,512]{1,0:T(1,128)S(1)}) custom-call(f32[1,512]{1,0:T(1,128)S(1)} %get-tuple-element.35.after.first.refs_0_, f32[16,512]{1,0:T(8,128)S(1)} %get-tuple-element.42.info, bf16[2,256,512]{2,1,0:T(8,128)(2,1)S(1)} %get-tuple-element.43.a_far, ...), custom_call_target="tpu_custom_call", output_to_operand_aliasing={{0}: (3, {}), {1}: (4, {})} | custom-call | tf_op jit(solution)/shard_map/late/pallas_call | solution.py:366
  22.8 1.0 %pair.1.early.refs_12_ = f32[520,512]{1,0:T(8,128)S(1)} custom-call(f32[16,512]{1,0:T(8,128)S(1)} %get-tuple-element.42.info, f32[512,512]{1,0:T(8,128)S(1)} %get-tuple-element.55.ga, f32[512,512]{1,0:T(8,128)S(1)} %get-tuple-element.60.gb.refs_13_), custom_call_target="tpu_custom_call" | custom-call | tf_op jit(solution)/shard_map/pair/pallas_call | solution.py:366
  23.9 0.4 collective-permute-start.10
  24.4 0.3 two.1
  24.8 1.9 %collective-permute-done.9.x.refs_1_ = f32[1,512]{1,0:T(1,128)S(1)} collective-permute-done((f32[1,512]{1,0:T(1,128)S(1)}, f32[1,512]{1,0:T(1,128)S(1)}, u32[]{:S(2)}, u32[]{:S(2)}) %collective-permute-start.9) | collective-permute-done | bytes 2080 | tf_op jit(solution)/shard_map/ppermute | solution.py:481
  26.7 0.3 pair_hop.1
  27.0 0.4 collective-permute-start.11
  27.4 1.0 %block.1 = (f32[512,512]{1,0:T(8,128)S(1)}, f32[8,512]{1,0:T(8,128)S(1)}) custom-call(f32[520,512]{1,0:T(8,128)S(1)} %collective-permute-done.10.late.refs_10_, f32[520,512]{1,0:T(8,128)S(1)} %pair.1.early.refs_12_), custom_call_target="tpu_custom_call" | custom-call | tf_op jit(solution)/shard_map/block/pallas_call | solution.py:366
  28.7 1.0 %collective-permute-done.12.x.refs_3_ = f32[1,512]{1,0:T(1,128)S(1)} collective-permute-done((f32[1,512]{1,0:T(1,128)S(1)}, f32[1,512]{1,0:T(1,128)S(1)}, u32[]{:S(2)}, u32[]{:S(2)}) %collective-permute-start.12) | collective-permute-done | bytes 2080 | tf_op jit(solution)/shard_map/ppermute | solution.py:481
  30.1 0.4 collective-permute-start.13
  30.5 1.9 %collective-permute-done.13.x.refs_4_ = f32[1,512]{1,0:T(1,128)S(1)} collective-permute-done((f32[1,512]{1,0:T(1,128)S(1)}, f32[1,512]{1,0:T(1,128)S(1)}, u32[]{:S(2)}, u32[]{:S(2)}) %collective-permute-start.13) | collective-permute-done | bytes 2080 | tf_op jit(solution)/shard_map/ppermute | solution.py:481
  32.8 1.0 %collective-permute-done.14.x.refs_5_ = f32[1,512]{1,0:T(1,128)S(1)} collective-permute-done((f32[1,512]{1,0:T(1,128)S(1)}, f32[1,512]{1,0:T(1,128)S(1)}, u32[]{:S(2)}, u32[]{:S(2)}) %collective-permute-start.14) | collective-permute-done | bytes 2080 | tf_op jit(solution)/shard_map/ppermute | solution.py:481
  34.2 1.0 %collective-permute-done.15.x.refs_6_ = f32[1,512]{1,0:T(1,128)S(1)} collective-permute-done((f32[1,512]{1,0:T(1,128)S(1)}, f32[1,512]{1,0:T(1,128)S(1)}, u32[]{:S(2)}, u32[]{:S(2)}) %collective-permute-start.15) | collective-permute-done | bytes 2080 | tf_op jit(solution)/shard_map/ppermute | solution.py:481
  35.3 1.2 %collective-permute-start.16 = (f32[1,512]{1,0:T(1,128)S(1)}, f32[1,512]{1,0:T(1,128)S(1)}, u32[]{:S(2)}, u32[]{:S(2)}) collective-permute-start(f32[1,512]{1,0:T(1,128)S(1)} %hop.9), channel_id=1, source_target_pairs={{0,2},{1,5},{2,3},{3,0},{4,6},{5,1},{6,7},{7,4},{8,9},{9,8},{10,11... | collective-permute-start | bytes 6152 | tf_op jit(solution)/shard_map/ppermute | solution.py:481
  36.5 1.9 %collective-permute-done.16.refs_7_ = f32[1,512]{1,0:T(1,128)S(1)} collective-permute-done((f32[1,512]{1,0:T(1,128)S(1)}, f32[1,512]{1,0:T(1,128)S(1)}, u32[]{:S(2)}, u32[]{:S(2)}) %collective-permute-start.16) | collective-permute-done | bytes 2080 | tf_op jit(solution)/shard_map/ppermute | solution.py:481
  38.4 0.4 last.1
  38.8 1.7 %collective-permute-start.18 = (f32[4,128]{1,0:T(4,128)S(1)}, f32[4,128]{1,0:T(4,128)S(1)}, u32[]{:S(2)}, u32[]{:S(2)}) collective-permute-start(f32[4,128]{1,0:T(4,128)S(1)} %get-tuple-element.62), channel_id=1, source_target_pairs={{0,2},{1,3},{2,0},{3,1},{4,6},{5,7},{6,4},{7,5},{8,10},{9,11},{10,... | collective-permute-start | bytes 6152 | tf_op jit(solution)/shard_map/ppermute | solution.py:360
  40.6 4.2 %collective-permute-start.19 = (f32[4,128]{1,0:T(4,128)S(1)}, f32[4,128]{1,0:T(4,128)S(1)}, u32[]{:S(2)}, u32[]{:S(2)}) collective-permute-start(f32[4,128]{1,0:T(4,128)S(1)} %get-tuple-element.63), channel_id=1, source_target_pairs={{0,3},{1,2},{2,0},{3,1},{4,7},{5,6},{6,4},{7,5},{8,11},{9,10},{10,... | collective-permute-start | bytes 6152 | tf_op jit(solution)/shard_map/ppermute | solution.py:506
  44.8 1.3 %collective-permute-done.19.refs_2_ = f32[4,128]{1,0:T(4,128)S(1)} collective-permute-done((f32[4,128]{1,0:T(4,128)S(1)}, f32[4,128]{1,0:T(4,128)S(1)}, u32[]{:S(2)}, u32[]{:S(2)}) %collective-permute-start.19) | collective-permute-done | bytes 2080 | tf_op jit(solution)/shard_map/ppermute | solution.py:506
  46.1 0.6 %out.1 = f32[4,128]{1,0:T(4,128)} custom-call(f32[4,128]{1,0:T(4,128)S(1)} %get-tuple-element.61.refs_0_, f32[4,128]{1,0:T(4,128)S(1)} %collective-permute-done.18.refs_1_, f32[4,128]{1,0:T(4,128)S(1)} %collective-permute-done.19.refs_2_, f32[4,128]{1,0:T(4,128)S(1)} %collective-permute-done.20.refs_3_), custom_call_target="tpu_custom_call" | custom-call | tf_op jit(solution)/shard_map/out/pallas_call | solution.py:366
  (30 shorter events, 2.5 us)
Async XLA Ops:
  1.6 5.1 %copy-start = (f32[128,512]{1,0:T(8,128)S(1)}, f32[128,512]{1,0:T(8,128)}, u32[]{:S(2)}) copy-start(f32[128,512]{1,0:T(8,128)} %trans.3) | copy-start | bytes 786436
  1.6 6.5 %collective-permute-start = (f32[64,512]{1,0:T(8,128)S(1)}, f32[64,512]{1,0:T(8,128)S(1)}, u32[]{:S(2)}, u32[]{:S(2)}) collective-permute-start(f32[64,512]{1,0:T(8,128)S(1)} %get-tuple-element.36), channel_id=1, source_target_pairs={{0,2},{1,3},{2,0},{3,1},{4,6},{5,7},{6,4},{7,5},{8,10},{9,11},{10,... | collective-permute-start | bytes 393224 | tf_op jit(solution)/shard_map/ppermute | solution.py:360
  6.1 9.7 %collective-permute-start.4 = (f32[256,512]{1,0:T(8,128)S(1)}, f32[256,512]{1,0:T(8,128)S(1)}, u32[]{:S(2)}, u32[]{:S(2)}) collective-permute-start(f32[256,512]{1,0:T(8,128)S(1)} %get-tuple-element.40), channel_id=1, source_target_pairs={{0,1},{1,0},{2,3},{3,2},{4,5},{5,4},{6,7},{7,6},{8,9},{9,8},{10,11... | collective-permute-start | bytes 1572872 | tf_op jit(solution)/shard_map/ppermute | solution.py:360
  6.2 9.6 %collective-permute-start.5 = (f32[256,512]{1,0:T(8,128)S(1)}, f32[256,512]{1,0:T(8,128)S(1)}, u32[]{:S(2)}, u32[]{:S(2)}) collective-permute-start(f32[256,512]{1,0:T(8,128)S(1)} %get-tuple-element.41), channel_id=1, source_target_pairs={{0,1},{1,0},{2,3},{3,2},{4,5},{5,4},{6,7},{7,6},{8,9},{9,8},{10,11... | collective-permute-start | bytes 1572872 | tf_op jit(solution)/shard_map/ppermute | solution.py:360
  6.7 12.3 %collective-permute-start.6 = (f32[4,200,128]{2,1,0:T(8,128)S(1)}, f32[4,200,128]{2,1,0:T(8,128)S(1)}, u32[]{:S(2)}, u32[]{:S(2)}) collective-permute-start(f32[4,200,128]{2,1,0:T(8,128)S(1)} %get-tuple-element.48), channel_id=1, source_target_pairs={{0,2},{1,3},{2,0},{3,1},{4,6},{5,7},{6,4},{7,5},{8,10},{9,11},{10,... | collective-permute-start | bytes 1228808 | tf_op jit(solution)/shard_map/ppermute | solution.py:360
  6.7 7.1 %collective-permute-start.1 = (f32[128,512]{1,0:T(8,128)S(1)}, f32[128,512]{1,0:T(8,128)S(1)}, u32[]{:S(2)}, u32[]{:S(2)}) collective-permute-start(f32[128,512]{1,0:T(8,128)S(1)} %copy-done), channel_id=1, source_target_pairs={{0,1},{1,0},{2,3},{3,2},{4,5},{5,4},{6,7},{7,6},{8,9},{9,8},{10,11... | collective-permute-start | bytes 786440 | tf_op jit(solution)/shard_map/ppermute | solution.py:360
  8.1 5.0 %collective-permute-start.2 = (f32[64,512]{1,0:T(8,128)S(1)}, f32[64,512]{1,0:T(8,128)S(1)}, u32[]{:S(2)}, u32[]{:S(2)}) collective-permute-start(f32[64,512]{1,0:T(8,128)S(1)} %collective-permute-done.after.refs_0_), channel_id=1, source_target_pairs={{0,4},{1,5},{2,6},{3,7},{4,0},{5,1},{6,2},{7,3},{8,12},{9,13},{10,... | collective-permute-start | bytes 393224 | tf_op jit(solution)/shard_map/ppermute | solution.py:360
  13.7 2.1 %collective-permute-start.3 = (f32[1,128,512]{2,1,0:T(8,128)S(1)}, f32[1,128,512]{2,1,0:T(8,128)S(1)}, u32[]{:S(2)}, u32[]{:S(2)}) collective-permute-start(f32[1,128,512]{2,1,0:T(8,128)S(1)} %join.1.joined), channel_id=1, source_target_pairs={{0,1},{1,0},{2,3},{3,2},{4,5},{5,4},{6,7},{7,6},{8,9},{9,8},{10,11... | collective-permute-start | bytes 786440 | tf_op jit(solution)/shard_map/ppermute | solution.py:360
  13.8 7.8 %collective-permute-start.7 = (f32[4,72,128]{2,1,0:T(8,128)S(1)}, f32[4,72,128]{2,1,0:T(8,128)S(1)}, u32[]{:S(2)}, u32[]{:S(2)}) collective-permute-start(f32[4,72,128]{2,1,0:T(8,128)S(1)} %get-tuple-element.53), channel_id=1, source_target_pairs={{0,3},{1,2},{2,1},{3,0},{4,7},{5,6},{6,5},{7,4},{8,11},{9,10},{10,... | collective-permute-start | bytes 442376 | tf_op jit(solution)/shard_map/ppermute | solution.py:360
  22.7 1.2 %collective-permute-start.8 = (f32[1,512]{1,0:T(1,128)S(1)}, f32[1,512]{1,0:T(1,128)S(1)}, u32[]{:S(2)}, u32[]{:S(2)}) collective-permute-start(f32[1,512]{1,0:T(1,128)S(1)} %get-tuple-element.54), channel_id=1, source_target_pairs={{0,1},{1,0},{2,3},{3,2},{4,5},{5,4},{6,7},{7,6},{8,9},{9,8},{10,11... | collective-permute-start | bytes 6152 | tf_op jit(solution)/shard_map/ppermute | solution.py:360
  23.9 2.7 %collective-permute-start.10 = (f32[520,512]{1,0:T(8,128)S(1)}, f32[520,512]{1,0:T(8,128)S(1)}, u32[]{:S(2)}, u32[]{:S(2)}) collective-permute-start(f32[520,512]{1,0:T(8,128)S(1)} %pair.1.early.refs_12_), channel_id=1, source_target_pairs={{0,1},{1,0},{2,3},{3,2},{4,5},{5,4},{6,7},{7,6},{8,9},{9,8},{10,11... | collective-permute-start | bytes 3194888 | tf_op jit(solution)/shard_map/ppermute | solution.py:360
  24.7 2.0 %collective-permute-start.9 = (f32[1,512]{1,0:T(1,128)S(1)}, f32[1,512]{1,0:T(1,128)S(1)}, u32[]{:S(2)}, u32[]{:S(2)}) collective-permute-start(f32[1,512]{1,0:T(1,128)S(1)} %two.1), channel_id=1, source_target_pairs={{0,1},{1,0},{2,3},{3,2},{4,5},{5,4},{6,7},{7,6},{8,9},{9,8},{10,11... | collective-permute-start | bytes 6152 | tf_op jit(solution)/shard_map/ppermute | solution.py:481
  27.0 1.4 %collective-permute-start.11 = (f32[1,512]{1,0:T(1,128)S(1)}, f32[1,512]{1,0:T(1,128)S(1)}, u32[]{:S(2)}, u32[]{:S(2)}) collective-permute-start(f32[1,512]{1,0:T(1,128)S(1)} %pair_hop.1), channel_id=1, source_target_pairs={{0,1},{1,0},{2,3},{3,2},{4,5},{5,4},{6,7},{7,6},{8,9},{9,8},{10,11... | collective-permute-start | bytes 6152 | tf_op jit(solution)/shard_map/ppermute | solution.py:481
  28.6 1.2 %collective-permute-start.12 = (f32[1,512]{1,0:T(1,128)S(1)}, f32[1,512]{1,0:T(1,128)S(1)}, u32[]{:S(2)}, u32[]{:S(2)}) collective-permute-start(f32[1,512]{1,0:T(1,128)S(1)} %hop.5), channel_id=1, source_target_pairs={{0,1},{1,0},{2,3},{3,2},{4,5},{5,4},{6,7},{7,6},{8,9},{9,8},{10,11... | collective-permute-start | bytes 6152 | tf_op jit(solution)/shard_map/ppermute | solution.py:481
  29.7 8.7 %collective-permute-start.17 = (f32[512,512]{1,0:T(8,128)S(1)}, f32[512,512]{1,0:T(8,128)S(1)}, u32[]{:S(2)}, u32[]{:S(2)}) collective-permute-start(f32[512,512]{1,0:T(8,128)S(1)} %get-tuple-element.60.gb.refs_13_), channel_id=1, source_target_pairs={{0,1},{1,0},{2,3},{3,2},{4,5},{5,4},{6,7},{7,6},{8,9},{9,8},{10,11... | collective-permute-start | bytes 3145736 | tf_op jit(solution)/shard_map/ppermute | solution.py:360
  30.1 2.3 %collective-permute-start.13 = (f32[1,512]{1,0:T(1,128)S(1)}, f32[1,512]{1,0:T(1,128)S(1)}, u32[]{:S(2)}, u32[]{:S(2)}) collective-permute-start(f32[1,512]{1,0:T(1,128)S(1)} %hop.6), channel_id=1, source_target_pairs={{0,1},{1,0},{2,3},{3,2},{4,5},{5,4},{6,7},{7,6},{8,9},{9,8},{10,11... | collective-permute-start | bytes 6152 | tf_op jit(solution)/shard_map/ppermute | solution.py:481
  32.6 1.2 %collective-permute-start.14 = (f32[1,512]{1,0:T(1,128)S(1)}, f32[1,512]{1,0:T(1,128)S(1)}, u32[]{:S(2)}, u32[]{:S(2)}) collective-permute-start(f32[1,512]{1,0:T(1,128)S(1)} %hop.7), channel_id=1, source_target_pairs={{0,1},{1,0},{2,3},{3,2},{4,5},{5,4},{6,7},{7,6},{8,10},{9,13},{10,... | collective-permute-start | bytes 6152 | tf_op jit(solution)/shard_map/ppermute | solution.py:481
  34.0 1.2 %collective-permute-start.15 = (f32[1,512]{1,0:T(1,128)S(1)}, f32[1,512]{1,0:T(1,128)S(1)}, u32[]{:S(2)}, u32[]{:S(2)}) collective-permute-start(f32[1,512]{1,0:T(1,128)S(1)} %hop.8), channel_id=1, source_target_pairs={{0,1},{1,0},{2,3},{3,2},{4,6},{5,9},{6,7},{7,4},{8,10},{9,5},{10,1... | collective-permute-start | bytes 6152 | tf_op jit(solution)/shard_map/ppermute | solution.py:481
  35.3 3.1 %collective-permute-start.16 = (f32[1,512]{1,0:T(1,128)S(1)}, f32[1,512]{1,0:T(1,128)S(1)}, u32[]{:S(2)}, u32[]{:S(2)}) collective-permute-start(f32[1,512]{1,0:T(1,128)S(1)} %hop.9), channel_id=1, source_target_pairs={{0,2},{1,5},{2,3},{3,0},{4,6},{5,1},{6,7},{7,4},{8,9},{9,8},{10,11... | collective-permute-start | bytes 6152 | tf_op jit(solution)/shard_map/ppermute | solution.py:481
  38.8 6.0 %collective-permute-start.18 = (f32[4,128]{1,0:T(4,128)S(1)}, f32[4,128]{1,0:T(4,128)S(1)}, u32[]{:S(2)}, u32[]{:S(2)}) collective-permute-start(f32[4,128]{1,0:T(4,128)S(1)} %get-tuple-element.62), channel_id=1, source_target_pairs={{0,2},{1,3},{2,0},{3,1},{4,6},{5,7},{6,4},{7,5},{8,10},{9,11},{10,... | collective-permute-start | bytes 6152 | tf_op jit(solution)/shard_map/ppermute | solution.py:360
  40.6 5.5 %collective-permute-start.19 = (f32[4,128]{1,0:T(4,128)S(1)}, f32[4,128]{1,0:T(4,128)S(1)}, u32[]{:S(2)}, u32[]{:S(2)}) collective-permute-start(f32[4,128]{1,0:T(4,128)S(1)} %get-tuple-element.63), channel_id=1, source_target_pairs={{0,3},{1,2},{2,0},{3,1},{4,7},{5,6},{6,4},{7,5},{8,11},{9,10},{10,... | collective-permute-start | bytes 6152 | tf_op jit(solution)/shard_map/ppermute | solution.py:506
  44.8 1.3 %collective-permute-start.20 = (f32[4,128]{1,0:T(4,128)S(1)}, f32[4,128]{1,0:T(4,128)S(1)}, u32[]{:S(2)}, u32[]{:S(2)}) collective-permute-start(f32[4,128]{1,0:T(4,128)S(1)} %get-tuple-element.64), channel_id=1, source_target_pairs={{0,1},{1,0},{2,3},{3,2},{4,5},{5,4},{6,7},{7,6},{8,9},{9,8},{10,11... | collective-permute-start | bytes 6152 | tf_op jit(solution)/shard_map/ppermute | solution.py:360
